TPU v7x, 32 devices: a whole 2x2x4 slice. The times are simulated.
32 devices in a mesh: groups: 2 (over y), lon: 16 (over z, x, core).
Axes of the slice: x: 2, y: 2, z: 4, core: 2. Of those that a mesh axis runs over, the one named last changes fastest.
Arguments:
- right_side: float32 [2048, 8192], P(('groups', 'lon')), parts along dimension 0, may hold values from -6 to 6
- texel_weight: bfloat16 [2048, 8192], P(('groups', 'lon')), parts along dimension 0, may hold values from 0.049804688 to 2
- seam_flags: int32 [64, 256], P(('groups', 'lon')), parts along dimension 0, may hold values 0 or 1
Outputs:
- fine_residual: float32 [2048, 8192], P(('groups', 'lon')), parts along dimension 0
- coarse_solution: float32 [512, 2048], P(('groups', 'lon')), parts along dimension 0
- coarse_residual: float32 [512, 2048], P(('groups', 'lon')), parts along dimension 0
There are 2 independent parts, one for each index of `groups`. A program takes and returns all parts, laid end to end along the dimension named above; each array names one. Nothing has to cross between parts.
Inputs may be any that keep to these rules, and one draw needn't show every extreme that they name: `seam_flags`: 1 marks a seam tile, 0 any other tile.
All inputs are finite; a program needn't handle non-finite values. No bound on the sum of `seam_flags` on one device may be relied on, other than what follows from the above.
Results may differ from a plain program's by a relative error of at most 0.0003.
Values sent between devices are 32-bit elements; how exact they have to be, the bound alone decides.
No kernel may reach another device: no remote copies, remote signals or barrier semaphores. Data moves between devices by JAX's collectives and lax.ppermute only.
A program may use at most 128 MiB of HBM per device.

v0:
```python
import jax
import jax.numpy as jnp
from jax import lax
from jax.sharding import PartitionSpec as P

TILE = 32


seam_scale = 0.1


def passed_along(shard, axis, by):
    size = lax.axis_size(axis)
    return lax.ppermute(shard, axis, [(i, (i + by) % size) for i in range(size)])


def padded(cells, sides, width):
    for axis, dim in sides:
        count = lax.axis_size(axis)
        head = lax.slice_in_dim(cells, 0, width, axis=dim)
        tail = lax.slice_in_dim(cells, cells.shape[dim] - width, cells.shape[dim], axis=dim)
        cells = jnp.concatenate(
            [
                lax.ppermute(tail, axis, [(i, (i + 1) % count) for i in range(count)]),
                cells,
                lax.ppermute(head, axis, [((i + 1) % count, i) for i in range(count)]),
            ],
            axis=dim,
        )
    return cells


def colour_mask(lon_count, lat_count, lon_start):
    lon_ids = lon_start + lax.iota(jnp.int32, lon_count)
    lat_ids = lax.iota(jnp.int32, lat_count)
    return (lon_ids[:, None] + lat_ids[None, :]) % 2 == 0


def take_even(values):
    lon_count, height = values.shape
    picker = (lax.iota(jnp.int32, 256)[:, None] == 2 * lax.iota(jnp.int32, 128)[None, :]).astype(
        jnp.float32
    )
    blocks = values.reshape(lon_count, height // 256, 256)
    picked = jnp.einsum(
        "cbk,km->cbm",
        blocks,
        picker,
        precision=lax.Precision.HIGHEST,
        preferred_element_type=jnp.float32,
    )
    return picked.reshape(lon_count, height // 2)


def pole_partner(field):
    return passed_along(jnp.stack([field[:, 0], field[:, -1]]), "lon", lax.axis_size("lon") // 2)


def lon_rim(field):
    return padded(field, (("lon", 0),), 1)


def sides_lon(field):
    height = field.shape[1]
    lat_ids = lax.iota(jnp.int32, height)[None, :]
    widened = lon_rim(field)
    partner = pole_partner(field)
    north = jnp.where(lat_ids == 0, partner[0][:, None], jnp.roll(field, 1, 1))
    south = jnp.where(lat_ids == height - 1, partner[1][:, None], jnp.roll(field, -1, 1))
    return (widened[:-2], widened[2:], north, south)


def relax_colour(field, parts, source, screen, update_mask):
    beside_all = parts[0] + parts[1] + (parts[2] + parts[3])
    return jnp.where(update_mask, (source + beside_all) / (4.0 + screen), field)


def residual_of(field, parts, source, screen):
    beside_all = parts[0] + parts[1] + (parts[2] + parts[3])
    return source - ((4.0 + screen) * field - beside_all)


def restrict(field):
    breadth, height = field.shape
    lat_ids = lax.iota(jnp.int32, height)[None, :]
    partner = pole_partner(field)
    north = jnp.where(lat_ids == 0, partner[0][:, None], jnp.roll(field, 1, 1))
    south = jnp.where(lat_ids == height - 1, partner[1][:, None], jnp.roll(field, -1, 1))
    twice = jnp.where(lat_ids == height - 2, partner[1][:, None], jnp.roll(field, -2, 1))
    lat_sum = north + 3.0 * field + 3.0 * south + twice
    widened = lon_rim(take_even(lat_sum))
    lon_sum = (
        widened[0:breadth:2]
        + 3.0 * widened[1 : breadth + 1 : 2]
        + 3.0 * widened[2 : breadth + 2 : 2]
        + widened[3 : breadth + 3 : 2]
    )
    return lon_sum / 16.0


def coarsen(screen):
    paired = take_even(screen + jnp.roll(screen, -1, 1))
    return paired[0::2] + paired[1::2]


def smooth(source, screen, sides_of, red_cells):
    black_cells = jnp.logical_not(red_cells)
    field = jnp.where(red_cells, source / (4.0 + screen), 0.0)
    field = relax_colour(field, sides_of(field), source, screen, black_cells)
    field = relax_colour(field, sides_of(field), source, screen, red_cells)
    field = relax_colour(field, sides_of(field), source, screen, black_cells)
    return field


def level_lon(source, screen):
    breadth = source.shape[0]
    red_cells = colour_mask(breadth, source.shape[1], lax.axis_index("lon") * breadth)
    field = smooth(source, screen, sides_lon, red_cells)
    misfit = residual_of(field, sides_lon(field), source, screen)
    return (field, misfit)


def body(right_side, texel_weight, seam_flags):
    tile_flags = jnp.repeat(jnp.repeat(seam_flags, TILE, 0), TILE, 1)
    screen = texel_weight.astype(jnp.float32) * jnp.where(tile_flags == 1, seam_scale, 1.0)
    source = right_side
    fine_residual = source
    for depth_level in range(2):
        field, misfit = level_lon(source, screen)
        if depth_level == 0:
            fine_residual = misfit
        source = restrict(misfit)
        screen = coarsen(screen)
    field, misfit = level_lon(source, screen)
    return (fine_residual, field, misfit)


def solution(mesh):
    return jax.shard_map(
        body,
        mesh=mesh,
        in_specs=(
            P(("groups", "lon"), None),
            P(("groups", "lon"), None),
            P(("groups", "lon"), None),
        ),
        out_specs=(
            P(("groups", "lon"), None),
            P(("groups", "lon"), None),
            P(("groups", "lon"), None),
        ),
        check_vma=False,
    )
```

profile of v0, /device:TPU:0, one launch (start us, length us, event | category | flops | bytes accessed | tf_op | source)
XLA Modules:
  0.0 305.2 jit_solution(6331627781852852409)
XLA Ops:
  1.4 2.0 copy.78
  3.8 2.3 slice.742
  6.0 3.8 %copy.100 = f32[64,8192]{0,1:T(8,128)} copy(f32[64,8192]{1,0:T(8,128)} %param.3) | data formatting | bytes 4194304 | tf_op args[0]
  9.9 8.4 %maximum_add_fusion = (f32[64,8192]{0,1:T(8,128)}, f32[64,8192]{0,1:T(8,128)S(1)}) fusion(f32[64,1]{0,1:T(1,128)S(1)} %slice.743, f32[64,8191]{0,1:T(8,128)} %slice.742, bf16[64,8192]{0,1:T(8,128)(2,1)S(1)} %copy.78, f32[64,256]{0,1:T(8,128)S(1)} %copy.79, f32[64,8192]{0,1:T(8,128)} %copy.100, s32[64]{0:T(128)S(1)} %iota_add_fusion.2), kind=kLoop, calls=%fused_computation.51 | loop fusion | flops 10485760 | bytes 9502976 | tf_op jit(solution)/shard_map/add | solution.py:102
  18.3 4.1 %collective-permute-start.2 = (f32[2,64]{1,0:T(2,128)S(1)}, f32[2,64]{1,0:T(2,128)S(1)}, u32[]{:S(2)}, u32[]{:S(2)}) collective-permute-start(f32[2,64]{1,0:T(2,128)S(1)} %pad_maximum_fusion.26), channel_id=1, source_target_pairs={{0,8},{1,9},{2,10},{3,11},{4,12},{5,13},{6,14},{7,15},{8,0},{9,1},... | collective-permute-start | bytes 1544 | tf_op jit(solution)/shard_map/ppermute | solution.py:14
  22.4 4.6 %fusion.114 = (f32[1,8192]{0,1:T(8,128)}, f32[1,8192]{0,1:T(8,128)}) fusion(f32[64,8192]{0,1:T(8,128)S(1)} %get-tuple-element.81), kind=kLoop, calls=%fused_computation.277 | loop fusion | bytes 131072 | tf_op jit(solution)/shard_map/slice | solution.py:21
  27.0 2.8 copy.83
  29.8 1.5 collective-permute-start.1
  31.3 2.8 copy.81
  34.8 7.2 %fusion.113 = (f32[64,8191]{0,1:T(8,128)}, f32[64,8191]{0,1:T(8,128)}) fusion(f32[64,8192]{0,1:T(8,128)} %copy-done.2), kind=kLoop, calls=%fused_computation.276 | loop fusion | bytes 8387584 | tf_op jit(solution)/shard_map/jit(_roll_static)/slice | solution.py:69
  42.0 5.6 %convolution_bitcast_fusion = f32[32,8,8,128]{3,2,1,0:T(8,128)S(1)} fusion(f32[64,32,256]{0,2,1:T(8,128)} %bitcast.153, s32[128]{0:T(128)S(1)} %iota_multiply_fusion), kind=kOutput, calls=%fused_computation.57 | convolution fusion | flops 805339136 | bytes 3146240 | tf_op jit(solution)/shard_map/cbk,km->cbm/dot_general | solution.py:45
  47.7 1.5 slice.609
  49.2 1.5 slice.608
  50.7 2.7 copy.82
  53.4 2.7 copy.84
  56.1 14.0 %fusion.20 = f32[64,8192]{0,1:T(8,128)S(1)} fusion(f32[64,8192]{0,1:T(8,128)} %copy-done.2, f32[64,8192]{0,1:T(8,128)} %copy.100, f32[1,8192]{0,1:T(8,128)} %copy.84, f32[1,8192]{0,1:T(8,128)} %copy.82, f32[64,8191]{0,1:T(8,128)} %get-tuple-element.77, f32[64,1]{0,1:T(1,128)S(1)} %get-tuple-element.74, f32[64,1]{0,1:T(1,128)S(1)} %get-tuple-element.75, ...), kind=kLoop, calls=%fused_computation.30 | loop fusion | flops 14680064 | bytes 11682560 | tf_op jit(solution)/shard_map/jit(_where)/select_n | solution.py:75
  70.2 4.2 %fusion.111 = (f32[64,8191]{0,1:T(8,128)}, f32[64,8191]{0,1:T(8,128)}) fusion(f32[64,8192]{0,1:T(8,128)S(1)} %fusion.20), kind=kLoop, calls=%fused_computation.274 | loop fusion | bytes 8387584 | tf_op jit(solution)/shard_map/jit(_roll_static)/slice | solution.py:69
  74.4 1.8 collective-permute-start.5
  76.2 4.6 %fusion.112 = (f32[1,8192]{0,1:T(8,128)}, f32[1,8192]{0,1:T(8,128)}) fusion(f32[64,8192]{0,1:T(8,128)S(1)} %fusion.20), kind=kLoop, calls=%fused_computation.275 | loop fusion | bytes 131072 | tf_op jit(solution)/shard_map/slice | solution.py:21
  80.8 2.8 copy.86
  83.6 2.8 copy.88
  86.5 3.3 %collective-permute-start.4 = (f32[1,8192]{1,0:T(1,128)S(1)}, f32[1,8192]{1,0:T(1,128)S(1)}, u32[]{:S(2)}, u32[]{:S(2)}) collective-permute-start(f32[1,8192]{1,0:T(1,128)S(1)} %copy.88), channel_id=1, source_target_pairs={{1,0},{2,1},{3,2},{4,3},{5,4},{6,5},{7,6},{8,7},{9,8},{10,9},{11,1... | collective-permute-start | bytes 98312 | tf_op jit(solution)/shard_map/ppermute | solution.py:26
  89.9 6.0 %collective-permute-done.3 = f32[1,8192]{1,0:T(1,128)S(1)} collective-permute-done((f32[1,8192]{1,0:T(1,128)S(1)}, f32[1,8192]{1,0:T(1,128)S(1)}, u32[]{:S(2)}, u32[]{:S(2)}) %collective-permute-start.3) | collective-permute-done | bytes 32800 | tf_op jit(solution)/shard_map/ppermute | solution.py:24
  95.9 2.7 copy.87
  98.6 2.7 copy.89
  101.3 14.0 %fusion.15 = f32[64,8192]{0,1:T(8,128)S(1)} fusion(f32[64,8192]{0,1:T(8,128)} %copy-done.5, f32[64,8192]{0,1:T(8,128)} %copy.100, f32[1,8192]{0,1:T(8,128)} %copy.89, f32[1,8192]{0,1:T(8,128)} %copy.87, f32[64,8191]{0,1:T(8,128)} %get-tuple-element.69, f32[64,1]{0,1:T(1,128)S(1)} %get-tuple-element.66, f32[64,1]{0,1:T(1,128)S(1)} %get-tuple-element.67, ...), kind=kLoop, calls=%fused_computation.23 | loop fusion | flops 14680064 | bytes 11682560 | tf_op jit(solution)/shard_map/jit(_where)/select_n | solution.py:75
  115.4 4.2 %fusion.109 = (f32[64,8191]{0,1:T(8,128)}, f32[64,8191]{0,1:T(8,128)}) fusion(f32[64,8192]{0,1:T(8,128)S(1)} %fusion.15), kind=kLoop, calls=%fused_computation.272 | loop fusion | bytes 8387584 | tf_op jit(solution)/shard_map/jit(_roll_static)/slice | solution.py:69
  119.8 4.6 %fusion.110 = (f32[1,8192]{0,1:T(8,128)}, f32[1,8192]{0,1:T(8,128)}) fusion(f32[64,8192]{0,1:T(8,128)S(1)} %fusion.15), kind=kLoop, calls=%fused_computation.273 | loop fusion | bytes 131072 | tf_op jit(solution)/shard_map/slice | solution.py:21
  124.5 2.8 copy.91
  127.3 2.8 copy.93
  130.7 5.6 %collective-permute-done.6 = f32[1,8192]{1,0:T(1,128)S(1)} collective-permute-done((f32[1,8192]{1,0:T(1,128)S(1)}, f32[1,8192]{1,0:T(1,128)S(1)}, u32[]{:S(2)}, u32[]{:S(2)}) %collective-permute-start.6) | collective-permute-done | bytes 32800 | tf_op jit(solution)/shard_map/ppermute | solution.py:24
  136.3 2.7 copy.92
  139.0 2.7 copy.94
  141.7 14.0 %fusion.10 = f32[64,8192]{0,1:T(8,128)S(1)} fusion(f32[64,8192]{0,1:T(8,128)} %copy-done.4, f32[64,8192]{0,1:T(8,128)} %copy.100, f32[1,8192]{0,1:T(8,128)} %copy.94, f32[1,8192]{0,1:T(8,128)} %copy.92, f32[64,8191]{0,1:T(8,128)} %get-tuple-element.61, f32[64,1]{0,1:T(1,128)S(1)} %get-tuple-element.58, f32[64,1]{0,1:T(1,128)S(1)} %get-tuple-element.59, ...), kind=kLoop, calls=%fused_computation.16 | loop fusion | flops 14680064 | bytes 11682560 | tf_op jit(solution)/shard_map/jit(_where)/select_n | solution.py:75
  155.7 4.2 %fusion.107 = (f32[64,8191]{0,1:T(8,128)}, f32[64,8191]{0,1:T(8,128)}) fusion(f32[64,8192]{0,1:T(8,128)S(1)} %fusion.10), kind=kLoop, calls=%fused_computation.270 | loop fusion | bytes 8387584 | tf_op jit(solution)/shard_map/jit(_roll_static)/slice | solution.py:69
  160.9 4.6 %fusion.108 = (f32[1,8192]{0,1:T(8,128)}, f32[1,8192]{0,1:T(8,128)}) fusion(f32[64,8192]{0,1:T(8,128)S(1)} %fusion.10), kind=kLoop, calls=%fused_computation.271 | loop fusion | bytes 131072 | tf_op jit(solution)/shard_map/slice | solution.py:21
  165.6 2.8 copy.96
  168.4 2.8 copy.98
  172.0 5.6 %collective-permute-done.9 = f32[1,8192]{1,0:T(1,128)S(1)} collective-permute-done((f32[1,8192]{1,0:T(1,128)S(1)}, f32[1,8192]{1,0:T(1,128)S(1)}, u32[]{:S(2)}, u32[]{:S(2)}) %collective-permute-start.9) | collective-permute-done | bytes 32800 | tf_op jit(solution)/shard_map/ppermute | solution.py:24
  177.6 2.7 copy.97
  180.3 2.7 copy.99
  183.0 14.0 %fusion.5 = f32[64,8192]{0,1:T(8,128)S(1)} fusion(f32[64,8192]{0,1:T(8,128)} %copy.100, f32[1,8192]{0,1:T(8,128)} %copy.99, f32[64,8192]{0,1:T(8,128)} %copy-done.3, f32[1,8192]{0,1:T(8,128)} %copy.97, f32[64,8191]{0,1:T(8,128)} %get-tuple-element.53, f32[64,1]{0,1:T(1,128)S(1)} %get-tuple-element.50, f32[64,1]{0,1:T(1,128)S(1)} %get-tuple-element.51, ...), kind=kLoop, calls=%fused_computation.9 | loop fusion | flops 7864320 | bytes 11682304 | tf_op jit(solution)/shard_map/sub | solution.py:80
  197.3 4.2 %fusion.106 = (f32[64,8191]{0,1:T(8,128)}, f32[64,8191]{0,1:T(8,128)}) fusion(f32[64,8192]{0,1:T(8,128)S(1)} %fusion.5), kind=kLoop, calls=%fused_computation.269 | loop fusion | bytes 8387584 | tf_op jit(solution)/shard_map/jit(_roll_static)/slice | solution.py:88
  201.5 3.8 %copy.109 = f32[64,8192]{1,0:T(8,128)} copy(f32[64,8192]{0,1:T(8,128)} %copy-done) | data formatting | bytes 4194304
  205.3 2.6 slice.738
  210.0 9.7 %fusion.27 = f32[64,8192]{0,1:T(8,128)S(1)} fusion(f32[64,8191]{0,1:T(8,128)} %get-tuple-element.47, f32[64,1]{0,1:T(1,128)S(1)} %get-tuple-element.44, f32[64,1]{0,1:T(1,128)S(1)} %get-tuple-element.45, f32[64,8191]{0,1:T(8,128)S(1)} %copy-done.6, f32[64,2]{0,1:T(2,128)S(1)} %slice-done, f32[64,8190]{0,1:T(8,128)S(1)} %slice.738, ...), kind=kLoop, calls=%fused_computation.47 | loop fusion | flops 5767168 | bytes 10510848 | tf_op jit(solution)/shard_map/add | solution.py:90
  219.7 3.5 %fusion.100 = f32[64,32,128]{2,0,1:T(8,128)S(1)} fusion(f32[64,32,256]{0,2,1:T(8,128)S(1)} %bitcast.154, s32[128]{0:T(128)S(1)} %iota_multiply_fusion), kind=kOutput, calls=%fused_computation.177 | convolution fusion | flops 805339136 | bytes 3146240 | tf_op jit(solution)/shard_map/cbk,km->cbm/dot_general | solution.py:45
  223.3 4.4 %collective-permute-start.14 = (f32[1,4096]{1,0:T(1,128)S(1)}, f32[1,4096]{1,0:T(1,128)S(1)}, u32[]{:S(2)}, u32[]{:S(2)}) collective-permute-start(f32[1,4096]{1,0:T(1,128)S(1)} %get-tuple-element.83), channel_id=1, source_target_pairs={{1,0},{2,1},{3,2},{4,3},{5,4},{6,5},{7,6},{8,7},{9,8},{10,9},{11,1... | collective-permute-start | bytes 49160 | tf_op jit(solution)/shard_map/ppermute | solution.py:26
  227.8 1.5 slice.603
  230.1 1.5 slice.602
  231.6 1.6 divide_select_fusion.1
  234.5 4.4 %collective-permute-start.16 = (f32[1,4096]{1,0:T(1,128)S(1)}, f32[1,4096]{1,0:T(1,128)S(1)}, u32[]{:S(2)}, u32[]{:S(2)}) collective-permute-start(f32[1,4096]{1,0:T(1,128)S(1)} %get-tuple-element.113), channel_id=1, source_target_pairs={{1,0},{2,1},{3,2},{4,3},{5,4},{6,5},{7,6},{8,7},{9,8},{10,9},{11,1... | collective-permute-start | bytes 49160 | tf_op jit(solution)/shard_map/ppermute | solution.py:26
  239.0 1.4 collective-permute-done.15
  242.7 4.4 %collective-permute-start.19 = (f32[1,4096]{1,0:T(1,128)S(1)}, f32[1,4096]{1,0:T(1,128)S(1)}, u32[]{:S(2)}, u32[]{:S(2)}) collective-permute-start(f32[1,4096]{1,0:T(1,128)S(1)} %get-tuple-element.107), channel_id=1, source_target_pairs={{1,0},{2,1},{3,2},{4,3},{5,4},{6,5},{7,6},{8,7},{9,8},{10,9},{11,1... | collective-permute-start | bytes 49160 | tf_op jit(solution)/shard_map/ppermute | solution.py:26
  250.3 4.4 %collective-permute-start.22 = (f32[1,4096]{1,0:T(1,128)S(1)}, f32[1,4096]{1,0:T(1,128)S(1)}, u32[]{:S(2)}, u32[]{:S(2)}) collective-permute-start(f32[1,4096]{1,0:T(1,128)S(1)} %get-tuple-element.101), channel_id=1, source_target_pairs={{1,0},{2,1},{3,2},{4,3},{5,4},{6,5},{7,6},{8,7},{9,8},{10,9},{11,1... | collective-permute-start | bytes 49160 | tf_op jit(solution)/shard_map/ppermute | solution.py:26
  258.5 4.7 %collective-permute-start.25 = (f32[1,4096]{1,0:T(1,128)S(1)}, f32[1,4096]{1,0:T(1,128)S(1)}, u32[]{:S(2)}, u32[]{:S(2)}) collective-permute-start(f32[1,4096]{1,0:T(1,128)S(1)} %get-tuple-element.95), channel_id=1, source_target_pairs={{1,0},{2,1},{3,2},{4,3},{5,4},{6,5},{7,6},{8,7},{9,8},{10,9},{11,1... | collective-permute-start | bytes 49160 | tf_op jit(solution)/shard_map/ppermute | solution.py:26
  267.1 3.4 %collective-permute-done.27 = f32[2,32]{1,0:T(2,128)S(1)} collective-permute-done((f32[2,32]{1,0:T(2,128)S(1)}, f32[2,32]{1,0:T(2,128)S(1)}, u32[]{:S(2)}, u32[]{:S(2)}) %collective-permute-start.27) | collective-permute-done | bytes 288 | tf_op jit(solution)/shard_map/ppermute | solution.py:14
  271.3 4.4 %collective-permute-start.29 = (f32[1,2048]{1,0:T(1,128)S(1)}, f32[1,2048]{1,0:T(1,128)S(1)}, u32[]{:S(2)}, u32[]{:S(2)}) collective-permute-start(f32[1,2048]{1,0:T(1,128)S(1)} %get-tuple-element.115), channel_id=1, source_target_pairs={{1,0},{2,1},{3,2},{4,3},{5,4},{6,5},{7,6},{8,7},{9,8},{10,9},{11,1... | collective-permute-start | bytes 24584 | tf_op jit(solution)/shard_map/ppermute | solution.py:26
  277.9 4.5 %collective-permute-start.31 = (f32[1,2048]{1,0:T(1,128)S(1)}, f32[1,2048]{1,0:T(1,128)S(1)}, u32[]{:S(2)}, u32[]{:S(2)}) collective-permute-start(f32[1,2048]{1,0:T(1,128)S(1)} %get-tuple-element.139), channel_id=1, source_target_pairs={{1,0},{2,1},{3,2},{4,3},{5,4},{6,5},{7,6},{8,7},{9,8},{10,9},{11,1... | collective-permute-start | bytes 24584 | tf_op jit(solution)/shard_map/ppermute | solution.py:26
  284.3 1.7 collective-permute-start.35
  286.1 3.2 %collective-permute-start.34 = (f32[1,2048]{1,0:T(1,128)S(1)}, f32[1,2048]{1,0:T(1,128)S(1)}, u32[]{:S(2)}, u32[]{:S(2)}) collective-permute-start(f32[1,2048]{1,0:T(1,128)S(1)} %get-tuple-element.133), channel_id=1, source_target_pairs={{1,0},{2,1},{3,2},{4,3},{5,4},{6,5},{7,6},{8,7},{9,8},{10,9},{11,1... | collective-permute-start | bytes 24584 | tf_op jit(solution)/shard_map/ppermute | solution.py:26
  292.6 3.2 %collective-permute-start.37 = (f32[1,2048]{1,0:T(1,128)S(1)}, f32[1,2048]{1,0:T(1,128)S(1)}, u32[]{:S(2)}, u32[]{:S(2)}) collective-permute-start(f32[1,2048]{1,0:T(1,128)S(1)} %get-tuple-element.127), channel_id=1, source_target_pairs={{1,0},{2,1},{3,2},{4,3},{5,4},{6,5},{7,6},{8,7},{9,8},{10,9},{11,1... | collective-permute-start | bytes 24584 | tf_op jit(solution)/shard_map/ppermute | solution.py:26
  297.8 1.7 collective-permute-start.41
  299.5 3.2 %collective-permute-start.40 = (f32[1,2048]{1,0:T(1,128)S(1)}, f32[1,2048]{1,0:T(1,128)S(1)}, u32[]{:S(2)}, u32[]{:S(2)}) collective-permute-start(f32[1,2048]{1,0:T(1,128)S(1)} %get-tuple-element.121), channel_id=1, source_target_pairs={{1,0},{2,1},{3,2},{4,3},{5,4},{6,5},{7,6},{8,7},{9,8},{10,9},{11,1... | collective-permute-start | bytes 24584 | tf_op jit(solution)/shard_map/ppermute | solution.py:26
  (191 shorter events, 34.3 us)
Async XLA Ops:
  18.3 8.7 %copy-start.2 = (f32[64,8192]{0,1:T(8,128)}, f32[64,8192]{0,1:T(8,128)S(1)}, u32[]{:S(2)}) copy-start(f32[64,8192]{0,1:T(8,128)S(1)} %get-tuple-element.81) | copy-start | bytes 6291460
  18.3 32.3 %collective-permute-start.2 = (f32[2,64]{1,0:T(2,128)S(1)}, f32[2,64]{1,0:T(2,128)S(1)}, u32[]{:S(2)}, u32[]{:S(2)}) collective-permute-start(f32[2,64]{1,0:T(2,128)S(1)} %pad_maximum_fusion.26), channel_id=1, source_target_pairs={{0,8},{1,9},{2,10},{3,11},{4,12},{5,13},{6,14},{7,15},{8,0},{9,1},... | collective-permute-start | bytes 1544 | tf_op jit(solution)/shard_map/ppermute | solution.py:14
  29.8 23.5 %collective-permute-start.1 = (f32[1,8192]{1,0:T(1,128)S(1)}, f32[1,8192]{1,0:T(1,128)S(1)}, u32[]{:S(2)}, u32[]{:S(2)}) collective-permute-start(f32[1,8192]{1,0:T(1,128)S(1)} %copy.83), channel_id=1, source_target_pairs={{1,0},{2,1},{3,2},{4,3},{5,4},{6,5},{7,6},{8,7},{9,8},{10,9},{11,1... | collective-permute-start | bytes 98312 | tf_op jit(solution)/shard_map/ppermute | solution.py:26
  34.1 16.5 %collective-permute-start = (f32[1,8192]{1,0:T(1,128)S(1)}, f32[1,8192]{1,0:T(1,128)S(1)}, u32[]{:S(2)}, u32[]{:S(2)}) collective-permute-start(f32[1,8192]{1,0:T(1,128)S(1)} %copy.81), channel_id=1, source_target_pairs={{0,1},{1,2},{2,3},{3,4},{4,5},{5,6},{6,7},{7,8},{8,9},{9,10},{10,1... | collective-permute-start | bytes 98312 | tf_op jit(solution)/shard_map/ppermute | solution.py:24
  70.1 6.0 %copy-start.5 = (f32[64,8192]{0,1:T(8,128)}, f32[64,8192]{0,1:T(8,128)S(1)}, u32[]{:S(2)}) copy-start(f32[64,8192]{0,1:T(8,128)S(1)} %fusion.20) | copy-start | bytes 6291460
  74.4 15.5 %collective-permute-start.5 = (f32[2,64]{1,0:T(2,128)S(1)}, f32[2,64]{1,0:T(2,128)S(1)}, u32[]{:S(2)}, u32[]{:S(2)}) collective-permute-start(f32[2,64]{1,0:T(2,128)S(1)} %pad_maximum_fusion.27), channel_id=1, source_target_pairs={{0,8},{1,9},{2,10},{3,11},{4,12},{5,13},{6,14},{7,15},{8,0},{9,1},... | collective-permute-start | bytes 1544 | tf_op jit(solution)/shard_map/ppermute | solution.py:14
  86.5 12.2 %collective-permute-start.4 = (f32[1,8192]{1,0:T(1,128)S(1)}, f32[1,8192]{1,0:T(1,128)S(1)}, u32[]{:S(2)}, u32[]{:S(2)}) collective-permute-start(f32[1,8192]{1,0:T(1,128)S(1)} %copy.88), channel_id=1, source_target_pairs={{1,0},{2,1},{3,2},{4,3},{5,4},{6,5},{7,6},{8,7},{9,8},{10,9},{11,1... | collective-permute-start | bytes 98312 | tf_op jit(solution)/shard_map/ppermute | solution.py:26
  89.7 6.2 %collective-permute-start.3 = (f32[1,8192]{1,0:T(1,128)S(1)}, f32[1,8192]{1,0:T(1,128)S(1)}, u32[]{:S(2)}, u32[]{:S(2)}) collective-permute-start(f32[1,8192]{1,0:T(1,128)S(1)} %copy.86), channel_id=1, source_target_pairs={{0,1},{1,2},{2,3},{3,4},{4,5},{5,6},{6,7},{7,8},{8,9},{9,10},{10,1... | collective-permute-start | bytes 98312 | tf_op jit(solution)/shard_map/ppermute | solution.py:24
  115.3 4.5 %copy-start.4 = (f32[64,8192]{0,1:T(8,128)}, f32[64,8192]{0,1:T(8,128)S(1)}, u32[]{:S(2)}) copy-start(f32[64,8192]{0,1:T(8,128)S(1)} %fusion.15) | copy-start | bytes 6291460
  119.6 11.1 %collective-permute-start.8 = (f32[2,64]{1,0:T(2,128)S(1)}, f32[2,64]{1,0:T(2,128)S(1)}, u32[]{:S(2)}, u32[]{:S(2)}) collective-permute-start(f32[2,64]{1,0:T(2,128)S(1)} %pad_maximum_fusion.28), channel_id=1, source_target_pairs={{0,8},{1,9},{2,10},{3,11},{4,12},{5,13},{6,14},{7,15},{8,0},{9,1},... | collective-permute-start | bytes 1544 | tf_op jit(solution)/shard_map/ppermute | solution.py:14
  130.2 8.8 %collective-permute-start.7 = (f32[1,8192]{1,0:T(1,128)S(1)}, f32[1,8192]{1,0:T(1,128)S(1)}, u32[]{:S(2)}, u32[]{:S(2)}) collective-permute-start(f32[1,8192]{1,0:T(1,128)S(1)} %copy.93), channel_id=1, source_target_pairs={{1,0},{2,1},{3,2},{4,3},{5,4},{6,5},{7,6},{8,7},{9,8},{10,9},{11,1... | collective-permute-start | bytes 98312 | tf_op jit(solution)/shard_map/ppermute | solution.py:26
  130.2 6.1 %collective-permute-start.6 = (f32[1,8192]{1,0:T(1,128)S(1)}, f32[1,8192]{1,0:T(1,128)S(1)}, u32[]{:S(2)}, u32[]{:S(2)}) collective-permute-start(f32[1,8192]{1,0:T(1,128)S(1)} %copy.91), channel_id=1, source_target_pairs={{0,1},{1,2},{2,3},{3,4},{4,5},{5,6},{6,7},{7,8},{8,9},{9,10},{10,1... | collective-permute-start | bytes 98312 | tf_op jit(solution)/shard_map/ppermute | solution.py:24
  155.7 5.2 %copy-start.3 = (f32[64,8192]{0,1:T(8,128)}, f32[64,8192]{0,1:T(8,128)S(1)}, u32[]{:S(2)}) copy-start(f32[64,8192]{0,1:T(8,128)S(1)} %fusion.10) | copy-start | bytes 6291460
  159.9 12.1 %collective-permute-start.11 = (f32[2,64]{1,0:T(2,128)S(1)}, f32[2,64]{1,0:T(2,128)S(1)}, u32[]{:S(2)}, u32[]{:S(2)}) collective-permute-start(f32[2,64]{1,0:T(2,128)S(1)} %pad_maximum_fusion.29), channel_id=1, source_target_pairs={{0,8},{1,9},{2,10},{3,11},{4,12},{5,13},{6,14},{7,15},{8,0},{9,1},... | collective-permute-start | bytes 1544 | tf_op jit(solution)/shard_map/ppermute | solution.py:14
  171.3 9.0 %collective-permute-start.10 = (f32[1,8192]{1,0:T(1,128)S(1)}, f32[1,8192]{1,0:T(1,128)S(1)}, u32[]{:S(2)}, u32[]{:S(2)}) collective-permute-start(f32[1,8192]{1,0:T(1,128)S(1)} %copy.98), channel_id=1, source_target_pairs={{1,0},{2,1},{3,2},{4,3},{5,4},{6,5},{7,6},{8,7},{9,8},{10,9},{11,1... | collective-permute-start | bytes 98312 | tf_op jit(solution)/shard_map/ppermute | solution.py:26
  171.4 6.3 %collective-permute-start.9 = (f32[1,8192]{1,0:T(1,128)S(1)}, f32[1,8192]{1,0:T(1,128)S(1)}, u32[]{:S(2)}, u32[]{:S(2)}) collective-permute-start(f32[1,8192]{1,0:T(1,128)S(1)} %copy.96), channel_id=1, source_target_pairs={{0,1},{1,2},{2,3},{3,4},{4,5},{5,6},{6,7},{7,8},{8,9},{9,10},{10,1... | collective-permute-start | bytes 98312 | tf_op jit(solution)/shard_map/ppermute | solution.py:24
  197.0 4.5 %copy-start = (f32[64,8192]{0,1:T(8,128)}, f32[64,8192]{0,1:T(8,128)S(1)}, u32[]{:S(2)}) copy-start(f32[64,8192]{0,1:T(8,128)S(1)} %fusion.5) | copy-start | bytes 6291460
  197.0 10.9 %collective-permute-start.12 = (f32[2,64]{1,0:T(2,128)S(1)}, f32[2,64]{1,0:T(2,128)S(1)}, u32[]{:S(2)}, u32[]{:S(2)}) collective-permute-start(f32[2,64]{1,0:T(2,128)S(1)} %pad_maximum_fusion.30), channel_id=1, source_target_pairs={{0,8},{1,9},{2,10},{3,11},{4,12},{5,13},{6,14},{7,15},{8,0},{9,1},... | collective-permute-start | bytes 1544 | tf_op jit(solution)/shard_map/ppermute | solution.py:14
  205.3 3.4 %copy-start.1 = (f32[64,8192]{0,1:T(8,128)S(1)}, f32[64,8192]{0,1:T(8,128)}, u32[]{:S(2)}) copy-start(f32[64,8192]{0,1:T(8,128)} %copy-done) | copy-start | bytes 6291460
  205.3 3.4 %slice-start = ((f32[64,8192]{0,1:T(8,128)}), f32[64,2]{0,1:T(2,128)S(1)}, s32[]{:S(2)}) async-start(f32[64,8192]{0,1:T(8,128)} %copy-done), calls=%async_computation | async-start | bytes 2048 | tf_op jit(solution)/shard_map/jit(_roll_static)/slice | solution.py:89
  205.3 4.7 %copy-start.6 = (f32[64,8191]{0,1:T(8,128)S(1)}, f32[64,8191]{0,1:T(8,128)}, u32[]{:S(2)}) copy-start(f32[64,8191]{0,1:T(8,128)} %get-tuple-element.46) | copy-start | bytes 6290692
  223.2 6.1 %collective-permute-start.13 = (f32[1,4096]{1,0:T(1,128)S(1)}, f32[1,4096]{1,0:T(1,128)S(1)}, u32[]{:S(2)}, u32[]{:S(2)}) collective-permute-start(f32[1,4096]{1,0:T(1,128)S(1)} %get-tuple-element.82), channel_id=1, source_target_pairs={{0,1},{1,2},{2,3},{3,4},{4,5},{5,6},{6,7},{7,8},{8,9},{9,10},{10,1... | collective-permute-start | bytes 49160 | tf_op jit(solution)/shard_map/ppermute | solution.py:24
  223.3 8.3 %copy-start.8 = (f32[32,4096]{1,0:T(8,128)S(1)}, f32[32,4096]{1,0:T(8,128)}, u32[]{:S(2)}) copy-start(f32[32,4096]{1,0:T(8,128)} %slice.609) | copy-start | bytes 1572868
  223.3 8.3 %copy-start.9 = (f32[32,4096]{1,0:T(8,128)S(1)}, f32[32,4096]{1,0:T(8,128)}, u32[]{:S(2)}) copy-start(f32[32,4096]{1,0:T(8,128)} %slice.608) | copy-start | bytes 1572868
  223.3 6.0 %collective-permute-start.14 = (f32[1,4096]{1,0:T(1,128)S(1)}, f32[1,4096]{1,0:T(1,128)S(1)}, u32[]{:S(2)}, u32[]{:S(2)}) collective-permute-start(f32[1,4096]{1,0:T(1,128)S(1)} %get-tuple-element.83), channel_id=1, source_target_pairs={{1,0},{2,1},{3,2},{4,3},{5,4},{6,5},{7,6},{8,7},{9,8},{10,9},{11,1... | collective-permute-start | bytes 49160 | tf_op jit(solution)/shard_map/ppermute | solution.py:26
  233.6 5.3 %collective-permute-start.17 = (f32[2,32]{1,0:T(2,128)S(1)}, f32[2,32]{1,0:T(2,128)S(1)}, u32[]{:S(2)}, u32[]{:S(2)}) collective-permute-start(f32[2,32]{1,0:T(2,128)S(1)} %pad_maximum_fusion.31), channel_id=1, source_target_pairs={{0,8},{1,9},{2,10},{3,11},{4,12},{5,13},{6,14},{7,15},{8,0},{9,1},... | collective-permute-start | bytes 776 | tf_op jit(solution)/shard_map/ppermute | solution.py:14
  234.5 5.9 %collective-permute-start.15 = (f32[1,4096]{1,0:T(1,128)S(1)}, f32[1,4096]{1,0:T(1,128)S(1)}, u32[]{:S(2)}, u32[]{:S(2)}) collective-permute-start(f32[1,4096]{1,0:T(1,128)S(1)} %get-tuple-element.112), channel_id=1, source_target_pairs={{0,1},{1,2},{2,3},{3,4},{4,5},{5,6},{6,7},{7,8},{8,9},{9,10},{10,1... | collective-permute-start | bytes 49160 | tf_op jit(solution)/shard_map/ppermute | solution.py:24
  234.5 5.9 %collective-permute-start.16 = (f32[1,4096]{1,0:T(1,128)S(1)}, f32[1,4096]{1,0:T(1,128)S(1)}, u32[]{:S(2)}, u32[]{:S(2)}) collective-permute-start(f32[1,4096]{1,0:T(1,128)S(1)} %get-tuple-element.113), channel_id=1, source_target_pairs={{1,0},{2,1},{3,2},{4,3},{5,4},{6,5},{7,6},{8,7},{9,8},{10,9},{11,1... | collective-permute-start | bytes 49160 | tf_op jit(solution)/shard_map/ppermute | solution.py:26
  241.4 5.7 %collective-permute-start.20 = (f32[2,32]{1,0:T(2,128)S(1)}, f32[2,32]{1,0:T(2,128)S(1)}, u32[]{:S(2)}, u32[]{:S(2)}) collective-permute-start(f32[2,32]{1,0:T(2,128)S(1)} %pad_maximum_fusion.32), channel_id=1, source_target_pairs={{0,8},{1,9},{2,10},{3,11},{4,12},{5,13},{6,14},{7,15},{8,0},{9,1},... | collective-permute-start | bytes 776 | tf_op jit(solution)/shard_map/ppermute | solution.py:14
  242.6 5.9 %collective-permute-start.18 = (f32[1,4096]{1,0:T(1,128)S(1)}, f32[1,4096]{1,0:T(1,128)S(1)}, u32[]{:S(2)}, u32[]{:S(2)}) collective-permute-start(f32[1,4096]{1,0:T(1,128)S(1)} %get-tuple-element.106), channel_id=1, source_target_pairs={{0,1},{1,2},{2,3},{3,4},{4,5},{5,6},{6,7},{7,8},{8,9},{9,10},{10,1... | collective-permute-start | bytes 49160 | tf_op jit(solution)/shard_map/ppermute | solution.py:24
  242.7 5.9 %collective-permute-start.19 = (f32[1,4096]{1,0:T(1,128)S(1)}, f32[1,4096]{1,0:T(1,128)S(1)}, u32[]{:S(2)}, u32[]{:S(2)}) collective-permute-start(f32[1,4096]{1,0:T(1,128)S(1)} %get-tuple-element.107), channel_id=1, source_target_pairs={{1,0},{2,1},{3,2},{4,3},{5,4},{6,5},{7,6},{8,7},{9,8},{10,9},{11,1... | collective-permute-start | bytes 49160 | tf_op jit(solution)/shard_map/ppermute | solution.py:26
  249.5 5.2 %collective-permute-start.23 = (f32[2,32]{1,0:T(2,128)S(1)}, f32[2,32]{1,0:T(2,128)S(1)}, u32[]{:S(2)}, u32[]{:S(2)}) collective-permute-start(f32[2,32]{1,0:T(2,128)S(1)} %pad_maximum_fusion.33), channel_id=1, source_target_pairs={{0,8},{1,9},{2,10},{3,11},{4,12},{5,13},{6,14},{7,15},{8,0},{9,1},... | collective-permute-start | bytes 776 | tf_op jit(solution)/shard_map/ppermute | solution.py:14
  250.3 5.9 %collective-permute-start.21 = (f32[1,4096]{1,0:T(1,128)S(1)}, f32[1,4096]{1,0:T(1,128)S(1)}, u32[]{:S(2)}, u32[]{:S(2)}) collective-permute-start(f32[1,4096]{1,0:T(1,128)S(1)} %get-tuple-element.100), channel_id=1, source_target_pairs={{0,1},{1,2},{2,3},{3,4},{4,5},{5,6},{6,7},{7,8},{8,9},{9,10},{10,1... | collective-permute-start | bytes 49160 | tf_op jit(solution)/shard_map/ppermute | solution.py:24
  250.3 5.9 %collective-permute-start.22 = (f32[1,4096]{1,0:T(1,128)S(1)}, f32[1,4096]{1,0:T(1,128)S(1)}, u32[]{:S(2)}, u32[]{:S(2)}) collective-permute-start(f32[1,4096]{1,0:T(1,128)S(1)} %get-tuple-element.101), channel_id=1, source_target_pairs={{1,0},{2,1},{3,2},{4,3},{5,4},{6,5},{7,6},{8,7},{9,8},{10,9},{11,1... | collective-permute-start | bytes 49160 | tf_op jit(solution)/shard_map/ppermute | solution.py:26
  257.2 6.0 %collective-permute-start.26 = (f32[2,32]{1,0:T(2,128)S(1)}, f32[2,32]{1,0:T(2,128)S(1)}, u32[]{:S(2)}, u32[]{:S(2)}) collective-permute-start(f32[2,32]{1,0:T(2,128)S(1)} %pad_maximum_fusion.34), channel_id=1, source_target_pairs={{0,8},{1,9},{2,10},{3,11},{4,12},{5,13},{6,14},{7,15},{8,0},{9,1},... | collective-permute-start | bytes 776 | tf_op jit(solution)/shard_map/ppermute | solution.py:14
  258.4 5.9 %collective-permute-start.24 = (f32[1,4096]{1,0:T(1,128)S(1)}, f32[1,4096]{1,0:T(1,128)S(1)}, u32[]{:S(2)}, u32[]{:S(2)}) collective-permute-start(f32[1,4096]{1,0:T(1,128)S(1)} %get-tuple-element.94), channel_id=1, source_target_pairs={{0,1},{1,2},{2,3},{3,4},{4,5},{5,6},{6,7},{7,8},{8,9},{9,10},{10,1... | collective-permute-start | bytes 49160 | tf_op jit(solution)/shard_map/ppermute | solution.py:24
  258.5 6.1 %collective-permute-start.25 = (f32[1,4096]{1,0:T(1,128)S(1)}, f32[1,4096]{1,0:T(1,128)S(1)}, u32[]{:S(2)}, u32[]{:S(2)}) collective-permute-start(f32[1,4096]{1,0:T(1,128)S(1)} %get-tuple-element.95), channel_id=1, source_target_pairs={{1,0},{2,1},{3,2},{4,3},{5,4},{6,5},{7,6},{8,7},{9,8},{10,9},{11,1... | collective-permute-start | bytes 49160 | tf_op jit(solution)/shard_map/ppermute | solution.py:26
  266.0 4.5 %collective-permute-start.27 = (f32[2,32]{1,0:T(2,128)S(1)}, f32[2,32]{1,0:T(2,128)S(1)}, u32[]{:S(2)}, u32[]{:S(2)}) collective-permute-start(f32[2,32]{1,0:T(2,128)S(1)} %pad_maximum_fusion.35), channel_id=1, source_target_pairs={{0,8},{1,9},{2,10},{3,11},{4,12},{5,13},{6,14},{7,15},{8,0},{9,1},... | collective-permute-start | bytes 776 | tf_op jit(solution)/shard_map/ppermute | solution.py:14
  271.2 5.8 %collective-permute-start.28 = (f32[1,2048]{1,0:T(1,128)S(1)}, f32[1,2048]{1,0:T(1,128)S(1)}, u32[]{:S(2)}, u32[]{:S(2)}) collective-permute-start(f32[1,2048]{1,0:T(1,128)S(1)} %get-tuple-element.114), channel_id=1, source_target_pairs={{0,1},{1,2},{2,3},{3,4},{4,5},{5,6},{6,7},{7,8},{8,9},{9,10},{10,1... | collective-permute-start | bytes 24584 | tf_op jit(solution)/shard_map/ppermute | solution.py:24
  271.3 5.8 %collective-permute-start.29 = (f32[1,2048]{1,0:T(1,128)S(1)}, f32[1,2048]{1,0:T(1,128)S(1)}, u32[]{:S(2)}, u32[]{:S(2)}) collective-permute-start(f32[1,2048]{1,0:T(1,128)S(1)} %get-tuple-element.115), channel_id=1, source_target_pairs={{1,0},{2,1},{3,2},{4,3},{5,4},{6,5},{7,6},{8,7},{9,8},{10,9},{11,1... | collective-permute-start | bytes 24584 | tf_op jit(solution)/shard_map/ppermute | solution.py:26
  277.8 5.8 %collective-permute-start.30 = (f32[1,2048]{1,0:T(1,128)S(1)}, f32[1,2048]{1,0:T(1,128)S(1)}, u32[]{:S(2)}, u32[]{:S(2)}) collective-permute-start(f32[1,2048]{1,0:T(1,128)S(1)} %get-tuple-element.138), channel_id=1, source_target_pairs={{0,1},{1,2},{2,3},{3,4},{4,5},{5,6},{6,7},{7,8},{8,9},{9,10},{10,1... | collective-permute-start | bytes 24584 | tf_op jit(solution)/shard_map/ppermute | solution.py:24
  277.9 4.5 %collective-permute-start.32 = (f32[2,16]{1,0:T(2,128)S(1)}, f32[2,16]{1,0:T(2,128)S(1)}, u32[]{:S(2)}, u32[]{:S(2)}) collective-permute-start(f32[2,16]{1,0:T(2,128)S(1)} %pad_maximum_fusion.36), channel_id=1, source_target_pairs={{0,8},{1,9},{2,10},{3,11},{4,12},{5,13},{6,14},{7,15},{8,0},{9,1},... | collective-permute-start | bytes 392 | tf_op jit(solution)/shard_map/ppermute | solution.py:14
  277.9 5.8 %collective-permute-start.31 = (f32[1,2048]{1,0:T(1,128)S(1)}, f32[1,2048]{1,0:T(1,128)S(1)}, u32[]{:S(2)}, u32[]{:S(2)}) collective-permute-start(f32[1,2048]{1,0:T(1,128)S(1)} %get-tuple-element.139), channel_id=1, source_target_pairs={{1,0},{2,1},{3,2},{4,3},{5,4},{6,5},{7,6},{8,7},{9,8},{10,9},{11,1... | collective-permute-start | bytes 24584 | tf_op jit(solution)/shard_map/ppermute | solution.py:26
  284.3 5.8 %collective-permute-start.33 = (f32[1,2048]{1,0:T(1,128)S(1)}, f32[1,2048]{1,0:T(1,128)S(1)}, u32[]{:S(2)}, u32[]{:S(2)}) collective-permute-start(f32[1,2048]{1,0:T(1,128)S(1)} %get-tuple-element.132), channel_id=1, source_target_pairs={{0,1},{1,2},{2,3},{3,4},{4,5},{5,6},{6,7},{7,8},{8,9},{9,10},{10,1... | collective-permute-start | bytes 24584 | tf_op jit(solution)/shard_map/ppermute | solution.py:24
  284.3 5.0 %collective-permute-start.35 = (f32[2,16]{1,0:T(2,128)S(1)}, f32[2,16]{1,0:T(2,128)S(1)}, u32[]{:S(2)}, u32[]{:S(2)}) collective-permute-start(f32[2,16]{1,0:T(2,128)S(1)} %pad_maximum_fusion.37), channel_id=1, source_target_pairs={{0,8},{1,9},{2,10},{3,11},{4,12},{5,13},{6,14},{7,15},{8,0},{9,1},... | collective-permute-start | bytes 392 | tf_op jit(solution)/shard_map/ppermute | solution.py:14
  286.1 4.6 %collective-permute-start.34 = (f32[1,2048]{1,0:T(1,128)S(1)}, f32[1,2048]{1,0:T(1,128)S(1)}, u32[]{:S(2)}, u32[]{:S(2)}) collective-permute-start(f32[1,2048]{1,0:T(1,128)S(1)} %get-tuple-element.133), channel_id=1, source_target_pairs={{1,0},{2,1},{3,2},{4,3},{5,4},{6,5},{7,6},{8,7},{9,8},{10,9},{11,1... | collective-permute-start | bytes 24584 | tf_op jit(solution)/shard_map/ppermute | solution.py:26
  291.2 5.8 %collective-permute-start.36 = (f32[1,2048]{1,0:T(1,128)S(1)}, f32[1,2048]{1,0:T(1,128)S(1)}, u32[]{:S(2)}, u32[]{:S(2)}) collective-permute-start(f32[1,2048]{1,0:T(1,128)S(1)} %get-tuple-element.126), channel_id=1, source_target_pairs={{0,1},{1,2},{2,3},{3,4},{4,5},{5,6},{6,7},{7,8},{8,9},{9,10},{10,1... | collective-permute-start | bytes 24584 | tf_op jit(solution)/shard_map/ppermute | solution.py:24
  291.3 4.5 %collective-permute-start.38 = (f32[2,16]{1,0:T(2,128)S(1)}, f32[2,16]{1,0:T(2,128)S(1)}, u32[]{:S(2)}, u32[]{:S(2)}) collective-permute-start(f32[2,16]{1,0:T(2,128)S(1)} %pad_maximum_fusion.38), channel_id=1, source_target_pairs={{0,8},{1,9},{2,10},{3,11},{4,12},{5,13},{6,14},{7,15},{8,0},{9,1},... | collective-permute-start | bytes 392 | tf_op jit(solution)/shard_map/ppermute | solution.py:14
  292.6 4.6 %collective-permute-start.37 = (f32[1,2048]{1,0:T(1,128)S(1)}, f32[1,2048]{1,0:T(1,128)S(1)}, u32[]{:S(2)}, u32[]{:S(2)}) collective-permute-start(f32[1,2048]{1,0:T(1,128)S(1)} %get-tuple-element.127), channel_id=1, source_target_pairs={{1,0},{2,1},{3,2},{4,3},{5,4},{6,5},{7,6},{8,7},{9,8},{10,9},{11,1... | collective-permute-start | bytes 24584 | tf_op jit(solution)/shard_map/ppermute | solution.py:26
  297.4 7.5 %copy-start.7 = (f32[16,2048]{1,0:T(8,128)}, f32[16,2048]{1,0:T(8,128)S(1)}, u32[]{:S(2)}) copy-start(f32[16,2048]{1,0:T(8,128)S(1)} %fusion.77) | copy-start | bytes 393220
  297.7 5.8 %collective-permute-start.39 = (f32[1,2048]{1,0:T(1,128)S(1)}, f32[1,2048]{1,0:T(1,128)S(1)}, u32[]{:S(2)}, u32[]{:S(2)}) collective-permute-start(f32[1,2048]{1,0:T(1,128)S(1)} %get-tuple-element.120), channel_id=1, source_target_pairs={{0,1},{1,2},{2,3},{3,4},{4,5},{5,6},{6,7},{7,8},{8,9},{9,10},{10,1... | collective-permute-start | bytes 24584 | tf_op jit(solution)/shard_map/ppermute | solution.py:24
  297.8 5.0 %collective-permute-start.41 = (f32[2,16]{1,0:T(2,128)S(1)}, f32[2,16]{1,0:T(2,128)S(1)}, u32[]{:S(2)}, u32[]{:S(2)}) collective-permute-start(f32[2,16]{1,0:T(2,128)S(1)} %pad_maximum_fusion.39), channel_id=1, source_target_pairs={{0,8},{1,9},{2,10},{3,11},{4,12},{5,13},{6,14},{7,15},{8,0},{9,1},... | collective-permute-start | bytes 392 | tf_op jit(solution)/shard_map/ppermute | solution.py:14
  299.5 4.6 %collective-permute-start.40 = (f32[1,2048]{1,0:T(1,128)S(1)}, f32[1,2048]{1,0:T(1,128)S(1)}, u32[]{:S(2)}, u32[]{:S(2)}) collective-permute-start(f32[1,2048]{1,0:T(1,128)S(1)} %get-tuple-element.121), channel_id=1, source_target_pairs={{1,0},{2,1},{3,2},{4,3},{5,4},{6,5},{7,6},{8,7},{9,8},{10,9},{11,1... | collective-permute-start | bytes 24584 | tf_op jit(solution)/shard_map/ppermute | solution.py:26
where the time goes:
time: 310 us; the launch traced here: 305 us
  local copies, waits for them, and re-layouts  115 us (37%)
  other arithmetic  81 us (26%)
  starting transfers between devices  64.8 us (21%)
  waiting for transfers between devices  33.1 us (11%)
  matrix products  9.86 us (3%)
    ppermute x14, starting transfers between devices, padded(): lax.ppermute(head, axis, [((i + 1) % count, i) for i in range(count)])  45.8 us
    select_n x9, other arithmetic, relax_colour(): return jnp.where(update_mask, (source + beside_all) / (4.0 + screen), field)  44.4 us
    slice x18, local copies, waits for them, and re-layouts, padded(): lax.slice_in_dim(cells, cells.shape[dim] - width, cells.shape[dim], axis=...  30 us
    ppermute x14, waiting for transfers between devices, padded(): lax.ppermute(tail, axis, [(i, (i + 1) % count) for i in range(count)])  27.8 us
    slice x12, local copies, waits for them, and re-layouts, sides_lon(): jnp.roll(field, -1, 1)  21.1 us
    ppermute x14, starting transfers between devices, passed_along(): lax.ppermute(shard, axis, [(i, (i + by) % size) for i in range(size)])  16.5 us
    sub x3, other arithmetic, residual_of(): return source - ((4.0 + screen) * field - beside_all)  15.2 us
    unnamed x25, local copies, waits for them, and re-layouts  12.2 us
  transfers between devices with their start and end apart: 42, of which 18 were waited for; matrix products, arithmetic and copies ran while one was open for 26% of the time, Pallas kernels for 0%

commit v1 on v0

v1 whole, which is shorter than its diff:
```python
import functools

import jax
import jax.numpy as jnp
from jax import lax
from jax.experimental import pallas as pl
from jax.experimental.pallas import tpu as pltpu
from jax.sharding import PartitionSpec as P

TILE = 32
SEAM_SCALE = 0.1
LANES = 128
F32 = jnp.float32
BF16 = jnp.bfloat16


def lane_ids(rows):
    return lax.broadcasted_iota(jnp.int32, (rows, LANES), 1)


def row_ids(rows):
    return lax.broadcasted_iota(jnp.int32, (rows, LANES), 0)


def roll_up(x):
    return pltpu.roll(x, 1, 1)


def roll_down(x):
    return pltpu.roll(x, LANES - 1, 1)


def col_prev(x):
    return pltpu.roll(x, 1, 0)


def col_next(x):
    return pltpu.roll(x, x.shape[0] - 1, 0)


def splitter():
    a = lax.broadcasted_iota(jnp.int32, (256, 256), 0)
    b = lax.broadcasted_iota(jnp.int32, (256, 256), 1)
    return jnp.where(a == 2 * (b % LANES) + b // LANES, 1.0, 0.0).astype(BF16)


def merger():
    a = lax.broadcasted_iota(jnp.int32, (256, 256), 0)
    b = lax.broadcasted_iota(jnp.int32, (256, 256), 1)
    return jnp.where(b == 2 * (a % LANES) + a // LANES, 1.0, 0.0).astype(BF16)


def virtual_splitter():
    a = lax.broadcasted_iota(jnp.int32, (LANES, 256), 0)
    b = lax.broadcasted_iota(jnp.int32, (LANES, 256), 1)
    place = a // 2 + jnp.where(a >= 64, 64, 0) + LANES * (a % 2)
    return jnp.where(place == b, 1.0, 0.0).astype(BF16)


def moved(x, matrix):
    high = x.astype(BF16)
    low = (x - high.astype(F32)).astype(BF16)
    return jnp.dot(high, matrix, preferred_element_type=F32) + jnp.dot(
        low, matrix, preferred_element_type=F32
    )


def quarters_of(parts, temp):
    count = parts.shape[0] // 2
    temp[0] = parts[:, :LANES]
    temp[1] = parts[:, LANES:]
    return [temp[pr, pl.ds(pc, count, 2), :] for pc in (0, 1) for pr in (0, 1)]


def prepare_kernel(
    right_ref, weight_ref, flag_ref,
    s_ref, d_ref, low_ref, high_ref, to_left, to_right, polar_ref, corner_low, corner_high,
    temp_s, temp_d, scale_ref,
):
    tiles, rows = s_ref.shape[1], s_ref.shape[2]
    flag_cols = flag_ref.shape[0]
    flag_lats = flag_ref.shape[1]
    per_tile = rows // flag_cols
    matrix = splitter()
    flags = jnp.concatenate(
        [flag_ref[...].astype(F32), jnp.zeros((8 - flag_cols, flag_lats), F32)], 0
    )
    lat = lax.broadcasted_iota(jnp.int32, (8, flag_lats), 1)
    stacked = jnp.concatenate(
        [jnp.where(lat // 8 == c, flags, 0.0) for c in range(tiles)], 0
    ).astype(BF16)
    a = lax.broadcasted_iota(jnp.int32, (flag_lats, LANES), 0)
    b = lax.broadcasted_iota(jnp.int32, (flag_lats, LANES), 1)
    spread = jnp.where(a % 8 == b // (TILE // 2), 1.0, 0.0).astype(BF16)
    spread_flags = jnp.dot(stacked, spread, preferred_element_type=F32)
    scale_ref[...] = jnp.where(spread_flags > 0.5, SEAM_SCALE, 1.0).reshape(tiles, 8, LANES)

    sub = row_ids(8)

    def edge(group, first, shift_of):
        packed = group[0] if shift_of(0) == 0 else pltpu.roll(group[0], shift_of(0), 0)
        for q in range(1, 4):
            shift = shift_of(q) % 8
            moved_q = group[q] if shift == 0 else pltpu.roll(group[q], shift, 0)
            packed = jnp.where(sub // 2 == q, moved_q, packed)
        return packed

    def body(c, _):
        where = pl.ds(pl.multiple_of(c * 256, 256), 256)
        source = quarters_of(moved(right_ref[:, where], matrix), temp_s)
        weight = quarters_of(
            jnp.dot(weight_ref[:, where], matrix, preferred_element_type=F32), temp_d
        )
        scales = scale_ref[c]
        scale = jnp.concatenate(
            [jnp.broadcast_to(scales[i : i + 1], (per_tile, LANES)) for i in range(flag_cols)], 0
        )
        screen = [w * scale for w in weight]
        coarse = (screen[0] + screen[1]) + (screen[2] + screen[3])
        half = rows // 2
        low_ref[c] = coarse[:half]
        high_ref[c] = coarse[half:]
        diag = [4.0 + s for s in screen]
        for q in range(4):
            s_ref[q, c] = source[q]
            d_ref[q, c] = diag[q]
        gs = [x[rows - 8 :] for x in source]
        gd = [x[rows - 8 :] for x in diag]
        first = pltpu.roll(gs[0] / gd[0], 2, 0)
        second = pltpu.roll(gs[3] / gd[3], 3, 0)
        to_right[0, c] = jnp.where(sub == 0, first, edge(gs, 0, lambda q: 2 * q + 2))
        to_right[1, c] = jnp.where(sub == 0, second, edge(gd, 0, lambda q: 2 * q + 2))
        gs = [x[:8] for x in source]
        gd = [x[:8] for x in diag]
        first = pltpu.roll(gs[3] / gd[3], 6, 0)
        second = pltpu.roll(gs[0] / gd[0], 5, 0)
        to_left[0, c] = jnp.where(sub == 7, first, edge(gs, 0, lambda q: 2 * q))
        to_left[1, c] = jnp.where(sub == 7, second, edge(gd, 0, lambda q: 2 * q))
        return 0

    lax.fori_loop(0, tiles, body, 0)

    a = lax.broadcasted_iota(jnp.int32, (LANES, LANES), 0)
    b = lax.broadcasted_iota(jnp.int32, (LANES, LANES), 1)
    mirror = jnp.where(a + b == LANES - 1, 1.0, 0.0).astype(BF16)
    lane = lane_ids(rows)
    for pc in (0, 1):
        for pr in (0, 1):
            q, from_q = 2 * pc + pr, 2 * pc + 1 - pr
            both = jnp.where(lane >= 64, s_ref[from_q, tiles - 1], s_ref[from_q, 0])
            diag = jnp.where(lane >= 64, d_ref[from_q, tiles - 1], d_ref[from_q, 0])
            both = jnp.where((lane >= 32) & (lane < 96), pltpu.roll(diag, 64, 1), both)
            both = moved(both, mirror)
            polar_ref[q] = both
            corner_low[q] = both[: rows // 2]
            corner_high[q] = both[rows // 2 :]


def inverse_kernel(d_ref, i_ref):
    def body(t, _):
        for q in range(4):
            i_ref[q, t] = 1.0 / d_ref[q, t]
        return 0

    lax.fori_loop(0, d_ref.shape[1], body, 0)


def half_sweep(v, load_s, load_i, tiles, red):
    rows = v.shape[2]
    lane = lane_ids(rows)
    y, z, qa, qb = (1, 2, 0, 3) if red else (3, 0, 2, 1)
    col_a, col_b = (col_prev, col_next) if red else (col_next, col_prev)

    def beside_virtual(q):
        ns, we = q ^ 1, q ^ 2
        here = v[ns, tiles]
        if q % 2 == 0:
            lat = jnp.where(lane == 0, roll_up(v[ns, tiles - 1]), roll_up(here))
        else:
            lat = jnp.where(lane == LANES - 1, roll_down(v[ns, 0]), roll_down(here))
        cols = v[we, tiles]
        return (here + lat) + (cols + (col_prev if q < 2 else col_next)(cols))

    held = [
        (q, (load_s(q, tiles) + beside_virtual(q)) * load_i(q, tiles)) for q in (y, z)
    ]

    def body(t, carry):
        y_before, z_here = carry
        vy, vz = v[y, t], v[z, t]
        y_here = roll_up(vy)
        z_after = roll_down(v[z, t + 1])
        lat_a = vy + jnp.where(lane == 0, y_before, y_here)
        lat_b = vz + jnp.where(lane == LANES - 1, z_after, z_here)
        v[qa, t] = (load_s(qa, t) + (lat_a + (vz + col_a(vz)))) * load_i(qa, t)
        v[qb, t] = (load_s(qb, t) + (lat_b + (vy + col_b(vy)))) * load_i(qb, t)
        return y_here, z_after

    lax.fori_loop(0, tiles, body, (roll_up(v[y, tiles]), roll_down(v[z, 0])))
    for q, value in held:
        v[q, tiles] = value


def smooth(v, load_s, load_i, tiles):
    rows = v.shape[2]
    zeros = jnp.zeros((rows, LANES), F32)

    def first(t, _):
        for q in (0, 3):
            v[q, t] = load_s(q, t) * load_i(q, t)
        return 0

    lax.fori_loop(0, tiles, first, 0)
    for q in (1, 2):
        v[q, 0] = zeros
        v[q, tiles - 1] = zeros
        v[q, tiles] = load_s(q, tiles) * load_i(q, tiles)
        v[3 * (q - 1), tiles] = zeros
    half_sweep(v, load_s, load_i, tiles, False)
    half_sweep(v, load_s, load_i, tiles, True)
    half_sweep(v, load_s, load_i, tiles, False)


def residual_and_columns(v, load_s, load_d, tiles, c_ref, keep):
    rows = v.shape[2]
    lane = lane_ids(rows)

    def body(t, _):
        before = jnp.where(t == 0, tiles, t - 1)
        after = jnp.where(t == tiles, 0, t + 1)
        x = [v[q, t] for q in range(4)]

        def north(q):
            return jnp.where(lane == 0, roll_up(v[q, before]), roll_up(x[q]))

        def south(q):
            return jnp.where(lane == LANES - 1, roll_down(v[q, after]), roll_down(x[q]))

        beside = [
            (x[1] + north(1)) + (x[2] + col_prev(x[2])),
            (x[0] + south(0)) + (x[3] + col_prev(x[3])),
            (x[3] + north(3)) + (x[0] + col_next(x[0])),
            (x[2] + south(2)) + (x[1] + col_next(x[1])),
        ]
        r = [load_s(q, t) - (load_d(q, t) * x[q] - beside[q]) for q in range(4)]
        keep(t, r)
        c_ref[0, t] = (col_prev(r[2]) + col_next(r[0])) + 3.0 * (r[0] + r[2])
        c_ref[1, t] = (col_prev(r[3]) + col_next(r[1])) + 3.0 * (r[1] + r[3])
        return 0

    lax.fori_loop(0, tiles + 1, body, 0)


def restricted(c_ref, t, tiles):
    lane = lane_ids(c_ref.shape[2])
    before = jnp.where(t == 0, tiles, t - 1)
    after = jnp.where(t == tiles, 0, t + 1)
    c0, c1 = c_ref[0, t], c_ref[1, t]
    north = jnp.where(lane == 0, roll_up(c_ref[1, before]), roll_up(c1))
    south = jnp.where(lane == LANES - 1, roll_down(c_ref[0, after]), roll_down(c0))
    return ((north + south) + 3.0 * (c0 + c1)) * (1.0 / 16.0)


def fine_kernel(
    s_ref, d_ref, i_ref, from_left, from_right, polar_ref, corner_left, corner_right,
    r_ref, low_ref, high_ref, screen_virtual,
    v, c_ref, hs, hd, hi, ps, pd, pi,
):
    tiles, rows = s_ref.shape[1], s_ref.shape[2]
    sub = row_ids(8)

    def rolled(x, shift):
        return x if shift % 8 == 0 else pltpu.roll(x, shift % 8, 0)

    def halo(t, _):
        al, bl, ar, br = from_left[0, t], from_left[1, t], from_right[0, t], from_right[1, t]
        for q in range(4):
            source = jnp.where(
                sub >= 6, rolled(al, 6 - 2 * q), jnp.where(sub <= 1, rolled(ar, -2 * q), 0.0)
            )
            diag = jnp.where(
                sub >= 6, rolled(bl, 6 - 2 * q), jnp.where(sub <= 1, rolled(br, -2 * q), 4.0)
            )
            if q == 0:
                source = jnp.where(sub == 2, rolled(br, 3), source)
                diag = jnp.where((sub == 2) | (sub == 6), 1.0, diag)
            if q == 3:
                source = jnp.where(sub == 5, rolled(bl, 5), source)
                diag = jnp.where((sub == 5) | (sub == 1), 1.0, diag)
            hs[q, t] = source
            hd[q, t] = diag
            hi[q, t] = 1.0 / diag
        return 0

    lax.fori_loop(0, tiles, halo, 0)

    def unpacked(x):
        lane = lane_ids(x.shape[0])
        used = (lane < 32) | (lane >= 96)
        return jnp.where(used, x, 0.0), jnp.where(used, pltpu.roll(x, 64, 1), 4.0)

    half = rows // 2
    totals = [0.0, 0.0, 0.0]
    for q in range(4):
        left_s, left_d = unpacked(corner_left[q])
        own_s, own_d = unpacked(polar_ref[q])
        right_s, right_d = unpacked(corner_right[q])
        totals = [totals[0] + left_d, totals[1] + own_d, totals[2] + right_d]
        ps[q] = own_s
        pd[q] = own_d
        pi[q] = 1.0 / own_d
        source = jnp.where(sub >= 5, left_s[half - 8 :], jnp.where(sub <= 2, right_s[:8], 0.0))
        diag = jnp.where(sub >= 5, left_d[half - 8 :], jnp.where(sub <= 2, right_d[:8], 4.0))
        hs[q, tiles] = source
        hd[q, tiles] = diag
        hi[q, tiles] = 1.0 / diag
    screen_virtual[:half] = totals[0] - 16.0
    screen_virtual[half : half + rows] = totals[1] - 16.0
    screen_virtual[half + rows :] = totals[2] - 16.0

    def loader(own, halo_ref, virtual):
        def load(q, t):
            if isinstance(t, int) and t == tiles:
                return jnp.concatenate([virtual[q], halo_ref[q, t]], 0)
            return jnp.concatenate([own[q, t], halo_ref[q, t]], 0)

        return load

    smooth(v, loader(s_ref, hs, ps), loader(i_ref, hi, pi), tiles)

    def residual(t, before, after, own_s, own_d):
        lane = lane_ids(v.shape[2])
        x = [v[q, t] for q in range(4)]

        def north(q):
            return jnp.where(lane == 0, roll_up(v[q, before]), roll_up(x[q]))

        def south(q):
            return jnp.where(lane == LANES - 1, roll_down(v[q, after]), roll_down(x[q]))

        beside = [
            (x[1] + north(1)) + (x[2] + col_prev(x[2])),
            (x[0] + south(0)) + (x[3] + col_prev(x[3])),
            (x[3] + north(3)) + (x[0] + col_next(x[0])),
            (x[2] + south(2)) + (x[1] + col_next(x[1])),
        ]
        r = [
            jnp.concatenate([own_s[q], hs[q, t]], 0)
            - (jnp.concatenate([own_d[q], hd[q, t]], 0) * x[q] - beside[q])
            for q in range(4)
        ]
        c_ref[0, t] = (col_prev(r[2]) + col_next(r[0])) + 3.0 * (r[0] + r[2])
        c_ref[1, t] = (col_prev(r[3]) + col_next(r[1])) + 3.0 * (r[1] + r[3])
        return r

    def main(t, _):
        before = jnp.where(t == 0, tiles, t - 1)
        r = residual(
            t, before, t + 1, [s_ref[q, t] for q in range(4)], [d_ref[q, t] for q in range(4)]
        )
        for q in range(4):
            r_ref[q, t] = r[q][:rows]
        return 0

    lax.fori_loop(0, tiles, main, 0)
    residual(tiles, tiles - 1, 0, [ps[q] for q in range(4)], [pd[q] for q in range(4)])

    def coarse(t, _):
        value = restricted(c_ref, t, tiles)
        low_ref[t] = value[:half]
        high_ref[t] = value[half:rows]
        return 0

    lax.fori_loop(0, tiles + 1, coarse, 0)


def merge_kernel(r_ref, out_ref, temp):
    tiles = r_ref.shape[1]
    rows = r_ref.shape[2]
    matrix = merger()

    def body(c, _):
        for pr in (0, 1):
            for pc in (0, 1):
                temp[pr, pl.ds(pc, rows, 2), :] = r_ref[2 * pc + pr, c]
        both = jnp.concatenate([temp[0], temp[1]], 1)
        out_ref[:, pl.ds(pl.multiple_of(c * 256, 256), 256)] = moved(both, matrix)
        return 0

    lax.fori_loop(0, tiles, body, 0)


def coarse_kernel(
    s_left, s_low, s_high, s_right, e_left, e_low, e_high, e_right, e_virtual,
    solution_ref, residual_ref,
    s, d, inv, v, c_ref, temp, s2, d2, i2, v2,
):
    tiles = s.shape[1] - 1
    rows = s.shape[2]
    matrix = splitter()

    def fill(t, source, screen):
        for q, value in enumerate(source):
            s[q, t] = value
        for q, value in enumerate(screen):
            diag = 4.0 + value
            d[q, t] = diag
            inv[q, t] = 1.0 / diag
        total = (screen[0] + screen[1]) + (screen[2] + screen[3])
        d2[t] = 4.0 + total
        i2[t] = 1.0 / (4.0 + total)

    def split(c, _):
        def wide(refs):
            return jnp.concatenate(
                [jnp.concatenate([ref[2 * c + h] for ref in refs], 0) for h in (0, 1)], 1
            )

        source = quarters_of(moved(wide((s_left, s_low, s_high, s_right)), matrix), temp)
        screen = quarters_of(moved(wide((e_left, e_low, e_high, e_right)), matrix), temp)
        fill(c, source, screen)
        return 0

    lax.fori_loop(0, tiles, split, 0)
    last = 2 * tiles
    matrix = virtual_splitter()
    source = jnp.concatenate([s_left[last], s_low[last], s_high[last], s_right[last]], 0)
    source = quarters_of(moved(source, matrix), temp)
    screen = quarters_of(moved(e_virtual[...], matrix), temp)
    fill(tiles, source, screen)

    smooth(v, lambda q, t: s[q, t], lambda q, t: inv[q, t], tiles)
    residual_and_columns(
        v, lambda q, t: s[q, t], lambda q, t: d[q, t], tiles, c_ref, lambda t, r: None
    )

    lane, sub = lane_ids(rows), row_ids(rows)
    even = (lane + sub) % 2 == 0

    def start(t, _):
        value = restricted(c_ref, t, tiles)
        s2[t] = value
        v2[t] = jnp.where(even, value * i2[t], 0.0)
        return 0

    lax.fori_loop(0, tiles, start, 0)
    value = restricted(c_ref, tiles, tiles)
    s2[tiles] = value
    v2[tiles] = jnp.where(even, 0.0, value * i2[tiles])

    def beside(t, before, after):
        x = v2[t]
        north = jnp.where(lane == 0, roll_up(v2[before]), roll_up(x))
        south = jnp.where(lane == LANES - 1, roll_down(v2[after]), roll_down(x))
        return (col_prev(x) + col_next(x)) + (north + south)

    def relaxed(t, before, after, mask):
        return jnp.where(mask, (s2[t] + beside(t, before, after)) * i2[t], v2[t])

    for mask, other in ((~even, even), (even, ~even), (~even, even)):
        held = relaxed(tiles, tiles - 1, 0, other)

        def sweep(t, _, mask=mask):
            v2[t] = relaxed(t, jnp.where(t == 0, tiles, t - 1), t + 1, mask)
            return 0

        lax.fori_loop(0, tiles, sweep, 0)
        v2[tiles] = held

    own = solution_ref.shape[0]
    skip = (rows - own) // 2

    def finish(t, _):
        x = v2[t]
        r = s2[t] - (d2[t] * x - beside(t, jnp.where(t == 0, tiles, t - 1), t + 1))
        where = pl.ds(pl.multiple_of(t * LANES, LANES), LANES)
        solution_ref[:, where] = x[skip : skip + own]
        residual_ref[:, where] = r[skip : skip + own]
        return 0

    lax.fori_loop(0, tiles, finish, 0)


def call(kernel, out_shapes, scratch, *args):
    vmem = pl.BlockSpec(memory_space=pltpu.VMEM)
    return pl.pallas_call(
        kernel,
        out_shape=[jax.ShapeDtypeStruct(shape, F32) for shape in out_shapes],
        in_specs=[vmem] * len(args),
        out_specs=[vmem] * len(out_shapes),
        scratch_shapes=[pltpu.VMEM(shape, F32) for shape in scratch],
        compiler_params=pltpu.CompilerParams(vmem_limit_bytes=40 * 2**20),
    )(*args)


def shifted(x, by):
    count = lax.axis_size("lon")
    return lax.ppermute(x, "lon", [(i, (i + by) % count) for i in range(count)])


def body(right_side, texel_weight, seam_flags):
    columns, height = right_side.shape
    half_turn = lax.axis_size("lon") // 2
    tiles, rows = height // 256, columns // 2
    half = rows // 2
    quarters = (4, tiles, rows, LANES)
    part = (tiles, half, LANES)
    s, d, e_low, e_high, to_left, to_right, polar, corner_low, corner_high = call(
        prepare_kernel,
        [quarters, quarters, part, part, (2, tiles, 8, LANES), (2, tiles, 8, LANES)]
        + [(4, rows, LANES), (4, half, LANES), (4, half, LANES)],
        [(2, columns, LANES), (2, columns, LANES), (tiles, 8, LANES)],
        right_side, texel_weight, seam_flags,
    )
    from_left = shifted(to_right, 1)
    from_right = shifted(to_left, -1)
    polar = shifted(polar, half_turn)
    corner_left = shifted(corner_high, half_turn + 1)
    corner_right = shifted(corner_low, half_turn - 1)
    e_left = shifted(e_high, 1)
    e_right = shifted(e_low, -1)
    (inverse,) = call(inverse_kernel, [quarters], [], d)
    wide = rows + 8
    halo = (4, tiles + 1, 8, LANES)
    own = (4, rows, LANES)
    part = (tiles + 1, half, LANES)
    r, s_low, s_high, e_virtual = call(
        fine_kernel,
        [quarters, part, part, (2 * rows, LANES)],
        [(4, tiles + 1, wide, LANES), (2, tiles + 1, wide, LANES), halo, halo, halo, own, own, own],
        s, d, inverse, from_left, from_right, polar, corner_left, corner_right,
    )
    s_left = shifted(s_high, 1)
    s_right = shifted(s_low, -1)
    (fine_residual,) = call(merge_kernel, [(columns, height)], [(2, columns, LANES)], r)
    coarse = (4, tiles // 2 + 1, rows, LANES)
    single = coarse[1:]
    solution_2, residual_2 = call(
        coarse_kernel,
        [(columns // 4, height // 4)] * 2,
        [coarse, coarse, coarse, coarse, (2,) + single, (2, columns, LANES)]
        + [single, single, single, single],
        s_left, s_low, s_high, s_right, e_left, e_low, e_high, e_right, e_virtual,
    )
    return fine_residual, solution_2, residual_2


def solution(mesh):
    spec = P(("groups", "lon"), None)
    return jax.shard_map(
        body, mesh=mesh, in_specs=(spec,) * 3, out_specs=(spec,) * 3, check_vma=False
    )
```

time: 310 us -> 76.4 us (0.25); the launches traced: 305 us -> 76.2 us
  local copies, waits for them, and re-layouts: 115 us -> 3.49 us
  other arithmetic: 81 us -> 0 us
  Pallas kernels: 0 us -> 48.9 us
  starting transfers between devices: 64.8 us -> 18.3 us
  waiting for transfers between devices: 33.1 us -> 4.76 us
  matrix products: 9.86 us -> 0 us
    slice x66 -> x0, local copies, waits for them, and re-layouts: 80.6 us -> none  [the longest x18 30 us: padded(): lax.slice_in_dim(cells, cells.shape[dim] - width, cells.shape[dim], axis=...]
    pallas_call x0 -> x5, Pallas kernels: none -> 48.9 us  [call(): pl.pallas_call(kernel, out_shape=[jax.ShapeDtypeStruct(shape, F32) for sh...]
    select_n x12 -> x0, other arithmetic: 46.8 us -> none  [the longest x9 44.4 us: relax_colour(): return jnp.where(update_mask, (source + beside_all) / (4.0 + screen), field)]
    ppermute x42 -> x9, starting transfers between devices: 64.8 us -> 18.3 us  [shifted(): return lax.ppermute(x, 'lon', [(i, (i + by) % count) for i in range(count)])]
    ppermute x42 -> x9, waiting for transfers between devices: 33.1 us -> 4.76 us  [shifted(): return lax.ppermute(x, 'lon', [(i, (i + by) % count) for i in range(count)])]
    ppermute x8 -> x0, local copies, waits for them, and re-layouts: 21.5 us -> none  [the longest x4 10.8 us: padded(): lax.ppermute(tail, axis, [(i, (i + 1) % count) for i in range(count)])]
    add x6 -> x0, other arithmetic: 18.4 us -> none  [the longest x2 9.97 us: restrict(): lat_sum = north + 3.0 * field + 3.0 * south + twice]
    sub x3 -> x0, other arithmetic: 15.2 us -> none  [residual_of(): return source - ((4.0 + screen) * field - beside_all)]
  transfers between devices with their start and end apart: 42 -> 9, of which waited for: 18 -> 3; matrix products, arithmetic and copies ran while one was open for 26% -> 0% of each run, Pallas kernels for 0% -> 10%
where the time goes in v1:
time: 76.4 us; the launch traced here: 76.2 us
  Pallas kernels  48.9 us (64%)
  starting transfers between devices  18.3 us (24%)
  waiting for transfers between devices  4.76 us (6%)
  local copies, waits for them, and re-layouts  3.49 us (5%)
    pallas_call x5, Pallas kernels, call(): pl.pallas_call(kernel, out_shape=[jax.ShapeDtypeStruct(shape, F32) for sh...  48.9 us
    ppermute x9, starting transfers between devices, shifted(): return lax.ppermute(x, 'lon', [(i, (i + by) % count) for i in range(count)])  18.3 us
    ppermute x9, waiting for transfers between devices, shifted(): return lax.ppermute(x, 'lon', [(i, (i + by) % count) for i in range(count)])  4.76 us
    unnamed x6, local copies, waits for them, and re-layouts  3.49 us
  transfers between devices with their start and end apart: 9, of which 3 were waited for; matrix products, arithmetic and copies ran while one was open for 0% of the time, Pallas kernels for 10%

profile of v1, /device:TPU:0, one launch (start us, length us, event | category | flops | bytes accessed | tf_op | source)
XLA Modules:
  0.0 76.2 jit_solution(3505848804847972657)
XLA Ops:
  0.6 0.0 copy-start
  0.6 1.6 %copy-done = f32[64,8192]{1,0:T(8,128)S(1)} copy-done((f32[64,8192]{1,0:T(8,128)S(1)}, f32[64,8192]{1,0:T(8,128)}, u32[]{:S(2)}) %copy-start) | copy-done | bytes 2097176
  2.2 0.0 copy-start.1
  2.2 1.2 %copy-done.1 = bf16[64,8192]{1,0:T(8,128)(2,1)S(1)} copy-done((bf16[64,8192]{1,0:T(8,128)(2,1)S(1)}, bf16[64,8192]{1,0:T(8,128)(2,1)}, u32[]{:S(2)}) %copy-start.1) | copy-done | bytes 1048600
  3.4 0.0 copy-start.2
  3.5 0.7 copy-done.2
  4.1 7.6 %shard_map.58 = (f32[4,32,32,128]{3,2,1,0:T(8,128)S(1)}, f32[4,32,32,128]{3,2,1,0:T(8,128)S(1)}, f32[32,16,128]{2,1,0:T(8,128)S(1)}, f32[32,16,128]{2,1,0:T(8,12...) custom-call(f32[64,8192]{1,0:T(8,128)S(1)} %copy-done, ...), custom_call_target="tpu_custom_call" | custom-call | tf_op jit(solution)/shard_map/pallas_call | solution.py:486
  11.7 0.5 collective-permute-start
  12.2 5.0 %collective-permute-start.1 = (f32[2,32,8,128]{3,2,1,0:T(8,128)S(1)}, f32[2,32,8,128]{3,2,1,0:T(8,128)S(1)}, u32[]{:S(2)}, u32[]{:S(2)}) collective-permute-start(f32[2,32,8,128]{3,2,1,0:T(8,128)S(1)} %get-tuple-element.21), channel_id=1, source_target_pairs={{0,15},{1,0},{2,1},{3,2},{4,3},{5,4},{6,5},{7,6},{8,7},{9,8},{10,9... | collective-permute-start | bytes 786440 | tf_op jit(solution)/shard_map/ppermute | solution.py:498
  17.2 1.2 %collective-permute-start.2 = (f32[4,32,128]{2,1,0:T(8,128)S(1)}, f32[4,32,128]{2,1,0:T(8,128)S(1)}, u32[]{:S(2)}, u32[]{:S(2)}) collective-permute-start(f32[4,32,128]{2,1,0:T(8,128)S(1)} %get-tuple-element.22), channel_id=1, source_target_pairs={{0,8},{1,9},{2,10},{3,11},{4,12},{5,13},{6,14},{7,15},{8,0},{9,1},... | collective-permute-start | bytes 196616 | tf_op jit(solution)/shard_map/ppermute | solution.py:498
  18.4 0.0 collective-permute-start.3
  18.4 2.6 %collective-permute-start.4 = (f32[4,16,128]{2,1,0:T(8,128)S(1)}, f32[4,16,128]{2,1,0:T(8,128)S(1)}, u32[]{:S(2)}, u32[]{:S(2)}) collective-permute-start(f32[4,16,128]{2,1,0:T(8,128)S(1)} %get-tuple-element.24), channel_id=1, source_target_pairs={{0,7},{1,8},{2,9},{3,10},{4,11},{5,12},{6,13},{7,14},{8,15},{9,0},... | collective-permute-start | bytes 98312 | tf_op jit(solution)/shard_map/ppermute | solution.py:498
  21.1 0.5 shard_map.59.i_ref
  21.6 1.3 %collective-permute-done.3.corner_left = f32[4,16,128]{2,1,0:T(8,128)S(1)} collective-permute-done((f32[4,16,128]{2,1,0:T(8,128)S(1)}, f32[4,16,128]{2,1,0:T(8,128)S(1)}, u32[]{:S(2)}, u32[]{:S(2)}) %collective-permute-start.3) | collective-permute-done | bytes 32800 | tf_op jit(solution)/shard_map/ppermute | solution.py:498
  22.9 1.3 %collective-permute-done.4.corner_right = f32[4,16,128]{2,1,0:T(8,128)S(1)} collective-permute-done((f32[4,16,128]{2,1,0:T(8,128)S(1)}, f32[4,16,128]{2,1,0:T(8,128)S(1)}, u32[]{:S(2)}, u32[]{:S(2)}) %collective-permute-start.4) | collective-permute-done | bytes 32800 | tf_op jit(solution)/shard_map/ppermute | solution.py:498
  24.2 2.2 %collective-permute-done.2.polar_ref = f32[4,32,128]{2,1,0:T(8,128)S(1)} collective-permute-done((f32[4,32,128]{2,1,0:T(8,128)S(1)}, f32[4,32,128]{2,1,0:T(8,128)S(1)}, u32[]{:S(2)}, u32[]{:S(2)}) %collective-permute-start.2) | collective-permute-done | bytes 65568 | tf_op jit(solution)/shard_map/ppermute | solution.py:498
  26.3 0.0 collective-permute-done.from_left
  26.3 0.0 collective-permute-done.1.from_right
  26.4 15.8 %shard_map.60 = (f32[4,32,32,128]{3,2,1,0:T(8,128)S(1)}, f32[33,16,128]{2,1,0:T(8,128)S(1)}, f32[33,16,128]{2,1,0:T(8,128)S(1)}, f32[64,128]{1,0:T(8,128)S(1)}) custom-call(f32[4,32,32,128]{3,2,1,0:T(8,128)S(1)} %get-tuple-element.18.s_ref, f32[4,32,32,128]{3,2,1,0:T(8,128)S(1)} %get-tuple-element.19.d_ref, f32[4,32,32,128]{3,2,1,0:T(8,128)S(1)} %shard_map.59.i_ref, ...), custom_call_target="tpu_custom_call" | custom-call | tf_op jit(solution)/shard_map/pallas_call | solution.py:486
  42.2 0.2 collective-permute-start.5
  42.4 4.2 %collective-permute-start.6 = (f32[33,16,128]{2,1,0:T(8,128)S(1)}, f32[33,16,128]{2,1,0:T(8,128)S(1)}, u32[]{:S(2)}, u32[]{:S(2)}) collective-permute-start(f32[33,16,128]{2,1,0:T(8,128)S(1)} %get-tuple-element.27.s_low), channel_id=1, source_target_pairs={{0,15},{1,0},{2,1},{3,2},{4,3},{5,4},{6,5},{7,6},{8,7},{9,8},{10,9... | collective-permute-start | bytes 811016 | tf_op jit(solution)/shard_map/ppermute | solution.py:498
  46.7 0.0 collective-permute-start.7
  46.7 4.4 %collective-permute-start.8 = (f32[32,16,128]{2,1,0:T(8,128)S(1)}, f32[32,16,128]{2,1,0:T(8,128)S(1)}, u32[]{:S(2)}, u32[]{:S(2)}) collective-permute-start(f32[32,16,128]{2,1,0:T(8,128)S(1)} %get-tuple-element.29.e_low), channel_id=1, source_target_pairs={{0,15},{1,0},{2,1},{3,2},{4,3},{5,4},{6,5},{7,6},{8,7},{9,8},{10,9... | collective-permute-start | bytes 786440 | tf_op jit(solution)/shard_map/ppermute | solution.py:498
  51.1 6.8 %shard_map.61 = f32[64,8192]{1,0:T(8,128)} custom-call(f32[4,32,32,128]{3,2,1,0:T(8,128)S(1)} %get-tuple-element.25.r_ref), custom_call_target="tpu_custom_call" | custom-call | tf_op jit(solution)/shard_map/pallas_call | solution.py:486
  57.9 0.0 collective-permute-done.7.e_left
  57.9 0.0 collective-permute-done.8.e_right
  57.9 0.0 collective-permute-done.5.s_left
  57.9 0.0 collective-permute-done.6.s_right
  57.9 18.2 %shard_map.62 = (f32[16,2048]{1,0:T(8,128)}, f32[16,2048]{1,0:T(8,128)}) custom-call(f32[33,16,128]{2,1,0:T(8,128)S(1)} %collective-permute-done.5.s_left, f32[33,16,128]{2,1,0:T(8,128)S(1)} %get-tuple-element.27.s_low, f32[33,16,128]{2,1,0:T(8,128)S(1)} %get-tuple-element.26.s_high, f32[33,16,128]{2,1,0:T(8,128)S(1)} %collective-permute-done.6.s_right, ...), custom_call_target="tpu_custom_call" | custom-call | tf_op jit(solution)/shard_map/pallas_call | solution.py:486
Async XLA Ops:
  0.6 1.6 %copy-start = (f32[64,8192]{1,0:T(8,128)S(1)}, f32[64,8192]{1,0:T(8,128)}, u32[]{:S(2)}) copy-start(f32[64,8192]{1,0:T(8,128)} %right_ref.1) | copy-start | bytes 6291460
  2.2 1.2 %copy-start.1 = (bf16[64,8192]{1,0:T(8,128)(2,1)S(1)}, bf16[64,8192]{1,0:T(8,128)(2,1)}, u32[]{:S(2)}) copy-start(bf16[64,8192]{1,0:T(8,128)(2,1)} %weight_ref.1) | copy-start | bytes 3145732
  3.4 0.7 copy-start.2
  11.7 14.6 %collective-permute-start = (f32[2,32,8,128]{3,2,1,0:T(8,128)S(1)}, f32[2,32,8,128]{3,2,1,0:T(8,128)S(1)}, u32[]{:S(2)}, u32[]{:S(2)}) collective-permute-start(f32[2,32,8,128]{3,2,1,0:T(8,128)S(1)} %get-tuple-element.20), channel_id=1, source_target_pairs={{0,1},{1,2},{2,3},{3,4},{4,5},{5,6},{6,7},{7,8},{8,9},{9,10},{10,1... | collective-permute-start | bytes 786440 | tf_op jit(solution)/shard_map/ppermute | solution.py:498
  12.2 14.1 %collective-permute-start.1 = (f32[2,32,8,128]{3,2,1,0:T(8,128)S(1)}, f32[2,32,8,128]{3,2,1,0:T(8,128)S(1)}, u32[]{:S(2)}, u32[]{:S(2)}) collective-permute-start(f32[2,32,8,128]{3,2,1,0:T(8,128)S(1)} %get-tuple-element.21), channel_id=1, source_target_pairs={{0,15},{1,0},{2,1},{3,2},{4,3},{5,4},{6,5},{7,6},{8,7},{9,8},{10,9... | collective-permute-start | bytes 786440 | tf_op jit(solution)/shard_map/ppermute | solution.py:498
  17.2 9.1 %collective-permute-start.2 = (f32[4,32,128]{2,1,0:T(8,128)S(1)}, f32[4,32,128]{2,1,0:T(8,128)S(1)}, u32[]{:S(2)}, u32[]{:S(2)}) collective-permute-start(f32[4,32,128]{2,1,0:T(8,128)S(1)} %get-tuple-element.22), channel_id=1, source_target_pairs={{0,8},{1,9},{2,10},{3,11},{4,12},{5,13},{6,14},{7,15},{8,0},{9,1},... | collective-permute-start | bytes 196616 | tf_op jit(solution)/shard_map/ppermute | solution.py:498
  18.4 4.4 %collective-permute-start.3 = (f32[4,16,128]{2,1,0:T(8,128)S(1)}, f32[4,16,128]{2,1,0:T(8,128)S(1)}, u32[]{:S(2)}, u32[]{:S(2)}) collective-permute-start(f32[4,16,128]{2,1,0:T(8,128)S(1)} %get-tuple-element.23), channel_id=1, source_target_pairs={{0,9},{1,10},{2,11},{3,12},{4,13},{5,14},{6,15},{7,0},{8,1},{9,2},... | collective-permute-start | bytes 98312 | tf_op jit(solution)/shard_map/ppermute | solution.py:498
  18.4 5.7 %collective-permute-start.4 = (f32[4,16,128]{2,1,0:T(8,128)S(1)}, f32[4,16,128]{2,1,0:T(8,128)S(1)}, u32[]{:S(2)}, u32[]{:S(2)}) collective-permute-start(f32[4,16,128]{2,1,0:T(8,128)S(1)} %get-tuple-element.24), channel_id=1, source_target_pairs={{0,7},{1,8},{2,9},{3,10},{4,11},{5,12},{6,13},{7,14},{8,15},{9,0},... | collective-permute-start | bytes 98312 | tf_op jit(solution)/shard_map/ppermute | solution.py:498
  42.2 15.7 %collective-permute-start.5 = (f32[33,16,128]{2,1,0:T(8,128)S(1)}, f32[33,16,128]{2,1,0:T(8,128)S(1)}, u32[]{:S(2)}, u32[]{:S(2)}) collective-permute-start(f32[33,16,128]{2,1,0:T(8,128)S(1)} %get-tuple-element.26.s_high), channel_id=1, source_target_pairs={{0,1},{1,2},{2,3},{3,4},{4,5},{5,6},{6,7},{7,8},{8,9},{9,10},{10,1... | collective-permute-start | bytes 811016 | tf_op jit(solution)/shard_map/ppermute | solution.py:498
  42.4 15.5 %collective-permute-start.6 = (f32[33,16,128]{2,1,0:T(8,128)S(1)}, f32[33,16,128]{2,1,0:T(8,128)S(1)}, u32[]{:S(2)}, u32[]{:S(2)}) collective-permute-start(f32[33,16,128]{2,1,0:T(8,128)S(1)} %get-tuple-element.27.s_low), channel_id=1, source_target_pairs={{0,15},{1,0},{2,1},{3,2},{4,3},{5,4},{6,5},{7,6},{8,7},{9,8},{10,9... | collective-permute-start | bytes 811016 | tf_op jit(solution)/shard_map/ppermute | solution.py:498
  46.7 11.2 %collective-permute-start.7 = (f32[32,16,128]{2,1,0:T(8,128)S(1)}, f32[32,16,128]{2,1,0:T(8,128)S(1)}, u32[]{:S(2)}, u32[]{:S(2)}) collective-permute-start(f32[32,16,128]{2,1,0:T(8,128)S(1)} %get-tuple-element.28.e_high), channel_id=1, source_target_pairs={{0,1},{1,2},{2,3},{3,4},{4,5},{5,6},{6,7},{7,8},{8,9},{9,10},{10,1... | collective-permute-start | bytes 786440 | tf_op jit(solution)/shard_map/ppermute | solution.py:498
  46.7 11.2 %collective-permute-start.8 = (f32[32,16,128]{2,1,0:T(8,128)S(1)}, f32[32,16,128]{2,1,0:T(8,128)S(1)}, u32[]{:S(2)}, u32[]{:S(2)}) collective-permute-start(f32[32,16,128]{2,1,0:T(8,128)S(1)} %get-tuple-element.29.e_low), channel_id=1, source_target_pairs={{0,15},{1,0},{2,1},{3,2},{4,3},{5,4},{6,5},{7,6},{8,7},{9,8},{10,9... | collective-permute-start | bytes 786440 | tf_op jit(solution)/shard_map/ppermute | solution.py:498

commit v2 on v1

--- a/solution.py
+++ b/solution.py
@@ -10,6 +10,8 @@
 TILE = 32
 SEAM_SCALE = 0.1
 LANES = 128
+GROUPS = 4
+BATCH = 4
 F32 = jnp.float32
 BF16 = jnp.bfloat16
 
@@ -36,6 +38,18 @@
 
 def col_next(x):
     return pltpu.roll(x, x.shape[0] - 1, 0)
+
+
+def loop(count, body, carry=0, unroll=4):
+    def steps(block, carry):
+        for i in range(unroll):
+            carry = body(block * unroll + i, carry)
+        return carry
+
+    carry = lax.fori_loop(0, count // unroll, steps, carry)
+    for t in range(count - count % unroll, count):
+        carry = body(t, carry)
+    return carry
 
 
 def splitter():
@@ -57,12 +71,14 @@
     return jnp.where(place == b, 1.0, 0.0).astype(BF16)
 
 
-def moved(x, matrix):
+def moved(x, matrix, exact=None):
+    rows = x.shape[0]
     high = x.astype(BF16)
     low = (x - high.astype(F32)).astype(BF16)
-    return jnp.dot(high, matrix, preferred_element_type=F32) + jnp.dot(
-        low, matrix, preferred_element_type=F32
-    )
+    terms = [high, low] if exact is None else [high, low, exact]
+    out = jnp.dot(jnp.concatenate(terms, 0), matrix, preferred_element_type=F32)
+    both = out[:rows] + out[rows : 2 * rows]
+    return both if exact is None else (both, out[2 * rows :])
 
 
 def quarters_of(parts, temp):
@@ -75,9 +91,21 @@
 def prepare_kernel(
     right_ref, weight_ref, flag_ref,
     s_ref, d_ref, low_ref, high_ref, to_left, to_right, polar_ref, corner_low, corner_high,
-    temp_s, temp_d, scale_ref,
+    right_buf, weight_buf, temp_s, temp_d, scale_ref, sems,
 ):
     tiles, rows = s_ref.shape[1], s_ref.shape[2]
+    chunk = right_ref.shape[1] // GROUPS
+    copies = []
+    for group in range(GROUPS):
+        part = pl.ds(group * chunk, chunk)
+        copies.append(
+            [
+                pltpu.make_async_copy(src.at[:, part], dst.at[:, part], sems.at[i, group])
+                for i, (src, dst) in enumerate(((right_ref, right_buf), (weight_ref, weight_buf)))
+            ]
+        )
+        for copy in copies[group]:
+            copy.start()
     flag_cols = flag_ref.shape[0]
     flag_lats = flag_ref.shape[1]
     per_tile = rows // flag_cols
@@ -105,12 +133,7 @@
             packed = jnp.where(sub // 2 == q, moved_q, packed)
         return packed
 
-    def body(c, _):
-        where = pl.ds(pl.multiple_of(c * 256, 256), 256)
-        source = quarters_of(moved(right_ref[:, where], matrix), temp_s)
-        weight = quarters_of(
-            jnp.dot(weight_ref[:, where], matrix, preferred_element_type=F32), temp_d
-        )
+    def piece(c, source, weight):
         scales = scale_ref[c]
         scale = jnp.concatenate(
             [jnp.broadcast_to(scales[i : i + 1], (per_tile, LANES)) for i in range(flag_cols)], 0
@@ -136,9 +159,24 @@
         second = pltpu.roll(gs[0] / gd[0], 5, 0)
         to_left[0, c] = jnp.where(sub == 7, first, edge(gs, 0, lambda q: 2 * q))
         to_left[1, c] = jnp.where(sub == 7, second, edge(gd, 0, lambda q: 2 * q))
-        return 0
-
-    lax.fori_loop(0, tiles, body, 0)
+
+    columns = right_ref.shape[0]
+    for group in range(GROUPS):
+        for copy in copies[group]:
+            copy.wait()
+        for batch in range(tiles // GROUPS // BATCH):
+            start = group * (tiles // GROUPS) + batch * BATCH
+            lanes = [slice((start + i) * 256, (start + i + 1) * 256) for i in range(BATCH)]
+            source = jnp.concatenate([right_buf[:, w] for w in lanes], 0)
+            weight = jnp.concatenate([weight_buf[:, w] for w in lanes], 0)
+            source, weight = moved(source, matrix, weight)
+            for i in range(BATCH):
+                here = slice(i * columns, (i + 1) * columns)
+                piece(
+                    start + i,
+                    quarters_of(source[here], temp_s.at[i]),
+                    quarters_of(weight[here], temp_d.at[i]),
+                )
 
     a = lax.broadcasted_iota(jnp.int32, (LANES, LANES), 0)
     b = lax.broadcasted_iota(jnp.int32, (LANES, LANES), 1)
@@ -162,23 +200,23 @@
             i_ref[q, t] = 1.0 / d_ref[q, t]
         return 0
 
-    lax.fori_loop(0, d_ref.shape[1], body, 0)
+    loop(d_ref.shape[1], body)
 
 
 def half_sweep(v, load_s, load_i, tiles, red):
-    rows = v.shape[2]
+    rows = v[0].shape[1]
     lane = lane_ids(rows)
     y, z, qa, qb = (1, 2, 0, 3) if red else (3, 0, 2, 1)
     col_a, col_b = (col_prev, col_next) if red else (col_next, col_prev)
 
     def beside_virtual(q):
         ns, we = q ^ 1, q ^ 2
-        here = v[ns, tiles]
+        here = v[ns][tiles]
         if q % 2 == 0:
-            lat = jnp.where(lane == 0, roll_up(v[ns, tiles - 1]), roll_up(here))
+            lat = jnp.where(lane == 0, roll_up(v[ns][tiles - 1]), roll_up(here))
         else:
-            lat = jnp.where(lane == LANES - 1, roll_down(v[ns, 0]), roll_down(here))
-        cols = v[we, tiles]
+            lat = jnp.where(lane == LANES - 1, roll_down(v[ns][0]), roll_down(here))
+        cols = v[we][tiles]
         return (here + lat) + (cols + (col_prev if q < 2 else col_next)(cols))
 
     held = [
@@ -187,54 +225,54 @@
 
     def body(t, carry):
         y_before, z_here = carry
-        vy, vz = v[y, t], v[z, t]
+        vy, vz = v[y][t], v[z][t]
         y_here = roll_up(vy)
-        z_after = roll_down(v[z, t + 1])
+        z_after = roll_down(v[z][t + 1])
         lat_a = vy + jnp.where(lane == 0, y_before, y_here)
         lat_b = vz + jnp.where(lane == LANES - 1, z_after, z_here)
-        v[qa, t] = (load_s(qa, t) + (lat_a + (vz + col_a(vz)))) * load_i(qa, t)
-        v[qb, t] = (load_s(qb, t) + (lat_b + (vy + col_b(vy)))) * load_i(qb, t)
+        v[qa][t] = (load_s(qa, t) + (lat_a + (vz + col_a(vz)))) * load_i(qa, t)
+        v[qb][t] = (load_s(qb, t) + (lat_b + (vy + col_b(vy)))) * load_i(qb, t)
         return y_here, z_after
 
-    lax.fori_loop(0, tiles, body, (roll_up(v[y, tiles]), roll_down(v[z, 0])))
+    loop(tiles, body, (roll_up(v[y][tiles]), roll_down(v[z][0])))
     for q, value in held:
-        v[q, tiles] = value
+        v[q][tiles] = value
 
 
 def smooth(v, load_s, load_i, tiles):
-    rows = v.shape[2]
+    rows = v[0].shape[1]
     zeros = jnp.zeros((rows, LANES), F32)
 
     def first(t, _):
         for q in (0, 3):
-            v[q, t] = load_s(q, t) * load_i(q, t)
-        return 0
-
-    lax.fori_loop(0, tiles, first, 0)
+            v[q][t] = load_s(q, t) * load_i(q, t)
+        return 0
+
+    loop(tiles, first)
     for q in (1, 2):
-        v[q, 0] = zeros
-        v[q, tiles - 1] = zeros
-        v[q, tiles] = load_s(q, tiles) * load_i(q, tiles)
-        v[3 * (q - 1), tiles] = zeros
+        v[q][0] = zeros
+        v[q][tiles - 1] = zeros
+        v[q][tiles] = load_s(q, tiles) * load_i(q, tiles)
+        v[3 * (q - 1)][tiles] = zeros
     half_sweep(v, load_s, load_i, tiles, False)
     half_sweep(v, load_s, load_i, tiles, True)
     half_sweep(v, load_s, load_i, tiles, False)
 
 
 def residual_and_columns(v, load_s, load_d, tiles, c_ref, keep):
-    rows = v.shape[2]
+    rows = v[0].shape[1]
     lane = lane_ids(rows)
 
     def body(t, _):
         before = jnp.where(t == 0, tiles, t - 1)
         after = jnp.where(t == tiles, 0, t + 1)
-        x = [v[q, t] for q in range(4)]
+        x = [v[q][t] for q in range(4)]
 
         def north(q):
-            return jnp.where(lane == 0, roll_up(v[q, before]), roll_up(x[q]))
+            return jnp.where(lane == 0, roll_up(v[q][before]), roll_up(x[q]))
 
         def south(q):
-            return jnp.where(lane == LANES - 1, roll_down(v[q, after]), roll_down(x[q]))
+            return jnp.where(lane == LANES - 1, roll_down(v[q][after]), roll_down(x[q]))
 
         beside = [
             (x[1] + north(1)) + (x[2] + col_prev(x[2])),
@@ -248,7 +286,7 @@
         c_ref[1, t] = (col_prev(r[3]) + col_next(r[1])) + 3.0 * (r[1] + r[3])
         return 0
 
-    lax.fori_loop(0, tiles + 1, body, 0)
+    loop(tiles + 1, body)
 
 
 def restricted(c_ref, t, tiles):
@@ -264,8 +302,9 @@
 def fine_kernel(
     s_ref, d_ref, i_ref, from_left, from_right, polar_ref, corner_left, corner_right,
     r_ref, low_ref, high_ref, screen_virtual,
-    v, c_ref, hs, hd, hi, ps, pd, pi,
+    v0, v1, v2, v3, c_ref, hs, hd, hi, ps, pd, pi,
 ):
+    v = [v0, v1, v2, v3]
     tiles, rows = s_ref.shape[1], s_ref.shape[2]
     sub = row_ids(8)
 
@@ -292,7 +331,7 @@
             hi[q, t] = 1.0 / diag
         return 0
 
-    lax.fori_loop(0, tiles, halo, 0)
+    loop(tiles, halo)
 
     def unpacked(x):
         lane = lane_ids(x.shape[0])
@@ -329,14 +368,14 @@
     smooth(v, loader(s_ref, hs, ps), loader(i_ref, hi, pi), tiles)
 
     def residual(t, before, after, own_s, own_d):
-        lane = lane_ids(v.shape[2])
-        x = [v[q, t] for q in range(4)]
+        lane = lane_ids(v[0].shape[1])
+        x = [v[q][t] for q in range(4)]
 
         def north(q):
-            return jnp.where(lane == 0, roll_up(v[q, before]), roll_up(x[q]))
+            return jnp.where(lane == 0, roll_up(v[q][before]), roll_up(x[q]))
 
         def south(q):
-            return jnp.where(lane == LANES - 1, roll_down(v[q, after]), roll_down(x[q]))
+            return jnp.where(lane == LANES - 1, roll_down(v[q][after]), roll_down(x[q]))
 
         beside = [
             (x[1] + north(1)) + (x[2] + col_prev(x[2])),
@@ -362,7 +401,7 @@
             r_ref[q, t] = r[q][:rows]
         return 0
 
-    lax.fori_loop(0, tiles, main, 0)
+    loop(tiles, main)
     residual(tiles, tiles - 1, 0, [ps[q] for q in range(4)], [pd[q] for q in range(4)])
 
     def coarse(t, _):
@@ -371,30 +410,42 @@
         high_ref[t] = value[half:rows]
         return 0
 
-    lax.fori_loop(0, tiles + 1, coarse, 0)
-
-
-def merge_kernel(r_ref, out_ref, temp):
+    loop(tiles + 1, coarse)
+
+
+def merge_kernel(r_ref, out_ref, temp, out_buf, sems):
     tiles = r_ref.shape[1]
     rows = r_ref.shape[2]
     matrix = merger()
-
-    def body(c, _):
-        for pr in (0, 1):
-            for pc in (0, 1):
-                temp[pr, pl.ds(pc, rows, 2), :] = r_ref[2 * pc + pr, c]
-        both = jnp.concatenate([temp[0], temp[1]], 1)
-        out_ref[:, pl.ds(pl.multiple_of(c * 256, 256), 256)] = moved(both, matrix)
-        return 0
-
-    lax.fori_loop(0, tiles, body, 0)
+    chunk = out_ref.shape[1] // GROUPS
+    copies = []
+    for group in range(GROUPS):
+        for batch in range(tiles // GROUPS // BATCH):
+            start = group * (tiles // GROUPS) + batch * BATCH
+            both = []
+            for i in range(BATCH):
+                for pr in (0, 1):
+                    for pc in (0, 1):
+                        temp[i, pr, pl.ds(pc, rows, 2), :] = r_ref[2 * pc + pr, start + i]
+                both.append(jnp.concatenate([temp[i, 0], temp[i, 1]], 1))
+            out = moved(jnp.concatenate(both, 0), matrix)
+            for i in range(BATCH):
+                where = slice((start + i) * 256, (start + i + 1) * 256)
+                out_buf[:, where] = out[2 * rows * i : 2 * rows * (i + 1)]
+        part = pl.ds(group * chunk, chunk)
+        copy = pltpu.make_async_copy(out_buf.at[:, part], out_ref.at[:, part], sems.at[group])
+        copy.start()
+        copies.append(copy)
+    for copy in copies:
+        copy.wait()
 
 
 def coarse_kernel(
     s_left, s_low, s_high, s_right, e_left, e_low, e_high, e_right, e_virtual,
     solution_ref, residual_ref,
-    s, d, inv, v, c_ref, temp, s2, d2, i2, v2,
+    s, d, inv, qv0, qv1, qv2, qv3, c_ref, temp, s2, d2, i2, v2,
 ):
+    v = [qv0, qv1, qv2, qv3]
     tiles = s.shape[1] - 1
     rows = s.shape[2]
     matrix = splitter()
@@ -410,23 +461,31 @@
         d2[t] = 4.0 + total
         i2[t] = 1.0 / (4.0 + total)
 
-    def split(c, _):
-        def wide(refs):
+    def split(batch, _):
+        def wide(refs, c):
             return jnp.concatenate(
                 [jnp.concatenate([ref[2 * c + h] for ref in refs], 0) for h in (0, 1)], 1
             )
 
-        source = quarters_of(moved(wide((s_left, s_low, s_high, s_right)), matrix), temp)
-        screen = quarters_of(moved(wide((e_left, e_low, e_high, e_right)), matrix), temp)
-        fill(c, source, screen)
-        return 0
-
-    lax.fori_loop(0, tiles, split, 0)
+        both = []
+        for i in range(BATCH):
+            both.append(wide((s_left, s_low, s_high, s_right), batch * BATCH + i))
+            both.append(wide((e_left, e_low, e_high, e_right), batch * BATCH + i))
+        out = moved(jnp.concatenate(both, 0), matrix)
+        size = 2 * rows
+        for i in range(BATCH):
+            at = 2 * i * size
+            source = quarters_of(out[at : at + size], temp.at[2 * i])
+            screen = quarters_of(out[at + size : at + 2 * size], temp.at[2 * i + 1])
+            fill(batch * BATCH + i, source, screen)
+        return 0
+
+    loop(tiles // BATCH, split, unroll=1)
     last = 2 * tiles
     matrix = virtual_splitter()
     source = jnp.concatenate([s_left[last], s_low[last], s_high[last], s_right[last]], 0)
-    source = quarters_of(moved(source, matrix), temp)
-    screen = quarters_of(moved(e_virtual[...], matrix), temp)
+    source = quarters_of(moved(source, matrix), temp.at[0])
+    screen = quarters_of(moved(e_virtual[...], matrix), temp.at[1])
     fill(tiles, source, screen)
 
     smooth(v, lambda q, t: s[q, t], lambda q, t: inv[q, t], tiles)
@@ -443,7 +502,7 @@
         v2[t] = jnp.where(even, value * i2[t], 0.0)
         return 0
 
-    lax.fori_loop(0, tiles, start, 0)
+    loop(tiles, start)
     value = restricted(c_ref, tiles, tiles)
     s2[tiles] = value
     v2[tiles] = jnp.where(even, 0.0, value * i2[tiles])
@@ -464,7 +523,7 @@
             v2[t] = relaxed(t, jnp.where(t == 0, tiles, t - 1), t + 1, mask)
             return 0
 
-        lax.fori_loop(0, tiles, sweep, 0)
+        loop(tiles, sweep)
         v2[tiles] = held
 
     own = solution_ref.shape[0]
@@ -478,17 +537,23 @@
         residual_ref[:, where] = r[skip : skip + own]
         return 0
 
-    lax.fori_loop(0, tiles, finish, 0)
-
-
-def call(kernel, out_shapes, scratch, *args):
-    vmem = pl.BlockSpec(memory_space=pltpu.VMEM)
+    loop(tiles, finish)
+
+
+VMEM = pl.BlockSpec(memory_space=pltpu.VMEM)
+HBM = pl.BlockSpec(memory_space=pltpu.HBM)
+
+
+def call(kernel, out_shapes, scratch, *args, sems=None, far_in=0, far_out=0):
+    scratch = [pltpu.VMEM(x, F32) if isinstance(x, tuple) else x for x in scratch]
+    if sems is not None:
+        scratch.append(pltpu.SemaphoreType.DMA(sems))
     return pl.pallas_call(
         kernel,
         out_shape=[jax.ShapeDtypeStruct(shape, F32) for shape in out_shapes],
-        in_specs=[vmem] * len(args),
-        out_specs=[vmem] * len(out_shapes),
-        scratch_shapes=[pltpu.VMEM(shape, F32) for shape in scratch],
+        in_specs=[HBM] * far_in + [VMEM] * (len(args) - far_in),
+        out_specs=[HBM] * far_out + [VMEM] * (len(out_shapes) - far_out),
+        scratch_shapes=scratch,
         compiler_params=pltpu.CompilerParams(vmem_limit_bytes=40 * 2**20),
     )(*args)
 
@@ -509,8 +574,11 @@
         prepare_kernel,
         [quarters, quarters, part, part, (2, tiles, 8, LANES), (2, tiles, 8, LANES)]
         + [(4, rows, LANES), (4, half, LANES), (4, half, LANES)],
-        [(2, columns, LANES), (2, columns, LANES), (tiles, 8, LANES)],
+        [(columns, height), pltpu.VMEM((columns, height), BF16)]
+        + [(BATCH, 2, columns, LANES)] * 2
+        + [(tiles, 8, LANES)],
         right_side, texel_weight, seam_flags,
+        sems=(2, GROUPS), far_in=2,
     )
     from_left = shifted(to_right, 1)
     from_right = shifted(to_left, -1)
@@ -527,18 +595,24 @@
     r, s_low, s_high, e_virtual = call(
         fine_kernel,
         [quarters, part, part, (2 * rows, LANES)],
-        [(4, tiles + 1, wide, LANES), (2, tiles + 1, wide, LANES), halo, halo, halo, own, own, own],
+        [(tiles + 1, wide, LANES)] * 4 + [(2, tiles + 1, wide, LANES), halo, halo, halo, own, own, own],
         s, d, inverse, from_left, from_right, polar, corner_left, corner_right,
     )
     s_left = shifted(s_high, 1)
     s_right = shifted(s_low, -1)
-    (fine_residual,) = call(merge_kernel, [(columns, height)], [(2, columns, LANES)], r)
+    (fine_residual,) = call(
+        merge_kernel,
+        [(columns, height)],
+        [(BATCH, 2, columns, LANES), (columns, height)],
+        r,
+        sems=(GROUPS,), far_out=1,
+    )
     coarse = (4, tiles // 2 + 1, rows, LANES)
     single = coarse[1:]
     solution_2, residual_2 = call(
         coarse_kernel,
         [(columns // 4, height // 4)] * 2,
-        [coarse, coarse, coarse, coarse, (2,) + single, (2, columns, LANES)]
+        [coarse, coarse, coarse, single, single, single, single, (2,) + single, (2 * BATCH, 2, columns, LANES)]
         + [single, single, single, single],
         s_left, s_low, s_high, s_right, e_left, e_low, e_high, e_right, e_virtual,
     )

time: 76.4 us -> 53.8 us (0.70)
  the two profiles are of different devices: /device:TPU:0 before, /device:TPU:1 now
where the time goes in v2:
time: 53.8 us; the launch traced here: 53.5 us
  Pallas kernels  22.1 us (41%)
  waiting for transfers between devices  14.3 us (27%)
  starting transfers between devices  12.9 us (24%)
  local copies, waits for them, and re-layouts  3.49 us (6%)
  between operations  0.69 us (1%)
    pallas_call x5, Pallas kernels, call(): pl.pallas_call(kernel, out_shape=[jax.ShapeDtypeStruct(shape, F32) for sh...  22.1 us
    ppermute x9, waiting for transfers between devices, shifted(): return lax.ppermute(x, 'lon', [(i, (i + by) % count) for i in range(count)])  14.3 us
    ppermute x9, starting transfers between devices, shifted(): return lax.ppermute(x, 'lon', [(i, (i + by) % count) for i in range(count)])  12.9 us
    unnamed x6, local copies, waits for them, and re-layouts  3.49 us
  transfers between devices with their start and end apart: 9, of which 3 were waited for; matrix products, arithmetic and copies ran while one was open for 0% of the time, Pallas kernels for 4%

profile of v2, /device:TPU:1, one launch (start us, length us, event | category | flops | bytes accessed | tf_op | source)
XLA Modules:
  0.0 53.5 jit_solution(16906152567000620264)
XLA Ops:
  0.6 0.0 copy-start
  0.6 1.6 %copy-done = f32[64,8192]{1,0:T(8,128)S(1)} copy-done((f32[64,8192]{1,0:T(8,128)S(1)}, f32[64,8192]{1,0:T(8,128)}, u32[]{:S(2)}) %copy-start) | copy-done | bytes 2097176
  2.2 0.0 copy-start.1
  2.2 1.2 %copy-done.1 = bf16[64,8192]{1,0:T(8,128)(2,1)S(1)} copy-done((bf16[64,8192]{1,0:T(8,128)(2,1)S(1)}, bf16[64,8192]{1,0:T(8,128)(2,1)}, u32[]{:S(2)}) %copy-start.1) | copy-done | bytes 1048600
  3.4 0.0 copy-start.2
  3.5 0.7 %copy-done.2 = s32[2,256]{1,0:T(2,128)S(1)} copy-done((s32[2,256]{1,0:T(2,128)S(1)}, s32[2,256]{1,0:T(2,128)}, u32[]{:S(2)}) %copy-start.2) | copy-done | bytes 2072
  4.1 2.7 %shard_map.58 = (f32[4,32,32,128]{3,2,1,0:T(8,128)S(1)}, f32[4,32,32,128]{3,2,1,0:T(8,128)S(1)}, f32[32,16,128]{2,1,0:T(8,128)S(1)}, f32[32,16,128]{2,1,0:T(8,12...) custom-call(f32[64,8192]{1,0:T(8,128)S(1)} %copy-done, ...), custom_call_target="tpu_custom_call" | custom-call | tf_op jit(solution)/shard_map/pallas_call | solution.py:551
  6.8 2.6 %collective-permute-start = (f32[2,32,8,128]{3,2,1,0:T(8,128)S(1)}, f32[2,32,8,128]{3,2,1,0:T(8,128)S(1)}, u32[]{:S(2)}, u32[]{:S(2)}) collective-permute-start(f32[2,32,8,128]{3,2,1,0:T(8,128)S(1)} %get-tuple-element.20), channel_id=1, source_target_pairs={{0,1},{1,2},{2,3},{3,4},{4,5},{5,6},{6,7},{7,8},{8,9},{9,10},{10,1... | collective-permute-start | bytes 786440 | tf_op jit(solution)/shard_map/ppermute | solution.py:563
  9.5 0.0 collective-permute-start.1
  9.5 2.3 %collective-permute-start.2 = (f32[4,32,128]{2,1,0:T(8,128)S(1)}, f32[4,32,128]{2,1,0:T(8,128)S(1)}, u32[]{:S(2)}, u32[]{:S(2)}) collective-permute-start(f32[4,32,128]{2,1,0:T(8,128)S(1)} %get-tuple-element.22), channel_id=1, source_target_pairs={{0,8},{1,9},{2,10},{3,11},{4,12},{5,13},{6,14},{7,15},{8,0},{9,1},... | collective-permute-start | bytes 196616 | tf_op jit(solution)/shard_map/ppermute | solution.py:563
  11.8 1.8 %collective-permute-start.3 = (f32[4,16,128]{2,1,0:T(8,128)S(1)}, f32[4,16,128]{2,1,0:T(8,128)S(1)}, u32[]{:S(2)}, u32[]{:S(2)}) collective-permute-start(f32[4,16,128]{2,1,0:T(8,128)S(1)} %get-tuple-element.23), channel_id=1, source_target_pairs={{0,9},{1,10},{2,11},{3,12},{4,13},{5,14},{6,15},{7,0},{8,1},{9,2},... | collective-permute-start | bytes 98312 | tf_op jit(solution)/shard_map/ppermute | solution.py:563
  13.6 1.4 %collective-permute-start.4 = (f32[4,16,128]{2,1,0:T(8,128)S(1)}, f32[4,16,128]{2,1,0:T(8,128)S(1)}, u32[]{:S(2)}, u32[]{:S(2)}) collective-permute-start(f32[4,16,128]{2,1,0:T(8,128)S(1)} %get-tuple-element.24), channel_id=1, source_target_pairs={{0,7},{1,8},{2,9},{3,10},{4,11},{5,12},{6,13},{7,14},{8,15},{9,0},... | collective-permute-start | bytes 98312 | tf_op jit(solution)/shard_map/ppermute | solution.py:563
  15.0 0.3 shard_map.59.i_ref
  15.3 5.9 %collective-permute-done.3.corner_left = f32[4,16,128]{2,1,0:T(8,128)S(1)} collective-permute-done((f32[4,16,128]{2,1,0:T(8,128)S(1)}, f32[4,16,128]{2,1,0:T(8,128)S(1)}, u32[]{:S(2)}, u32[]{:S(2)}) %collective-permute-start.3) | collective-permute-done | bytes 32800 | tf_op jit(solution)/shard_map/ppermute | solution.py:563
  21.2 0.0 collective-permute-done.4.corner_right
  21.2 0.0 collective-permute-done.2.polar_ref
  21.2 0.0 collective-permute-done.from_left
  21.2 0.0 collective-permute-done.1.from_right
  21.2 7.0 %shard_map.60 = (f32[4,32,32,128]{3,2,1,0:T(8,128)S(1)}, f32[33,16,128]{2,1,0:T(8,128)S(1)}, f32[33,16,128]{2,1,0:T(8,128)S(1)}, f32[64,128]{1,0:T(8,128)S(1)}) custom-call(f32[4,32,32,128]{3,2,1,0:T(8,128)S(1)} %get-tuple-element.18.s_ref, f32[4,32,32,128]{3,2,1,0:T(8,128)S(1)} %get-tuple-element.19.d_ref, f32[4,32,32,128]{3,2,1,0:T(8,128)S(1)} %shard_map.59.i_ref, ...), custom_call_target="tpu_custom_call" | custom-call | tf_op jit(solution)/shard_map/pallas_call | solution.py:551
  28.2 0.6 %collective-permute-start.5 = (f32[33,16,128]{2,1,0:T(8,128)S(1)}, f32[33,16,128]{2,1,0:T(8,128)S(1)}, u32[]{:S(2)}, u32[]{:S(2)}) collective-permute-start(f32[33,16,128]{2,1,0:T(8,128)S(1)} %get-tuple-element.26.s_high), channel_id=1, source_target_pairs={{0,1},{1,2},{2,3},{3,4},{4,5},{5,6},{6,7},{7,8},{8,9},{9,10},{10,1... | collective-permute-start | bytes 811016 | tf_op jit(solution)/shard_map/ppermute | solution.py:563
  28.8 0.0 collective-permute-start.6
  28.8 1.7 %collective-permute-start.7 = (f32[32,16,128]{2,1,0:T(8,128)S(1)}, f32[32,16,128]{2,1,0:T(8,128)S(1)}, u32[]{:S(2)}, u32[]{:S(2)}) collective-permute-start(f32[32,16,128]{2,1,0:T(8,128)S(1)} %get-tuple-element.28.e_high), channel_id=1, source_target_pairs={{0,1},{1,2},{2,3},{3,4},{4,5},{5,6},{6,7},{7,8},{8,9},{9,10},{10,1... | collective-permute-start | bytes 786440 | tf_op jit(solution)/shard_map/ppermute | solution.py:563
  30.6 2.5 %collective-permute-start.8 = (f32[32,16,128]{2,1,0:T(8,128)S(1)}, f32[32,16,128]{2,1,0:T(8,128)S(1)}, u32[]{:S(2)}, u32[]{:S(2)}) collective-permute-start(f32[32,16,128]{2,1,0:T(8,128)S(1)} %get-tuple-element.29.e_low), channel_id=1, source_target_pairs={{0,15},{1,0},{2,1},{3,2},{4,3},{5,4},{6,5},{7,6},{8,7},{9,8},{10,9... | collective-permute-start | bytes 786440 | tf_op jit(solution)/shard_map/ppermute | solution.py:563
  33.0 1.8 %shard_map.61 = f32[64,8192]{1,0:T(8,128)} custom-call(f32[4,32,32,128]{3,2,1,0:T(8,128)S(1)} %get-tuple-element.25.r_ref), custom_call_target="tpu_custom_call" | custom-call | tf_op jit(solution)/shard_map/pallas_call | solution.py:551
  34.8 5.9 %collective-permute-done.7.e_left = f32[32,16,128]{2,1,0:T(8,128)S(1)} collective-permute-done((f32[32,16,128]{2,1,0:T(8,128)S(1)}, f32[32,16,128]{2,1,0:T(8,128)S(1)}, u32[]{:S(2)}, u32[]{:S(2)}) %collective-permute-start.7) | collective-permute-done | bytes 262176 | tf_op jit(solution)/shard_map/ppermute | solution.py:563
  40.8 2.5 %collective-permute-done.8.e_right = f32[32,16,128]{2,1,0:T(8,128)S(1)} collective-permute-done((f32[32,16,128]{2,1,0:T(8,128)S(1)}, f32[32,16,128]{2,1,0:T(8,128)S(1)}, u32[]{:S(2)}, u32[]{:S(2)}) %collective-permute-start.8) | collective-permute-done | bytes 262176 | tf_op jit(solution)/shard_map/ppermute | solution.py:563
  43.2 0.0 collective-permute-done.5.s_left
  43.2 0.0 collective-permute-done.6.s_right
  43.2 10.3 %shard_map.62 = (f32[16,2048]{1,0:T(8,128)}, f32[16,2048]{1,0:T(8,128)}) custom-call(f32[33,16,128]{2,1,0:T(8,128)S(1)} %collective-permute-done.5.s_left, f32[33,16,128]{2,1,0:T(8,128)S(1)} %get-tuple-element.27.s_low, f32[33,16,128]{2,1,0:T(8,128)S(1)} %get-tuple-element.26.s_high, f32[33,16,128]{2,1,0:T(8,128)S(1)} %collective-permute-done.6.s_right, ...), custom_call_target="tpu_custom_call" | custom-call | tf_op jit(solution)/shard_map/pallas_call | solution.py:551
Async XLA Ops:
  0.6 1.6 %copy-start = (f32[64,8192]{1,0:T(8,128)S(1)}, f32[64,8192]{1,0:T(8,128)}, u32[]{:S(2)}) copy-start(f32[64,8192]{1,0:T(8,128)} %right_ref.1) | copy-start | bytes 6291460
  2.2 1.2 %copy-start.1 = (bf16[64,8192]{1,0:T(8,128)(2,1)S(1)}, bf16[64,8192]{1,0:T(8,128)(2,1)}, u32[]{:S(2)}) copy-start(bf16[64,8192]{1,0:T(8,128)(2,1)} %weight_ref.1) | copy-start | bytes 3145732
  3.4 0.7 %copy-start.2 = (s32[2,256]{1,0:T(2,128)S(1)}, s32[2,256]{1,0:T(2,128)}, u32[]{:S(2)}) copy-start(s32[2,256]{1,0:T(2,128)} %flag_ref.1) | copy-start | bytes 6148
  6.8 14.4 %collective-permute-start = (f32[2,32,8,128]{3,2,1,0:T(8,128)S(1)}, f32[2,32,8,128]{3,2,1,0:T(8,128)S(1)}, u32[]{:S(2)}, u32[]{:S(2)}) collective-permute-start(f32[2,32,8,128]{3,2,1,0:T(8,128)S(1)} %get-tuple-element.20), channel_id=1, source_target_pairs={{0,1},{1,2},{2,3},{3,4},{4,5},{5,6},{6,7},{7,8},{8,9},{9,10},{10,1... | collective-permute-start | bytes 786440 | tf_op jit(solution)/shard_map/ppermute | solution.py:563
  9.5 11.7 %collective-permute-start.1 = (f32[2,32,8,128]{3,2,1,0:T(8,128)S(1)}, f32[2,32,8,128]{3,2,1,0:T(8,128)S(1)}, u32[]{:S(2)}, u32[]{:S(2)}) collective-permute-start(f32[2,32,8,128]{3,2,1,0:T(8,128)S(1)} %get-tuple-element.21), channel_id=1, source_target_pairs={{0,15},{1,0},{2,1},{3,2},{4,3},{5,4},{6,5},{7,6},{8,7},{9,8},{10,9... | collective-permute-start | bytes 786440 | tf_op jit(solution)/shard_map/ppermute | solution.py:563
  9.5 11.7 %collective-permute-start.2 = (f32[4,32,128]{2,1,0:T(8,128)S(1)}, f32[4,32,128]{2,1,0:T(8,128)S(1)}, u32[]{:S(2)}, u32[]{:S(2)}) collective-permute-start(f32[4,32,128]{2,1,0:T(8,128)S(1)} %get-tuple-element.22), channel_id=1, source_target_pairs={{0,8},{1,9},{2,10},{3,11},{4,12},{5,13},{6,14},{7,15},{8,0},{9,1},... | collective-permute-start | bytes 196616 | tf_op jit(solution)/shard_map/ppermute | solution.py:563
  11.8 9.4 %collective-permute-start.3 = (f32[4,16,128]{2,1,0:T(8,128)S(1)}, f32[4,16,128]{2,1,0:T(8,128)S(1)}, u32[]{:S(2)}, u32[]{:S(2)}) collective-permute-start(f32[4,16,128]{2,1,0:T(8,128)S(1)} %get-tuple-element.23), channel_id=1, source_target_pairs={{0,9},{1,10},{2,11},{3,12},{4,13},{5,14},{6,15},{7,0},{8,1},{9,2},... | collective-permute-start | bytes 98312 | tf_op jit(solution)/shard_map/ppermute | solution.py:563
  13.6 7.6 %collective-permute-start.4 = (f32[4,16,128]{2,1,0:T(8,128)S(1)}, f32[4,16,128]{2,1,0:T(8,128)S(1)}, u32[]{:S(2)}, u32[]{:S(2)}) collective-permute-start(f32[4,16,128]{2,1,0:T(8,128)S(1)} %get-tuple-element.24), channel_id=1, source_target_pairs={{0,7},{1,8},{2,9},{3,10},{4,11},{5,12},{6,13},{7,14},{8,15},{9,0},... | collective-permute-start | bytes 98312 | tf_op jit(solution)/shard_map/ppermute | solution.py:563
  28.2 15.0 %collective-permute-start.5 = (f32[33,16,128]{2,1,0:T(8,128)S(1)}, f32[33,16,128]{2,1,0:T(8,128)S(1)}, u32[]{:S(2)}, u32[]{:S(2)}) collective-permute-start(f32[33,16,128]{2,1,0:T(8,128)S(1)} %get-tuple-element.26.s_high), channel_id=1, source_target_pairs={{0,1},{1,2},{2,3},{3,4},{4,5},{5,6},{6,7},{7,8},{8,9},{9,10},{10,1... | collective-permute-start | bytes 811016 | tf_op jit(solution)/shard_map/ppermute | solution.py:563
  28.8 14.4 %collective-permute-start.6 = (f32[33,16,128]{2,1,0:T(8,128)S(1)}, f32[33,16,128]{2,1,0:T(8,128)S(1)}, u32[]{:S(2)}, u32[]{:S(2)}) collective-permute-start(f32[33,16,128]{2,1,0:T(8,128)S(1)} %get-tuple-element.27.s_low), channel_id=1, source_target_pairs={{0,15},{1,0},{2,1},{3,2},{4,3},{5,4},{6,5},{7,6},{8,7},{9,8},{10,9... | collective-permute-start | bytes 811016 | tf_op jit(solution)/shard_map/ppermute | solution.py:563
  28.8 11.9 %collective-permute-start.7 = (f32[32,16,128]{2,1,0:T(8,128)S(1)}, f32[32,16,128]{2,1,0:T(8,128)S(1)}, u32[]{:S(2)}, u32[]{:S(2)}) collective-permute-start(f32[32,16,128]{2,1,0:T(8,128)S(1)} %get-tuple-element.28.e_high), channel_id=1, source_target_pairs={{0,1},{1,2},{2,3},{3,4},{4,5},{5,6},{6,7},{7,8},{8,9},{9,10},{10,1... | collective-permute-start | bytes 786440 | tf_op jit(solution)/shard_map/ppermute | solution.py:563
  30.6 12.7 %collective-permute-start.8 = (f32[32,16,128]{2,1,0:T(8,128)S(1)}, f32[32,16,128]{2,1,0:T(8,128)S(1)}, u32[]{:S(2)}, u32[]{:S(2)}) collective-permute-start(f32[32,16,128]{2,1,0:T(8,128)S(1)} %get-tuple-element.29.e_low), channel_id=1, source_target_pairs={{0,15},{1,0},{2,1},{3,2},{4,3},{5,4},{6,5},{7,6},{8,7},{9,8},{10,9... | collective-permute-start | bytes 786440 | tf_op jit(solution)/shard_map/ppermute | solution.py:563

commit v3 on v2

v3 whole, which is shorter than its diff:
```python
import jax
import jax.numpy as jnp
from jax import lax
from jax.experimental import pallas as pl
from jax.experimental.pallas import tpu as pltpu
from jax.sharding import PartitionSpec as P

TILE = 32
SEAM_SCALE = 0.1
LANES = 128
GROUPS = 4
BATCH = 4
F32 = jnp.float32
BF16 = jnp.bfloat16


def loop(count, body, carry=0, unroll=4):
    unroll = min(unroll, count)

    def steps(block, carry):
        for i in range(unroll):
            carry = body(block * unroll + i, carry)
        return carry

    whole = count // unroll
    carry = steps(0, carry) if whole == 1 else lax.fori_loop(0, whole, steps, carry)
    for t in range(whole * unroll, count):
        carry = body(t, carry)
    return carry


def before(t, tiles):
    return (tiles if t == 0 else t - 1) if isinstance(t, int) else jnp.where(t == 0, tiles, t - 1)


def after(t, tiles):
    return (0 if t == tiles else t + 1) if isinstance(t, int) else t + 1


def lane_ids(rows):
    return lax.broadcasted_iota(jnp.int32, (rows, LANES), 1)


def row_ids(rows):
    return lax.broadcasted_iota(jnp.int32, (rows, LANES), 0)


def roll_up(x):
    return pltpu.roll(x, 1, 1)


def roll_down(x):
    return pltpu.roll(x, LANES - 1, 1)


def roll_rows(x, by):
    by %= x.shape[0]
    return x if by == 0 else pltpu.roll(x, by, 0)


def roll_lanes(x, by):
    by %= LANES
    return x if by == 0 else pltpu.roll(x, by, 1)


def col_prev(x):
    return pltpu.roll(x, 1, 0)


def col_next(x):
    return pltpu.roll(x, x.shape[0] - 1, 0)


def selector(shape, rule):
    a = lax.broadcasted_iota(jnp.int32, shape, 0)
    b = lax.broadcasted_iota(jnp.int32, shape, 1)
    return jnp.where(rule(a, b), 1.0, 0.0).astype(BF16)


def splitter():
    return selector((256, 256), lambda a, b: a == 2 * (b % LANES) + b // LANES)


def merger():
    return selector((256, 256), lambda a, b: b == 2 * (a % LANES) + a // LANES)


def virtual_splitter():
    return selector(
        (LANES, 256),
        lambda a, b: a // 2 + jnp.where(a >= 64, 64, 0) + LANES * (a % 2) == b,
    )


def moved(x, matrix, exact=None):
    rows = x.shape[0]
    high = x.astype(BF16)
    low = (x - high.astype(F32)).astype(BF16)
    terms = [high, low] if exact is None else [high, low, exact]
    out = jnp.dot(jnp.concatenate(terms, 0), matrix, preferred_element_type=F32)
    both = out[:rows] + out[rows : 2 * rows]
    return both if exact is None else (both, out[2 * rows :])


def quarters_of(parts, temp):
    count = parts.shape[0] // 2
    temp[0] = parts[:, :LANES]
    temp[1] = parts[:, LANES:]
    return [temp[pr, pl.ds(pc, count, 2), :] for pc in (0, 1) for pr in (0, 1)]


def reds(swapped):
    return (1, 2) if swapped else (0, 3)


def interleaved(group, offset):
    sub = row_ids(8)
    packed = roll_rows(group[0], offset)
    for q in range(1, 4):
        packed = jnp.where(sub // 2 == q, roll_rows(group[q], 2 * q + offset), packed)
    return packed


def edge_packs(source, diag, swapped):
    sub = row_ids(8)
    even, odd = reds(swapped)
    rows = source[0].shape[0]
    packs = []
    for here, first, second, row, step in (
        (slice(rows - 8, rows), even, odd, 6, 1),
        (slice(0, 8), odd, even, 1, -1),
    ):
        gs = [x[here] for x in source]
        gd = [x[here] for x in diag]
        near = gs[first] / gd[first]
        far = roll_rows(gs[second] / gd[second], step)
        gs[first] = jnp.where(sub == row, near, gs[first])
        gd[first] = jnp.where(sub == row, far, gd[first])
        offset = 2 if row == 6 else 0
        packs.append((interleaved(gs, offset), interleaved(gd, offset)))
    return packs


def unpacked_halo(left, right, swapped):
    sub = row_ids(8)
    even, odd = reds(swapped)
    (al, bl), (ar, br) = left, right
    source, diag = [], []
    for q in range(4):
        s = jnp.where(
            sub >= 6,
            roll_rows(al, 6 - 2 * q),
            jnp.where(sub <= 1, roll_rows(ar, -2 * q), 0.0),
        )
        d = jnp.where(
            sub >= 6,
            roll_rows(bl, 6 - 2 * q),
            jnp.where(sub <= 1, roll_rows(br, -2 * q), 4.0),
        )
        if q == even:
            s = jnp.where(sub == 2, roll_rows(br, 1 - 2 * odd), s)
            d = jnp.where((sub == 2) | (sub == 6), 1.0, d)
        if q == odd:
            s = jnp.where(sub == 5, roll_rows(bl, 5 - 2 * even), s)
            d = jnp.where((sub == 5) | (sub == 1), 1.0, d)
        source.append(s)
        diag.append(d)
    return source, diag


def fill_halo(t, left, right, swapped, hs, hd, hi):
    source, diag = unpacked_halo(
        (left[0, t], left[1, t]), (right[0, t], right[1, t]), swapped
    )
    for q in range(4):
        hs[q, t] = source[q]
        hd[q, t] = diag[q]
        hi[q, t] = 1.0 / diag[q]


def loader(own, halo, virtual, tiles):
    def load(q, t):
        if isinstance(t, int) and t == tiles:
            return jnp.concatenate([virtual[q], halo[q, t]], 0)
        return jnp.concatenate([own[q, t], halo[q, t]], 0)

    return load


def polar_packs(tiles_of):
    lane = lane_ids(tiles_of[0][0].shape[0])
    packs = []
    for pc in (0, 1):
        parts = [*tiles_of[2 * pc], *tiles_of[2 * pc + 1]]
        packed = parts[0]
        for m in range(1, 4):
            mine = (lane + (16 - 32 * m) % LANES) % LANES < 32
            packed = jnp.where(mine, roll_lanes(parts[m], 32 * m), packed)
        packs.append(packed)
    return packs


def polar_unpacked(x, q):
    lane = lane_ids(x.shape[1])
    used = (lane < 16) | (lane >= LANES - 16)
    m = 2 * (q % 2)
    return (
        jnp.where(used, roll_lanes(x[q // 2], 32 * m), 0.0),
        jnp.where(used, roll_lanes(x[q // 2], 32 * (m + 1)), 4.0),
    )


def prepare_kernel(
    right_ref, weight_ref, flag_ref,
    s_ref, d_ref, e_ref, to_left, to_right, polar_ref, corner_low, corner_high,
    right_buf, weight_buf, temp_s, temp_d, scale_ref, sems,
):
    tiles, rows = s_ref.shape[1], s_ref.shape[2]
    chunk = right_ref.shape[1] // GROUPS
    copies = []
    for group in range(GROUPS):
        part = pl.ds(group * chunk, chunk)
        copies.append(
            [
                pltpu.make_async_copy(src.at[:, part], dst.at[:, part], sems.at[i, group])
                for i, (src, dst) in enumerate(((right_ref, right_buf), (weight_ref, weight_buf)))
            ]
        )
        for copy in copies[group]:
            copy.start()
    flag_cols = flag_ref.shape[0]
    flag_lats = flag_ref.shape[1]
    per_tile = rows // flag_cols
    matrix = splitter()
    flags = jnp.concatenate(
        [flag_ref[...].astype(F32), jnp.zeros((8 - flag_cols, flag_lats), F32)], 0
    )
    lat = lax.broadcasted_iota(jnp.int32, (8, flag_lats), 1)
    stacked = jnp.concatenate(
        [jnp.where(lat // 8 == c, flags, 0.0) for c in range(tiles)], 0
    ).astype(BF16)
    spread = selector((flag_lats, LANES), lambda a, b: a % 8 == b // (TILE // 2))
    spread_flags = jnp.dot(stacked, spread, preferred_element_type=F32)
    scale_ref[...] = jnp.where(spread_flags > 0.5, SEAM_SCALE, 1.0).reshape(tiles, 8, LANES)

    def piece(c, source, weight):
        scales = scale_ref[c]
        scale = jnp.concatenate(
            [jnp.broadcast_to(scales[i : i + 1], (per_tile, LANES)) for i in range(flag_cols)], 0
        )
        screen = [w * scale for w in weight]
        e_ref[c] = (screen[0] + screen[1]) + (screen[2] + screen[3])
        diag = [4.0 + s for s in screen]
        for q in range(4):
            s_ref[q, c] = source[q]
            d_ref[q, c] = diag[q]
        right, left = edge_packs(source, diag, False)
        to_right[0, c], to_right[1, c] = right
        to_left[0, c], to_left[1, c] = left

    columns = right_ref.shape[0]
    for group in range(GROUPS):
        for copy in copies[group]:
            copy.wait()
        for batch in range(tiles // GROUPS // BATCH):
            start = group * (tiles // GROUPS) + batch * BATCH
            lanes = [slice((start + i) * 256, (start + i + 1) * 256) for i in range(BATCH)]
            source = jnp.concatenate([right_buf[:, w] for w in lanes], 0)
            weight = jnp.concatenate([weight_buf[:, w] for w in lanes], 0)
            source, weight = moved(source, matrix, weight)
            for i in range(BATCH):
                here = slice(i * columns, (i + 1) * columns)
                piece(
                    start + i,
                    quarters_of(source[here], temp_s.at[i]),
                    quarters_of(weight[here], temp_d.at[i]),
                )

    mirror = selector((LANES, LANES), lambda a, b: a + b == LANES - 1)
    lane = lane_ids(rows)
    ends = [
        [jnp.where(lane >= 64, ref[q ^ 1, tiles - 1], ref[q ^ 1, 0]) for ref in (s_ref, d_ref)]
        for q in range(4)
    ]
    both = moved(jnp.concatenate(polar_packs(ends), 0), mirror)
    for pc in (0, 1):
        pack = both[pc * rows : (pc + 1) * rows]
        polar_ref[pc] = pack
        corner_low[pc] = pack[:8]
        corner_high[pc] = pack[rows - 8 :]


def split_tiles(load, tiles, rows, matrix, temp, use):
    for start in range(0, tiles, BATCH):
        wide = [
            jnp.concatenate([load(2 * c), load(2 * c + 1)], 1)
            for c in range(start, start + BATCH)
        ]
        out = moved(jnp.concatenate(wide, 0), matrix)
        for i in range(BATCH):
            use(start + i, quarters_of(out[i * rows : (i + 1) * rows], temp.at[i]))


def screens_kernel(d_ref, e_ref, i_ref, d1_ref, i1_ref, d2_ref, temp):
    def inverse(t, _):
        for q in range(4):
            i_ref[q, t] = 1.0 / d_ref[q, t]
        return 0

    loop(d_ref.shape[1], inverse)

    def use(c, screen):
        for q in range(4):
            d1_ref[q, c] = 4.0 + screen[q]
            i1_ref[q, c] = 1.0 / (4.0 + screen[q])
        d2_ref[c] = 4.0 + ((screen[0] + screen[1]) + (screen[2] + screen[3]))

    tiles, rows = d1_ref.shape[1], e_ref.shape[1]
    split_tiles(lambda t: e_ref[t], tiles, rows, splitter(), temp, use)


def half_sweep(v, load_s, load_i, tiles, red, unroll):
    rows = v[0].shape[1]
    lane = lane_ids(rows)
    y, z, qa, qb = (1, 2, 0, 3) if red else (3, 0, 2, 1)
    col_a, col_b = (col_prev, col_next) if red else (col_next, col_prev)

    def beside_virtual(q):
        ns, we = q ^ 1, q ^ 2
        here = v[ns][tiles]
        if q % 2 == 0:
            lat = jnp.where(lane == 0, roll_up(v[ns][tiles - 1]), roll_up(here))
        else:
            lat = jnp.where(lane == LANES - 1, roll_down(v[ns][0]), roll_down(here))
        cols = v[we][tiles]
        return (here + lat) + (cols + (col_prev if q < 2 else col_next)(cols))

    held = [
        (q, (load_s(q, tiles) + beside_virtual(q)) * load_i(q, tiles)) for q in (y, z)
    ]

    def body(t, carry):
        y_before, z_here = carry
        vy, vz = v[y][t], v[z][t]
        y_here = roll_up(vy)
        z_after = roll_down(v[z][t + 1])
        lat_a = vy + jnp.where(lane == 0, y_before, y_here)
        lat_b = vz + jnp.where(lane == LANES - 1, z_after, z_here)
        v[qa][t] = (load_s(qa, t) + (lat_a + (vz + col_a(vz)))) * load_i(qa, t)
        v[qb][t] = (load_s(qb, t) + (lat_b + (vy + col_b(vy)))) * load_i(qb, t)
        return y_here, z_after

    loop(tiles, body, (roll_up(v[y][tiles]), roll_down(v[z][0])), unroll)
    for q, value in held:
        v[q][tiles] = value


def smooth(v, load_s, load_i, tiles, unroll):
    zeros = jnp.zeros(v[0].shape[1:], F32)

    def first(t, _):
        for q in (0, 3):
            v[q][t] = load_s(q, t) * load_i(q, t)
        return 0

    loop(tiles, first, 0, unroll)
    for q in (1, 2):
        v[q][0] = zeros
        v[q][tiles - 1] = zeros
        v[q][tiles] = load_s(q, tiles) * load_i(q, tiles)
        v[3 * (q - 1)][tiles] = zeros
    half_sweep(v, load_s, load_i, tiles, False, unroll)
    half_sweep(v, load_s, load_i, tiles, True, unroll)
    half_sweep(v, load_s, load_i, tiles, False, unroll)


def residuals(v, load_s, load_d, tiles, c0, c1, keep, unroll):
    lane = lane_ids(v[0].shape[1])

    def body(t, _):
        x = [v[q][t] for q in range(4)]

        def north(q):
            return jnp.where(lane == 0, roll_up(v[q][before(t, tiles)]), roll_up(x[q]))

        def south(q):
            return jnp.where(
                lane == LANES - 1, roll_down(v[q][after(t, tiles)]), roll_down(x[q])
            )

        beside = [
            (x[1] + north(1)) + (x[2] + col_prev(x[2])),
            (x[0] + south(0)) + (x[3] + col_prev(x[3])),
            (x[3] + north(3)) + (x[0] + col_next(x[0])),
            (x[2] + south(2)) + (x[1] + col_next(x[1])),
        ]
        r = [load_s(q, t) - (load_d(q, t) * x[q] - beside[q]) for q in range(4)]
        keep(t, r)
        c0[t] = (col_prev(r[2]) + col_next(r[0])) + 3.0 * (r[0] + r[2])
        c1[t] = (col_prev(r[3]) + col_next(r[1])) + 3.0 * (r[1] + r[3])
        return 0

    loop(tiles, body, 0, unroll)
    body(tiles, 0)


def restricted(c0, c1, t, tiles, rows):
    lane = lane_ids(rows)
    here, other = c0[t, :rows], c1[t, :rows]
    north = jnp.where(lane == 0, roll_up(c1[before(t, tiles), :rows]), roll_up(other))
    south = jnp.where(
        lane == LANES - 1, roll_down(c0[after(t, tiles), :rows]), roll_down(here)
    )
    return ((north + south) + 3.0 * (here + other)) * (1.0 / 16.0)


def fine_kernel(
    s_ref, d_ref, i_ref, d1_ref, from_left, from_right, polar_ref, corner_left, corner_right,
    r_ref, s1_ref, d1_virtual, d2_virtual, to_left, to_right,
    v0, v1, v2, v3, c0, c1, hs, hd, hi, ps, pd, pi, n1, temp,
):
    v = [v0, v1, v2, v3]
    tiles, rows = s_ref.shape[1], s_ref.shape[2]
    sub = row_ids(8)

    def halo(t, _):
        fill_halo(t, from_left, from_right, False, hs, hd, hi)
        return 0

    loop(tiles, halo)
    total = -16.0
    for q in range(4):
        left_s, left_d = polar_unpacked(corner_left, q)
        own_s, own_d = polar_unpacked(polar_ref, q)
        right_s, right_d = polar_unpacked(corner_right, q)
        total = total + own_d
        ps[q] = own_s
        pd[q] = own_d
        pi[q] = 1.0 / own_d
        source = jnp.where(sub >= 5, left_s, jnp.where(sub <= 2, right_s, 0.0))
        diag = jnp.where(sub >= 5, left_d, jnp.where(sub <= 2, right_d, 4.0))
        hs[q, tiles] = source
        hd[q, tiles] = diag
        hi[q, tiles] = 1.0 / diag

    load_s = loader(s_ref, hs, ps, tiles)
    smooth(v, load_s, loader(i_ref, hi, pi, tiles), tiles, 8)

    def keep(t, r):
        if not (isinstance(t, int) and t == tiles):
            for q in range(4):
                r_ref[q, t] = r[q][:rows]

    residuals(v, load_s, loader(d_ref, hd, pd, tiles), tiles, c0, c1, keep, 4)

    def coarse(t, _):
        n1[t] = restricted(c0, c1, t, tiles, rows)
        return 0

    loop(tiles, coarse, 0, 8)
    coarse(tiles, 0)

    def edges(t, source, diag, swapped):
        right, left = edge_packs(source, diag, swapped)
        to_right[0, t], to_right[1, t] = right
        to_left[0, t], to_left[1, t] = left

    def use(c, source):
        for q in range(4):
            s1_ref[q, c] = source[q]
        edges(c, source, [d1_ref[q, c] for q in range(4)], False)

    tiles1 = tiles // 2
    split_tiles(lambda t: n1[t], tiles1, rows, splitter(), temp, use)
    out = moved(jnp.concatenate([n1[tiles], total], 0), virtual_splitter())
    source = quarters_of(out[:rows], temp.at[0])
    screen = quarters_of(out[rows:], temp.at[1])
    diag = [4.0 + x for x in screen]
    for q in range(4):
        s1_ref[q, tiles1] = source[q]
        d1_virtual[q] = diag[q]
    d2_virtual[...] = 4.0 + ((screen[0] + screen[1]) + (screen[2] + screen[3]))
    edges(tiles1, source, diag, True)


def merge_kernel(r_ref, out_ref, temp, out_buf, sems):
    tiles = r_ref.shape[1]
    rows = r_ref.shape[2]
    matrix = merger()
    chunk = out_ref.shape[1] // GROUPS
    copies = []
    for group in range(GROUPS):
        for batch in range(tiles // GROUPS // BATCH):
            start = group * (tiles // GROUPS) + batch * BATCH
            both = []
            for i in range(BATCH):
                for pr in (0, 1):
                    for pc in (0, 1):
                        temp[i, pr, pl.ds(pc, rows, 2), :] = r_ref[2 * pc + pr, start + i]
                both.append(jnp.concatenate([temp[i, 0], temp[i, 1]], 1))
            out = moved(jnp.concatenate(both, 0), matrix)
            for i in range(BATCH):
                where = slice((start + i) * 256, (start + i + 1) * 256)
                out_buf[:, where] = out[2 * rows * i : 2 * rows * (i + 1)]
        part = pl.ds(group * chunk, chunk)
        copy = pltpu.make_async_copy(out_buf.at[:, part], out_ref.at[:, part], sems.at[group])
        copy.start()
        copies.append(copy)
    for copy in copies:
        copy.wait()


def middle_kernel(
    s_ref, d_ref, i_ref, d_virtual, d2_ref, d2_virtual, from_left, from_right,
    s2_ref, to_left, to_right,
    v0, v1, v2, v3, c0, c1, hs, hd, hi, pi,
):
    v = [v0, v1, v2, v3]
    tiles, rows = d_ref.shape[1], d_ref.shape[2]
    for t in range(tiles + 1):
        fill_halo(t, from_left, from_right, t == tiles, hs, hd, hi)
    for q in range(4):
        pi[q] = 1.0 / d_virtual[q]

    def load_s(q, t):
        return jnp.concatenate([s_ref[q, t], hs[q, t]], 0)

    smooth(v, load_s, loader(i_ref, hi, pi, tiles), tiles, 16)
    residuals(
        v, load_s, loader(d_ref, hd, d_virtual, tiles), tiles, c0, c1, lambda t, r: None, 16
    )
    sub = row_ids(8)
    for t in range(tiles + 1):
        value = restricted(c0, c1, t, tiles, rows)
        diag = d2_virtual[...] if t == tiles else d2_ref[t]
        s2_ref[t] = value
        to_right[t] = jnp.where(sub < 4, roll_rows(value[rows - 8 :], 4), diag[rows - 8 :])
        to_left[t] = jnp.where(sub < 4, value[:8], roll_rows(diag[:8], 4))


def last_kernel(
    s_ref, d_ref, d_virtual, from_left, from_right,
    solution_ref, residual_ref,
    s, d, inv, va, vb,
):
    tiles, own = d_ref.shape[0], d_ref.shape[1]
    rows = own + 8
    sub = row_ids(8)
    lane, row = lane_ids(rows), row_ids(rows)
    even = (lane + row) % 2 == 0
    odd = jnp.logical_not(even)
    for t in range(tiles + 1):
        left, right = from_left[t], from_right[t]
        diag = d_virtual[...] if t == tiles else d_ref[t]
        source = jnp.concatenate(
            [s_ref[t], jnp.where(sub < 4, right, roll_rows(left, 4))], 0
        )
        diag = jnp.concatenate([diag, jnp.where(sub < 4, roll_rows(right, 4), left)], 0)
        inverse = 1.0 / diag
        s[t] = source
        d[t] = diag
        inv[t] = inverse
        va[t] = jnp.where(odd if t == tiles else even, source * inverse, 0.0)

    def beside(v, t):
        x = v[t]
        north = jnp.where(lane == 0, roll_up(v[before(t, tiles)]), roll_up(x))
        south = jnp.where(lane == LANES - 1, roll_down(v[after(t, tiles)]), roll_down(x))
        return (col_prev(x) + col_next(x)) + (north + south)

    old, new = va, vb
    for mask, other in ((odd, even), (even, odd), (odd, even)):
        for t in range(tiles + 1):
            value = (s[t] + beside(old, t)) * inv[t]
            new[t] = jnp.where(other if t == tiles else mask, value, old[t])
        old, new = new, old
    for t in range(tiles):
        x = old[t]
        r = s[t] - (d[t] * x - beside(old, t))
        where = slice(t * LANES, (t + 1) * LANES)
        solution_ref[:, where] = x[:own]
        residual_ref[:, where] = r[:own]


VMEM = pl.BlockSpec(memory_space=pltpu.VMEM)
HBM = pl.BlockSpec(memory_space=pltpu.HBM)


def call(kernel, out_shapes, scratch, *args, sems=None, far_in=0, far_out=0):
    scratch = [pltpu.VMEM(x, F32) if isinstance(x, tuple) else x for x in scratch]
    if sems is not None:
        scratch.append(pltpu.SemaphoreType.DMA(sems))
    return pl.pallas_call(
        kernel,
        out_shape=[jax.ShapeDtypeStruct(shape, F32) for shape in out_shapes],
        in_specs=[HBM] * far_in + [VMEM] * (len(args) - far_in),
        out_specs=[HBM] * far_out + [VMEM] * (len(out_shapes) - far_out),
        scratch_shapes=scratch,
        compiler_params=pltpu.CompilerParams(vmem_limit_bytes=40 * 2**20),
    )(*args)


def shifted(x, by):
    count = lax.axis_size("lon")
    return lax.ppermute(x, "lon", [(i, (i + by) % count) for i in range(count)])


def body(right_side, texel_weight, seam_flags):
    columns, height = right_side.shape
    half_turn = lax.axis_size("lon") // 2
    tiles, rows = height // 256, columns // 2
    tiles1, rows1 = tiles // 2, rows // 2
    temp = (BATCH, 2, columns, LANES)
    right_side = pltpu.with_memory_space_constraint(right_side, pltpu.HBM)
    texel_weight = pltpu.with_memory_space_constraint(texel_weight, pltpu.HBM)

    quarters = (4, tiles, rows, LANES)
    s, d, e, to_left, to_right, polar, corner_low, corner_high = call(
        prepare_kernel,
        [quarters, quarters, quarters[1:], (2, tiles, 8, LANES), (2, tiles, 8, LANES)]
        + [(2, rows, LANES), (2, 8, LANES), (2, 8, LANES)],
        [(columns, height), pltpu.VMEM((columns, height), BF16), temp, temp, (tiles, 8, LANES)],
        right_side, texel_weight, seam_flags,
        sems=(2, GROUPS), far_in=2,
    )
    from_left = shifted(to_right, 1)
    from_right = shifted(to_left, -1)
    polar = shifted(polar, half_turn)
    corner_left = shifted(corner_high, half_turn + 1)
    corner_right = shifted(corner_low, half_turn - 1)
    quarters1 = (4, tiles1, rows1, LANES)
    inverse, d1, i1, d2 = call(
        screens_kernel,
        [quarters, quarters1, quarters1, quarters1[1:]],
        [(BATCH, 2, rows, LANES)],
        d, e,
    )

    def level_scratch(tiles, rows):
        halo = (4, tiles + 1, 8, LANES)
        return [(tiles + 1, rows + 8, LANES)] * 6 + [halo] * 3

    pack1 = (2, tiles1 + 1, 8, LANES)
    r, s1, d1_virtual, d2_virtual, to_left, to_right = call(
        fine_kernel,
        [quarters, (4, tiles1 + 1, rows1, LANES), (4, rows1, LANES), (rows1, LANES), pack1, pack1],
        level_scratch(tiles, rows)
        + [(4, rows, LANES)] * 3
        + [(tiles + 1, rows, LANES), (BATCH, 2, rows, LANES)],
        s, d, inverse, d1, from_left, from_right, polar, corner_left, corner_right,
    )
    from_left = shifted(to_right, 1)
    from_right = shifted(to_left, -1)
    (fine_residual,) = call(
        merge_kernel, [(columns, height)], [temp, (columns, height)], r,
        sems=(GROUPS,), far_out=1,
    )
    pack2 = (tiles1 + 1, 8, LANES)
    s2, to_left, to_right = call(
        middle_kernel,
        [(tiles1 + 1, rows1, LANES), pack2, pack2],
        level_scratch(tiles1, rows1) + [(4, rows1, LANES)],
        s1, d1, i1, d1_virtual, d2, d2_virtual, from_left, from_right,
    )
    from_left = shifted(to_right, 1)
    from_right = shifted(to_left, -1)
    solution_2, residual_2 = call(
        last_kernel,
        [(columns // 4, height // 4)] * 2,
        [(tiles1 + 1, rows1 + 8, LANES)] * 5,
        s2, d2, d2_virtual, from_left, from_right,
    )
    return fine_residual, solution_2, residual_2


def solution(mesh):
    spec = P(("groups", "lon"), None)
    return jax.shard_map(
        body, mesh=mesh, in_specs=(spec,) * 3, out_specs=(spec,) * 3, check_vma=False
    )
```

time: 53.8 us -> 39.5 us (0.73)
  the two profiles are of different devices: /device:TPU:1 before, /device:TPU:0 now
where the time goes in v3:
time: 39.5 us; the launch traced here: 39.3 us
  starting transfers between devices  18.4 us (47%)
  Pallas kernels  14.9 us (38%)
  waiting for transfers between devices  4.61 us (12%)
  between operations  0.68 us (2%)
  local copies, waits for them, and re-layouts  0.67 us (2%)
    ppermute x9, starting transfers between devices, shifted(): return lax.ppermute(x, 'lon', [(i, (i + by) % count) for i in range(count)])  18.4 us
    pallas_call x6, Pallas kernels, call(): pl.pallas_call(kernel, out_shape=[jax.ShapeDtypeStruct(shape, F32) for sh...  14.9 us
    ppermute x9, waiting for transfers between devices, shifted(): return lax.ppermute(x, 'lon', [(i, (i + by) % count) for i in range(count)])  4.61 us
  transfers between devices with their start and end apart: 9, of which 4 were waited for; matrix products, arithmetic and copies ran while one was open for 0% of the time, Pallas kernels for 6%

profile of v3, /device:TPU:0, one launch (start us, length us, event | category | flops | bytes accessed | tf_op | source)
XLA Modules:
  0.0 39.3 jit_solution(11717172451925612599)
XLA Ops:
  0.6 0.0 copy-start
  0.6 0.7 %copy-done = s32[2,256]{1,0:T(2,128)S(1)} copy-done((s32[2,256]{1,0:T(2,128)S(1)}, s32[2,256]{1,0:T(2,128)}, u32[]{:S(2)}) %copy-start) | copy-done | bytes 2072
  1.3 3.3 %shard_map.58 = (f32[4,32,32,128]{3,2,1,0:T(8,128)S(1)}, f32[4,32,32,128]{3,2,1,0:T(8,128)S(1)}, f32[32,32,128]{2,1,0:T(8,128)S(1)}, f32[2,32,8,128]{3,2,1,0:T(8...) custom-call(f32[64,8192]{1,0:T(8,128)} %right_ref.1, ...), custom_call_target="tpu_custom_call" | custom-call | tf_op jit(solution)/shard_map/pallas_call | solution.py:593
  4.6 0.5 %collective-permute-start = (f32[2,32,8,128]{3,2,1,0:T(8,128)S(1)}, f32[2,32,8,128]{3,2,1,0:T(8,128)S(1)}, u32[]{:S(2)}, u32[]{:S(2)}) collective-permute-start(f32[2,32,8,128]{3,2,1,0:T(8,128)S(1)} %get-tuple-element.31), channel_id=1, source_target_pairs={{0,1},{1,2},{2,3},{3,4},{4,5},{5,6},{6,7},{7,8},{8,9},{9,10},{10,1... | collective-permute-start | bytes 786440 | tf_op jit(solution)/shard_map/ppermute | solution.py:605
  5.1 5.0 %collective-permute-start.1 = (f32[2,32,8,128]{3,2,1,0:T(8,128)S(1)}, f32[2,32,8,128]{3,2,1,0:T(8,128)S(1)}, u32[]{:S(2)}, u32[]{:S(2)}) collective-permute-start(f32[2,32,8,128]{3,2,1,0:T(8,128)S(1)} %get-tuple-element.32), channel_id=1, source_target_pairs={{0,15},{1,0},{2,1},{3,2},{4,3},{5,4},{6,5},{7,6},{8,7},{9,8},{10,9... | collective-permute-start | bytes 786440 | tf_op jit(solution)/shard_map/ppermute | solution.py:605
  10.2 1.2 %collective-permute-start.2 = (f32[2,32,128]{2,1,0:T(8,128)S(1)}, f32[2,32,128]{2,1,0:T(8,128)S(1)}, u32[]{:S(2)}, u32[]{:S(2)}) collective-permute-start(f32[2,32,128]{2,1,0:T(8,128)S(1)} %get-tuple-element.33), channel_id=1, source_target_pairs={{0,8},{1,9},{2,10},{3,11},{4,12},{5,13},{6,14},{7,15},{8,0},{9,1},... | collective-permute-start | bytes 98312 | tf_op jit(solution)/shard_map/ppermute | solution.py:605
  11.4 0.0 collective-permute-start.3
  11.4 2.6 %collective-permute-start.4 = (f32[2,8,128]{2,1,0:T(8,128)S(1)}, f32[2,8,128]{2,1,0:T(8,128)S(1)}, u32[]{:S(2)}, u32[]{:S(2)}) collective-permute-start(f32[2,8,128]{2,1,0:T(8,128)S(1)} %get-tuple-element.35), channel_id=1, source_target_pairs={{0,7},{1,8},{2,9},{3,10},{4,11},{5,12},{6,13},{7,14},{8,15},{9,0},... | collective-permute-start | bytes 24584 | tf_op jit(solution)/shard_map/ppermute | solution.py:605
  14.0 0.7 %shard_map.59 = (f32[4,32,32,128]{3,2,1,0:T(8,128)S(1)}, f32[4,16,16,128]{3,2,1,0:T(8,128)S(1)}, f32[4,16,16,128]{3,2,1,0:T(8,128)S(1)}, f32[16,16,128]{2,1,0:T(8,128)S(1)}) custom-call(f32[4,32,32,128]{3,2,1,0:T(8,128)S(1)} %get-tuple-element.27.d_ref, f32[32,32,128]{2,1,0:T(8,128)S(1)} %get-tuple-element.28.e_ref), custom_call_target="tpu_custom_call" | custom-call | tf_op jit(solution)/shard_map/pallas_call | solution.py:593
  14.7 1.2 %collective-permute-done.3.corner_left = f32[2,8,128]{2,1,0:T(8,128)S(1)} collective-permute-done((f32[2,8,128]{2,1,0:T(8,128)S(1)}, f32[2,8,128]{2,1,0:T(8,128)S(1)}, u32[]{:S(2)}, u32[]{:S(2)}) %collective-permute-start.3) | collective-permute-done | bytes 8224 | tf_op jit(solution)/shard_map/ppermute | solution.py:605
  15.9 0.0 collective-permute-done.4.corner_right
  15.9 0.3 collective-permute-done.2.polar_ref
  16.3 0.0 collective-permute-done.from_left
  16.3 0.0 collective-permute-done.1.from_right
  16.3 6.2 %shard_map.60 = (f32[4,32,32,128]{3,2,1,0:T(8,128)S(1)}, f32[4,17,16,128]{3,2,1,0:T(8,128)S(1)}, f32[4,16,128]{2,1,0:T(8,128)S(1)}, f32[16,128]{1,0:T(8,128)S(1)...) custom-call(f32[4,32,32,128]{3,2,1,0:T(8,128)S(1)} %get-tuple-element.26.s_ref, ...), custom_call_target="tpu_custom_call" | custom-call | tf_op jit(solution)/shard_map/pallas_call | solution.py:593
  22.5 0.5 %collective-permute-start.5 = (f32[2,17,8,128]{3,2,1,0:T(8,128)S(1)}, f32[2,17,8,128]{3,2,1,0:T(8,128)S(1)}, u32[]{:S(2)}, u32[]{:S(2)}) collective-permute-start(f32[2,17,8,128]{3,2,1,0:T(8,128)S(1)} %get-tuple-element.42), channel_id=1, source_target_pairs={{0,1},{1,2},{2,3},{3,4},{4,5},{5,6},{6,7},{7,8},{8,9},{9,10},{10,1... | collective-permute-start | bytes 417800 | tf_op jit(solution)/shard_map/ppermute | solution.py:605
  23.0 4.0 %collective-permute-start.6 = (f32[2,17,8,128]{3,2,1,0:T(8,128)S(1)}, f32[2,17,8,128]{3,2,1,0:T(8,128)S(1)}, u32[]{:S(2)}, u32[]{:S(2)}) collective-permute-start(f32[2,17,8,128]{3,2,1,0:T(8,128)S(1)} %get-tuple-element.43), channel_id=1, source_target_pairs={{0,15},{1,0},{2,1},{3,2},{4,3},{5,4},{6,5},{7,6},{8,7},{9,8},{10,9... | collective-permute-start | bytes 417800 | tf_op jit(solution)/shard_map/ppermute | solution.py:605
  27.0 2.8 %collective-permute-done.5.from_left = f32[2,17,8,128]{3,2,1,0:T(8,128)S(1)} collective-permute-done((f32[2,17,8,128]{3,2,1,0:T(8,128)S(1)}, f32[2,17,8,128]{3,2,1,0:T(8,128)S(1)}, u32[]{:S(2)}, u32[]{:S(2)}) %collective-permute-start.5) | collective-permute-done | bytes 139296 | tf_op jit(solution)/shard_map/ppermute | solution.py:605
  29.9 0.0 collective-permute-done.6.from_right
  29.9 1.2 %shard_map.62 = (f32[17,16,128]{2,1,0:T(8,128)S(1)}, f32[17,8,128]{2,1,0:T(8,128)S(1)}, f32[17,8,128]{2,1,0:T(8,128)S(1)}) custom-call(f32[4,17,16,128]{3,2,1,0:T(8,128)S(1)} %get-tuple-element.37.s_ref, f32[4,16,16,128]{3,2,1,0:T(8,128)S(1)} %get-tuple-element.30.d1_ref.d_ref, f32[4,16,16,128]{3,2,1,0:T(8,128)S(1)} %get-tuple-element.38.i_ref, ...), custom_call_target="tpu_custom_call" | custom-call | tf_op jit(solution)/shard_map/pallas_call | solution.py:593
  31.1 0.9 %collective-permute-start.7 = (f32[17,8,128]{2,1,0:T(8,128)S(1)}, f32[17,8,128]{2,1,0:T(8,128)S(1)}, u32[]{:S(2)}, u32[]{:S(2)}) collective-permute-start(f32[17,8,128]{2,1,0:T(8,128)S(1)} %get-tuple-element.45), channel_id=1, source_target_pairs={{0,1},{1,2},{2,3},{3,4},{4,5},{5,6},{6,7},{7,8},{8,9},{9,10},{10,1... | collective-permute-start | bytes 208904 | tf_op jit(solution)/shard_map/ppermute | solution.py:605
  32.0 3.6 %collective-permute-start.8 = (f32[17,8,128]{2,1,0:T(8,128)S(1)}, f32[17,8,128]{2,1,0:T(8,128)S(1)}, u32[]{:S(2)}, u32[]{:S(2)}) collective-permute-start(f32[17,8,128]{2,1,0:T(8,128)S(1)} %get-tuple-element.46), channel_id=1, source_target_pairs={{0,15},{1,0},{2,1},{3,2},{4,3},{5,4},{6,5},{7,6},{8,7},{9,8},{10,9... | collective-permute-start | bytes 208904 | tf_op jit(solution)/shard_map/ppermute | solution.py:605
  35.6 1.8 %shard_map.61 = f32[64,8192]{1,0:T(8,128)} custom-call(f32[4,32,32,128]{3,2,1,0:T(8,128)S(1)} %get-tuple-element.36.r_ref), custom_call_target="tpu_custom_call" | custom-call | tf_op jit(solution)/shard_map/pallas_call | solution.py:593
  37.3 0.2 collective-permute-done.7.from_left
  37.6 0.0 collective-permute-done.8.from_right
  37.6 1.7 %shard_map.63 = (f32[16,2048]{1,0:T(8,128)}, f32[16,2048]{1,0:T(8,128)}) custom-call(f32[17,16,128]{2,1,0:T(8,128)S(1)} %get-tuple-element.44.s_ref, f32[16,16,128]{2,1,0:T(8,128)S(1)} %get-tuple-element.40.d2_ref.d_ref, f32[16,128]{1,0:T(8,128)S(1)} %get-tuple-element.41.d2_virtual.d_virtual, f32[17,8,128]{2,1,0:T(8,128)S(1)} %collective-permute-done.7.from_left, ...), custom_call_target="tpu_custom_call" | custom-call | tf_op jit(solution)/shard_map/pallas_call | solution.py:593
Async XLA Ops:
  0.6 0.7 %copy-start = (s32[2,256]{1,0:T(2,128)S(1)}, s32[2,256]{1,0:T(2,128)}, u32[]{:S(2)}) copy-start(s32[2,256]{1,0:T(2,128)} %flag_ref.1) | copy-start | bytes 6148
  4.6 11.6 %collective-permute-start = (f32[2,32,8,128]{3,2,1,0:T(8,128)S(1)}, f32[2,32,8,128]{3,2,1,0:T(8,128)S(1)}, u32[]{:S(2)}, u32[]{:S(2)}) collective-permute-start(f32[2,32,8,128]{3,2,1,0:T(8,128)S(1)} %get-tuple-element.31), channel_id=1, source_target_pairs={{0,1},{1,2},{2,3},{3,4},{4,5},{5,6},{6,7},{7,8},{8,9},{9,10},{10,1... | collective-permute-start | bytes 786440 | tf_op jit(solution)/shard_map/ppermute | solution.py:605
  5.1 11.1 %collective-permute-start.1 = (f32[2,32,8,128]{3,2,1,0:T(8,128)S(1)}, f32[2,32,8,128]{3,2,1,0:T(8,128)S(1)}, u32[]{:S(2)}, u32[]{:S(2)}) collective-permute-start(f32[2,32,8,128]{3,2,1,0:T(8,128)S(1)} %get-tuple-element.32), channel_id=1, source_target_pairs={{0,15},{1,0},{2,1},{3,2},{4,3},{5,4},{6,5},{7,6},{8,7},{9,8},{10,9... | collective-permute-start | bytes 786440 | tf_op jit(solution)/shard_map/ppermute | solution.py:605
  10.2 6.1 %collective-permute-start.2 = (f32[2,32,128]{2,1,0:T(8,128)S(1)}, f32[2,32,128]{2,1,0:T(8,128)S(1)}, u32[]{:S(2)}, u32[]{:S(2)}) collective-permute-start(f32[2,32,128]{2,1,0:T(8,128)S(1)} %get-tuple-element.33), channel_id=1, source_target_pairs={{0,8},{1,9},{2,10},{3,11},{4,12},{5,13},{6,14},{7,15},{8,0},{9,1},... | collective-permute-start | bytes 98312 | tf_op jit(solution)/shard_map/ppermute | solution.py:605
  11.4 4.5 %collective-permute-start.3 = (f32[2,8,128]{2,1,0:T(8,128)S(1)}, f32[2,8,128]{2,1,0:T(8,128)S(1)}, u32[]{:S(2)}, u32[]{:S(2)}) collective-permute-start(f32[2,8,128]{2,1,0:T(8,128)S(1)} %get-tuple-element.34), channel_id=1, source_target_pairs={{0,9},{1,10},{2,11},{3,12},{4,13},{5,14},{6,15},{7,0},{8,1},{9,2},... | collective-permute-start | bytes 24584 | tf_op jit(solution)/shard_map/ppermute | solution.py:605
  11.4 4.5 %collective-permute-start.4 = (f32[2,8,128]{2,1,0:T(8,128)S(1)}, f32[2,8,128]{2,1,0:T(8,128)S(1)}, u32[]{:S(2)}, u32[]{:S(2)}) collective-permute-start(f32[2,8,128]{2,1,0:T(8,128)S(1)} %get-tuple-element.35), channel_id=1, source_target_pairs={{0,7},{1,8},{2,9},{3,10},{4,11},{5,12},{6,13},{7,14},{8,15},{9,0},... | collective-permute-start | bytes 24584 | tf_op jit(solution)/shard_map/ppermute | solution.py:605
  22.5 7.3 %collective-permute-start.5 = (f32[2,17,8,128]{3,2,1,0:T(8,128)S(1)}, f32[2,17,8,128]{3,2,1,0:T(8,128)S(1)}, u32[]{:S(2)}, u32[]{:S(2)}) collective-permute-start(f32[2,17,8,128]{3,2,1,0:T(8,128)S(1)} %get-tuple-element.42), channel_id=1, source_target_pairs={{0,1},{1,2},{2,3},{3,4},{4,5},{5,6},{6,7},{7,8},{8,9},{9,10},{10,1... | collective-permute-start | bytes 417800 | tf_op jit(solution)/shard_map/ppermute | solution.py:605
  23.0 6.8 %collective-permute-start.6 = (f32[2,17,8,128]{3,2,1,0:T(8,128)S(1)}, f32[2,17,8,128]{3,2,1,0:T(8,128)S(1)}, u32[]{:S(2)}, u32[]{:S(2)}) collective-permute-start(f32[2,17,8,128]{3,2,1,0:T(8,128)S(1)} %get-tuple-element.43), channel_id=1, source_target_pairs={{0,15},{1,0},{2,1},{3,2},{4,3},{5,4},{6,5},{7,6},{8,7},{9,8},{10,9... | collective-permute-start | bytes 417800 | tf_op jit(solution)/shard_map/ppermute | solution.py:605
  31.1 6.5 %collective-permute-start.7 = (f32[17,8,128]{2,1,0:T(8,128)S(1)}, f32[17,8,128]{2,1,0:T(8,128)S(1)}, u32[]{:S(2)}, u32[]{:S(2)}) collective-permute-start(f32[17,8,128]{2,1,0:T(8,128)S(1)} %get-tuple-element.45), channel_id=1, source_target_pairs={{0,1},{1,2},{2,3},{3,4},{4,5},{5,6},{6,7},{7,8},{8,9},{9,10},{10,1... | collective-permute-start | bytes 208904 | tf_op jit(solution)/shard_map/ppermute | solution.py:605
  32.0 5.5 %collective-permute-start.8 = (f32[17,8,128]{2,1,0:T(8,128)S(1)}, f32[17,8,128]{2,1,0:T(8,128)S(1)}, u32[]{:S(2)}, u32[]{:S(2)}) collective-permute-start(f32[17,8,128]{2,1,0:T(8,128)S(1)} %get-tuple-element.46), channel_id=1, source_target_pairs={{0,15},{1,0},{2,1},{3,2},{4,3},{5,4},{6,5},{7,6},{8,7},{9,8},{10,9... | collective-permute-start | bytes 208904 | tf_op jit(solution)/shard_map/ppermute | solution.py:605

commit v4 on v3

--- a/solution.py
+++ b/solution.py
@@ -210,9 +210,75 @@
     )
 
 
+def seam_scales(flag_ref, chunks):
+    flag_cols, flag_lats = flag_ref.shape
+    flags = jnp.concatenate(
+        [flag_ref[...].astype(F32), jnp.zeros((8 - flag_cols, flag_lats), F32)], 0
+    )
+    lat = lax.broadcasted_iota(jnp.int32, (8, flag_lats), 1)
+    stacked = jnp.concatenate([jnp.where(lat // 8 == c, flags, 0.0) for c in chunks], 0)
+    spread = selector((flag_lats, LANES), lambda a, b: a % 8 == b // (TILE // 2))
+    spread_flags = jnp.dot(stacked.astype(BF16), spread, preferred_element_type=F32)
+    scale = jnp.where(spread_flags > 0.5, SEAM_SCALE, 1.0)
+    return scale.reshape(len(chunks), 8, LANES)
+
+
+def seam_rows(scales, flag_cols, rows):
+    size = (rows // flag_cols, LANES)
+    return jnp.concatenate(
+        [jnp.broadcast_to(scales[i : i + 1], size) for i in range(flag_cols)], 0
+    )
+
+
+def polar_kernel(
+    right_ref, weight_ref, flag_ref, polar_ref, corner_ref, right_buf, weight_buf, temp_s, temp_d, sems
+):
+    columns, height = right_ref.shape
+    rows = columns // 2
+    copies = []
+    for end, start in enumerate((0, height - 256)):
+        for i, (src, dst) in enumerate(((right_ref, right_buf), (weight_ref, weight_buf))):
+            copies.append(
+                pltpu.make_async_copy(src.at[:, pl.ds(start, 256)], dst.at[end], sems.at[i, end])
+            )
+    for copy in copies:
+        copy.start()
+    scales = seam_scales(flag_ref, (0, height // 256 - 1))
+    mirror = selector((LANES, LANES), lambda a, b: a + b == LANES - 1)
+    matrix = splitter()
+    lane = lane_ids(rows)
+    for copy in copies:
+        copy.wait()
+    source, weight = moved(
+        jnp.concatenate([right_buf[0], right_buf[1]], 0),
+        matrix,
+        jnp.concatenate([weight_buf[0], weight_buf[1]], 0),
+    )
+    found = []
+    for end in (0, 1):
+        here = slice(end * columns, (end + 1) * columns)
+        scale = seam_rows(scales[end], flag_ref.shape[0], rows)
+        found.append(
+            (
+                quarters_of(source[here], temp_s.at[end]),
+                [4.0 + w * scale for w in quarters_of(weight[here], temp_d.at[end])],
+            )
+        )
+    ends = [
+        [jnp.where(lane >= 64, found[1][i][q ^ 1], found[0][i][q ^ 1]) for i in (0, 1)]
+        for q in range(4)
+    ]
+    both = moved(jnp.concatenate(polar_packs(ends), 0), mirror)
+    for pc in (0, 1):
+        pack = both[pc * rows : (pc + 1) * rows]
+        polar_ref[pc] = pack
+        corner_ref[pc, :8] = pack[:8]
+        corner_ref[pc, 8:] = pack[rows - 8 :]
+
+
 def prepare_kernel(
-    right_ref, weight_ref, flag_ref,
-    s_ref, d_ref, e_ref, to_left, to_right, polar_ref, corner_low, corner_high,
+    right_ref, weight_ref, polar_first, flag_ref,
+    s_ref, d_ref, e_ref, to_left, to_right,
     right_buf, weight_buf, temp_s, temp_d, scale_ref, sems,
 ):
     tiles, rows = s_ref.shape[1], s_ref.shape[2]
@@ -228,26 +294,11 @@
         )
         for copy in copies[group]:
             copy.start()
-    flag_cols = flag_ref.shape[0]
-    flag_lats = flag_ref.shape[1]
-    per_tile = rows // flag_cols
     matrix = splitter()
-    flags = jnp.concatenate(
-        [flag_ref[...].astype(F32), jnp.zeros((8 - flag_cols, flag_lats), F32)], 0
-    )
-    lat = lax.broadcasted_iota(jnp.int32, (8, flag_lats), 1)
-    stacked = jnp.concatenate(
-        [jnp.where(lat // 8 == c, flags, 0.0) for c in range(tiles)], 0
-    ).astype(BF16)
-    spread = selector((flag_lats, LANES), lambda a, b: a % 8 == b // (TILE // 2))
-    spread_flags = jnp.dot(stacked, spread, preferred_element_type=F32)
-    scale_ref[...] = jnp.where(spread_flags > 0.5, SEAM_SCALE, 1.0).reshape(tiles, 8, LANES)
+    scale_ref[...] = seam_scales(flag_ref, range(tiles))
 
     def piece(c, source, weight):
-        scales = scale_ref[c]
-        scale = jnp.concatenate(
-            [jnp.broadcast_to(scales[i : i + 1], (per_tile, LANES)) for i in range(flag_cols)], 0
-        )
+        scale = seam_rows(scale_ref[c], flag_ref.shape[0], rows)
         screen = [w * scale for w in weight]
         e_ref[c] = (screen[0] + screen[1]) + (screen[2] + screen[3])
         diag = [4.0 + s for s in screen]
@@ -276,19 +327,6 @@
                     quarters_of(weight[here], temp_d.at[i]),
                 )
 
-    mirror = selector((LANES, LANES), lambda a, b: a + b == LANES - 1)
-    lane = lane_ids(rows)
-    ends = [
-        [jnp.where(lane >= 64, ref[q ^ 1, tiles - 1], ref[q ^ 1, 0]) for ref in (s_ref, d_ref)]
-        for q in range(4)
-    ]
-    both = moved(jnp.concatenate(polar_packs(ends), 0), mirror)
-    for pc in (0, 1):
-        pack = both[pc * rows : (pc + 1) * rows]
-        polar_ref[pc] = pack
-        corner_low[pc] = pack[:8]
-        corner_high[pc] = pack[rows - 8 :]
-
 
 def split_tiles(load, tiles, rows, matrix, temp, use):
     for start in range(0, tiles, BATCH):
@@ -415,13 +453,21 @@
 
 
 def fine_kernel(
-    s_ref, d_ref, i_ref, d1_ref, from_left, from_right, polar_ref, corner_left, corner_right,
+    s_ref, d_ref, i_ref, d1_ref, from_left, from_right, mates, others,
     r_ref, s1_ref, d1_virtual, d2_virtual, to_left, to_right,
     v0, v1, v2, v3, c0, c1, hs, hd, hi, ps, pd, pi, n1, temp,
 ):
     v = [v0, v1, v2, v3]
     tiles, rows = s_ref.shape[1], s_ref.shape[2]
     sub = row_ids(8)
+    count = lax.axis_size("lon")
+    me = lax.axis_index("lon")
+    odd = lax.rem(me, 2)
+    across = 2 * (1 - me // (count // 2))
+    polar_ref = mates.at[odd + across]
+    beside = mates.at[1 - odd + across]
+    behind = lax.rem(me + count - 1 + odd, count) // (count // 2)
+    far = others.at[2 * (1 - behind) + odd]
 
     def halo(t, _):
         fill_halo(t, from_left, from_right, False, hs, hd, hi)
@@ -430,9 +476,14 @@
     loop(tiles, halo)
     total = -16.0
     for q in range(4):
-        left_s, left_d = polar_unpacked(corner_left, q)
         own_s, own_d = polar_unpacked(polar_ref, q)
-        right_s, right_d = polar_unpacked(corner_right, q)
+        beside_s, beside_d = polar_unpacked(beside, q)
+        low_s, low_d = polar_unpacked(far.at[:, :8], q)
+        high_s, high_d = polar_unpacked(far.at[:, 8:], q)
+        left_s = jnp.where(odd == 1, beside_s[rows - 8 :], high_s)
+        left_d = jnp.where(odd == 1, beside_d[rows - 8 :], high_d)
+        right_s = jnp.where(odd == 1, low_s, beside_s[:8])
+        right_d = jnp.where(odd == 1, low_d, beside_d[:8])
         total = total + own_d
         ps[q] = own_s
         pd[q] = own_d
@@ -511,7 +562,7 @@
 
 
 def middle_kernel(
-    s_ref, d_ref, i_ref, d_virtual, d2_ref, d2_virtual, from_left, from_right,
+    merged_first, s_ref, d_ref, i_ref, d_virtual, d2_ref, d2_virtual, from_left, from_right,
     s2_ref, to_left, to_right,
     v0, v1, v2, v3, c0, c1, hs, hd, hi, pi,
 ):
@@ -597,6 +648,7 @@
         out_specs=[HBM] * far_out + [VMEM] * (len(out_shapes) - far_out),
         scratch_shapes=scratch,
         compiler_params=pltpu.CompilerParams(vmem_limit_bytes=40 * 2**20),
+        cost_estimate=pl.CostEstimate(flops=2**10, bytes_accessed=2**10, transcendentals=0),
     )(*args)
 
 
@@ -614,20 +666,29 @@
     right_side = pltpu.with_memory_space_constraint(right_side, pltpu.HBM)
     texel_weight = pltpu.with_memory_space_constraint(texel_weight, pltpu.HBM)
 
+    polar, corners = call(
+        polar_kernel,
+        [(2, rows, LANES), (2, 16, LANES)],
+        [(2, columns, 256), pltpu.VMEM((2, columns, 256), BF16)] + [(2, 2, columns, LANES)] * 2,
+        right_side, texel_weight, seam_flags,
+        sems=(2, 2), far_in=2,
+    )
+    count = lax.axis_size("lon")
+    pairs = [(i, i + 1, i + half_turn, i + half_turn + 1) for i in range(half_turn)]
+    groups = [[i % count for i in pair] for pair in pairs]
+    mates = lax.all_gather(polar, "lon", axis_index_groups=groups[0::2])
+    others = lax.all_gather(corners, "lon", axis_index_groups=groups[1::2])
+
     quarters = (4, tiles, rows, LANES)
-    s, d, e, to_left, to_right, polar, corner_low, corner_high = call(
+    s, d, e, to_left, to_right = call(
         prepare_kernel,
-        [quarters, quarters, quarters[1:], (2, tiles, 8, LANES), (2, tiles, 8, LANES)]
-        + [(2, rows, LANES), (2, 8, LANES), (2, 8, LANES)],
+        [quarters, quarters, quarters[1:], (2, tiles, 8, LANES), (2, tiles, 8, LANES)],
         [(columns, height), pltpu.VMEM((columns, height), BF16), temp, temp, (tiles, 8, LANES)],
-        right_side, texel_weight, seam_flags,
-        sems=(2, GROUPS), far_in=2,
+        right_side, texel_weight, polar, seam_flags,
+        sems=(2, GROUPS), far_in=3,
     )
     from_left = shifted(to_right, 1)
     from_right = shifted(to_left, -1)
-    polar = shifted(polar, half_turn)
-    corner_left = shifted(corner_high, half_turn + 1)
-    corner_right = shifted(corner_low, half_turn - 1)
     quarters1 = (4, tiles1, rows1, LANES)
     inverse, d1, i1, d2 = call(
         screens_kernel,
@@ -647,7 +708,7 @@
         level_scratch(tiles, rows)
         + [(4, rows, LANES)] * 3
         + [(tiles + 1, rows, LANES), (BATCH, 2, rows, LANES)],
-        s, d, inverse, d1, from_left, from_right, polar, corner_left, corner_right,
+        s, d, inverse, d1, from_left, from_right, mates, others,
     )
     from_left = shifted(to_right, 1)
     from_right = shifted(to_left, -1)
@@ -660,7 +721,8 @@
         middle_kernel,
         [(tiles1 + 1, rows1, LANES), pack2, pack2],
         level_scratch(tiles1, rows1) + [(4, rows1, LANES)],
-        s1, d1, i1, d1_virtual, d2, d2_virtual, from_left, from_right,
+        fine_residual, s1, d1, i1, d1_virtual, d2, d2_virtual, from_left, from_right,
+        far_in=1,
     )
     from_left = shifted(to_right, 1)
     from_right = shifted(to_left, -1)

time: 39.5 us -> 56.9 us (1.44)
  blocking collectives: 0 us -> 20.1 us
  starting transfers between devices: 18.4 us -> 14.6 us
  waiting for transfers between devices: 4.61 us -> 2.91 us
  local copies, waits for them, and re-layouts: 0.67 us -> 2.27 us
  Pallas kernels: 14.9 us -> 16.2 us
    all_gather x0 -> x2, blocking collectives: none -> 20.1 us  [the longest x1 13.5 us: body(): others = lax.all_gather(corners, 'lon', axis_index_groups=groups[1::2])]
    ppermute x9 -> x6, starting transfers between devices: 18.4 us -> 14.6 us  [shifted(): return lax.ppermute(x, 'lon', [(i, (i + by) % count) for i in range(count)])]
    ppermute x9 -> x6, waiting for transfers between devices: 4.61 us -> 2.91 us  [shifted(): return lax.ppermute(x, 'lon', [(i, (i + by) % count) for i in range(count)])]
    unnamed x2 -> x4, local copies, waits for them, and re-layouts: 0.67 us -> 2.27 us
    pallas_call x6 -> x7, Pallas kernels: 14.9 us -> 16.2 us  [call(): pl.pallas_call(kernel, out_shape=[jax.ShapeDtypeStruct(shape, F32) for sh...]
  transfers between devices with their start and end apart: 9 -> 6, of which waited for: 4 -> 2; matrix products, arithmetic and copies ran while one was open for 0% -> 0% of each run, Pallas kernels for 6% -> 4%
where the time goes in v4:
time: 56.9 us; the launch traced here: 56.7 us
  blocking collectives  20.1 us (35%)
  Pallas kernels  16.2 us (28%)
  starting transfers between devices  14.6 us (26%)
  waiting for transfers between devices  2.91 us (5%)
  local copies, waits for them, and re-layouts  2.27 us (4%)
  between operations  0.7 us (1%)
    pallas_call x7, Pallas kernels, call(): pl.pallas_call(kernel, out_shape=[jax.ShapeDtypeStruct(shape, F32) for sh...  16.2 us
    ppermute x6, starting transfers between devices, shifted(): return lax.ppermute(x, 'lon', [(i, (i + by) % count) for i in range(count)])  14.6 us
    all_gather x1, blocking collectives, body(): others = lax.all_gather(corners, 'lon', axis_index_groups=groups[1::2])  13.5 us
    all_gather x1, blocking collectives, body(): mates = lax.all_gather(polar, 'lon', axis_index_groups=groups[0::2])  6.62 us
    ppermute x6, waiting for transfers between devices, shifted(): return lax.ppermute(x, 'lon', [(i, (i + by) % count) for i in range(count)])  2.91 us
    unnamed x4, local copies, waits for them, and re-layouts  2.27 us
  transfers between devices with their start and end apart: 6, of which 2 were waited for; matrix products, arithmetic and copies ran while one was open for 0% of the time, Pallas kernels for 4%

profile of v4, /device:TPU:0, one launch (start us, length us, event | category | flops | bytes accessed | tf_op | source)
XLA Modules:
  0.0 56.7 jit_solution(8027085898736077751)
XLA Ops:
  0.6 0.0 copy-start.1
  0.6 0.7 %copy-done.1 = s32[2,256]{1,0:T(2,128)S(1)} copy-done((s32[2,256]{1,0:T(2,128)S(1)}, s32[2,256]{1,0:T(2,128)}, u32[]{:S(2)}) %copy-start.1) | copy-done | bytes 2072
  1.3 1.4 %shard_map.58 = (f32[2,32,128]{2,1,0:T(8,128)S(1)}, f32[2,16,128]{2,1,0:T(8,128)S(1)}) custom-call(f32[64,8192]{1,0:T(8,128)} %right_ref.3, bf16[64,8192]{1,0:T(8,128)(2,1)} %weight_ref.3, s32[2,256]{1,0:T(2,128)S(1)} %copy-done.1), custom_call_target="tpu_custom_call" | custom-call | flops 1024 | bytes 1024 | tf_op jit(solution)/shard_map/pallas_call | solution.py:644
  2.7 3.1 %shard_map.59 = (f32[4,32,32,128]{3,2,1,0:T(8,128)S(1)}, f32[4,32,32,128]{3,2,1,0:T(8,128)S(1)}, f32[32,32,128]{2,1,0:T(8,128)S(1)}, f32[2,32,8,128]{3,2,1,0:T(8,128)S(1)}, f32[2,32,8,128]{3,2,1,0:T(8,128)S(1)}) custom-call(f32[64,8192]{1,0:T(8,128)} %right_ref.3, bf16[64,8192]{1,0:T(8,128)(2,1)} %weight_ref.3, ...), custom_call_target="tpu_custom_call" | custom-call | flops 1024 | bytes 1024 | tf_op jit(solution)/shard_map/pallas_call | solution.py:644
  5.8 0.5 collective-permute-start
  6.3 5.0 %collective-permute-start.1 = (f32[2,32,8,128]{3,2,1,0:T(8,128)S(1)}, f32[2,32,8,128]{3,2,1,0:T(8,128)S(1)}, u32[]{:S(2)}, u32[]{:S(2)}) collective-permute-start(f32[2,32,8,128]{3,2,1,0:T(8,128)S(1)} %get-tuple-element.32), channel_id=1, source_target_pairs={{0,15},{1,0},{2,1},{3,2},{4,3},{5,4},{6,5},{7,6},{8,7},{9,8},{10,9... | collective-permute-start | bytes 786440 | tf_op jit(solution)/shard_map/ppermute | solution.py:657
  11.4 0.7 %shard_map.60 = (f32[4,32,32,128]{3,2,1,0:T(8,128)S(1)}, f32[4,16,16,128]{3,2,1,0:T(8,128)S(1)}, f32[4,16,16,128]{3,2,1,0:T(8,128)S(1)}, f32[16,16,128]{2,1,0:T(8,128)S(1)}) custom-call(f32[4,32,32,128]{3,2,1,0:T(8,128)S(1)} %get-tuple-element.27.d_ref, f32[32,32,128]{2,1,0:T(8,128)S(1)} %get-tuple-element.28.e_ref), custom_call_target="tpu_custom_call" | custom-call | flops 1024 | bytes 1024 | tf_op jit(solution)/shard_map/pallas_call | solution.py:644
  12.0 13.5 %all-gather.1 = f32[8,16,128]{2,1,0:T(8,128)S(1)} all-gather(f32[2,16,128]{2,1,0:T(8,128)S(1)} %get-tuple-element.33), channel_id=3, replica_groups={{1,2,9,10},{3,4,11,12},{5,6,13,14},{7,8,15,0},{17,18,25,26},{19,20,27,2..., dimensions={0}, use_global_device_ids=true | all-gather | bytes 81920 | tf_op jit(solution)/shard_map/all_gather | solution.py:680
  25.5 6.6 %all-gather = f32[8,32,128]{2,1,0:T(8,128)S(1)} all-gather(f32[2,32,128]{2,1,0:T(8,128)S(1)} %get-tuple-element.25.polar_first), channel_id=2, replica_groups={{0,1,8,9},{2,3,10,11},{4,5,12,13},{6,7,14,15},{16,17,24,25},{18,19,26,2..., dimensions={0}, use_global_device_ids=true | all-gather | bytes 163840 | tf_op jit(solution)/shard_map/all_gather | solution.py:679
  32.1 0.0 collective-permute-done.from_left
  32.1 0.0 collective-permute-done.1.from_right
  32.1 6.3 %shard_map.61 = (f32[4,32,32,128]{3,2,1,0:T(8,128)S(1)}, f32[4,17,16,128]{3,2,1,0:T(8,128)S(1)}, f32[4,16,128]{2,1,0:T(8,128)S(1)}, f32[16,128]{1,0:T(8,128)S(1)...) custom-call(f32[4,32,32,128]{3,2,1,0:T(8,128)S(1)} %get-tuple-element.26.s_ref, ...), custom_call_target="tpu_custom_call" | custom-call | flops 1024 | bytes 1024 | tf_op jit(solution)/shard_map/pallas_call | solution.py:644
  38.4 0.4 collective-permute-start.2
  38.8 4.1 %collective-permute-start.3 = (f32[2,17,8,128]{3,2,1,0:T(8,128)S(1)}, f32[2,17,8,128]{3,2,1,0:T(8,128)S(1)}, u32[]{:S(2)}, u32[]{:S(2)}) collective-permute-start(f32[2,17,8,128]{3,2,1,0:T(8,128)S(1)} %get-tuple-element.41), channel_id=1, source_target_pairs={{0,15},{1,0},{2,1},{3,2},{4,3},{5,4},{6,5},{7,6},{8,7},{9,8},{10,9... | collective-permute-start | bytes 417800 | tf_op jit(solution)/shard_map/ppermute | solution.py:657
  42.9 1.8 %shard_map.62.merged_first = f32[64,8192]{1,0:T(8,128)} custom-call(f32[4,32,32,128]{3,2,1,0:T(8,128)S(1)} %get-tuple-element.34.r_ref), custom_call_target="tpu_custom_call" | custom-call | flops 1024 | bytes 1024 | tf_op jit(solution)/shard_map/pallas_call | solution.py:644
  44.7 1.0 %collective-permute-done.2.from_left = f32[2,17,8,128]{3,2,1,0:T(8,128)S(1)} collective-permute-done((f32[2,17,8,128]{3,2,1,0:T(8,128)S(1)}, f32[2,17,8,128]{3,2,1,0:T(8,128)S(1)}, u32[]{:S(2)}, u32[]{:S(2)}) %collective-permute-start.2) | collective-permute-done | bytes 139296 | tf_op jit(solution)/shard_map/ppermute | solution.py:657
  45.6 0.0 collective-permute-done.3.from_right
  45.6 0.0 copy-start
  45.6 1.6 %copy-done = f32[64,8192]{1,0:T(8,128)S(1)} copy-done((f32[64,8192]{1,0:T(8,128)S(1)}, f32[64,8192]{1,0:T(8,128)}, u32[]{:S(2)}) %copy-start) | copy-done | bytes 2097176
  47.2 1.2 %shard_map.63 = (f32[17,16,128]{2,1,0:T(8,128)S(1)}, f32[17,8,128]{2,1,0:T(8,128)S(1)}, f32[17,8,128]{2,1,0:T(8,128)S(1)}) custom-call(f32[64,8192]{1,0:T(8,128)S(1)} %copy-done, f32[4,17,16,128]{3,2,1,0:T(8,128)S(1)} %get-tuple-element.35.s_ref, f32[4,16,16,128]{3,2,1,0:T(8,128)S(1)} %get-tuple-element.30.d1_ref.d_ref, ...), custom_call_target="tpu_custom_call" | custom-call | flops 1024 | bytes 1024 | tf_op jit(solution)/shard_map/pallas_call | solution.py:644
  48.5 0.1 collective-permute-start.4
  48.5 4.5 %collective-permute-start.5 = (f32[17,8,128]{2,1,0:T(8,128)S(1)}, f32[17,8,128]{2,1,0:T(8,128)S(1)}, u32[]{:S(2)}, u32[]{:S(2)}) collective-permute-start(f32[17,8,128]{2,1,0:T(8,128)S(1)} %get-tuple-element.44), channel_id=1, source_target_pairs={{0,15},{1,0},{2,1},{3,2},{4,3},{5,4},{6,5},{7,6},{8,7},{9,8},{10,9... | collective-permute-start | bytes 208904 | tf_op jit(solution)/shard_map/ppermute | solution.py:657
  53.0 1.9 %collective-permute-done.4.from_left = f32[17,8,128]{2,1,0:T(8,128)S(1)} collective-permute-done((f32[17,8,128]{2,1,0:T(8,128)S(1)}, f32[17,8,128]{2,1,0:T(8,128)S(1)}, u32[]{:S(2)}, u32[]{:S(2)}) %collective-permute-start.4) | collective-permute-done | bytes 69664 | tf_op jit(solution)/shard_map/ppermute | solution.py:657
  55.0 0.0 collective-permute-done.5.from_right
  55.0 1.7 %shard_map.64 = (f32[16,2048]{1,0:T(8,128)}, f32[16,2048]{1,0:T(8,128)}) custom-call(f32[17,16,128]{2,1,0:T(8,128)S(1)} %get-tuple-element.42.s_ref, f32[16,16,128]{2,1,0:T(8,128)S(1)} %get-tuple-element.38.d2_ref.d_ref, f32[16,128]{1,0:T(8,128)S(1)} %get-tuple-element.39.d2_virtual.d_virtual, f32[17,8,128]{2,1,0:T(8,128)S(1)} %collective-permute-done.4.from_left, ...), custom_call_target="tpu_custom_call" | custom-call | flops 1024 | bytes 1024 | tf_op jit(solution)/shard_map/pallas_call | solution.py:644
Async XLA Ops:
  0.6 0.7 %copy-start.1 = (s32[2,256]{1,0:T(2,128)S(1)}, s32[2,256]{1,0:T(2,128)}, u32[]{:S(2)}) copy-start(s32[2,256]{1,0:T(2,128)} %flag_ref.3) | copy-start | bytes 6148
  5.8 26.3 %collective-permute-start = (f32[2,32,8,128]{3,2,1,0:T(8,128)S(1)}, f32[2,32,8,128]{3,2,1,0:T(8,128)S(1)}, u32[]{:S(2)}, u32[]{:S(2)}) collective-permute-start(f32[2,32,8,128]{3,2,1,0:T(8,128)S(1)} %get-tuple-element.31), channel_id=1, source_target_pairs={{0,1},{1,2},{2,3},{3,4},{4,5},{5,6},{6,7},{7,8},{8,9},{9,10},{10,1... | collective-permute-start | bytes 786440 | tf_op jit(solution)/shard_map/ppermute | solution.py:657
  6.3 25.8 %collective-permute-start.1 = (f32[2,32,8,128]{3,2,1,0:T(8,128)S(1)}, f32[2,32,8,128]{3,2,1,0:T(8,128)S(1)}, u32[]{:S(2)}, u32[]{:S(2)}) collective-permute-start(f32[2,32,8,128]{3,2,1,0:T(8,128)S(1)} %get-tuple-element.32), channel_id=1, source_target_pairs={{0,15},{1,0},{2,1},{3,2},{4,3},{5,4},{6,5},{7,6},{8,7},{9,8},{10,9... | collective-permute-start | bytes 786440 | tf_op jit(solution)/shard_map/ppermute | solution.py:657
  38.4 7.2 %collective-permute-start.2 = (f32[2,17,8,128]{3,2,1,0:T(8,128)S(1)}, f32[2,17,8,128]{3,2,1,0:T(8,128)S(1)}, u32[]{:S(2)}, u32[]{:S(2)}) collective-permute-start(f32[2,17,8,128]{3,2,1,0:T(8,128)S(1)} %get-tuple-element.40), channel_id=1, source_target_pairs={{0,1},{1,2},{2,3},{3,4},{4,5},{5,6},{6,7},{7,8},{8,9},{9,10},{10,1... | collective-permute-start | bytes 417800 | tf_op jit(solution)/shard_map/ppermute | solution.py:657
  38.8 6.8 %collective-permute-start.3 = (f32[2,17,8,128]{3,2,1,0:T(8,128)S(1)}, f32[2,17,8,128]{3,2,1,0:T(8,128)S(1)}, u32[]{:S(2)}, u32[]{:S(2)}) collective-permute-start(f32[2,17,8,128]{3,2,1,0:T(8,128)S(1)} %get-tuple-element.41), channel_id=1, source_target_pairs={{0,15},{1,0},{2,1},{3,2},{4,3},{5,4},{6,5},{7,6},{8,7},{9,8},{10,9... | collective-permute-start | bytes 417800 | tf_op jit(solution)/shard_map/ppermute | solution.py:657
  45.6 1.6 %copy-start = (f32[64,8192]{1,0:T(8,128)S(1)}, f32[64,8192]{1,0:T(8,128)}, u32[]{:S(2)}) copy-start(f32[64,8192]{1,0:T(8,128)} %shard_map.62.merged_first) | copy-start | bytes 6291460
  48.5 6.5 %collective-permute-start.4 = (f32[17,8,128]{2,1,0:T(8,128)S(1)}, f32[17,8,128]{2,1,0:T(8,128)S(1)}, u32[]{:S(2)}, u32[]{:S(2)}) collective-permute-start(f32[17,8,128]{2,1,0:T(8,128)S(1)} %get-tuple-element.43), channel_id=1, source_target_pairs={{0,1},{1,2},{2,3},{3,4},{4,5},{5,6},{6,7},{7,8},{8,9},{9,10},{10,1... | collective-permute-start | bytes 208904 | tf_op jit(solution)/shard_map/ppermute | solution.py:657
  48.5 6.4 %collective-permute-start.5 = (f32[17,8,128]{2,1,0:T(8,128)S(1)}, f32[17,8,128]{2,1,0:T(8,128)S(1)}, u32[]{:S(2)}, u32[]{:S(2)}) collective-permute-start(f32[17,8,128]{2,1,0:T(8,128)S(1)} %get-tuple-element.44), channel_id=1, source_target_pairs={{0,15},{1,0},{2,1},{3,2},{4,3},{5,4},{6,5},{7,6},{8,7},{9,8},{10,9... | collective-permute-start | bytes 208904 | tf_op jit(solution)/shard_map/ppermute | solution.py:657

commit v5 on v3

--- a/solution.py
+++ b/solution.py
@@ -168,10 +168,24 @@
     return source, diag
 
 
-def fill_halo(t, left, right, swapped, hs, hd, hi):
-    source, diag = unpacked_halo(
-        (left[0, t], left[1, t]), (right[0, t], right[1, t]), swapped
-    )
+def is_odd():
+    return lax.rem(lax.axis_index("lon"), 2) == 1
+
+
+def chosen(odd, a, b):
+    return jnp.where(odd, a, b), jnp.where(odd, b, a)
+
+
+def store_edges(t, packs, odd, to_mate, to_other):
+    right, left = packs
+    for i in (0, 1):
+        to_mate[i, t], to_other[i, t] = chosen(odd, left[i], right[i])
+
+
+def fill_halo(t, from_mate, from_other, odd, swapped, hs, hd, hi):
+    al, ar = chosen(odd, from_mate[0, t], from_other[0, t])
+    bl, br = chosen(odd, from_mate[1, t], from_other[1, t])
+    source, diag = unpacked_halo((al, bl), (ar, br), swapped)
     for q in range(4):
         hs[q, t] = source[q]
         hd[q, t] = diag[q]
@@ -212,9 +226,12 @@
 
 def prepare_kernel(
     right_ref, weight_ref, flag_ref,
-    s_ref, d_ref, e_ref, to_left, to_right, polar_ref, corner_low, corner_high,
-    right_buf, weight_buf, temp_s, temp_d, scale_ref, sems,
+    s_ref, d_ref, e_ref, to_mate, to_other, polar_ref, corner_near, corner_far,
+    right_buf, weight_buf, flag_buf, temp_s, temp_d, scale_ref, sems,
 ):
+    flag_copy = pltpu.make_async_copy(flag_ref, flag_buf, sems.at[0, GROUPS])
+    flag_copy.start()
+    odd = is_odd()
     tiles, rows = s_ref.shape[1], s_ref.shape[2]
     chunk = right_ref.shape[1] // GROUPS
     copies = []
@@ -228,12 +245,13 @@
         )
         for copy in copies[group]:
             copy.start()
+    flag_copy.wait()
     flag_cols = flag_ref.shape[0]
     flag_lats = flag_ref.shape[1]
     per_tile = rows // flag_cols
     matrix = splitter()
     flags = jnp.concatenate(
-        [flag_ref[...].astype(F32), jnp.zeros((8 - flag_cols, flag_lats), F32)], 0
+        [flag_buf[...].astype(F32), jnp.zeros((8 - flag_cols, flag_lats), F32)], 0
     )
     lat = lax.broadcasted_iota(jnp.int32, (8, flag_lats), 1)
     stacked = jnp.concatenate(
@@ -254,9 +272,7 @@
         for q in range(4):
             s_ref[q, c] = source[q]
             d_ref[q, c] = diag[q]
-        right, left = edge_packs(source, diag, False)
-        to_right[0, c], to_right[1, c] = right
-        to_left[0, c], to_left[1, c] = left
+        store_edges(c, edge_packs(source, diag, False), odd, to_mate, to_other)
 
     columns = right_ref.shape[0]
     for group in range(GROUPS):
@@ -286,8 +302,7 @@
     for pc in (0, 1):
         pack = both[pc * rows : (pc + 1) * rows]
         polar_ref[pc] = pack
-        corner_low[pc] = pack[:8]
-        corner_high[pc] = pack[rows - 8 :]
+        corner_near[pc], corner_far[pc] = chosen(odd, pack[:8], pack[rows - 8 :])
 
 
 def split_tiles(load, tiles, rows, matrix, temp, use):
@@ -415,24 +430,27 @@
 
 
 def fine_kernel(
-    s_ref, d_ref, i_ref, d1_ref, from_left, from_right, polar_ref, corner_left, corner_right,
-    r_ref, s1_ref, d1_virtual, d2_virtual, to_left, to_right,
+    s_ref, d_ref, i_ref, d1_ref, from_mate, from_other, polar_ref, corner_near, corner_far,
+    r_ref, s1_ref, d1_virtual, d2_virtual, to_mate, to_other,
     v0, v1, v2, v3, c0, c1, hs, hd, hi, ps, pd, pi, n1, temp,
 ):
     v = [v0, v1, v2, v3]
     tiles, rows = s_ref.shape[1], s_ref.shape[2]
     sub = row_ids(8)
+    odd = is_odd()
 
     def halo(t, _):
-        fill_halo(t, from_left, from_right, False, hs, hd, hi)
+        fill_halo(t, from_mate, from_other, odd, False, hs, hd, hi)
         return 0
 
     loop(tiles, halo)
     total = -16.0
     for q in range(4):
-        left_s, left_d = polar_unpacked(corner_left, q)
         own_s, own_d = polar_unpacked(polar_ref, q)
-        right_s, right_d = polar_unpacked(corner_right, q)
+        near_s, near_d = polar_unpacked(corner_near, q)
+        far_s, far_d = polar_unpacked(corner_far, q)
+        left_s, right_s = chosen(odd, near_s, far_s)
+        left_d, right_d = chosen(odd, near_d, far_d)
         total = total + own_d
         ps[q] = own_s
         pd[q] = own_d
@@ -444,14 +462,14 @@
         hi[q, tiles] = 1.0 / diag
 
     load_s = loader(s_ref, hs, ps, tiles)
-    smooth(v, load_s, loader(i_ref, hi, pi, tiles), tiles, 8)
+    smooth(v, load_s, loader(i_ref, hi, pi, tiles), tiles, 16)
 
     def keep(t, r):
         if not (isinstance(t, int) and t == tiles):
             for q in range(4):
                 r_ref[q, t] = r[q][:rows]
 
-    residuals(v, load_s, loader(d_ref, hd, pd, tiles), tiles, c0, c1, keep, 4)
+    residuals(v, load_s, loader(d_ref, hd, pd, tiles), tiles, c0, c1, keep, 8)
 
     def coarse(t, _):
         n1[t] = restricted(c0, c1, t, tiles, rows)
@@ -461,9 +479,7 @@
     coarse(tiles, 0)
 
     def edges(t, source, diag, swapped):
-        right, left = edge_packs(source, diag, swapped)
-        to_right[0, t], to_right[1, t] = right
-        to_left[0, t], to_left[1, t] = left
+        store_edges(t, edge_packs(source, diag, swapped), odd, to_mate, to_other)
 
     def use(c, source):
         for q in range(4):
@@ -511,14 +527,15 @@
 
 
 def middle_kernel(
-    s_ref, d_ref, i_ref, d_virtual, d2_ref, d2_virtual, from_left, from_right,
-    s2_ref, to_left, to_right,
+    merged_first, s_ref, d_ref, i_ref, d_virtual, d2_ref, d2_virtual, from_mate, from_other,
+    s2_ref, to_mate, to_other,
     v0, v1, v2, v3, c0, c1, hs, hd, hi, pi,
 ):
     v = [v0, v1, v2, v3]
     tiles, rows = d_ref.shape[1], d_ref.shape[2]
+    odd = is_odd()
     for t in range(tiles + 1):
-        fill_halo(t, from_left, from_right, t == tiles, hs, hd, hi)
+        fill_halo(t, from_mate, from_other, odd, t == tiles, hs, hd, hi)
     for q in range(4):
         pi[q] = 1.0 / d_virtual[q]
 
@@ -534,12 +551,13 @@
         value = restricted(c0, c1, t, tiles, rows)
         diag = d2_virtual[...] if t == tiles else d2_ref[t]
         s2_ref[t] = value
-        to_right[t] = jnp.where(sub < 4, roll_rows(value[rows - 8 :], 4), diag[rows - 8 :])
-        to_left[t] = jnp.where(sub < 4, value[:8], roll_rows(diag[:8], 4))
+        right = jnp.where(sub < 4, roll_rows(value[rows - 8 :], 4), diag[rows - 8 :])
+        left = jnp.where(sub < 4, value[:8], roll_rows(diag[:8], 4))
+        to_mate[t], to_other[t] = chosen(odd, left, right)
 
 
 def last_kernel(
-    s_ref, d_ref, d_virtual, from_left, from_right,
+    s_ref, d_ref, d_virtual, from_mate, from_other,
     solution_ref, residual_ref,
     s, d, inv, va, vb,
 ):
@@ -549,8 +567,9 @@
     lane, row = lane_ids(rows), row_ids(rows)
     even = (lane + row) % 2 == 0
     odd = jnp.logical_not(even)
+    odd_band = is_odd()
     for t in range(tiles + 1):
-        left, right = from_left[t], from_right[t]
+        left, right = chosen(odd_band, from_mate[t], from_other[t])
         diag = d_virtual[...] if t == tiles else d_ref[t]
         source = jnp.concatenate(
             [s_ref[t], jnp.where(sub < 4, right, roll_rows(left, 4))], 0
@@ -600,9 +619,15 @@
     )(*args)
 
 
-def shifted(x, by):
+def swapped_with(x, by):
     count = lax.axis_size("lon")
-    return lax.ppermute(x, "lon", [(i, (i + by) % count) for i in range(count)])
+    pairs = [(i, (i + by) % count) for i in range(0, count, 2)]
+    return lax.ppermute(x, "lon", pairs + [(b, a) for a, b in pairs])
+
+
+def swapped_edges(to_mate, to_other):
+    from_other = swapped_with(to_other, -1)
+    return swapped_with(to_mate, 1), from_other
 
 
 def body(right_side, texel_weight, seam_flags):
@@ -613,21 +638,24 @@
     temp = (BATCH, 2, columns, LANES)
     right_side = pltpu.with_memory_space_constraint(right_side, pltpu.HBM)
     texel_weight = pltpu.with_memory_space_constraint(texel_weight, pltpu.HBM)
+    seam_flags = pltpu.with_memory_space_constraint(seam_flags, pltpu.HBM)
 
     quarters = (4, tiles, rows, LANES)
-    s, d, e, to_left, to_right, polar, corner_low, corner_high = call(
+    s, d, e, to_mate, to_other, polar, corner_near, corner_far = call(
         prepare_kernel,
         [quarters, quarters, quarters[1:], (2, tiles, 8, LANES), (2, tiles, 8, LANES)]
         + [(2, rows, LANES), (2, 8, LANES), (2, 8, LANES)],
-        [(columns, height), pltpu.VMEM((columns, height), BF16), temp, temp, (tiles, 8, LANES)],
+        [(columns, height), pltpu.VMEM((columns, height), BF16)]
+        + [pltpu.VMEM(seam_flags.shape, jnp.int32), temp, temp, (tiles, 8, LANES)],
         right_side, texel_weight, seam_flags,
-        sems=(2, GROUPS), far_in=2,
-    )
-    from_left = shifted(to_right, 1)
-    from_right = shifted(to_left, -1)
-    polar = shifted(polar, half_turn)
-    corner_left = shifted(corner_high, half_turn + 1)
-    corner_right = shifted(corner_low, half_turn - 1)
+        sems=(2, GROUPS + 1), far_in=3,
+    )
+    from_mate, from_other = swapped_edges(to_mate, to_other)
+    polar = lax.ppermute(
+        polar, "lon", [(i, (i + half_turn) % (2 * half_turn)) for i in range(2 * half_turn)]
+    )
+    corner_far = swapped_with(corner_far, half_turn - 1)
+    corner_near = swapped_with(corner_near, half_turn + 1)
     quarters1 = (4, tiles1, rows1, LANES)
     inverse, d1, i1, d2 = call(
         screens_kernel,
@@ -641,34 +669,34 @@
         return [(tiles + 1, rows + 8, LANES)] * 6 + [halo] * 3
 
     pack1 = (2, tiles1 + 1, 8, LANES)
-    r, s1, d1_virtual, d2_virtual, to_left, to_right = call(
+    r, s1, d1_virtual, d2_virtual, to_mate, to_other = call(
         fine_kernel,
         [quarters, (4, tiles1 + 1, rows1, LANES), (4, rows1, LANES), (rows1, LANES), pack1, pack1],
         level_scratch(tiles, rows)
         + [(4, rows, LANES)] * 3
         + [(tiles + 1, rows, LANES), (BATCH, 2, rows, LANES)],
-        s, d, inverse, d1, from_left, from_right, polar, corner_left, corner_right,
-    )
-    from_left = shifted(to_right, 1)
-    from_right = shifted(to_left, -1)
+        s, d, inverse, d1, from_mate, from_other, polar, corner_near, corner_far,
+    )
+    from_mate, from_other = swapped_edges(to_mate, to_other)
     (fine_residual,) = call(
         merge_kernel, [(columns, height)], [temp, (columns, height)], r,
         sems=(GROUPS,), far_out=1,
     )
     pack2 = (tiles1 + 1, 8, LANES)
-    s2, to_left, to_right = call(
+    s2, to_mate, to_other = call(
         middle_kernel,
         [(tiles1 + 1, rows1, LANES), pack2, pack2],
         level_scratch(tiles1, rows1) + [(4, rows1, LANES)],
-        s1, d1, i1, d1_virtual, d2, d2_virtual, from_left, from_right,
-    )
-    from_left = shifted(to_right, 1)
-    from_right = shifted(to_left, -1)
+        pltpu.with_memory_space_constraint(fine_residual, pltpu.HBM),
+        s1, d1, i1, d1_virtual, d2, d2_virtual, from_mate, from_other,
+        far_in=1,
+    )
+    from_mate, from_other = swapped_edges(to_mate, to_other)
     solution_2, residual_2 = call(
         last_kernel,
         [(columns // 4, height // 4)] * 2,
         [(tiles1 + 1, rows1 + 8, LANES)] * 5,
-        s2, d2, d2_virtual, from_left, from_right,
+        s2, d2, d2_virtual, from_mate, from_other,
     )
     return fine_residual, solution_2, residual_2
 

time: 39.5 us -> 40.6 us (1.028)
  waiting for transfers between devices: 4.61 us -> 10.8 us
  starting transfers between devices: 18.4 us -> 14.7 us
  local copies, waits for them, and re-layouts: 0.67 us -> 0 us
  Pallas kernels: 14.9 us -> 14.3 us
    ppermute x9, waiting for transfers between devices: 4.61 us -> 10.8 us  [the longest x8 10.5 us: swapped_with(): return lax.ppermute(x, 'lon', pairs + [(b, a) for a, b in pairs])]
    ppermute x9, starting transfers between devices: 18.4 us -> 14.7 us  [the longest x8 14.7 us: swapped_with(): return lax.ppermute(x, 'lon', pairs + [(b, a) for a, b in pairs])]
    unnamed x2 -> x0, local copies, waits for them, and re-layouts: 0.67 us -> none
    pallas_call x6, Pallas kernels: 14.9 us -> 14.3 us  [call(): pl.pallas_call(kernel, out_shape=[jax.ShapeDtypeStruct(shape, F32) for sh...]
  transfers between devices with their start and end apart: 9 -> 9, of which waited for: 4 -> 5; matrix products, arithmetic and copies ran while one was open for 0% -> 0% of each run, Pallas kernels for 6% -> 6%
where the time goes in v5:
time: 40.6 us; the launch traced here: 40.5 us
  starting transfers between devices  14.7 us (36%)
  Pallas kernels  14.3 us (35%)
  waiting for transfers between devices  10.8 us (27%)
  between operations  0.69 us (2%)
    ppermute x8, starting transfers between devices, swapped_with(): return lax.ppermute(x, 'lon', pairs + [(b, a) for a, b in pairs])  14.7 us
    pallas_call x6, Pallas kernels, call(): pl.pallas_call(kernel, out_shape=[jax.ShapeDtypeStruct(shape, F32) for sh...  14.3 us
    ppermute x8, waiting for transfers between devices, swapped_with(): return lax.ppermute(x, 'lon', pairs + [(b, a) for a, b in pairs])  10.5 us
  transfers between devices with their start and end apart: 9, of which 5 were waited for; matrix products, arithmetic and copies ran while one was open for 0% of the time, Pallas kernels for 6%

profile of v5, /device:TPU:0, one launch (start us, length us, event | category | flops | bytes accessed | tf_op | source)
XLA Modules:
  0.0 40.5 jit_solution(5774318009223568600)
XLA Ops:
  0.6 3.4 %shard_map.58 = (f32[4,32,32,128]{3,2,1,0:T(8,128)S(1)}, f32[4,32,32,128]{3,2,1,0:T(8,128)S(1)}, f32[32,32,128]{2,1,0:T(8,128)S(1)}, f32[2,32,8,128]{3,2,1,0:T(8...) custom-call(f32[64,8192]{1,0:T(8,128)} %right_ref.1, ...), custom_call_target="tpu_custom_call" | custom-call | tf_op jit(solution)/shard_map/pallas_call | solution.py:612
  4.0 0.5 %collective-permute-start = (f32[2,32,8,128]{3,2,1,0:T(8,128)S(1)}, f32[2,32,8,128]{3,2,1,0:T(8,128)S(1)}, u32[]{:S(2)}, u32[]{:S(2)}) collective-permute-start(f32[2,32,8,128]{3,2,1,0:T(8,128)S(1)} %get-tuple-element.31), channel_id=1, source_target_pairs={{0,1},{2,3},{4,5},{6,7},{8,9},{10,11},{12,13},{14,15},{1,0},{3,2},... | collective-permute-start | bytes 786440 | tf_op jit(solution)/shard_map/ppermute | solution.py:625
  4.5 5.6 %collective-permute-start.1 = (f32[2,32,8,128]{3,2,1,0:T(8,128)S(1)}, f32[2,32,8,128]{3,2,1,0:T(8,128)S(1)}, u32[]{:S(2)}, u32[]{:S(2)}) collective-permute-start(f32[2,32,8,128]{3,2,1,0:T(8,128)S(1)} %get-tuple-element.32), channel_id=1, source_target_pairs={{0,15},{2,1},{4,3},{6,5},{8,7},{10,9},{12,11},{14,13},{15,0},{1,2}... | collective-permute-start | bytes 786440 | tf_op jit(solution)/shard_map/ppermute | solution.py:625
  10.2 0.0 collective-permute-start.2
  10.2 0.0 collective-permute-start.3
  10.2 1.1 %collective-permute-start.4 = (f32[2,8,128]{2,1,0:T(8,128)S(1)}, f32[2,8,128]{2,1,0:T(8,128)S(1)}, u32[]{:S(2)}, u32[]{:S(2)}) collective-permute-start(f32[2,8,128]{2,1,0:T(8,128)S(1)} %get-tuple-element.35), channel_id=1, source_target_pairs={{0,7},{2,9},{4,11},{6,13},{8,15},{10,1},{12,3},{14,5},{7,0},{9,2},... | collective-permute-start | bytes 24584 | tf_op jit(solution)/shard_map/ppermute | solution.py:625
  11.3 0.7 %shard_map.59 = (f32[4,32,32,128]{3,2,1,0:T(8,128)S(1)}, f32[4,16,16,128]{3,2,1,0:T(8,128)S(1)}, f32[4,16,16,128]{3,2,1,0:T(8,128)S(1)}, f32[16,16,128]{2,1,0:T(8,128)S(1)}) custom-call(f32[4,32,32,128]{3,2,1,0:T(8,128)S(1)} %get-tuple-element.27.d_ref, f32[32,32,128]{2,1,0:T(8,128)S(1)} %get-tuple-element.28.e_ref), custom_call_target="tpu_custom_call" | custom-call | tf_op jit(solution)/shard_map/pallas_call | solution.py:612
  12.0 2.7 %collective-permute-done.3.corner_near = f32[2,8,128]{2,1,0:T(8,128)S(1)} collective-permute-done((f32[2,8,128]{2,1,0:T(8,128)S(1)}, f32[2,8,128]{2,1,0:T(8,128)S(1)}, u32[]{:S(2)}, u32[]{:S(2)}) %collective-permute-start.3) | collective-permute-done | bytes 8224 | tf_op jit(solution)/shard_map/ppermute | solution.py:625
  14.7 0.1 collective-permute-done.4.corner_far
  14.8 0.2 collective-permute-done.2.polar_ref
  15.0 0.0 collective-permute-done.from_mate
  15.0 0.0 collective-permute-done.1.from_other
  15.0 5.6 %shard_map.60 = (f32[4,32,32,128]{3,2,1,0:T(8,128)S(1)}, f32[4,17,16,128]{3,2,1,0:T(8,128)S(1)}, f32[4,16,128]{2,1,0:T(8,128)S(1)}, f32[16,128]{1,0:T(8,128)S(1)...) custom-call(f32[4,32,32,128]{3,2,1,0:T(8,128)S(1)} %get-tuple-element.26.s_ref, ...), custom_call_target="tpu_custom_call" | custom-call | tf_op jit(solution)/shard_map/pallas_call | solution.py:612
  20.6 3.1 %collective-permute-start.5 = (f32[2,17,8,128]{3,2,1,0:T(8,128)S(1)}, f32[2,17,8,128]{3,2,1,0:T(8,128)S(1)}, u32[]{:S(2)}, u32[]{:S(2)}) collective-permute-start(f32[2,17,8,128]{3,2,1,0:T(8,128)S(1)} %get-tuple-element.42), channel_id=1, source_target_pairs={{0,1},{2,3},{4,5},{6,7},{8,9},{10,11},{12,13},{14,15},{1,0},{3,2},... | collective-permute-start | bytes 417800 | tf_op jit(solution)/shard_map/ppermute | solution.py:625
  23.8 2.1 %collective-permute-start.6 = (f32[2,17,8,128]{3,2,1,0:T(8,128)S(1)}, f32[2,17,8,128]{3,2,1,0:T(8,128)S(1)}, u32[]{:S(2)}, u32[]{:S(2)}) collective-permute-start(f32[2,17,8,128]{3,2,1,0:T(8,128)S(1)} %get-tuple-element.43), channel_id=1, source_target_pairs={{0,15},{2,1},{4,3},{6,5},{8,7},{10,9},{12,11},{14,13},{15,0},{1,2}... | collective-permute-start | bytes 417800 | tf_op jit(solution)/shard_map/ppermute | solution.py:625
  25.8 1.8 %shard_map.61.merged_first = f32[64,8192]{1,0:T(8,128)} custom-call(f32[4,32,32,128]{3,2,1,0:T(8,128)S(1)} %get-tuple-element.36.r_ref), custom_call_target="tpu_custom_call" | custom-call | tf_op jit(solution)/shard_map/pallas_call | solution.py:612
  27.6 0.0 collective-permute-done.5.from_mate
  27.6 3.3 %collective-permute-done.6.from_other = f32[2,17,8,128]{3,2,1,0:T(8,128)S(1)} collective-permute-done((f32[2,17,8,128]{3,2,1,0:T(8,128)S(1)}, f32[2,17,8,128]{3,2,1,0:T(8,128)S(1)}, u32[]{:S(2)}, u32[]{:S(2)}) %collective-permute-start.6) | collective-permute-done | bytes 139296 | tf_op jit(solution)/shard_map/ppermute | solution.py:625
  30.9 1.2 %shard_map.62 = (f32[17,16,128]{2,1,0:T(8,128)S(1)}, f32[17,8,128]{2,1,0:T(8,128)S(1)}, f32[17,8,128]{2,1,0:T(8,128)S(1)}) custom-call(f32[64,8192]{1,0:T(8,128)} %shard_map.61.merged_first, f32[4,17,16,128]{3,2,1,0:T(8,128)S(1)} %get-tuple-element.37.s_ref, f32[4,16,16,128]{3,2,1,0:T(8,128)S(1)} %get-tuple-element.30.d1_ref.d_ref, ...), custom_call_target="tpu_custom_call" | custom-call | tf_op jit(solution)/shard_map/pallas_call | solution.py:612
  32.2 0.1 collective-permute-start.7
  32.2 2.1 %collective-permute-start.8 = (f32[17,8,128]{2,1,0:T(8,128)S(1)}, f32[17,8,128]{2,1,0:T(8,128)S(1)}, u32[]{:S(2)}, u32[]{:S(2)}) collective-permute-start(f32[17,8,128]{2,1,0:T(8,128)S(1)} %get-tuple-element.46), channel_id=1, source_target_pairs={{0,15},{2,1},{4,3},{6,5},{8,7},{10,9},{12,11},{14,13},{15,0},{1,2}... | collective-permute-start | bytes 208904 | tf_op jit(solution)/shard_map/ppermute | solution.py:625
  34.4 0.0 collective-permute-done.7.from_mate
  34.4 4.4 %collective-permute-done.8.from_other = f32[17,8,128]{2,1,0:T(8,128)S(1)} collective-permute-done((f32[17,8,128]{2,1,0:T(8,128)S(1)}, f32[17,8,128]{2,1,0:T(8,128)S(1)}, u32[]{:S(2)}, u32[]{:S(2)}) %collective-permute-start.8) | collective-permute-done | bytes 69664 | tf_op jit(solution)/shard_map/ppermute | solution.py:625
  38.7 1.7 %shard_map.63 = (f32[16,2048]{1,0:T(8,128)}, f32[16,2048]{1,0:T(8,128)}) custom-call(f32[17,16,128]{2,1,0:T(8,128)S(1)} %get-tuple-element.44.s_ref, f32[16,16,128]{2,1,0:T(8,128)S(1)} %get-tuple-element.40.d2_ref.d_ref, f32[16,128]{1,0:T(8,128)S(1)} %get-tuple-element.41.d2_virtual.d_virtual, f32[17,8,128]{2,1,0:T(8,128)S(1)} %collective-permute-done.7.from_mate, ...), custom_call_target="tpu_custom_call" | custom-call | tf_op jit(solution)/shard_map/pallas_call | solution.py:612
Async XLA Ops:
  4.0 11.0 %collective-permute-start = (f32[2,32,8,128]{3,2,1,0:T(8,128)S(1)}, f32[2,32,8,128]{3,2,1,0:T(8,128)S(1)}, u32[]{:S(2)}, u32[]{:S(2)}) collective-permute-start(f32[2,32,8,128]{3,2,1,0:T(8,128)S(1)} %get-tuple-element.31), channel_id=1, source_target_pairs={{0,1},{2,3},{4,5},{6,7},{8,9},{10,11},{12,13},{14,15},{1,0},{3,2},... | collective-permute-start | bytes 786440 | tf_op jit(solution)/shard_map/ppermute | solution.py:625
  4.5 10.5 %collective-permute-start.1 = (f32[2,32,8,128]{3,2,1,0:T(8,128)S(1)}, f32[2,32,8,128]{3,2,1,0:T(8,128)S(1)}, u32[]{:S(2)}, u32[]{:S(2)}) collective-permute-start(f32[2,32,8,128]{3,2,1,0:T(8,128)S(1)} %get-tuple-element.32), channel_id=1, source_target_pairs={{0,15},{2,1},{4,3},{6,5},{8,7},{10,9},{12,11},{14,13},{15,0},{1,2}... | collective-permute-start | bytes 786440 | tf_op jit(solution)/shard_map/ppermute | solution.py:625
  10.2 4.9 %collective-permute-start.2 = (f32[2,32,128]{2,1,0:T(8,128)S(1)}, f32[2,32,128]{2,1,0:T(8,128)S(1)}, u32[]{:S(2)}, u32[]{:S(2)}) collective-permute-start(f32[2,32,128]{2,1,0:T(8,128)S(1)} %get-tuple-element.33), channel_id=1, source_target_pairs={{0,8},{1,9},{2,10},{3,11},{4,12},{5,13},{6,14},{7,15},{8,0},{9,1},... | collective-permute-start | bytes 98312 | tf_op jit(solution)/shard_map/ppermute | solution.py:654
  10.2 4.5 %collective-permute-start.3 = (f32[2,8,128]{2,1,0:T(8,128)S(1)}, f32[2,8,128]{2,1,0:T(8,128)S(1)}, u32[]{:S(2)}, u32[]{:S(2)}) collective-permute-start(f32[2,8,128]{2,1,0:T(8,128)S(1)} %get-tuple-element.34), channel_id=1, source_target_pairs={{0,9},{2,11},{4,13},{6,15},{8,1},{10,3},{12,5},{14,7},{9,0},{11,2}... | collective-permute-start | bytes 24584 | tf_op jit(solution)/shard_map/ppermute | solution.py:625
  10.2 4.6 %collective-permute-start.4 = (f32[2,8,128]{2,1,0:T(8,128)S(1)}, f32[2,8,128]{2,1,0:T(8,128)S(1)}, u32[]{:S(2)}, u32[]{:S(2)}) collective-permute-start(f32[2,8,128]{2,1,0:T(8,128)S(1)} %get-tuple-element.35), channel_id=1, source_target_pairs={{0,7},{2,9},{4,11},{6,13},{8,15},{10,1},{12,3},{14,5},{7,0},{9,2},... | collective-permute-start | bytes 24584 | tf_op jit(solution)/shard_map/ppermute | solution.py:625
  20.6 7.0 %collective-permute-start.5 = (f32[2,17,8,128]{3,2,1,0:T(8,128)S(1)}, f32[2,17,8,128]{3,2,1,0:T(8,128)S(1)}, u32[]{:S(2)}, u32[]{:S(2)}) collective-permute-start(f32[2,17,8,128]{3,2,1,0:T(8,128)S(1)} %get-tuple-element.42), channel_id=1, source_target_pairs={{0,1},{2,3},{4,5},{6,7},{8,9},{10,11},{12,13},{14,15},{1,0},{3,2},... | collective-permute-start | bytes 417800 | tf_op jit(solution)/shard_map/ppermute | solution.py:625
  23.8 7.2 %collective-permute-start.6 = (f32[2,17,8,128]{3,2,1,0:T(8,128)S(1)}, f32[2,17,8,128]{3,2,1,0:T(8,128)S(1)}, u32[]{:S(2)}, u32[]{:S(2)}) collective-permute-start(f32[2,17,8,128]{3,2,1,0:T(8,128)S(1)} %get-tuple-element.43), channel_id=1, source_target_pairs={{0,15},{2,1},{4,3},{6,5},{8,7},{10,9},{12,11},{14,13},{15,0},{1,2}... | collective-permute-start | bytes 417800 | tf_op jit(solution)/shard_map/ppermute | solution.py:625
  32.2 2.2 %collective-permute-start.7 = (f32[17,8,128]{2,1,0:T(8,128)S(1)}, f32[17,8,128]{2,1,0:T(8,128)S(1)}, u32[]{:S(2)}, u32[]{:S(2)}) collective-permute-start(f32[17,8,128]{2,1,0:T(8,128)S(1)} %get-tuple-element.45), channel_id=1, source_target_pairs={{0,1},{2,3},{4,5},{6,7},{8,9},{10,11},{12,13},{14,15},{1,0},{3,2},... | collective-permute-start | bytes 208904 | tf_op jit(solution)/shard_map/ppermute | solution.py:625
  32.2 6.5 %collective-permute-start.8 = (f32[17,8,128]{2,1,0:T(8,128)S(1)}, f32[17,8,128]{2,1,0:T(8,128)S(1)}, u32[]{:S(2)}, u32[]{:S(2)}) collective-permute-start(f32[17,8,128]{2,1,0:T(8,128)S(1)} %get-tuple-element.46), channel_id=1, source_target_pairs={{0,15},{2,1},{4,3},{6,5},{8,7},{10,9},{12,11},{14,13},{15,0},{1,2}... | collective-permute-start | bytes 208904 | tf_op jit(solution)/shard_map/ppermute | solution.py:625

commit v6 on v5

--- a/solution.py
+++ b/solution.py
@@ -224,78 +224,95 @@
     )
 
 
-def prepare_kernel(
+def seam_scales(flags, chunks):
+    flag_cols, flag_lats = flags.shape
+    flags = jnp.concatenate(
+        [flags.astype(F32), jnp.zeros((8 - flag_cols, flag_lats), F32)], 0
+    )
+    lat = lax.broadcasted_iota(jnp.int32, (8, flag_lats), 1)
+    stacked = jnp.concatenate([jnp.where(lat // 8 == c, flags, 0.0) for c in chunks], 0)
+    spread = selector((flag_lats, LANES), lambda a, b: a % 8 == b // (TILE // 2))
+    spread_flags = jnp.dot(stacked.astype(BF16), spread, preferred_element_type=F32)
+    scale = jnp.where(spread_flags > 0.5, SEAM_SCALE, 1.0)
+    return scale.reshape(len(chunks), 8, LANES)
+
+
+def seam_rows(scales, flag_cols, rows):
+    size = (rows // flag_cols, LANES)
+    return jnp.concatenate(
+        [jnp.broadcast_to(scales[i : i + 1], size) for i in range(flag_cols)], 0
+    )
+
+
+def edge_kernel(
     right_ref, weight_ref, flag_ref,
-    s_ref, d_ref, e_ref, to_mate, to_other, polar_ref, corner_near, corner_far,
-    right_buf, weight_buf, flag_buf, temp_s, temp_d, scale_ref, sems,
+    to_mate, to_other, polar_ref, corner_near, corner_far,
+    edge_s, edge_w, end_s, end_w, flags, temp_s, temp_w, temp_p, temp_q, scale_ref, sems,
 ):
-    flag_copy = pltpu.make_async_copy(flag_ref, flag_buf, sems.at[0, GROUPS])
-    flag_copy.start()
+    columns, height = right_ref.shape
+    rows, tiles = columns // 2, height // 256
+    pairs = [(flag_ref, flags)]
+    for i, (src, dst, size) in enumerate(
+        ((right_ref, edge_s, 8), (weight_ref, edge_w, 16))
+    ):
+        pairs.append((src.at[pl.ds(0, size)], dst.at[pl.ds(0, size)]))
+        pairs.append((src.at[pl.ds(columns - size, size)], dst.at[pl.ds(size, size)]))
+    for src, dst in ((right_ref, end_s), (weight_ref, end_w)):
+        for end, start in enumerate((0, height - 256)):
+            pairs.append((src.at[:, pl.ds(start, 256)], dst.at[end]))
+    copies = [
+        pltpu.make_async_copy(src, dst, sems.at[i]) for i, (src, dst) in enumerate(pairs)
+    ]
+    for copy in copies:
+        copy.start()
     odd = is_odd()
-    tiles, rows = s_ref.shape[1], s_ref.shape[2]
-    chunk = right_ref.shape[1] // GROUPS
-    copies = []
-    for group in range(GROUPS):
-        part = pl.ds(group * chunk, chunk)
-        copies.append(
-            [
-                pltpu.make_async_copy(src.at[:, part], dst.at[:, part], sems.at[i, group])
-                for i, (src, dst) in enumerate(((right_ref, right_buf), (weight_ref, weight_buf)))
-            ]
+    matrix = splitter()
+    flag_cols = flag_ref.shape[0]
+    copies[0].wait()
+    scale_ref[...] = seam_scales(flags[...], range(tiles))
+    for copy in copies[1:5]:
+        copy.wait()
+    sub = row_ids(8)
+    lanes = [slice(c * 256, (c + 1) * 256) for c in range(tiles)]
+    source, weight = moved(
+        jnp.concatenate([edge_s[:, w] for w in lanes], 0),
+        matrix,
+        jnp.concatenate([edge_w[:, w] for w in lanes], 0),
+    )
+    weight = weight.reshape(tiles, 32, 256)
+    weight = jnp.concatenate([weight[:, :8], weight[:, 24:]], 1).reshape(tiles * 16, 256)
+    source = quarters_of(source, temp_s)
+    weight = quarters_of(weight, temp_w)
+    for c in range(tiles):
+        here = slice(c * 8, (c + 1) * 8)
+        scales = scale_ref[c]
+        scale = jnp.where(sub < 4, scales[:1], scales[flag_cols - 1 : flag_cols])
+        diag = [4.0 + w[here] * scale for w in weight]
+        store_edges(
+            c, edge_packs([x[here] for x in source], diag, False), odd, to_mate, to_other
         )
-        for copy in copies[group]:
-            copy.start()
-    flag_copy.wait()
-    flag_cols = flag_ref.shape[0]
-    flag_lats = flag_ref.shape[1]
-    per_tile = rows // flag_cols
-    matrix = splitter()
-    flags = jnp.concatenate(
-        [flag_buf[...].astype(F32), jnp.zeros((8 - flag_cols, flag_lats), F32)], 0
-    )
-    lat = lax.broadcasted_iota(jnp.int32, (8, flag_lats), 1)
-    stacked = jnp.concatenate(
-        [jnp.where(lat // 8 == c, flags, 0.0) for c in range(tiles)], 0
-    ).astype(BF16)
-    spread = selector((flag_lats, LANES), lambda a, b: a % 8 == b // (TILE // 2))
-    spread_flags = jnp.dot(stacked, spread, preferred_element_type=F32)
-    scale_ref[...] = jnp.where(spread_flags > 0.5, SEAM_SCALE, 1.0).reshape(tiles, 8, LANES)
-
-    def piece(c, source, weight):
-        scales = scale_ref[c]
-        scale = jnp.concatenate(
-            [jnp.broadcast_to(scales[i : i + 1], (per_tile, LANES)) for i in range(flag_cols)], 0
-        )
-        screen = [w * scale for w in weight]
-        e_ref[c] = (screen[0] + screen[1]) + (screen[2] + screen[3])
-        diag = [4.0 + s for s in screen]
-        for q in range(4):
-            s_ref[q, c] = source[q]
-            d_ref[q, c] = diag[q]
-        store_edges(c, edge_packs(source, diag, False), odd, to_mate, to_other)
-
-    columns = right_ref.shape[0]
-    for group in range(GROUPS):
-        for copy in copies[group]:
-            copy.wait()
-        for batch in range(tiles // GROUPS // BATCH):
-            start = group * (tiles // GROUPS) + batch * BATCH
-            lanes = [slice((start + i) * 256, (start + i + 1) * 256) for i in range(BATCH)]
-            source = jnp.concatenate([right_buf[:, w] for w in lanes], 0)
-            weight = jnp.concatenate([weight_buf[:, w] for w in lanes], 0)
-            source, weight = moved(source, matrix, weight)
-            for i in range(BATCH):
-                here = slice(i * columns, (i + 1) * columns)
-                piece(
-                    start + i,
-                    quarters_of(source[here], temp_s.at[i]),
-                    quarters_of(weight[here], temp_d.at[i]),
-                )
-
+
+    for copy in copies[5:]:
+        copy.wait()
     mirror = selector((LANES, LANES), lambda a, b: a + b == LANES - 1)
     lane = lane_ids(rows)
+    source, weight = moved(
+        jnp.concatenate([end_s[0], end_s[1]], 0),
+        matrix,
+        jnp.concatenate([end_w[0], end_w[1]], 0),
+    )
+    found = []
+    for end, c in enumerate((0, tiles - 1)):
+        here = slice(end * columns, (end + 1) * columns)
+        scale = seam_rows(scale_ref[c], flag_cols, rows)
+        found.append(
+            (
+                quarters_of(source[here], temp_p.at[end]),
+                [4.0 + w * scale for w in quarters_of(weight[here], temp_q.at[end])],
+            )
+        )
     ends = [
-        [jnp.where(lane >= 64, ref[q ^ 1, tiles - 1], ref[q ^ 1, 0]) for ref in (s_ref, d_ref)]
+        [jnp.where(lane >= 64, found[1][i][q ^ 1], found[0][i][q ^ 1]) for i in (0, 1)]
         for q in range(4)
     ]
     both = moved(jnp.concatenate(polar_packs(ends), 0), mirror)
@@ -303,6 +320,44 @@
         pack = both[pc * rows : (pc + 1) * rows]
         polar_ref[pc] = pack
         corner_near[pc], corner_far[pc] = chosen(odd, pack[:8], pack[rows - 8 :])
+
+
+def bulk_kernel(
+    right_ref, weight_ref, flag_ref, edges_first,
+    s_ref, d_ref, i_ref, d1_ref, i1_ref, d2_ref,
+    temp_s, temp_d, scale_ref, e_ref,
+):
+    tiles, rows = s_ref.shape[1], s_ref.shape[2]
+    columns = 2 * rows
+    matrix = splitter()
+    scale_ref[...] = seam_scales(flag_ref[...], range(tiles))
+    for start in range(0, tiles, BATCH):
+        lanes = [slice((start + i) * 256, (start + i + 1) * 256) for i in range(BATCH)]
+        source, weight = moved(
+            jnp.concatenate([right_ref[:, w] for w in lanes], 0),
+            matrix,
+            jnp.concatenate([weight_ref[:, w] for w in lanes], 0),
+        )
+        for i in range(BATCH):
+            c = start + i
+            here = slice(i * columns, (i + 1) * columns)
+            scale = seam_rows(scale_ref[c], flag_ref.shape[0], rows)
+            for q, value in enumerate(quarters_of(source[here], temp_s.at[i])):
+                s_ref[q, c] = value
+            screen = [w * scale for w in quarters_of(weight[here], temp_d.at[i])]
+            e_ref[c] = (screen[0] + screen[1]) + (screen[2] + screen[3])
+            for q in range(4):
+                diag = 4.0 + screen[q]
+                d_ref[q, c] = diag
+                i_ref[q, c] = 1.0 / diag
+
+    def use(c, screen):
+        for q in range(4):
+            d1_ref[q, c] = 4.0 + screen[q]
+            i1_ref[q, c] = 1.0 / (4.0 + screen[q])
+        d2_ref[c] = 4.0 + ((screen[0] + screen[1]) + (screen[2] + screen[3]))
+
+    split_tiles(lambda t: e_ref[t], tiles // 2, rows, matrix, temp_s, use)
 
 
 def split_tiles(load, tiles, rows, matrix, temp, use):
@@ -313,25 +368,7 @@
         ]
         out = moved(jnp.concatenate(wide, 0), matrix)
         for i in range(BATCH):
-            use(start + i, quarters_of(out[i * rows : (i + 1) * rows], temp.at[i]))
-
-
-def screens_kernel(d_ref, e_ref, i_ref, d1_ref, i1_ref, d2_ref, temp):
-    def inverse(t, _):
-        for q in range(4):
-            i_ref[q, t] = 1.0 / d_ref[q, t]
-        return 0
-
-    loop(d_ref.shape[1], inverse)
-
-    def use(c, screen):
-        for q in range(4):
-            d1_ref[q, c] = 4.0 + screen[q]
-            i1_ref[q, c] = 1.0 / (4.0 + screen[q])
-        d2_ref[c] = 4.0 + ((screen[0] + screen[1]) + (screen[2] + screen[3]))
-
-    tiles, rows = d1_ref.shape[1], e_ref.shape[1]
-    split_tiles(lambda t: e_ref[t], tiles, rows, splitter(), temp, use)
+            use(start + i, quarters_of(out[i * rows : (i + 1) * rows], temp.at[i, :, :rows]))
 
 
 def half_sweep(v, load_s, load_i, tiles, red, unroll):
@@ -636,32 +673,37 @@
     tiles, rows = height // 256, columns // 2
     tiles1, rows1 = tiles // 2, rows // 2
     temp = (BATCH, 2, columns, LANES)
-    right_side = pltpu.with_memory_space_constraint(right_side, pltpu.HBM)
-    texel_weight = pltpu.with_memory_space_constraint(texel_weight, pltpu.HBM)
-    seam_flags = pltpu.with_memory_space_constraint(seam_flags, pltpu.HBM)
-
     quarters = (4, tiles, rows, LANES)
-    s, d, e, to_mate, to_other, polar, corner_near, corner_far = call(
-        prepare_kernel,
-        [quarters, quarters, quarters[1:], (2, tiles, 8, LANES), (2, tiles, 8, LANES)]
-        + [(2, rows, LANES), (2, 8, LANES), (2, 8, LANES)],
-        [(columns, height), pltpu.VMEM((columns, height), BF16)]
-        + [pltpu.VMEM(seam_flags.shape, jnp.int32), temp, temp, (tiles, 8, LANES)],
-        right_side, texel_weight, seam_flags,
-        sems=(2, GROUPS + 1), far_in=3,
+    quarters1 = (4, tiles1, rows1, LANES)
+    pack = (2, tiles, 8, LANES)
+    corner = (2, 8, LANES)
+    split = (2, 16 * tiles, LANES)
+    to_mate, to_other, polar, corner_near, corner_far = call(
+        edge_kernel,
+        [pack, pack, (2, rows, LANES), corner, corner],
+        [(16, height), pltpu.VMEM((32, height), BF16)]
+        + [(2, columns, 256), pltpu.VMEM((2, columns, 256), BF16)]
+        + [pltpu.VMEM(seam_flags.shape, jnp.int32), split, split]
+        + [(2, 2, columns, LANES)] * 2
+        + [(tiles, 8, LANES)],
+        *[
+            pltpu.with_memory_space_constraint(x, pltpu.HBM)
+            for x in (right_side, texel_weight, seam_flags)
+        ],
+        sems=(9,), far_in=3,
     )
     from_mate, from_other = swapped_edges(to_mate, to_other)
     polar = lax.ppermute(
         polar, "lon", [(i, (i + half_turn) % (2 * half_turn)) for i in range(2 * half_turn)]
     )
+    corner_near_own = corner_near
     corner_far = swapped_with(corner_far, half_turn - 1)
     corner_near = swapped_with(corner_near, half_turn + 1)
-    quarters1 = (4, tiles1, rows1, LANES)
-    inverse, d1, i1, d2 = call(
-        screens_kernel,
-        [quarters, quarters1, quarters1, quarters1[1:]],
-        [(BATCH, 2, rows, LANES)],
-        d, e,
+    s, d, inverse, d1, i1, d2 = call(
+        bulk_kernel,
+        [quarters] * 3 + [quarters1, quarters1, quarters1[1:]],
+        [temp, temp, (tiles, 8, LANES), quarters[1:]],
+        right_side, texel_weight, seam_flags, corner_near_own,
     )
 
     def level_scratch(tiles, rows):

time: 40.6 us -> 37 us (0.911)
  waiting for transfers between devices: 10.8 us -> 4.92 us
  starting transfers between devices: 14.7 us -> 16.6 us
    ppermute x8, waiting for transfers between devices: 10.5 us -> 4.53 us  [swapped_with(): return lax.ppermute(x, 'lon', pairs + [(b, a) for a, b in pairs])]
    ppermute x8, starting transfers between devices: 14.7 us -> 16.6 us  [swapped_with(): return lax.ppermute(x, 'lon', pairs + [(b, a) for a, b in pairs])]
  transfers between devices with their start and end apart: 9 -> 9, of which waited for: 5 -> 4; matrix products, arithmetic and copies ran while one was open for 0% -> 0% of each run, Pallas kernels for 6% -> 10%
where the time goes in v6:
time: 37 us; the launch traced here: 36.9 us
  starting transfers between devices  16.6 us (45%)
  Pallas kernels  14.6 us (39%)
  waiting for transfers between devices  4.92 us (13%)
  between operations  0.72 us (2%)
    ppermute x8, starting transfers between devices, swapped_with(): return lax.ppermute(x, 'lon', pairs + [(b, a) for a, b in pairs])  16.6 us
    pallas_call x6, Pallas kernels, call(): pl.pallas_call(kernel, out_shape=[jax.ShapeDtypeStruct(shape, F32) for sh...  14.6 us
    ppermute x8, waiting for transfers between devices, swapped_with(): return lax.ppermute(x, 'lon', pairs + [(b, a) for a, b in pairs])  4.53 us
  transfers between devices with their start and end apart: 9, of which 4 were waited for; matrix products, arithmetic and copies ran while one was open for 0% of the time, Pallas kernels for 10%

profile of v6, /device:TPU:0, one launch (start us, length us, event | category | flops | bytes accessed | tf_op | source)
XLA Modules:
  0.0 36.9 jit_solution(7806206932409235443)
XLA Ops:
  0.6 0.0 copy-start.2
  0.6 0.0 copy-start.1
  0.7 0.0 copy-start
  0.7 2.5 %shard_map.58 = (f32[2,32,8,128]{3,2,1,0:T(8,128)S(1)}, f32[2,32,8,128]{3,2,1,0:T(8,128)S(1)}, f32[2,32,128]{2,1,0:T(8,128)S(1)}, f32[2,8,128]{2,1,0:T(8,128)S(1)}, f32[2,8,128]{2,1,0:T(8,128)S(1)}) custom-call(f32[64,8192]{1,0:T(8,128)} %right_ref.3, bf16[64,8192]{1,0:T(8,128)(2,1)} %weight_ref.3, s32[2,256]{1,0:T(2,128)} %flag_ref.3), custom_call_target="tpu_custom_call" | custom-call | tf_op jit(solution)/shard_map/pallas_call | solution.py:649
  3.2 0.5 %collective-permute-start = (f32[2,32,8,128]{3,2,1,0:T(8,128)S(1)}, f32[2,32,8,128]{3,2,1,0:T(8,128)S(1)}, u32[]{:S(2)}, u32[]{:S(2)}) collective-permute-start(f32[2,32,8,128]{3,2,1,0:T(8,128)S(1)} %get-tuple-element.30), channel_id=1, source_target_pairs={{0,1},{2,3},{4,5},{6,7},{8,9},{10,11},{12,13},{14,15},{1,0},{3,2},... | collective-permute-start | bytes 786440 | tf_op jit(solution)/shard_map/ppermute | solution.py:662
  3.7 5.6 %collective-permute-start.1 = (f32[2,32,8,128]{3,2,1,0:T(8,128)S(1)}, f32[2,32,8,128]{3,2,1,0:T(8,128)S(1)}, u32[]{:S(2)}, u32[]{:S(2)}) collective-permute-start(f32[2,32,8,128]{3,2,1,0:T(8,128)S(1)} %get-tuple-element.31), channel_id=1, source_target_pairs={{0,15},{2,1},{4,3},{6,5},{8,7},{10,9},{12,11},{14,13},{15,0},{1,2}... | collective-permute-start | bytes 786440 | tf_op jit(solution)/shard_map/ppermute | solution.py:662
  9.3 0.0 collective-permute-start.2
  9.3 0.3 collective-permute-start.4
  9.6 1.9 %collective-permute-start.3 = (f32[2,8,128]{2,1,0:T(8,128)S(1)}, f32[2,8,128]{2,1,0:T(8,128)S(1)}, u32[]{:S(2)}, u32[]{:S(2)}) collective-permute-start(f32[2,8,128]{2,1,0:T(8,128)S(1)} %get-tuple-element.25.edges_first), channel_id=1, source_target_pairs={{0,9},{2,11},{4,13},{6,15},{8,1},{10,3},{12,5},{14,7},{9,0},{11,2}... | collective-permute-start | bytes 24584 | tf_op jit(solution)/shard_map/ppermute | solution.py:662
  11.5 0.0 copy-done.2
  11.5 0.0 copy-done.1
  11.5 0.0 copy-done
  11.5 1.8 %shard_map.59 = (f32[4,32,32,128]{3,2,1,0:T(8,128)S(1)}, f32[4,32,32,128]{3,2,1,0:T(8,128)S(1)}, f32[4,32,32,128]{3,2,1,0:T(8,128)S(1)}, f32[4,16,16,128]{3,2,1,...) custom-call(f32[64,8192]{1,0:T(8,128)S(1)} %copy-done, bf16[64,8192]{1,0:T(8,128)(2,1)S(1)} %copy-done.1, ...), custom_call_target="tpu_custom_call" | custom-call | tf_op jit(solution)/shard_map/pallas_call | solution.py:649
  13.3 0.6 %collective-permute-done.4.corner_far = f32[2,8,128]{2,1,0:T(8,128)S(1)} collective-permute-done((f32[2,8,128]{2,1,0:T(8,128)S(1)}, f32[2,8,128]{2,1,0:T(8,128)S(1)}, u32[]{:S(2)}, u32[]{:S(2)}) %collective-permute-start.4) | collective-permute-done | bytes 8224 | tf_op jit(solution)/shard_map/ppermute | solution.py:662
  13.9 0.0 collective-permute-done.3.corner_near
  13.9 0.4 %collective-permute-done.2.polar_ref = f32[2,32,128]{2,1,0:T(8,128)S(1)} collective-permute-done((f32[2,32,128]{2,1,0:T(8,128)S(1)}, f32[2,32,128]{2,1,0:T(8,128)S(1)}, u32[]{:S(2)}, u32[]{:S(2)}) %collective-permute-start.2) | collective-permute-done | bytes 32800 | tf_op jit(solution)/shard_map/ppermute | solution.py:696
  14.3 0.0 collective-permute-done.from_mate
  14.3 0.0 collective-permute-done.1.from_other
  14.3 5.6 %shard_map.60 = (f32[4,32,32,128]{3,2,1,0:T(8,128)S(1)}, f32[4,17,16,128]{3,2,1,0:T(8,128)S(1)}, f32[4,16,128]{2,1,0:T(8,128)S(1)}, f32[16,128]{1,0:T(8,128)S(1)...) custom-call(f32[4,32,32,128]{3,2,1,0:T(8,128)S(1)} %get-tuple-element.26.s_ref, ...), custom_call_target="tpu_custom_call" | custom-call | tf_op jit(solution)/shard_map/pallas_call | solution.py:649
  19.9 0.2 collective-permute-start.5
  20.1 4.0 %collective-permute-start.6 = (f32[2,17,8,128]{3,2,1,0:T(8,128)S(1)}, f32[2,17,8,128]{3,2,1,0:T(8,128)S(1)}, u32[]{:S(2)}, u32[]{:S(2)}) collective-permute-start(f32[2,17,8,128]{3,2,1,0:T(8,128)S(1)} %get-tuple-element.41), channel_id=1, source_target_pairs={{0,15},{2,1},{4,3},{6,5},{8,7},{10,9},{12,11},{14,13},{15,0},{1,2}... | collective-permute-start | bytes 417800 | tf_op jit(solution)/shard_map/ppermute | solution.py:662
  24.1 1.8 %shard_map.61.merged_first = f32[64,8192]{1,0:T(8,128)} custom-call(f32[4,32,32,128]{3,2,1,0:T(8,128)S(1)} %get-tuple-element.34.r_ref), custom_call_target="tpu_custom_call" | custom-call | tf_op jit(solution)/shard_map/pallas_call | solution.py:649
  25.9 0.0 collective-permute-done.5.from_mate
  25.9 1.4 %collective-permute-done.6.from_other = f32[2,17,8,128]{3,2,1,0:T(8,128)S(1)} collective-permute-done((f32[2,17,8,128]{3,2,1,0:T(8,128)S(1)}, f32[2,17,8,128]{3,2,1,0:T(8,128)S(1)}, u32[]{:S(2)}, u32[]{:S(2)}) %collective-permute-start.6) | collective-permute-done | bytes 139296 | tf_op jit(solution)/shard_map/ppermute | solution.py:662
  27.3 1.2 %shard_map.62 = (f32[17,16,128]{2,1,0:T(8,128)S(1)}, f32[17,8,128]{2,1,0:T(8,128)S(1)}, f32[17,8,128]{2,1,0:T(8,128)S(1)}) custom-call(f32[64,8192]{1,0:T(8,128)} %shard_map.61.merged_first, f32[4,17,16,128]{3,2,1,0:T(8,128)S(1)} %get-tuple-element.35.s_ref, f32[4,16,16,128]{3,2,1,0:T(8,128)S(1)} %get-tuple-element.29.d1_ref.d_ref, ...), custom_call_target="tpu_custom_call" | custom-call | tf_op jit(solution)/shard_map/pallas_call | solution.py:649
  28.5 0.1 collective-permute-start.7
  28.6 4.0 %collective-permute-start.8 = (f32[17,8,128]{2,1,0:T(8,128)S(1)}, f32[17,8,128]{2,1,0:T(8,128)S(1)}, u32[]{:S(2)}, u32[]{:S(2)}) collective-permute-start(f32[17,8,128]{2,1,0:T(8,128)S(1)} %get-tuple-element.44), channel_id=1, source_target_pairs={{0,15},{2,1},{4,3},{6,5},{8,7},{10,9},{12,11},{14,13},{15,0},{1,2}... | collective-permute-start | bytes 208904 | tf_op jit(solution)/shard_map/ppermute | solution.py:662
  32.6 0.0 collective-permute-done.7.from_mate
  32.6 2.5 %collective-permute-done.8.from_other = f32[17,8,128]{2,1,0:T(8,128)S(1)} collective-permute-done((f32[17,8,128]{2,1,0:T(8,128)S(1)}, f32[17,8,128]{2,1,0:T(8,128)S(1)}, u32[]{:S(2)}, u32[]{:S(2)}) %collective-permute-start.8) | collective-permute-done | bytes 69664 | tf_op jit(solution)/shard_map/ppermute | solution.py:662
  35.1 1.7 %shard_map.63 = (f32[16,2048]{1,0:T(8,128)}, f32[16,2048]{1,0:T(8,128)}) custom-call(f32[17,16,128]{2,1,0:T(8,128)S(1)} %get-tuple-element.42.s_ref, f32[16,16,128]{2,1,0:T(8,128)S(1)} %get-tuple-element.38.d2_ref.d_ref, f32[16,128]{1,0:T(8,128)S(1)} %get-tuple-element.39.d2_virtual.d_virtual, f32[17,8,128]{2,1,0:T(8,128)S(1)} %collective-permute-done.7.from_mate, ...), custom_call_target="tpu_custom_call" | custom-call | tf_op jit(solution)/shard_map/pallas_call | solution.py:649
Async XLA Ops:
  0.6 10.9 %copy-start.2 = (s32[2,256]{1,0:T(2,128)S(1)}, s32[2,256]{1,0:T(2,128)}, u32[]{:S(2)}) copy-start(s32[2,256]{1,0:T(2,128)} %flag_ref.3) | copy-start | bytes 6148
  0.6 10.9 %copy-start.1 = (bf16[64,8192]{1,0:T(8,128)(2,1)S(1)}, bf16[64,8192]{1,0:T(8,128)(2,1)}, u32[]{:S(2)}) copy-start(bf16[64,8192]{1,0:T(8,128)(2,1)} %weight_ref.3) | copy-start | bytes 3145732
  0.7 10.9 %copy-start = (f32[64,8192]{1,0:T(8,128)S(1)}, f32[64,8192]{1,0:T(8,128)}, u32[]{:S(2)}) copy-start(f32[64,8192]{1,0:T(8,128)} %right_ref.3) | copy-start | bytes 6291460
  3.2 11.1 %collective-permute-start = (f32[2,32,8,128]{3,2,1,0:T(8,128)S(1)}, f32[2,32,8,128]{3,2,1,0:T(8,128)S(1)}, u32[]{:S(2)}, u32[]{:S(2)}) collective-permute-start(f32[2,32,8,128]{3,2,1,0:T(8,128)S(1)} %get-tuple-element.30), channel_id=1, source_target_pairs={{0,1},{2,3},{4,5},{6,7},{8,9},{10,11},{12,13},{14,15},{1,0},{3,2},... | collective-permute-start | bytes 786440 | tf_op jit(solution)/shard_map/ppermute | solution.py:662
  3.7 10.6 %collective-permute-start.1 = (f32[2,32,8,128]{3,2,1,0:T(8,128)S(1)}, f32[2,32,8,128]{3,2,1,0:T(8,128)S(1)}, u32[]{:S(2)}, u32[]{:S(2)}) collective-permute-start(f32[2,32,8,128]{3,2,1,0:T(8,128)S(1)} %get-tuple-element.31), channel_id=1, source_target_pairs={{0,15},{2,1},{4,3},{6,5},{8,7},{10,9},{12,11},{14,13},{15,0},{1,2}... | collective-permute-start | bytes 786440 | tf_op jit(solution)/shard_map/ppermute | solution.py:662
  9.3 5.0 %collective-permute-start.2 = (f32[2,32,128]{2,1,0:T(8,128)S(1)}, f32[2,32,128]{2,1,0:T(8,128)S(1)}, u32[]{:S(2)}, u32[]{:S(2)}) collective-permute-start(f32[2,32,128]{2,1,0:T(8,128)S(1)} %get-tuple-element.32), channel_id=1, source_target_pairs={{0,8},{1,9},{2,10},{3,11},{4,12},{5,13},{6,14},{7,15},{8,0},{9,1},... | collective-permute-start | bytes 98312 | tf_op jit(solution)/shard_map/ppermute | solution.py:696
  9.3 4.6 %collective-permute-start.4 = (f32[2,8,128]{2,1,0:T(8,128)S(1)}, f32[2,8,128]{2,1,0:T(8,128)S(1)}, u32[]{:S(2)}, u32[]{:S(2)}) collective-permute-start(f32[2,8,128]{2,1,0:T(8,128)S(1)} %get-tuple-element.33), channel_id=1, source_target_pairs={{0,7},{2,9},{4,11},{6,13},{8,15},{10,1},{12,3},{14,5},{7,0},{9,2},... | collective-permute-start | bytes 24584 | tf_op jit(solution)/shard_map/ppermute | solution.py:662
  9.6 4.3 %collective-permute-start.3 = (f32[2,8,128]{2,1,0:T(8,128)S(1)}, f32[2,8,128]{2,1,0:T(8,128)S(1)}, u32[]{:S(2)}, u32[]{:S(2)}) collective-permute-start(f32[2,8,128]{2,1,0:T(8,128)S(1)} %get-tuple-element.25.edges_first), channel_id=1, source_target_pairs={{0,9},{2,11},{4,13},{6,15},{8,1},{10,3},{12,5},{14,7},{9,0},{11,2}... | collective-permute-start | bytes 24584 | tf_op jit(solution)/shard_map/ppermute | solution.py:662
  19.9 5.9 %collective-permute-start.5 = (f32[2,17,8,128]{3,2,1,0:T(8,128)S(1)}, f32[2,17,8,128]{3,2,1,0:T(8,128)S(1)}, u32[]{:S(2)}, u32[]{:S(2)}) collective-permute-start(f32[2,17,8,128]{3,2,1,0:T(8,128)S(1)} %get-tuple-element.40), channel_id=1, source_target_pairs={{0,1},{2,3},{4,5},{6,7},{8,9},{10,11},{12,13},{14,15},{1,0},{3,2},... | collective-permute-start | bytes 417800 | tf_op jit(solution)/shard_map/ppermute | solution.py:662
  20.1 7.2 %collective-permute-start.6 = (f32[2,17,8,128]{3,2,1,0:T(8,128)S(1)}, f32[2,17,8,128]{3,2,1,0:T(8,128)S(1)}, u32[]{:S(2)}, u32[]{:S(2)}) collective-permute-start(f32[2,17,8,128]{3,2,1,0:T(8,128)S(1)} %get-tuple-element.41), channel_id=1, source_target_pairs={{0,15},{2,1},{4,3},{6,5},{8,7},{10,9},{12,11},{14,13},{15,0},{1,2}... | collective-permute-start | bytes 417800 | tf_op jit(solution)/shard_map/ppermute | solution.py:662
  28.5 4.1 %collective-permute-start.7 = (f32[17,8,128]{2,1,0:T(8,128)S(1)}, f32[17,8,128]{2,1,0:T(8,128)S(1)}, u32[]{:S(2)}, u32[]{:S(2)}) collective-permute-start(f32[17,8,128]{2,1,0:T(8,128)S(1)} %get-tuple-element.43), channel_id=1, source_target_pairs={{0,1},{2,3},{4,5},{6,7},{8,9},{10,11},{12,13},{14,15},{1,0},{3,2},... | collective-permute-start | bytes 208904 | tf_op jit(solution)/shard_map/ppermute | solution.py:662
  28.6 6.5 %collective-permute-start.8 = (f32[17,8,128]{2,1,0:T(8,128)S(1)}, f32[17,8,128]{2,1,0:T(8,128)S(1)}, u32[]{:S(2)}, u32[]{:S(2)}) collective-permute-start(f32[17,8,128]{2,1,0:T(8,128)S(1)} %get-tuple-element.44), channel_id=1, source_target_pairs={{0,15},{2,1},{4,3},{6,5},{8,7},{10,9},{12,11},{14,13},{15,0},{1,2}... | collective-permute-start | bytes 208904 | tf_op jit(solution)/shard_map/ppermute | solution.py:662

commit v7 on v6

--- a/solution.py
+++ b/solution.py
@@ -429,45 +429,48 @@
 def residuals(v, load_s, load_d, tiles, c0, c1, keep, unroll):
     lane = lane_ids(v[0].shape[1])
 
-    def body(t, _):
+    def body(t, carry):
+        up1, up3, down0, down2 = carry
         x = [v[q][t] for q in range(4)]
-
-        def north(q):
-            return jnp.where(lane == 0, roll_up(v[q][before(t, tiles)]), roll_up(x[q]))
-
-        def south(q):
-            return jnp.where(
-                lane == LANES - 1, roll_down(v[q][after(t, tiles)]), roll_down(x[q])
-            )
-
+        here1, here3 = roll_up(x[1]), roll_up(x[3])
+        next0, next2 = (roll_down(v[q][after(t, tiles)]) for q in (0, 2))
         beside = [
-            (x[1] + north(1)) + (x[2] + col_prev(x[2])),
-            (x[0] + south(0)) + (x[3] + col_prev(x[3])),
-            (x[3] + north(3)) + (x[0] + col_next(x[0])),
-            (x[2] + south(2)) + (x[1] + col_next(x[1])),
+            (x[1] + jnp.where(lane == 0, up1, here1)) + (x[2] + col_prev(x[2])),
+            (x[0] + jnp.where(lane == LANES - 1, next0, down0)) + (x[3] + col_prev(x[3])),
+            (x[3] + jnp.where(lane == 0, up3, here3)) + (x[0] + col_next(x[0])),
+            (x[2] + jnp.where(lane == LANES - 1, next2, down2)) + (x[1] + col_next(x[1])),
         ]
         r = [load_s(q, t) - (load_d(q, t) * x[q] - beside[q]) for q in range(4)]
         keep(t, r)
         c0[t] = (col_prev(r[2]) + col_next(r[0])) + 3.0 * (r[0] + r[2])
         c1[t] = (col_prev(r[3]) + col_next(r[1])) + 3.0 * (r[1] + r[3])
-        return 0
-
-    loop(tiles, body, 0, unroll)
-    body(tiles, 0)
-
-
-def restricted(c0, c1, t, tiles, rows):
+        return here1, here3, next0, next2
+
+    start = (
+        roll_up(v[1][tiles]), roll_up(v[3][tiles]), roll_down(v[0][0]), roll_down(v[2][0])
+    )
+    body(tiles, loop(tiles, body, start, unroll))
+
+
+def restrict(c0, c1, tiles, rows, use, unroll):
     lane = lane_ids(rows)
-    here, other = c0[t, :rows], c1[t, :rows]
-    north = jnp.where(lane == 0, roll_up(c1[before(t, tiles), :rows]), roll_up(other))
-    south = jnp.where(
-        lane == LANES - 1, roll_down(c0[after(t, tiles), :rows]), roll_down(here)
-    )
-    return ((north + south) + 3.0 * (here + other)) * (1.0 / 16.0)
+
+    def body(t, carry):
+        up, down = carry
+        here, other = c0[t, :rows], c1[t, :rows]
+        up_here = roll_up(other)
+        down_next = roll_down(c0[after(t, tiles), :rows])
+        north = jnp.where(lane == 0, up, up_here)
+        south = jnp.where(lane == LANES - 1, down_next, down)
+        use(t, ((north + south) + 3.0 * (here + other)) * (1.0 / 16.0))
+        return up_here, down_next
+
+    start = roll_up(c1[tiles, :rows]), roll_down(c0[0, :rows])
+    body(tiles, loop(tiles, body, start, unroll))
 
 
 def fine_kernel(
-    s_ref, d_ref, i_ref, d1_ref, from_mate, from_other, polar_ref, corner_near, corner_far,
+    s_ref, d_ref, i_ref, d1_ref, from_other, from_mate, polar_ref, corner_near, corner_far,
     r_ref, s1_ref, d1_virtual, d2_virtual, to_mate, to_other,
     v0, v1, v2, v3, c0, c1, hs, hd, hi, ps, pd, pi, n1, temp,
 ):
@@ -480,7 +483,7 @@
         fill_halo(t, from_mate, from_other, odd, False, hs, hd, hi)
         return 0
 
-    loop(tiles, halo)
+    loop(tiles, halo, 0, 8)
     total = -16.0
     for q in range(4):
         own_s, own_d = polar_unpacked(polar_ref, q)
@@ -499,21 +502,19 @@
         hi[q, tiles] = 1.0 / diag
 
     load_s = loader(s_ref, hs, ps, tiles)
-    smooth(v, load_s, loader(i_ref, hi, pi, tiles), tiles, 16)
+    smooth(v, load_s, loader(i_ref, hi, pi, tiles), tiles, 32)
 
     def keep(t, r):
         if not (isinstance(t, int) and t == tiles):
             for q in range(4):
                 r_ref[q, t] = r[q][:rows]
 
-    residuals(v, load_s, loader(d_ref, hd, pd, tiles), tiles, c0, c1, keep, 8)
-
-    def coarse(t, _):
-        n1[t] = restricted(c0, c1, t, tiles, rows)
-        return 0
-
-    loop(tiles, coarse, 0, 8)
-    coarse(tiles, 0)
+    residuals(v, load_s, loader(d_ref, hd, pd, tiles), tiles, c0, c1, keep, 16)
+
+    def coarse(t, value):
+        n1[t] = value
+
+    restrict(c0, c1, tiles, rows, coarse, 16)
 
     def edges(t, source, diag, swapped):
         store_edges(t, edge_packs(source, diag, swapped), odd, to_mate, to_other)
@@ -564,7 +565,7 @@
 
 
 def middle_kernel(
-    merged_first, s_ref, d_ref, i_ref, d_virtual, d2_ref, d2_virtual, from_mate, from_other,
+    merged_first, s_ref, d_ref, i_ref, d_virtual, d2_ref, d2_virtual, from_other, from_mate,
     s2_ref, to_mate, to_other,
     v0, v1, v2, v3, c0, c1, hs, hd, hi, pi,
 ):
@@ -584,17 +585,19 @@
         v, load_s, loader(d_ref, hd, d_virtual, tiles), tiles, c0, c1, lambda t, r: None, 16
     )
     sub = row_ids(8)
-    for t in range(tiles + 1):
-        value = restricted(c0, c1, t, tiles, rows)
+
+    def coarse(t, value):
         diag = d2_virtual[...] if t == tiles else d2_ref[t]
         s2_ref[t] = value
         right = jnp.where(sub < 4, roll_rows(value[rows - 8 :], 4), diag[rows - 8 :])
         left = jnp.where(sub < 4, value[:8], roll_rows(diag[:8], 4))
         to_mate[t], to_other[t] = chosen(odd, left, right)
 
+    restrict(c0, c1, tiles, rows, coarse, 16)
+
 
 def last_kernel(
-    s_ref, d_ref, d_virtual, from_mate, from_other,
+    s_ref, d_ref, d_virtual, from_other, from_mate,
     solution_ref, residual_ref,
     s, d, inv, va, vb,
 ):
@@ -618,24 +621,31 @@
         inv[t] = inverse
         va[t] = jnp.where(odd if t == tiles else even, source * inverse, 0.0)
 
-    def beside(v, t):
-        x = v[t]
-        north = jnp.where(lane == 0, roll_up(v[before(t, tiles)]), roll_up(x))
-        south = jnp.where(lane == LANES - 1, roll_down(v[after(t, tiles)]), roll_down(x))
-        return (col_prev(x) + col_next(x)) + (north + south)
-
-    old, new = va, vb
-    for mask, other in ((odd, even), (even, odd), (odd, even)):
+    def scan(v, use):
+        up, down = roll_up(v[tiles]), roll_down(v[0])
         for t in range(tiles + 1):
-            value = (s[t] + beside(old, t)) * inv[t]
-            new[t] = jnp.where(other if t == tiles else mask, value, old[t])
-        old, new = new, old
-    for t in range(tiles):
-        x = old[t]
-        r = s[t] - (d[t] * x - beside(old, t))
-        where = slice(t * LANES, (t + 1) * LANES)
-        solution_ref[:, where] = x[:own]
-        residual_ref[:, where] = r[:own]
+            x = v[t]
+            up_here, down_next = roll_up(x), roll_down(v[after(t, tiles)])
+            north = jnp.where(lane == 0, up, up_here)
+            south = jnp.where(lane == LANES - 1, down_next, down)
+            use(t, x, (col_prev(x) + col_next(x)) + (north + south))
+            up, down = up_here, down_next
+
+    for old, new, mask, other in ((va, vb, odd, even), (vb, va, even, odd), (va, vb, odd, even)):
+
+        def relax(t, x, beside):
+            update = other if t == tiles else mask
+            new[t] = jnp.where(update, (s[t] + beside) * inv[t], x)
+
+        scan(old, relax)
+
+    def finish(t, x, beside):
+        if t < tiles:
+            where = slice(t * LANES, (t + 1) * LANES)
+            solution_ref[:, where] = x[:own]
+            residual_ref[:, where] = (s[t] - (d[t] * x - beside))[:own]
+
+    scan(vb, finish)
 
 
 VMEM = pl.BlockSpec(memory_space=pltpu.VMEM)
@@ -663,8 +673,8 @@
 
 
 def swapped_edges(to_mate, to_other):
-    from_other = swapped_with(to_other, -1)
-    return swapped_with(to_mate, 1), from_other
+    from_mate = swapped_with(to_mate, 1)
+    return from_mate, swapped_with(to_other, -1)
 
 
 def body(right_side, texel_weight, seam_flags):
@@ -717,7 +727,7 @@
         level_scratch(tiles, rows)
         + [(4, rows, LANES)] * 3
         + [(tiles + 1, rows, LANES), (BATCH, 2, rows, LANES)],
-        s, d, inverse, d1, from_mate, from_other, polar, corner_near, corner_far,
+        s, d, inverse, d1, from_other, from_mate, polar, corner_near, corner_far,
     )
     from_mate, from_other = swapped_edges(to_mate, to_other)
     (fine_residual,) = call(
@@ -730,7 +740,7 @@
         [(tiles1 + 1, rows1, LANES), pack2, pack2],
         level_scratch(tiles1, rows1) + [(4, rows1, LANES)],
         pltpu.with_memory_space_constraint(fine_residual, pltpu.HBM),
-        s1, d1, i1, d1_virtual, d2, d2_virtual, from_mate, from_other,
+        s1, d1, i1, d1_virtual, d2, d2_virtual, from_other, from_mate,
         far_in=1,
     )
     from_mate, from_other = swapped_edges(to_mate, to_other)
@@ -738,7 +748,7 @@
         last_kernel,
         [(columns // 4, height // 4)] * 2,
         [(tiles1 + 1, rows1 + 8, LANES)] * 5,
-        s2, d2, d2_virtual, from_mate, from_other,
+        s2, d2, d2_virtual, from_other, from_mate,
     )
     return fine_residual, solution_2, residual_2
 

time: 37 us -> 34.9 us (0.943)
  Pallas kernels: 14.6 us -> 12.6 us
    pallas_call x6, Pallas kernels: 14.6 us -> 12.6 us  [call(): pl.pallas_call(kernel, out_shape=[jax.ShapeDtypeStruct(shape, F32) for sh...]
    ppermute x1, waiting for transfers between devices: 0.39 us -> 0.01 us  [body(): lax.ppermute(polar, 'lon', [(i, (i + half_turn) % (2 * half_turn)) for i...]
  transfers between devices with their start and end apart: 9 -> 9, of which waited for: 4 -> 2; matrix products, arithmetic and copies ran while one was open for 0% -> 0% of each run, Pallas kernels for 10% -> 10%
where the time goes in v7:
time: 34.9 us; the launch traced here: 34.7 us
  starting transfers between devices  16.6 us (48%)
  Pallas kernels  12.6 us (36%)
  waiting for transfers between devices  4.72 us (14%)
  between operations  0.74 us (2%)
    ppermute x8, starting transfers between devices, swapped_with(): return lax.ppermute(x, 'lon', pairs + [(b, a) for a, b in pairs])  16.4 us
    pallas_call x6, Pallas kernels, call(): pl.pallas_call(kernel, out_shape=[jax.ShapeDtypeStruct(shape, F32) for sh...  12.6 us
    ppermute x8, waiting for transfers between devices, swapped_with(): return lax.ppermute(x, 'lon', pairs + [(b, a) for a, b in pairs])  4.72 us
  transfers between devices with their start and end apart: 9, of which 2 were waited for; matrix products, arithmetic and copies ran while one was open for 0% of the time, Pallas kernels for 10%

profile of v7, /device:TPU:0, one launch (start us, length us, event | category | flops | bytes accessed | tf_op | source)
XLA Modules:
  0.0 34.7 jit_solution(5472692438402786813)
XLA Ops:
  0.6 0.0 copy-start.2
  0.6 0.0 copy-start.1
  0.7 0.0 copy-start
  0.7 2.5 %shard_map.58 = (f32[2,32,8,128]{3,2,1,0:T(8,128)S(1)}, f32[2,32,8,128]{3,2,1,0:T(8,128)S(1)}, f32[2,32,128]{2,1,0:T(8,128)S(1)}, f32[2,8,128]{2,1,0:T(8,128)S(1)}, f32[2,8,128]{2,1,0:T(8,128)S(1)}) custom-call(f32[64,8192]{1,0:T(8,128)} %right_ref.3, bf16[64,8192]{1,0:T(8,128)(2,1)} %weight_ref.3, s32[2,256]{1,0:T(2,128)} %flag_ref.3), custom_call_target="tpu_custom_call" | custom-call | tf_op jit(solution)/shard_map/pallas_call | solution.py:659
  3.2 5.5 %collective-permute-start = (f32[2,32,8,128]{3,2,1,0:T(8,128)S(1)}, f32[2,32,8,128]{3,2,1,0:T(8,128)S(1)}, u32[]{:S(2)}, u32[]{:S(2)}) collective-permute-start(f32[2,32,8,128]{3,2,1,0:T(8,128)S(1)} %get-tuple-element.30), channel_id=1, source_target_pairs={{0,15},{2,1},{4,3},{6,5},{8,7},{10,9},{12,11},{14,13},{15,0},{1,2}... | collective-permute-start | bytes 786440 | tf_op jit(solution)/shard_map/ppermute | solution.py:672
  8.7 0.0 collective-permute-start.1
  8.7 0.2 collective-permute-start.2
  8.9 0.8 %collective-permute-start.4 = (f32[2,8,128]{2,1,0:T(8,128)S(1)}, f32[2,8,128]{2,1,0:T(8,128)S(1)}, u32[]{:S(2)}, u32[]{:S(2)}) collective-permute-start(f32[2,8,128]{2,1,0:T(8,128)S(1)} %get-tuple-element.33), channel_id=1, source_target_pairs={{0,7},{2,9},{4,11},{6,13},{8,15},{10,1},{12,3},{14,5},{7,0},{9,2},... | collective-permute-start | bytes 24584 | tf_op jit(solution)/shard_map/ppermute | solution.py:672
  9.7 2.8 %collective-permute-start.3 = (f32[2,8,128]{2,1,0:T(8,128)S(1)}, f32[2,8,128]{2,1,0:T(8,128)S(1)}, u32[]{:S(2)}, u32[]{:S(2)}) collective-permute-start(f32[2,8,128]{2,1,0:T(8,128)S(1)} %get-tuple-element.25.edges_first), channel_id=1, source_target_pairs={{0,9},{2,11},{4,13},{6,15},{8,1},{10,3},{12,5},{14,7},{9,0},{11,2}... | collective-permute-start | bytes 24584 | tf_op jit(solution)/shard_map/ppermute | solution.py:672
  12.5 0.0 copy-done.2
  12.5 0.0 copy-done.1
  12.5 0.0 copy-done
  12.5 1.8 %shard_map.59 = (f32[4,32,32,128]{3,2,1,0:T(8,128)S(1)}, f32[4,32,32,128]{3,2,1,0:T(8,128)S(1)}, f32[4,32,32,128]{3,2,1,0:T(8,128)S(1)}, f32[4,16,16,128]{3,2,1,...) custom-call(f32[64,8192]{1,0:T(8,128)S(1)} %copy-done, bf16[64,8192]{1,0:T(8,128)(2,1)S(1)} %copy-done.1, ...), custom_call_target="tpu_custom_call" | custom-call | tf_op jit(solution)/shard_map/pallas_call | solution.py:659
  14.3 0.0 collective-permute-done.4.corner_far
  14.3 0.0 collective-permute-done.3.corner_near
  14.4 0.0 collective-permute-done.2.polar_ref
  14.4 0.0 collective-permute-done.from_other
  14.4 0.0 collective-permute-done.1.from_mate
  14.4 4.2 %shard_map.60 = (f32[4,32,32,128]{3,2,1,0:T(8,128)S(1)}, f32[4,17,16,128]{3,2,1,0:T(8,128)S(1)}, f32[4,16,128]{2,1,0:T(8,128)S(1)}, f32[16,128]{1,0:T(8,128)S(1)...) custom-call(f32[4,32,32,128]{3,2,1,0:T(8,128)S(1)} %get-tuple-element.26.s_ref, ...), custom_call_target="tpu_custom_call" | custom-call | tf_op jit(solution)/shard_map/pallas_call | solution.py:659
  18.6 3.6 %collective-permute-start.5 = (f32[2,17,8,128]{3,2,1,0:T(8,128)S(1)}, f32[2,17,8,128]{3,2,1,0:T(8,128)S(1)}, u32[]{:S(2)}, u32[]{:S(2)}) collective-permute-start(f32[2,17,8,128]{3,2,1,0:T(8,128)S(1)} %get-tuple-element.40), channel_id=1, source_target_pairs={{0,15},{2,1},{4,3},{6,5},{8,7},{10,9},{12,11},{14,13},{15,0},{1,2}... | collective-permute-start | bytes 417800 | tf_op jit(solution)/shard_map/ppermute | solution.py:672
  22.2 0.0 collective-permute-start.6
  22.2 1.8 %shard_map.61.merged_first = f32[64,8192]{1,0:T(8,128)} custom-call(f32[4,32,32,128]{3,2,1,0:T(8,128)S(1)} %get-tuple-element.34.r_ref), custom_call_target="tpu_custom_call" | custom-call | tf_op jit(solution)/shard_map/pallas_call | solution.py:659
  24.0 1.8 %collective-permute-done.5.from_other = f32[2,17,8,128]{3,2,1,0:T(8,128)S(1)} collective-permute-done((f32[2,17,8,128]{3,2,1,0:T(8,128)S(1)}, f32[2,17,8,128]{3,2,1,0:T(8,128)S(1)}, u32[]{:S(2)}, u32[]{:S(2)}) %collective-permute-start.5) | collective-permute-done | bytes 139296 | tf_op jit(solution)/shard_map/ppermute | solution.py:672
  25.8 0.0 collective-permute-done.6.from_mate
  25.8 1.0 %shard_map.62 = (f32[17,16,128]{2,1,0:T(8,128)S(1)}, f32[17,8,128]{2,1,0:T(8,128)S(1)}, f32[17,8,128]{2,1,0:T(8,128)S(1)}) custom-call(f32[64,8192]{1,0:T(8,128)} %shard_map.61.merged_first, f32[4,17,16,128]{3,2,1,0:T(8,128)S(1)} %get-tuple-element.35.s_ref, f32[4,16,16,128]{3,2,1,0:T(8,128)S(1)} %get-tuple-element.29.d1_ref.d_ref, ...), custom_call_target="tpu_custom_call" | custom-call | tf_op jit(solution)/shard_map/pallas_call | solution.py:659
  26.8 3.6 %collective-permute-start.7 = (f32[17,8,128]{2,1,0:T(8,128)S(1)}, f32[17,8,128]{2,1,0:T(8,128)S(1)}, u32[]{:S(2)}, u32[]{:S(2)}) collective-permute-start(f32[17,8,128]{2,1,0:T(8,128)S(1)} %get-tuple-element.43), channel_id=1, source_target_pairs={{0,15},{2,1},{4,3},{6,5},{8,7},{10,9},{12,11},{14,13},{15,0},{1,2}... | collective-permute-start | bytes 208904 | tf_op jit(solution)/shard_map/ppermute | solution.py:672
  30.5 0.0 collective-permute-start.8
  30.5 2.9 %collective-permute-done.7.from_other = f32[17,8,128]{2,1,0:T(8,128)S(1)} collective-permute-done((f32[17,8,128]{2,1,0:T(8,128)S(1)}, f32[17,8,128]{2,1,0:T(8,128)S(1)}, u32[]{:S(2)}, u32[]{:S(2)}) %collective-permute-start.7) | collective-permute-done | bytes 69664 | tf_op jit(solution)/shard_map/ppermute | solution.py:672
  33.3 0.0 collective-permute-done.8.from_mate
  33.3 1.4 %shard_map.63 = (f32[16,2048]{1,0:T(8,128)}, f32[16,2048]{1,0:T(8,128)}) custom-call(f32[17,16,128]{2,1,0:T(8,128)S(1)} %get-tuple-element.42.s_ref, f32[16,16,128]{2,1,0:T(8,128)S(1)} %get-tuple-element.38.d2_ref.d_ref, f32[16,128]{1,0:T(8,128)S(1)} %get-tuple-element.39.d2_virtual.d_virtual, f32[17,8,128]{2,1,0:T(8,128)S(1)} %collective-permute-done.7.from_other, ...), custom_call_target="tpu_custom_call" | custom-call | tf_op jit(solution)/shard_map/pallas_call | solution.py:659
Async XLA Ops:
  0.6 11.9 %copy-start.2 = (s32[2,256]{1,0:T(2,128)S(1)}, s32[2,256]{1,0:T(2,128)}, u32[]{:S(2)}) copy-start(s32[2,256]{1,0:T(2,128)} %flag_ref.3) | copy-start | bytes 6148
  0.6 11.9 %copy-start.1 = (bf16[64,8192]{1,0:T(8,128)(2,1)S(1)}, bf16[64,8192]{1,0:T(8,128)(2,1)}, u32[]{:S(2)}) copy-start(bf16[64,8192]{1,0:T(8,128)(2,1)} %weight_ref.3) | copy-start | bytes 3145732
  0.7 11.9 %copy-start = (f32[64,8192]{1,0:T(8,128)S(1)}, f32[64,8192]{1,0:T(8,128)}, u32[]{:S(2)}) copy-start(f32[64,8192]{1,0:T(8,128)} %right_ref.3) | copy-start | bytes 6291460
  3.2 11.2 %collective-permute-start = (f32[2,32,8,128]{3,2,1,0:T(8,128)S(1)}, f32[2,32,8,128]{3,2,1,0:T(8,128)S(1)}, u32[]{:S(2)}, u32[]{:S(2)}) collective-permute-start(f32[2,32,8,128]{3,2,1,0:T(8,128)S(1)} %get-tuple-element.30), channel_id=1, source_target_pairs={{0,15},{2,1},{4,3},{6,5},{8,7},{10,9},{12,11},{14,13},{15,0},{1,2}... | collective-permute-start | bytes 786440 | tf_op jit(solution)/shard_map/ppermute | solution.py:672
  8.7 5.7 %collective-permute-start.1 = (f32[2,32,8,128]{3,2,1,0:T(8,128)S(1)}, f32[2,32,8,128]{3,2,1,0:T(8,128)S(1)}, u32[]{:S(2)}, u32[]{:S(2)}) collective-permute-start(f32[2,32,8,128]{3,2,1,0:T(8,128)S(1)} %get-tuple-element.31), channel_id=1, source_target_pairs={{0,1},{2,3},{4,5},{6,7},{8,9},{10,11},{12,13},{14,15},{1,0},{3,2},... | collective-permute-start | bytes 786440 | tf_op jit(solution)/shard_map/ppermute | solution.py:672
  8.7 5.7 %collective-permute-start.2 = (f32[2,32,128]{2,1,0:T(8,128)S(1)}, f32[2,32,128]{2,1,0:T(8,128)S(1)}, u32[]{:S(2)}, u32[]{:S(2)}) collective-permute-start(f32[2,32,128]{2,1,0:T(8,128)S(1)} %get-tuple-element.32), channel_id=1, source_target_pairs={{0,8},{1,9},{2,10},{3,11},{4,12},{5,13},{6,14},{7,15},{8,0},{9,1},... | collective-permute-start | bytes 98312 | tf_op jit(solution)/shard_map/ppermute | solution.py:706
  8.9 5.5 %collective-permute-start.4 = (f32[2,8,128]{2,1,0:T(8,128)S(1)}, f32[2,8,128]{2,1,0:T(8,128)S(1)}, u32[]{:S(2)}, u32[]{:S(2)}) collective-permute-start(f32[2,8,128]{2,1,0:T(8,128)S(1)} %get-tuple-element.33), channel_id=1, source_target_pairs={{0,7},{2,9},{4,11},{6,13},{8,15},{10,1},{12,3},{14,5},{7,0},{9,2},... | collective-permute-start | bytes 24584 | tf_op jit(solution)/shard_map/ppermute | solution.py:672
  9.7 4.6 %collective-permute-start.3 = (f32[2,8,128]{2,1,0:T(8,128)S(1)}, f32[2,8,128]{2,1,0:T(8,128)S(1)}, u32[]{:S(2)}, u32[]{:S(2)}) collective-permute-start(f32[2,8,128]{2,1,0:T(8,128)S(1)} %get-tuple-element.25.edges_first), channel_id=1, source_target_pairs={{0,9},{2,11},{4,13},{6,15},{8,1},{10,3},{12,5},{14,7},{9,0},{11,2}... | collective-permute-start | bytes 24584 | tf_op jit(solution)/shard_map/ppermute | solution.py:672
  18.6 7.2 %collective-permute-start.5 = (f32[2,17,8,128]{3,2,1,0:T(8,128)S(1)}, f32[2,17,8,128]{3,2,1,0:T(8,128)S(1)}, u32[]{:S(2)}, u32[]{:S(2)}) collective-permute-start(f32[2,17,8,128]{3,2,1,0:T(8,128)S(1)} %get-tuple-element.40), channel_id=1, source_target_pairs={{0,15},{2,1},{4,3},{6,5},{8,7},{10,9},{12,11},{14,13},{15,0},{1,2}... | collective-permute-start | bytes 417800 | tf_op jit(solution)/shard_map/ppermute | solution.py:672
  22.2 3.6 %collective-permute-start.6 = (f32[2,17,8,128]{3,2,1,0:T(8,128)S(1)}, f32[2,17,8,128]{3,2,1,0:T(8,128)S(1)}, u32[]{:S(2)}, u32[]{:S(2)}) collective-permute-start(f32[2,17,8,128]{3,2,1,0:T(8,128)S(1)} %get-tuple-element.41), channel_id=1, source_target_pairs={{0,1},{2,3},{4,5},{6,7},{8,9},{10,11},{12,13},{14,15},{1,0},{3,2},... | collective-permute-start | bytes 417800 | tf_op jit(solution)/shard_map/ppermute | solution.py:672
  26.8 6.5 %collective-permute-start.7 = (f32[17,8,128]{2,1,0:T(8,128)S(1)}, f32[17,8,128]{2,1,0:T(8,128)S(1)}, u32[]{:S(2)}, u32[]{:S(2)}) collective-permute-start(f32[17,8,128]{2,1,0:T(8,128)S(1)} %get-tuple-element.43), channel_id=1, source_target_pairs={{0,15},{2,1},{4,3},{6,5},{8,7},{10,9},{12,11},{14,13},{15,0},{1,2}... | collective-permute-start | bytes 208904 | tf_op jit(solution)/shard_map/ppermute | solution.py:672
  30.5 2.9 %collective-permute-start.8 = (f32[17,8,128]{2,1,0:T(8,128)S(1)}, f32[17,8,128]{2,1,0:T(8,128)S(1)}, u32[]{:S(2)}, u32[]{:S(2)}) collective-permute-start(f32[17,8,128]{2,1,0:T(8,128)S(1)} %get-tuple-element.44), channel_id=1, source_target_pairs={{0,1},{2,3},{4,5},{6,7},{8,9},{10,11},{12,13},{14,15},{1,0},{3,2},... | collective-permute-start | bytes 208904 | tf_op jit(solution)/shard_map/ppermute | solution.py:672

commit v8 on v7

--- a/solution.py
+++ b/solution.py
@@ -469,10 +469,25 @@
     body(tiles, loop(tiles, body, start, unroll))
 
 
-def fine_kernel(
+def ends_of(x, rows):
+    return x[rows - 8 : rows], x[:8]
+
+
+def virtual_tiles(polar_ref, ps, pd, pi):
+    total = -16.0
+    for q in range(4):
+        source, diag = polar_unpacked(polar_ref, q)
+        total = total + diag
+        ps[q] = source
+        pd[q] = diag
+        pi[q] = 1.0 / diag
+    return total
+
+
+def rim_kernel(
     s_ref, d_ref, i_ref, d1_ref, from_other, from_mate, polar_ref, corner_near, corner_far,
-    r_ref, s1_ref, d1_virtual, d2_virtual, to_mate, to_other,
-    v0, v1, v2, v3, c0, c1, hs, hd, hi, ps, pd, pi, n1, temp,
+    r_ref, n_ref, to_mate, to_other,
+    v0, v1, v2, v3, c0, c1, hs, hd, hi, ps, pd, pi, temp,
 ):
     v = [v0, v1, v2, v3]
     tiles, rows = s_ref.shape[1], s_ref.shape[2]
@@ -484,57 +499,115 @@
         return 0
 
     loop(tiles, halo, 0, 8)
-    total = -16.0
+    total = virtual_tiles(polar_ref, ps, pd, pi)
     for q in range(4):
-        own_s, own_d = polar_unpacked(polar_ref, q)
         near_s, near_d = polar_unpacked(corner_near, q)
         far_s, far_d = polar_unpacked(corner_far, q)
         left_s, right_s = chosen(odd, near_s, far_s)
         left_d, right_d = chosen(odd, near_d, far_d)
-        total = total + own_d
-        ps[q] = own_s
-        pd[q] = own_d
-        pi[q] = 1.0 / own_d
         source = jnp.where(sub >= 5, left_s, jnp.where(sub <= 2, right_s, 0.0))
         diag = jnp.where(sub >= 5, left_d, jnp.where(sub <= 2, right_d, 4.0))
         hs[q, tiles] = source
         hd[q, tiles] = diag
         hi[q, tiles] = 1.0 / diag
 
-    load_s = loader(s_ref, hs, ps, tiles)
-    smooth(v, load_s, loader(i_ref, hi, pi, tiles), tiles, 32)
+    def rim(own, halo, virtual):
+        def load(q, t):
+            if isinstance(t, int) and t == tiles:
+                last, first = virtual[q, rows - 8 :], virtual[q, :8]
+            else:
+                last, first = own[q, t, rows - 8 :], own[q, t, :8]
+            return jnp.concatenate([last, halo[q, t], first], 0)
+
+        return load
+
+    load_s = rim(s_ref, hs, ps)
+    smooth(v, load_s, rim(i_ref, hi, pi), tiles, 32)
 
     def keep(t, r):
         if not (isinstance(t, int) and t == tiles):
             for q in range(4):
-                r_ref[q, t] = r[q][:rows]
-
-    residuals(v, load_s, loader(d_ref, hd, pd, tiles), tiles, c0, c1, keep, 16)
+                r_ref[q, t] = jnp.concatenate([r[q][16:], r[q][:8]], 0)
+
+    residuals(v, load_s, rim(d_ref, hd, pd), tiles, c0, c1, keep, 16)
 
     def coarse(t, value):
-        n1[t] = value
+        n_ref[t] = jnp.concatenate([value[16:], value[:8]], 0)
+
+    restrict(c0, c1, tiles, 24, coarse, 16)
+
+    rows1 = rows // 2
+
+    def use(c, source):
+        diag = [
+            jnp.where(sub < 4, d1_ref[q, c, :8], d1_ref[q, c, rows1 - 8 :]) for q in range(4)
+        ]
+        store_edges(c, edge_packs(source, diag, False), odd, to_mate, to_other)
+
+    tiles1 = tiles // 2
+    split_tiles(lambda t: n_ref[t], tiles1, 16, splitter(), temp, use)
+    out = moved(
+        jnp.concatenate([n_ref[tiles], total[:8], total[rows - 8 :]], 0), virtual_splitter()
+    )
+    source = quarters_of(out[:16], temp.at[0])
+    diag = [4.0 + x for x in quarters_of(out[16:], temp.at[1])]
+    store_edges(tiles1, edge_packs(source, diag, True), odd, to_mate, to_other)
+
+
+def core_kernel(
+    s_ref, d_ref, i_ref, polar_ref, rim_r, rim_n,
+    r_ref, s1_ref, d1_virtual, d2_virtual,
+    v0, v1, v2, v3, c0, c1, ps, pd, pi, n1, temp,
+):
+    v = [v0, v1, v2, v3]
+    tiles, rows = s_ref.shape[1], s_ref.shape[2]
+    sub = row_ids(8)
+    total = virtual_tiles(polar_ref, ps, pd, pi)
+
+    def core(own, virtual):
+        def load(q, t):
+            return virtual[q] if isinstance(t, int) and t == tiles else own[q, t]
+
+        return load
+
+    def stitched(first, value, last):
+        return jnp.concatenate(
+            [
+                jnp.where(sub < 3, first, value[:8]),
+                value[8 : rows - 8],
+                jnp.where(sub > 4, last, value[rows - 8 :]),
+            ],
+            0,
+        )
+
+    load_s = core(s_ref, ps)
+    smooth(v, load_s, core(i_ref, pi), tiles, 32)
+
+    def keep(t, r):
+        if not (isinstance(t, int) and t == tiles):
+            for q in range(4):
+                r_ref[q, t] = stitched(rim_r[q, t, :8], r[q], rim_r[q, t, 8:])
+
+    residuals(v, load_s, core(d_ref, pd), tiles, c0, c1, keep, 16)
+
+    def coarse(t, value):
+        n1[t] = stitched(rim_n[t, :8], value, rim_n[t, 8:])
 
     restrict(c0, c1, tiles, rows, coarse, 16)
-
-    def edges(t, source, diag, swapped):
-        store_edges(t, edge_packs(source, diag, swapped), odd, to_mate, to_other)
 
     def use(c, source):
         for q in range(4):
             s1_ref[q, c] = source[q]
-        edges(c, source, [d1_ref[q, c] for q in range(4)], False)
 
     tiles1 = tiles // 2
     split_tiles(lambda t: n1[t], tiles1, rows, splitter(), temp, use)
     out = moved(jnp.concatenate([n1[tiles], total], 0), virtual_splitter())
     source = quarters_of(out[:rows], temp.at[0])
     screen = quarters_of(out[rows:], temp.at[1])
-    diag = [4.0 + x for x in screen]
     for q in range(4):
         s1_ref[q, tiles1] = source[q]
-        d1_virtual[q] = diag[q]
+        d1_virtual[q] = 4.0 + screen[q]
     d2_virtual[...] = 4.0 + ((screen[0] + screen[1]) + (screen[2] + screen[3]))
-    edges(tiles1, source, diag, True)
 
 
 def merge_kernel(r_ref, out_ref, temp, out_buf, sems):
@@ -565,7 +638,7 @@
 
 
 def middle_kernel(
-    merged_first, s_ref, d_ref, i_ref, d_virtual, d2_ref, d2_virtual, from_other, from_mate,
+    s_ref, d_ref, i_ref, d_virtual, d2_ref, d2_virtual, from_other, from_mate,
     s2_ref, to_mate, to_other,
     v0, v1, v2, v3, c0, c1, hs, hd, hi, pi,
 ):
@@ -717,19 +790,28 @@
     )
 
     def level_scratch(tiles, rows):
-        halo = (4, tiles + 1, 8, LANES)
-        return [(tiles + 1, rows + 8, LANES)] * 6 + [halo] * 3
+        return [(tiles + 1, rows, LANES)] * 6
+
+    def halo_scratch(tiles):
+        return [(4, tiles + 1, 8, LANES)] * 3
 
     pack1 = (2, tiles1 + 1, 8, LANES)
-    r, s1, d1_virtual, d2_virtual, to_mate, to_other = call(
-        fine_kernel,
-        [quarters, (4, tiles1 + 1, rows1, LANES), (4, rows1, LANES), (rows1, LANES), pack1, pack1],
+    virtual = [(4, rows, LANES)] * 3
+    rim_r, rim_n, to_mate, to_other = call(
+        rim_kernel,
+        [(4, tiles, 16, LANES), (tiles + 1, 16, LANES), pack1, pack1],
+        level_scratch(tiles, 24) + halo_scratch(tiles) + virtual + [(BATCH, 2, 16, LANES)],
+        s, d, inverse, d1, from_other, from_mate, polar, corner_near, corner_far,
+    )
+    from_mate, from_other = swapped_edges(to_mate, to_other)
+    r, s1, d1_virtual, d2_virtual = call(
+        core_kernel,
+        [quarters, (4, tiles1 + 1, rows1, LANES), (4, rows1, LANES), (rows1, LANES)],
         level_scratch(tiles, rows)
-        + [(4, rows, LANES)] * 3
+        + virtual
         + [(tiles + 1, rows, LANES), (BATCH, 2, rows, LANES)],
-        s, d, inverse, d1, from_other, from_mate, polar, corner_near, corner_far,
-    )
-    from_mate, from_other = swapped_edges(to_mate, to_other)
+        s, d, inverse, polar, rim_r, rim_n,
+    )
     (fine_residual,) = call(
         merge_kernel, [(columns, height)], [temp, (columns, height)], r,
         sems=(GROUPS,), far_out=1,
@@ -738,10 +820,8 @@
     s2, to_mate, to_other = call(
         middle_kernel,
         [(tiles1 + 1, rows1, LANES), pack2, pack2],
-        level_scratch(tiles1, rows1) + [(4, rows1, LANES)],
-        pltpu.with_memory_space_constraint(fine_residual, pltpu.HBM),
+        level_scratch(tiles1, rows1 + 8) + halo_scratch(tiles1) + [(4, rows1, LANES)],
         s1, d1, i1, d1_virtual, d2, d2_virtual, from_other, from_mate,
-        far_in=1,
     )
     from_mate, from_other = swapped_edges(to_mate, to_other)
     solution_2, residual_2 = call(

time: 34.9 us -> 33.5 us (0.960)
  waiting for transfers between devices: 4.72 us -> 1.41 us
  Pallas kernels: 12.6 us -> 14.5 us
    ppermute x8, waiting for transfers between devices: 4.72 us -> 1.41 us  [swapped_with(): return lax.ppermute(x, 'lon', pairs + [(b, a) for a, b in pairs])]
    pallas_call x6 -> x7, Pallas kernels: 12.6 us -> 14.5 us  [call(): pl.pallas_call(kernel, out_shape=[jax.ShapeDtypeStruct(shape, F32) for sh...]
  transfers between devices with their start and end apart: 9 -> 9, of which waited for: 2 -> 2; matrix products, arithmetic and copies ran while one was open for 0% -> 0% of each run, Pallas kernels for 10% -> 21%
where the time goes in v8:
time: 33.5 us; the launch traced here: 33.3 us
  starting transfers between devices  16.6 us (50%)
  Pallas kernels  14.5 us (43%)
  waiting for transfers between devices  1.41 us (4%)
  between operations  0.74 us (2%)
    ppermute x8, starting transfers between devices, swapped_with(): return lax.ppermute(x, 'lon', pairs + [(b, a) for a, b in pairs])  16.4 us
    pallas_call x7, Pallas kernels, call(): pl.pallas_call(kernel, out_shape=[jax.ShapeDtypeStruct(shape, F32) for sh...  14.5 us
    ppermute x8, waiting for transfers between devices, swapped_with(): return lax.ppermute(x, 'lon', pairs + [(b, a) for a, b in pairs])  1.41 us
  transfers between devices with their start and end apart: 9, of which 2 were waited for; matrix products, arithmetic and copies ran while one was open for 0% of the time, Pallas kernels for 21%

profile of v8, /device:TPU:0, one launch (start us, length us, event | category | flops | bytes accessed | tf_op | source)
XLA Modules:
  0.0 33.3 jit_solution(16847624311463581174)
XLA Ops:
  0.6 0.0 copy-start.2
  0.6 0.0 copy-start.1
  0.7 0.0 copy-start
  0.7 2.5 %shard_map.58 = (f32[2,32,8,128]{3,2,1,0:T(8,128)S(1)}, f32[2,32,8,128]{3,2,1,0:T(8,128)S(1)}, f32[2,32,128]{2,1,0:T(8,128)S(1)}, f32[2,8,128]{2,1,0:T(8,128)S(1)}, f32[2,8,128]{2,1,0:T(8,128)S(1)}) custom-call(f32[64,8192]{1,0:T(8,128)} %right_ref.3, bf16[64,8192]{1,0:T(8,128)(2,1)} %weight_ref.3, s32[2,256]{1,0:T(2,128)} %flag_ref.3), custom_call_target="tpu_custom_call" | custom-call | tf_op jit(solution)/shard_map/pallas_call | solution.py:732
  3.2 5.5 %collective-permute-start.1 = (f32[2,32,8,128]{3,2,1,0:T(8,128)S(1)}, f32[2,32,8,128]{3,2,1,0:T(8,128)S(1)}, u32[]{:S(2)}, u32[]{:S(2)}) collective-permute-start(f32[2,32,8,128]{3,2,1,0:T(8,128)S(1)} %get-tuple-element.33), channel_id=1, source_target_pairs={{0,15},{2,1},{4,3},{6,5},{8,7},{10,9},{12,11},{14,13},{15,0},{1,2}... | collective-permute-start | bytes 786440 | tf_op jit(solution)/shard_map/ppermute | solution.py:745
  8.7 0.0 collective-permute-start.2
  8.7 0.2 collective-permute-start
  8.9 0.8 %collective-permute-start.4 = (f32[2,8,128]{2,1,0:T(8,128)S(1)}, f32[2,8,128]{2,1,0:T(8,128)S(1)}, u32[]{:S(2)}, u32[]{:S(2)}) collective-permute-start(f32[2,8,128]{2,1,0:T(8,128)S(1)} %get-tuple-element.35), channel_id=1, source_target_pairs={{0,7},{2,9},{4,11},{6,13},{8,15},{10,1},{12,3},{14,5},{7,0},{9,2},... | collective-permute-start | bytes 24584 | tf_op jit(solution)/shard_map/ppermute | solution.py:745
  9.7 2.8 %collective-permute-start.3 = (f32[2,8,128]{2,1,0:T(8,128)S(1)}, f32[2,8,128]{2,1,0:T(8,128)S(1)}, u32[]{:S(2)}, u32[]{:S(2)}) collective-permute-start(f32[2,8,128]{2,1,0:T(8,128)S(1)} %get-tuple-element.27.edges_first), channel_id=1, source_target_pairs={{0,9},{2,11},{4,13},{6,15},{8,1},{10,3},{12,5},{14,7},{9,0},{11,2}... | collective-permute-start | bytes 24584 | tf_op jit(solution)/shard_map/ppermute | solution.py:745
  12.5 0.0 copy-done.2
  12.5 0.0 copy-done.1
  12.5 0.0 copy-done
  12.5 1.8 %shard_map.59 = (f32[4,32,32,128]{3,2,1,0:T(8,128)S(1)}, f32[4,32,32,128]{3,2,1,0:T(8,128)S(1)}, f32[4,32,32,128]{3,2,1,0:T(8,128)S(1)}, f32[4,16,16,128]{3,2,1,...) custom-call(f32[64,8192]{1,0:T(8,128)S(1)} %copy-done, bf16[64,8192]{1,0:T(8,128)(2,1)S(1)} %copy-done.1, ...), custom_call_target="tpu_custom_call" | custom-call | tf_op jit(solution)/shard_map/pallas_call | solution.py:732
  14.3 0.0 collective-permute-done.4.corner_far
  14.3 0.0 collective-permute-done.3.corner_near
  14.3 0.0 collective-permute-done.polar_ref
  14.4 0.0 collective-permute-done.1.from_other
  14.4 0.0 collective-permute-done.2.from_mate
  14.4 2.8 %shard_map.60 = (f32[4,32,16,128]{3,2,1,0:T(8,128)S(1)}, f32[33,16,128]{2,1,0:T(8,128)S(1)}, f32[2,17,8,128]{3,2,1,0:T(8,128)S(1)}, f32[2,17,8,128]{3,2,1,0:T(8,128)S(1)}) custom-call(f32[4,32,32,128]{3,2,1,0:T(8,128)S(1)} %get-tuple-element.28.s_ref, f32[4,32,32,128]{3,2,1,0:T(8,128)S(1)} %get-tuple-element.29.d_ref, ...), custom_call_target="tpu_custom_call" | custom-call | tf_op jit(solution)/shard_map/pallas_call | solution.py:732
  17.1 3.6 %collective-permute-start.5 = (f32[2,17,8,128]{3,2,1,0:T(8,128)S(1)}, f32[2,17,8,128]{3,2,1,0:T(8,128)S(1)}, u32[]{:S(2)}, u32[]{:S(2)}) collective-permute-start(f32[2,17,8,128]{3,2,1,0:T(8,128)S(1)} %get-tuple-element.44), channel_id=1, source_target_pairs={{0,15},{2,1},{4,3},{6,5},{8,7},{10,9},{12,11},{14,13},{15,0},{1,2}... | collective-permute-start | bytes 417800 | tf_op jit(solution)/shard_map/ppermute | solution.py:745
  20.8 0.0 collective-permute-start.6
  20.8 3.3 %shard_map.61 = (f32[4,32,32,128]{3,2,1,0:T(8,128)S(1)}, f32[4,17,16,128]{3,2,1,0:T(8,128)S(1)}, f32[4,16,128]{2,1,0:T(8,128)S(1)}, f32[16,128]{1,0:T(8,128)S(1)}) custom-call(f32[4,32,32,128]{3,2,1,0:T(8,128)S(1)} %get-tuple-element.28.s_ref, f32[4,32,32,128]{3,2,1,0:T(8,128)S(1)} %get-tuple-element.29.d_ref, ...), custom_call_target="tpu_custom_call" | custom-call | tf_op jit(solution)/shard_map/pallas_call | solution.py:732
  24.1 0.3 %collective-permute-done.5.from_other = f32[2,17,8,128]{3,2,1,0:T(8,128)S(1)} collective-permute-done((f32[2,17,8,128]{3,2,1,0:T(8,128)S(1)}, f32[2,17,8,128]{3,2,1,0:T(8,128)S(1)}, u32[]{:S(2)}, u32[]{:S(2)}) %collective-permute-start.5) | collective-permute-done | bytes 139296 | tf_op jit(solution)/shard_map/ppermute | solution.py:745
  24.4 0.0 collective-permute-done.6.from_mate
  24.4 1.0 %shard_map.63 = (f32[17,16,128]{2,1,0:T(8,128)S(1)}, f32[17,8,128]{2,1,0:T(8,128)S(1)}, f32[17,8,128]{2,1,0:T(8,128)S(1)}) custom-call(f32[4,17,16,128]{3,2,1,0:T(8,128)S(1)} %get-tuple-element.39.s_ref, f32[4,16,16,128]{3,2,1,0:T(8,128)S(1)} %get-tuple-element.32.d1_ref.d_ref, f32[4,16,16,128]{3,2,1,0:T(8,128)S(1)} %get-tuple-element.40.i_ref, ...), custom_call_target="tpu_custom_call" | custom-call | tf_op jit(solution)/shard_map/pallas_call | solution.py:732
  25.4 3.6 %collective-permute-start.7 = (f32[17,8,128]{2,1,0:T(8,128)S(1)}, f32[17,8,128]{2,1,0:T(8,128)S(1)}, u32[]{:S(2)}, u32[]{:S(2)}) collective-permute-start(f32[17,8,128]{2,1,0:T(8,128)S(1)} %get-tuple-element.47), channel_id=1, source_target_pairs={{0,15},{2,1},{4,3},{6,5},{8,7},{10,9},{12,11},{14,13},{15,0},{1,2}... | collective-permute-start | bytes 208904 | tf_op jit(solution)/shard_map/ppermute | solution.py:745
  29.1 0.0 collective-permute-start.8
  29.1 1.8 %shard_map.62 = f32[64,8192]{1,0:T(8,128)} custom-call(f32[4,32,32,128]{3,2,1,0:T(8,128)S(1)} %get-tuple-element.38.r_ref), custom_call_target="tpu_custom_call" | custom-call | tf_op jit(solution)/shard_map/pallas_call | solution.py:732
  30.9 1.1 %collective-permute-done.7.from_other = f32[17,8,128]{2,1,0:T(8,128)S(1)} collective-permute-done((f32[17,8,128]{2,1,0:T(8,128)S(1)}, f32[17,8,128]{2,1,0:T(8,128)S(1)}, u32[]{:S(2)}, u32[]{:S(2)}) %collective-permute-start.7) | collective-permute-done | bytes 69664 | tf_op jit(solution)/shard_map/ppermute | solution.py:745
  31.9 0.0 collective-permute-done.8.from_mate
  31.9 1.4 %shard_map.64 = (f32[16,2048]{1,0:T(8,128)}, f32[16,2048]{1,0:T(8,128)}) custom-call(f32[17,16,128]{2,1,0:T(8,128)S(1)} %get-tuple-element.46.s_ref, f32[16,16,128]{2,1,0:T(8,128)S(1)} %get-tuple-element.42.d2_ref.d_ref, f32[16,128]{1,0:T(8,128)S(1)} %get-tuple-element.43.d2_virtual.d_virtual, f32[17,8,128]{2,1,0:T(8,128)S(1)} %collective-permute-done.7.from_other, ...), custom_call_target="tpu_custom_call" | custom-call | tf_op jit(solution)/shard_map/pallas_call | solution.py:732
Async XLA Ops:
  0.6 11.9 %copy-start.2 = (s32[2,256]{1,0:T(2,128)S(1)}, s32[2,256]{1,0:T(2,128)}, u32[]{:S(2)}) copy-start(s32[2,256]{1,0:T(2,128)} %flag_ref.3) | copy-start | bytes 6148
  0.6 11.9 %copy-start.1 = (bf16[64,8192]{1,0:T(8,128)(2,1)S(1)}, bf16[64,8192]{1,0:T(8,128)(2,1)}, u32[]{:S(2)}) copy-start(bf16[64,8192]{1,0:T(8,128)(2,1)} %weight_ref.3) | copy-start | bytes 3145732
  0.7 11.9 %copy-start = (f32[64,8192]{1,0:T(8,128)S(1)}, f32[64,8192]{1,0:T(8,128)}, u32[]{:S(2)}) copy-start(f32[64,8192]{1,0:T(8,128)} %right_ref.3) | copy-start | bytes 6291460
  3.2 11.2 %collective-permute-start.1 = (f32[2,32,8,128]{3,2,1,0:T(8,128)S(1)}, f32[2,32,8,128]{3,2,1,0:T(8,128)S(1)}, u32[]{:S(2)}, u32[]{:S(2)}) collective-permute-start(f32[2,32,8,128]{3,2,1,0:T(8,128)S(1)} %get-tuple-element.33), channel_id=1, source_target_pairs={{0,15},{2,1},{4,3},{6,5},{8,7},{10,9},{12,11},{14,13},{15,0},{1,2}... | collective-permute-start | bytes 786440 | tf_op jit(solution)/shard_map/ppermute | solution.py:745
  8.7 5.7 %collective-permute-start.2 = (f32[2,32,8,128]{3,2,1,0:T(8,128)S(1)}, f32[2,32,8,128]{3,2,1,0:T(8,128)S(1)}, u32[]{:S(2)}, u32[]{:S(2)}) collective-permute-start(f32[2,32,8,128]{3,2,1,0:T(8,128)S(1)} %get-tuple-element.34), channel_id=1, source_target_pairs={{0,1},{2,3},{4,5},{6,7},{8,9},{10,11},{12,13},{14,15},{1,0},{3,2},... | collective-permute-start | bytes 786440 | tf_op jit(solution)/shard_map/ppermute | solution.py:745
  8.7 5.7 %collective-permute-start = (f32[2,32,128]{2,1,0:T(8,128)S(1)}, f32[2,32,128]{2,1,0:T(8,128)S(1)}, u32[]{:S(2)}, u32[]{:S(2)}) collective-permute-start(f32[2,32,128]{2,1,0:T(8,128)S(1)} %get-tuple-element.31), channel_id=1, source_target_pairs={{0,8},{1,9},{2,10},{3,11},{4,12},{5,13},{6,14},{7,15},{8,0},{9,1},... | collective-permute-start | bytes 98312 | tf_op jit(solution)/shard_map/ppermute | solution.py:779
  8.9 5.5 %collective-permute-start.4 = (f32[2,8,128]{2,1,0:T(8,128)S(1)}, f32[2,8,128]{2,1,0:T(8,128)S(1)}, u32[]{:S(2)}, u32[]{:S(2)}) collective-permute-start(f32[2,8,128]{2,1,0:T(8,128)S(1)} %get-tuple-element.35), channel_id=1, source_target_pairs={{0,7},{2,9},{4,11},{6,13},{8,15},{10,1},{12,3},{14,5},{7,0},{9,2},... | collective-permute-start | bytes 24584 | tf_op jit(solution)/shard_map/ppermute | solution.py:745
  9.7 4.6 %collective-permute-start.3 = (f32[2,8,128]{2,1,0:T(8,128)S(1)}, f32[2,8,128]{2,1,0:T(8,128)S(1)}, u32[]{:S(2)}, u32[]{:S(2)}) collective-permute-start(f32[2,8,128]{2,1,0:T(8,128)S(1)} %get-tuple-element.27.edges_first), channel_id=1, source_target_pairs={{0,9},{2,11},{4,13},{6,15},{8,1},{10,3},{12,5},{14,7},{9,0},{11,2}... | collective-permute-start | bytes 24584 | tf_op jit(solution)/shard_map/ppermute | solution.py:745
  17.1 7.2 %collective-permute-start.5 = (f32[2,17,8,128]{3,2,1,0:T(8,128)S(1)}, f32[2,17,8,128]{3,2,1,0:T(8,128)S(1)}, u32[]{:S(2)}, u32[]{:S(2)}) collective-permute-start(f32[2,17,8,128]{3,2,1,0:T(8,128)S(1)} %get-tuple-element.44), channel_id=1, source_target_pairs={{0,15},{2,1},{4,3},{6,5},{8,7},{10,9},{12,11},{14,13},{15,0},{1,2}... | collective-permute-start | bytes 417800 | tf_op jit(solution)/shard_map/ppermute | solution.py:745
  20.8 3.6 %collective-permute-start.6 = (f32[2,17,8,128]{3,2,1,0:T(8,128)S(1)}, f32[2,17,8,128]{3,2,1,0:T(8,128)S(1)}, u32[]{:S(2)}, u32[]{:S(2)}) collective-permute-start(f32[2,17,8,128]{3,2,1,0:T(8,128)S(1)} %get-tuple-element.45), channel_id=1, source_target_pairs={{0,1},{2,3},{4,5},{6,7},{8,9},{10,11},{12,13},{14,15},{1,0},{3,2},... | collective-permute-start | bytes 417800 | tf_op jit(solution)/shard_map/ppermute | solution.py:745
  25.4 6.5 %collective-permute-start.7 = (f32[17,8,128]{2,1,0:T(8,128)S(1)}, f32[17,8,128]{2,1,0:T(8,128)S(1)}, u32[]{:S(2)}, u32[]{:S(2)}) collective-permute-start(f32[17,8,128]{2,1,0:T(8,128)S(1)} %get-tuple-element.47), channel_id=1, source_target_pairs={{0,15},{2,1},{4,3},{6,5},{8,7},{10,9},{12,11},{14,13},{15,0},{1,2}... | collective-permute-start | bytes 208904 | tf_op jit(solution)/shard_map/ppermute | solution.py:745
  29.1 2.9 %collective-permute-start.8 = (f32[17,8,128]{2,1,0:T(8,128)S(1)}, f32[17,8,128]{2,1,0:T(8,128)S(1)}, u32[]{:S(2)}, u32[]{:S(2)}) collective-permute-start(f32[17,8,128]{2,1,0:T(8,128)S(1)} %get-tuple-element.48), channel_id=1, source_target_pairs={{0,1},{2,3},{4,5},{6,7},{8,9},{10,11},{12,13},{14,15},{1,0},{3,2},... | collective-permute-start | bytes 208904 | tf_op jit(solution)/shard_map/ppermute | solution.py:745

commit v9 on v8

--- a/solution.py
+++ b/solution.py
@@ -246,20 +246,17 @@
 
 def edge_kernel(
     right_ref, weight_ref, flag_ref,
-    to_mate, to_other, polar_ref, corner_near, corner_far,
-    edge_s, edge_w, end_s, end_w, flags, temp_s, temp_w, temp_p, temp_q, scale_ref, sems,
+    to_mate, to_other, corner_ref,
+    edge_s, edge_w, flags, temp_s, temp_w, scale_ref, sems,
 ):
     columns, height = right_ref.shape
-    rows, tiles = columns // 2, height // 256
+    tiles = height // 256
     pairs = [(flag_ref, flags)]
     for i, (src, dst, size) in enumerate(
         ((right_ref, edge_s, 8), (weight_ref, edge_w, 16))
     ):
         pairs.append((src.at[pl.ds(0, size)], dst.at[pl.ds(0, size)]))
         pairs.append((src.at[pl.ds(columns - size, size)], dst.at[pl.ds(size, size)]))
-    for src, dst in ((right_ref, end_s), (weight_ref, end_w)):
-        for end, start in enumerate((0, height - 256)):
-            pairs.append((src.at[:, pl.ds(start, 256)], dst.at[end]))
     copies = [
         pltpu.make_async_copy(src, dst, sems.at[i]) for i, (src, dst) in enumerate(pairs)
     ]
@@ -270,7 +267,7 @@
     flag_cols = flag_ref.shape[0]
     copies[0].wait()
     scale_ref[...] = seam_scales(flags[...], range(tiles))
-    for copy in copies[1:5]:
+    for copy in copies[1:]:
         copy.wait()
     sub = row_ids(8)
     lanes = [slice(c * 256, (c + 1) * 256) for c in range(tiles)]
@@ -283,47 +280,60 @@
     weight = jnp.concatenate([weight[:, :8], weight[:, 24:]], 1).reshape(tiles * 16, 256)
     source = quarters_of(source, temp_s)
     weight = quarters_of(weight, temp_w)
+    found = []
     for c in range(tiles):
         here = slice(c * 8, (c + 1) * 8)
         scales = scale_ref[c]
         scale = jnp.where(sub < 4, scales[:1], scales[flag_cols - 1 : flag_cols])
-        diag = [4.0 + w[here] * scale for w in weight]
-        store_edges(
-            c, edge_packs([x[here] for x in source], diag, False), odd, to_mate, to_other
-        )
-
-    for copy in copies[5:]:
-        copy.wait()
+        pair = [x[here] for x in source], [4.0 + w[here] * scale for w in weight]
+        store_edges(c, edge_packs(*pair, False), odd, to_mate, to_other)
+        if c in (0, tiles - 1):
+            found.append(pair)
+    both = mirrored_ends(*found)
+    for pc in (0, 1):
+        corner = both[8 * pc : 8 * (pc + 1)]
+        corner_ref[pc] = corner
+        to_mate[pc, tiles] = corner
+
+
+def mirrored_ends(first, last):
     mirror = selector((LANES, LANES), lambda a, b: a + b == LANES - 1)
-    lane = lane_ids(rows)
+    lane = lane_ids(first[0][0].shape[0])
+    ends = [
+        [jnp.where(lane >= 64, last[i][q ^ 1], first[i][q ^ 1]) for i in (0, 1)]
+        for q in range(4)
+    ]
+    return moved(jnp.concatenate(polar_packs(ends), 0), mirror)
+
+
+def polar_kernel(right_ref, weight_ref, flag_ref, from_mate, polar_ref, temp_s, temp_w):
+    columns, height = right_ref.shape
+    rows, tiles = columns // 2, height // 256
+    scales = seam_scales(flag_ref[...], (0, tiles - 1))
+    lanes = slice(0, 256), slice(height - 256, height)
     source, weight = moved(
-        jnp.concatenate([end_s[0], end_s[1]], 0),
-        matrix,
-        jnp.concatenate([end_w[0], end_w[1]], 0),
+        jnp.concatenate([right_ref[:, w] for w in lanes], 0),
+        splitter(),
+        jnp.concatenate([weight_ref[:, w] for w in lanes], 0),
     )
     found = []
-    for end, c in enumerate((0, tiles - 1)):
+    for end in (0, 1):
         here = slice(end * columns, (end + 1) * columns)
-        scale = seam_rows(scale_ref[c], flag_cols, rows)
+        scale = seam_rows(scales[end], flag_ref.shape[0], rows)
         found.append(
             (
-                quarters_of(source[here], temp_p.at[end]),
-                [4.0 + w * scale for w in quarters_of(weight[here], temp_q.at[end])],
+                quarters_of(source[here], temp_s.at[end]),
+                [4.0 + w * scale for w in quarters_of(weight[here], temp_w.at[end])],
             )
         )
-    ends = [
-        [jnp.where(lane >= 64, found[1][i][q ^ 1], found[0][i][q ^ 1]) for i in (0, 1)]
-        for q in range(4)
-    ]
-    both = moved(jnp.concatenate(polar_packs(ends), 0), mirror)
+    both = mirrored_ends(*found)
     for pc in (0, 1):
-        pack = both[pc * rows : (pc + 1) * rows]
-        polar_ref[pc] = pack
-        corner_near[pc], corner_far[pc] = chosen(odd, pack[:8], pack[rows - 8 :])
+        polar_ref[pc, :rows] = both[pc * rows : (pc + 1) * rows]
+        polar_ref[pc, rows:] = from_mate[pc, tiles]
 
 
 def bulk_kernel(
-    right_ref, weight_ref, flag_ref, edges_first,
+    right_ref, weight_ref, flag_ref, polar_first,
     s_ref, d_ref, i_ref, d1_ref, i1_ref, d2_ref,
     temp_s, temp_d, scale_ref, e_ref,
 ):
@@ -476,7 +486,7 @@
 def virtual_tiles(polar_ref, ps, pd, pi):
     total = -16.0
     for q in range(4):
-        source, diag = polar_unpacked(polar_ref, q)
+        source, diag = polar_unpacked(polar_ref.at[:, : ps.shape[1]], q)
         total = total + diag
         ps[q] = source
         pd[q] = diag
@@ -485,7 +495,7 @@
 
 
 def rim_kernel(
-    s_ref, d_ref, i_ref, d1_ref, from_other, from_mate, polar_ref, corner_near, corner_far,
+    s_ref, d_ref, i_ref, d1_ref, from_other, from_mate, polar_ref, corner_far,
     r_ref, n_ref, to_mate, to_other,
     v0, v1, v2, v3, c0, c1, hs, hd, hi, ps, pd, pi, temp,
 ):
@@ -501,7 +511,7 @@
     loop(tiles, halo, 0, 8)
     total = virtual_tiles(polar_ref, ps, pd, pi)
     for q in range(4):
-        near_s, near_d = polar_unpacked(corner_near, q)
+        near_s, near_d = polar_unpacked(polar_ref.at[:, rows:], q)
         far_s, far_d = polar_unpacked(corner_far, q)
         left_s, right_s = chosen(odd, near_s, far_s)
         left_d, right_d = chosen(odd, near_d, far_d)
@@ -758,35 +768,33 @@
     temp = (BATCH, 2, columns, LANES)
     quarters = (4, tiles, rows, LANES)
     quarters1 = (4, tiles1, rows1, LANES)
-    pack = (2, tiles, 8, LANES)
-    corner = (2, 8, LANES)
     split = (2, 16 * tiles, LANES)
-    to_mate, to_other, polar, corner_near, corner_far = call(
+    to_mate, to_other, corner = call(
         edge_kernel,
-        [pack, pack, (2, rows, LANES), corner, corner],
+        [(2, tiles + 1, 8, LANES), (2, tiles, 8, LANES), (2, 8, LANES)],
         [(16, height), pltpu.VMEM((32, height), BF16)]
-        + [(2, columns, 256), pltpu.VMEM((2, columns, 256), BF16)]
-        + [pltpu.VMEM(seam_flags.shape, jnp.int32), split, split]
-        + [(2, 2, columns, LANES)] * 2
-        + [(tiles, 8, LANES)],
+        + [pltpu.VMEM(seam_flags.shape, jnp.int32), split, split, (tiles, 8, LANES)],
         *[
             pltpu.with_memory_space_constraint(x, pltpu.HBM)
             for x in (right_side, texel_weight, seam_flags)
         ],
-        sems=(9,), far_in=3,
+        sems=(5,), far_in=3,
     )
     from_mate, from_other = swapped_edges(to_mate, to_other)
+    corner_far = swapped_with(corner, half_turn - 1)
+    ends = (2, 2, columns, LANES)
+    (polar_own,) = call(
+        polar_kernel, [(2, rows + 8, LANES)], [ends, ends],
+        right_side, texel_weight, seam_flags, from_mate,
+    )
     polar = lax.ppermute(
-        polar, "lon", [(i, (i + half_turn) % (2 * half_turn)) for i in range(2 * half_turn)]
-    )
-    corner_near_own = corner_near
-    corner_far = swapped_with(corner_far, half_turn - 1)
-    corner_near = swapped_with(corner_near, half_turn + 1)
+        polar_own, "lon", [(i, (i + half_turn) % (2 * half_turn)) for i in range(2 * half_turn)]
+    )
     s, d, inverse, d1, i1, d2 = call(
         bulk_kernel,
         [quarters] * 3 + [quarters1, quarters1, quarters1[1:]],
         [temp, temp, (tiles, 8, LANES), quarters[1:]],
-        right_side, texel_weight, seam_flags, corner_near_own,
+        right_side, texel_weight, seam_flags, polar_own,
     )
 
     def level_scratch(tiles, rows):
@@ -801,7 +809,7 @@
         rim_kernel,
         [(4, tiles, 16, LANES), (tiles + 1, 16, LANES), pack1, pack1],
         level_scratch(tiles, 24) + halo_scratch(tiles) + virtual + [(BATCH, 2, 16, LANES)],
-        s, d, inverse, d1, from_other, from_mate, polar, corner_near, corner_far,
+        s, d, inverse, d1, from_other, from_mate, polar, corner_far,
     )
     from_mate, from_other = swapped_edges(to_mate, to_other)
     r, s1, d1_virtual, d2_virtual = call(

time: 33.5 us -> 34 us (1.015)
  waiting for transfers between devices: 1.41 us -> 5.45 us
  starting transfers between devices: 16.6 us -> 13.1 us
    ppermute x8 -> x7, starting transfers between devices: 16.4 us -> 13.1 us  [swapped_with(): return lax.ppermute(x, 'lon', pairs + [(b, a) for a, b in pairs])]
    ppermute x8 -> x7, waiting for transfers between devices: 1.41 us -> 3.97 us  [swapped_with(): return lax.ppermute(x, 'lon', pairs + [(b, a) for a, b in pairs])]
    ppermute x1, waiting for transfers between devices: 0.01 us -> 1.48 us  [body(): lax.ppermute(polar_own, 'lon', [(i, (i + half_turn) % (2 * half_turn)) fo...]
    pallas_call x7 -> x8, Pallas kernels: 14.5 us -> 14.5 us  [call(): pl.pallas_call(kernel, out_shape=[jax.ShapeDtypeStruct(shape, F32) for sh...]
  transfers between devices with their start and end apart: 9 -> 8, of which waited for: 2 -> 4; matrix products, arithmetic and copies ran while one was open for 0% -> 0% of each run, Pallas kernels for 21% -> 22%
where the time goes in v9:
time: 34 us; the launch traced here: 33.8 us
  Pallas kernels  14.5 us (43%)
  starting transfers between devices  13.1 us (39%)
  waiting for transfers between devices  5.45 us (16%)
  between operations  0.72 us (2%)
    pallas_call x8, Pallas kernels, call(): pl.pallas_call(kernel, out_shape=[jax.ShapeDtypeStruct(shape, F32) for sh...  14.5 us
    ppermute x7, starting transfers between devices, swapped_with(): return lax.ppermute(x, 'lon', pairs + [(b, a) for a, b in pairs])  13.1 us
    ppermute x7, waiting for transfers between devices, swapped_with(): return lax.ppermute(x, 'lon', pairs + [(b, a) for a, b in pairs])  3.97 us
    ppermute x1, waiting for transfers between devices, body(): lax.ppermute(polar_own, 'lon', [(i, (i + half_turn) % (2 * half_turn)) fo...  1.48 us
  transfers between devices with their start and end apart: 8, of which 4 were waited for; matrix products, arithmetic and copies ran while one was open for 0% of the time, Pallas kernels for 22%

profile of v9, /device:TPU:0, one launch (start us, length us, event | category | flops | bytes accessed | tf_op | source)
XLA Modules:
  0.0 33.8 jit_solution(11779826319771349932)
XLA Ops:
  0.6 0.0 copy-start.2
  0.6 0.0 copy-start.1
  0.7 0.0 copy-start
  0.7 2.1 %shard_map.58 = (f32[2,33,8,128]{3,2,1,0:T(8,128)S(1)}, f32[2,32,8,128]{3,2,1,0:T(8,128)S(1)}, f32[2,8,128]{2,1,0:T(8,128)S(1)}) custom-call(f32[64,8192]{1,0:T(8,128)} %right_ref.5, bf16[64,8192]{1,0:T(8,128)(2,1)} %weight_ref.5, s32[2,256]{1,0:T(2,128)} %flag_ref.5), custom_call_target="tpu_custom_call" | custom-call | tf_op jit(solution)/shard_map/pallas_call | solution.py:742
  2.8 0.5 %collective-permute-start = (f32[2,33,8,128]{3,2,1,0:T(8,128)S(1)}, f32[2,33,8,128]{3,2,1,0:T(8,128)S(1)}, u32[]{:S(2)}, u32[]{:S(2)}) collective-permute-start(f32[2,33,8,128]{3,2,1,0:T(8,128)S(1)} %get-tuple-element.25), channel_id=1, source_target_pairs={{0,1},{2,3},{4,5},{6,7},{8,9},{10,11},{12,13},{14,15},{1,0},{3,2},... | collective-permute-start | bytes 811016 | tf_op jit(solution)/shard_map/ppermute | solution.py:755
  3.3 5.6 %collective-permute-start.2 = (f32[2,32,8,128]{3,2,1,0:T(8,128)S(1)}, f32[2,32,8,128]{3,2,1,0:T(8,128)S(1)}, u32[]{:S(2)}, u32[]{:S(2)}) collective-permute-start(f32[2,32,8,128]{3,2,1,0:T(8,128)S(1)} %get-tuple-element.30), channel_id=1, source_target_pairs={{0,15},{2,1},{4,3},{6,5},{8,7},{10,9},{12,11},{14,13},{15,0},{1,2}... | collective-permute-start | bytes 786440 | tf_op jit(solution)/shard_map/ppermute | solution.py:755
  8.9 0.0 collective-permute-done.from_mate
  8.9 0.0 copy-done.2
  8.9 0.0 copy-done.1
  8.9 0.0 copy-done
  8.9 0.4 %shard_map.59.polar_first = f32[2,40,128]{2,1,0:T(8,128)S(1)} custom-call(f32[64,8192]{1,0:T(8,128)S(1)} %copy-done, bf16[64,8192]{1,0:T(8,128)(2,1)S(1)} %copy-done.1, s32[2,256]{1,0:T(2,128)S(1)} %copy-done.2, f32[2,33,8,128]{3,2,1,0:T(8,128)S(1)} %collective-permute-done.from_mate), custom_call_target="tpu_custom_call" | custom-call | tf_op jit(solution)/shard_map/pallas_call | solution.py:742
  9.4 0.0 collective-permute-start.1
  9.4 1.5 %collective-permute-start.3 = (f32[2,8,128]{2,1,0:T(8,128)S(1)}, f32[2,8,128]{2,1,0:T(8,128)S(1)}, u32[]{:S(2)}, u32[]{:S(2)}) collective-permute-start(f32[2,8,128]{2,1,0:T(8,128)S(1)} %get-tuple-element.31), channel_id=1, source_target_pairs={{0,7},{2,9},{4,11},{6,13},{8,15},{10,1},{12,3},{14,5},{7,0},{9,2},... | collective-permute-start | bytes 24584 | tf_op jit(solution)/shard_map/ppermute | solution.py:755
  10.8 1.8 %shard_map.60 = (f32[4,32,32,128]{3,2,1,0:T(8,128)S(1)}, f32[4,32,32,128]{3,2,1,0:T(8,128)S(1)}, f32[4,32,32,128]{3,2,1,0:T(8,128)S(1)}, f32[4,16,16,128]{3,2,1,...) custom-call(f32[64,8192]{1,0:T(8,128)S(1)} %copy-done, bf16[64,8192]{1,0:T(8,128)(2,1)S(1)} %copy-done.1, ...), custom_call_target="tpu_custom_call" | custom-call | tf_op jit(solution)/shard_map/pallas_call | solution.py:742
  12.6 0.8 %collective-permute-done.3.corner_far = f32[2,8,128]{2,1,0:T(8,128)S(1)} collective-permute-done((f32[2,8,128]{2,1,0:T(8,128)S(1)}, f32[2,8,128]{2,1,0:T(8,128)S(1)}, u32[]{:S(2)}, u32[]{:S(2)}) %collective-permute-start.3) | collective-permute-done | bytes 8224 | tf_op jit(solution)/shard_map/ppermute | solution.py:755
  13.4 0.0 collective-permute-done.2.from_other
  13.4 1.5 %collective-permute-done.1.polar_ref = f32[2,40,128]{2,1,0:T(8,128)S(1)} collective-permute-done((f32[2,40,128]{2,1,0:T(8,128)S(1)}, f32[2,40,128]{2,1,0:T(8,128)S(1)}, u32[]{:S(2)}, u32[]{:S(2)}) %collective-permute-start.1) | collective-permute-done | bytes 40992 | tf_op jit(solution)/shard_map/ppermute | solution.py:790
  14.9 2.8 %shard_map.61 = (f32[4,32,16,128]{3,2,1,0:T(8,128)S(1)}, f32[33,16,128]{2,1,0:T(8,128)S(1)}, f32[2,17,8,128]{3,2,1,0:T(8,128)S(1)}, f32[2,17,8,128]{3,2,1,0:T(8,128)S(1)}) custom-call(f32[4,32,32,128]{3,2,1,0:T(8,128)S(1)} %get-tuple-element.26.s_ref, f32[4,32,32,128]{3,2,1,0:T(8,128)S(1)} %get-tuple-element.27.d_ref, ...), custom_call_target="tpu_custom_call" | custom-call | tf_op jit(solution)/shard_map/pallas_call | solution.py:742
  17.7 2.8 %collective-permute-start.4 = (f32[2,17,8,128]{3,2,1,0:T(8,128)S(1)}, f32[2,17,8,128]{3,2,1,0:T(8,128)S(1)}, u32[]{:S(2)}, u32[]{:S(2)}) collective-permute-start(f32[2,17,8,128]{3,2,1,0:T(8,128)S(1)} %get-tuple-element.40), channel_id=1, source_target_pairs={{0,15},{2,1},{4,3},{6,5},{8,7},{10,9},{12,11},{14,13},{15,0},{1,2}... | collective-permute-start | bytes 417800 | tf_op jit(solution)/shard_map/ppermute | solution.py:755
  20.4 0.0 collective-permute-start.5
  20.4 3.3 %shard_map.62 = (f32[4,32,32,128]{3,2,1,0:T(8,128)S(1)}, f32[4,17,16,128]{3,2,1,0:T(8,128)S(1)}, f32[4,16,128]{2,1,0:T(8,128)S(1)}, f32[16,128]{1,0:T(8,128)S(1)}) custom-call(f32[4,32,32,128]{3,2,1,0:T(8,128)S(1)} %get-tuple-element.26.s_ref, f32[4,32,32,128]{3,2,1,0:T(8,128)S(1)} %get-tuple-element.27.d_ref, ...), custom_call_target="tpu_custom_call" | custom-call | tf_op jit(solution)/shard_map/pallas_call | solution.py:742
  23.7 1.2 %collective-permute-done.4.from_other = f32[2,17,8,128]{3,2,1,0:T(8,128)S(1)} collective-permute-done((f32[2,17,8,128]{3,2,1,0:T(8,128)S(1)}, f32[2,17,8,128]{3,2,1,0:T(8,128)S(1)}, u32[]{:S(2)}, u32[]{:S(2)}) %collective-permute-start.4) | collective-permute-done | bytes 139296 | tf_op jit(solution)/shard_map/ppermute | solution.py:755
  24.9 0.0 collective-permute-done.5.from_mate
  24.9 1.0 %shard_map.64 = (f32[17,16,128]{2,1,0:T(8,128)S(1)}, f32[17,8,128]{2,1,0:T(8,128)S(1)}, f32[17,8,128]{2,1,0:T(8,128)S(1)}) custom-call(f32[4,17,16,128]{3,2,1,0:T(8,128)S(1)} %get-tuple-element.35.s_ref, f32[4,16,16,128]{3,2,1,0:T(8,128)S(1)} %get-tuple-element.29.d1_ref.d_ref, f32[4,16,16,128]{3,2,1,0:T(8,128)S(1)} %get-tuple-element.36.i_ref, ...), custom_call_target="tpu_custom_call" | custom-call | tf_op jit(solution)/shard_map/pallas_call | solution.py:742
  25.9 2.8 %collective-permute-start.6 = (f32[17,8,128]{2,1,0:T(8,128)S(1)}, f32[17,8,128]{2,1,0:T(8,128)S(1)}, u32[]{:S(2)}, u32[]{:S(2)}) collective-permute-start(f32[17,8,128]{2,1,0:T(8,128)S(1)} %get-tuple-element.43), channel_id=1, source_target_pairs={{0,15},{2,1},{4,3},{6,5},{8,7},{10,9},{12,11},{14,13},{15,0},{1,2}... | collective-permute-start | bytes 208904 | tf_op jit(solution)/shard_map/ppermute | solution.py:755
  28.7 0.0 collective-permute-start.7
  28.7 1.8 %shard_map.63 = f32[64,8192]{1,0:T(8,128)} custom-call(f32[4,32,32,128]{3,2,1,0:T(8,128)S(1)} %get-tuple-element.34.r_ref), custom_call_target="tpu_custom_call" | custom-call | tf_op jit(solution)/shard_map/pallas_call | solution.py:742
  30.5 2.0 %collective-permute-done.6.from_other = f32[17,8,128]{2,1,0:T(8,128)S(1)} collective-permute-done((f32[17,8,128]{2,1,0:T(8,128)S(1)}, f32[17,8,128]{2,1,0:T(8,128)S(1)}, u32[]{:S(2)}, u32[]{:S(2)}) %collective-permute-start.6) | collective-permute-done | bytes 69664 | tf_op jit(solution)/shard_map/ppermute | solution.py:755
  32.4 0.0 collective-permute-done.7.from_mate
  32.4 1.4 %shard_map.65 = (f32[16,2048]{1,0:T(8,128)}, f32[16,2048]{1,0:T(8,128)}) custom-call(f32[17,16,128]{2,1,0:T(8,128)S(1)} %get-tuple-element.42.s_ref, f32[16,16,128]{2,1,0:T(8,128)S(1)} %get-tuple-element.38.d2_ref.d_ref, f32[16,128]{1,0:T(8,128)S(1)} %get-tuple-element.39.d2_virtual.d_virtual, f32[17,8,128]{2,1,0:T(8,128)S(1)} %collective-permute-done.6.from_other, ...), custom_call_target="tpu_custom_call" | custom-call | tf_op jit(solution)/shard_map/pallas_call | solution.py:742
Async XLA Ops:
  0.6 8.3 %copy-start.2 = (s32[2,256]{1,0:T(2,128)S(1)}, s32[2,256]{1,0:T(2,128)}, u32[]{:S(2)}) copy-start(s32[2,256]{1,0:T(2,128)} %flag_ref.5) | copy-start | bytes 6148
  0.6 8.3 %copy-start.1 = (bf16[64,8192]{1,0:T(8,128)(2,1)S(1)}, bf16[64,8192]{1,0:T(8,128)(2,1)}, u32[]{:S(2)}) copy-start(bf16[64,8192]{1,0:T(8,128)(2,1)} %weight_ref.5) | copy-start | bytes 3145732
  0.7 8.3 %copy-start = (f32[64,8192]{1,0:T(8,128)S(1)}, f32[64,8192]{1,0:T(8,128)}, u32[]{:S(2)}) copy-start(f32[64,8192]{1,0:T(8,128)} %right_ref.5) | copy-start | bytes 6291460
  2.8 6.2 %collective-permute-start = (f32[2,33,8,128]{3,2,1,0:T(8,128)S(1)}, f32[2,33,8,128]{3,2,1,0:T(8,128)S(1)}, u32[]{:S(2)}, u32[]{:S(2)}) collective-permute-start(f32[2,33,8,128]{3,2,1,0:T(8,128)S(1)} %get-tuple-element.25), channel_id=1, source_target_pairs={{0,1},{2,3},{4,5},{6,7},{8,9},{10,11},{12,13},{14,15},{1,0},{3,2},... | collective-permute-start | bytes 811016 | tf_op jit(solution)/shard_map/ppermute | solution.py:755
  3.3 10.2 %collective-permute-start.2 = (f32[2,32,8,128]{3,2,1,0:T(8,128)S(1)}, f32[2,32,8,128]{3,2,1,0:T(8,128)S(1)}, u32[]{:S(2)}, u32[]{:S(2)}) collective-permute-start(f32[2,32,8,128]{3,2,1,0:T(8,128)S(1)} %get-tuple-element.30), channel_id=1, source_target_pairs={{0,15},{2,1},{4,3},{6,5},{8,7},{10,9},{12,11},{14,13},{15,0},{1,2}... | collective-permute-start | bytes 786440 | tf_op jit(solution)/shard_map/ppermute | solution.py:755
  9.4 5.5 %collective-permute-start.1 = (f32[2,40,128]{2,1,0:T(8,128)S(1)}, f32[2,40,128]{2,1,0:T(8,128)S(1)}, u32[]{:S(2)}, u32[]{:S(2)}) collective-permute-start(f32[2,40,128]{2,1,0:T(8,128)S(1)} %shard_map.59.polar_first), channel_id=1, source_target_pairs={{0,8},{1,9},{2,10},{3,11},{4,12},{5,13},{6,14},{7,15},{8,0},{9,1},... | collective-permute-start | bytes 122888 | tf_op jit(solution)/shard_map/ppermute | solution.py:790
  9.4 4.0 %collective-permute-start.3 = (f32[2,8,128]{2,1,0:T(8,128)S(1)}, f32[2,8,128]{2,1,0:T(8,128)S(1)}, u32[]{:S(2)}, u32[]{:S(2)}) collective-permute-start(f32[2,8,128]{2,1,0:T(8,128)S(1)} %get-tuple-element.31), channel_id=1, source_target_pairs={{0,7},{2,9},{4,11},{6,13},{8,15},{10,1},{12,3},{14,5},{7,0},{9,2},... | collective-permute-start | bytes 24584 | tf_op jit(solution)/shard_map/ppermute | solution.py:755
  17.7 7.2 %collective-permute-start.4 = (f32[2,17,8,128]{3,2,1,0:T(8,128)S(1)}, f32[2,17,8,128]{3,2,1,0:T(8,128)S(1)}, u32[]{:S(2)}, u32[]{:S(2)}) collective-permute-start(f32[2,17,8,128]{3,2,1,0:T(8,128)S(1)} %get-tuple-element.40), channel_id=1, source_target_pairs={{0,15},{2,1},{4,3},{6,5},{8,7},{10,9},{12,11},{14,13},{15,0},{1,2}... | collective-permute-start | bytes 417800 | tf_op jit(solution)/shard_map/ppermute | solution.py:755
  20.4 4.5 %collective-permute-start.5 = (f32[2,17,8,128]{3,2,1,0:T(8,128)S(1)}, f32[2,17,8,128]{3,2,1,0:T(8,128)S(1)}, u32[]{:S(2)}, u32[]{:S(2)}) collective-permute-start(f32[2,17,8,128]{3,2,1,0:T(8,128)S(1)} %get-tuple-element.41), channel_id=1, source_target_pairs={{0,1},{2,3},{4,5},{6,7},{8,9},{10,11},{12,13},{14,15},{1,0},{3,2},... | collective-permute-start | bytes 417800 | tf_op jit(solution)/shard_map/ppermute | solution.py:755
  25.9 6.5 %collective-permute-start.6 = (f32[17,8,128]{2,1,0:T(8,128)S(1)}, f32[17,8,128]{2,1,0:T(8,128)S(1)}, u32[]{:S(2)}, u32[]{:S(2)}) collective-permute-start(f32[17,8,128]{2,1,0:T(8,128)S(1)} %get-tuple-element.43), channel_id=1, source_target_pairs={{0,15},{2,1},{4,3},{6,5},{8,7},{10,9},{12,11},{14,13},{15,0},{1,2}... | collective-permute-start | bytes 208904 | tf_op jit(solution)/shard_map/ppermute | solution.py:755
  28.7 3.7 %collective-permute-start.7 = (f32[17,8,128]{2,1,0:T(8,128)S(1)}, f32[17,8,128]{2,1,0:T(8,128)S(1)}, u32[]{:S(2)}, u32[]{:S(2)}) collective-permute-start(f32[17,8,128]{2,1,0:T(8,128)S(1)} %get-tuple-element.44), channel_id=1, source_target_pairs={{0,1},{2,3},{4,5},{6,7},{8,9},{10,11},{12,13},{14,15},{1,0},{3,2},... | collective-permute-start | bytes 208904 | tf_op jit(solution)/shard_map/ppermute | solution.py:755

commit v10 on v7

--- a/solution.py
+++ b/solution.py
@@ -180,6 +180,58 @@
     right, left = packs
     for i in (0, 1):
         to_mate[i, t], to_other[i, t] = chosen(odd, left[i], right[i])
+
+
+def wide_packs(source, diag, partial, diag2, swapped):
+    sub = row_ids(8)
+    even, odd = reds(swapped)
+    rows = source[0].shape[0]
+    packs = []
+    for here, far, near, row, step in (
+        (slice(rows - 8, rows), even, odd, 4, -1),
+        (slice(0, 8), odd, even, 3, 1),
+    ):
+        gs = [x[here] for x in source]
+        gd = [x[here] for x in diag]
+        part = partial[here]
+        at = sub == row
+        for q in (far, near):
+            gs[q] = jnp.where(at, gs[q] / gd[q], gs[q])
+        gd[far] = jnp.where(at, part / diag2[here], gd[far])
+        gs[far ^ 1] = jnp.where(at, roll_rows(part, step), gs[far ^ 1])
+        gd[far ^ 1] = jnp.where(at, roll_rows(part, 2 * step), gd[far ^ 1])
+        shift = 4 if row == 4 else 0
+        packs.append(
+            [
+                jnp.where(sub < 4, roll_rows(g[q], shift), roll_rows(g[q + 1], 4 - shift))
+                for g in (gs, gd)
+                for q in (0, 2)
+            ]
+        )
+    return packs
+
+
+def wide_unpacked(left, right, swapped):
+    sub = row_ids(8)
+    even, odd = reds(swapped)
+    groups = []
+    for k in (0, 2):
+        group = []
+        for l, r in zip(left[k : k + 2], right[k : k + 2]):
+            group.append(jnp.where(sub < 4, r, roll_rows(l, 4)))
+            group.append(jnp.where(sub < 4, roll_rows(r, 4), l))
+        groups.append(group)
+    source, diag = groups
+    partial = jnp.zeros_like(sub, F32)
+    for far, near, row, step in ((even, odd, 4, 1), (odd, even, 3, -1)):
+        at = sub == row
+        for i, part in enumerate((diag[far], source[far ^ 1], diag[far ^ 1])):
+            partial = jnp.where(sub == row + i * step, roll_rows(part, i * step), partial)
+        source[far ^ 1] = jnp.where(at, 0.0, source[far ^ 1])
+        diag[far ^ 1] = jnp.where(at, 4.0, diag[far ^ 1])
+        for q in (far, near):
+            diag[q] = jnp.where(at, 1.0, diag[q])
+    return source, diag, partial
 
 
 def fill_halo(t, from_mate, from_other, odd, swapped, hs, hd, hi):
@@ -426,7 +478,7 @@
     half_sweep(v, load_s, load_i, tiles, False, unroll)
 
 
-def residuals(v, load_s, load_d, tiles, c0, c1, keep, unroll):
+def residuals(v, load_s, load_d, tiles, c0, c1, keep, unroll, valid=None):
     lane = lane_ids(v[0].shape[1])
 
     def body(t, carry):
@@ -442,6 +494,8 @@
         ]
         r = [load_s(q, t) - (load_d(q, t) * x[q] - beside[q]) for q in range(4)]
         keep(t, r)
+        if valid is not None:
+            r = [jnp.where(valid, x, 0.0) for x in r]
         c0[t] = (col_prev(r[2]) + col_next(r[0])) + 3.0 * (r[0] + r[2])
         c1[t] = (col_prev(r[3]) + col_next(r[1])) + 3.0 * (r[1] + r[3])
         return here1, here3, next0, next2
@@ -470,9 +524,11 @@
 
 
 def fine_kernel(
-    s_ref, d_ref, i_ref, d1_ref, from_other, from_mate, polar_ref, corner_near, corner_far,
+    s_ref, d_ref, i_ref, d1_ref, i1_ref, d2_ref,
+    from_other, from_mate, polar_ref, corner_near, corner_far,
     r_ref, s1_ref, d1_virtual, d2_virtual, to_mate, to_other,
     v0, v1, v2, v3, c0, c1, hs, hd, hi, ps, pd, pi, n1, temp,
+    w0, w1, w2, w3, e0, e1, pi1,
 ):
     v = [v0, v1, v2, v3]
     tiles, rows = s_ref.shape[1], s_ref.shape[2]
@@ -516,25 +572,42 @@
 
     restrict(c0, c1, tiles, rows, coarse, 16)
 
-    def edges(t, source, diag, swapped):
-        store_edges(t, edge_packs(source, diag, swapped), odd, to_mate, to_other)
-
     def use(c, source):
         for q in range(4):
             s1_ref[q, c] = source[q]
-        edges(c, source, [d1_ref[q, c] for q in range(4)], False)
 
     tiles1 = tiles // 2
     split_tiles(lambda t: n1[t], tiles1, rows, splitter(), temp, use)
     out = moved(jnp.concatenate([n1[tiles], total], 0), virtual_splitter())
     source = quarters_of(out[:rows], temp.at[0])
     screen = quarters_of(out[rows:], temp.at[1])
-    diag = [4.0 + x for x in screen]
     for q in range(4):
         s1_ref[q, tiles1] = source[q]
-        d1_virtual[q] = diag[q]
+        d1_virtual[q] = 4.0 + screen[q]
+        pi1[q] = 1.0 / (4.0 + screen[q])
     d2_virtual[...] = 4.0 + ((screen[0] + screen[1]) + (screen[2] + screen[3]))
-    edges(tiles1, source, diag, True)
+
+    def own(main, virtual):
+        return lambda q, t: virtual[q] if isinstance(t, int) and t == tiles1 else main[q, t]
+
+    w = [w0, w1, w2, w3]
+    rows1 = rows // 2
+    row = row_ids(rows1)
+    load_s, load_d = own(s1_ref, s1_ref.at[:, tiles1]), own(d1_ref, d1_virtual)
+    smooth(w, load_s, own(i1_ref, pi1), tiles1, 16)
+    valid = (row >= 2) & (row < rows1 - 2)
+    residuals(w, load_s, load_d, tiles1, e0, e1, lambda t, r: None, 16, valid)
+
+    def edges(t, partial):
+        virtual = isinstance(t, int) and t == tiles1
+        source = [s1_ref[q, t] for q in range(4)]
+        diag = [load_d(q, t) for q in range(4)]
+        diag2 = d2_virtual[...] if virtual else d2_ref[t]
+        right, left = wide_packs(source, diag, partial, diag2, virtual)
+        for i in range(4):
+            to_mate[i, t], to_other[i, t] = chosen(odd, left[i], right[i])
+
+    restrict(e0, e1, tiles1, rows1, edges, 16)
 
 
 def merge_kernel(r_ref, out_ref, temp, out_buf, sems):
@@ -564,16 +637,28 @@
         copy.wait()
 
 
-def middle_kernel(
-    merged_first, s_ref, d_ref, i_ref, d_virtual, d2_ref, d2_virtual, from_other, from_mate,
-    s2_ref, to_mate, to_other,
-    v0, v1, v2, v3, c0, c1, hs, hd, hi, pi,
+def coarse_kernel(
+    s_ref, d_ref, i_ref, d_virtual, d2_ref, d2_virtual, from_other, from_mate,
+    solution_ref, residual_ref,
+    v0, v1, v2, v3, c0, c1, hs, hd, hi, pi, part, s, d, inv, va, vb,
 ):
     v = [v0, v1, v2, v3]
-    tiles, rows = d_ref.shape[1], d_ref.shape[2]
-    odd = is_odd()
+    tiles, own = d_ref.shape[1], d_ref.shape[2]
+    rows = own + 8
+    sub = row_ids(8)
+    odd_band = is_odd()
     for t in range(tiles + 1):
-        fill_halo(t, from_mate, from_other, odd, t == tiles, hs, hd, hi)
+        pairs = [chosen(odd_band, from_mate[i, t], from_other[i, t]) for i in range(4)]
+        left, right = zip(*pairs)
+        source, diag, part[t] = wide_unpacked(left, right, t == tiles)
+        for q in range(4):
+            hs[q, t] = source[q]
+            hd[q, t] = diag[q]
+            hi[q, t] = 1.0 / diag[q]
+        total = (diag[0] + diag[1]) + (diag[2] + diag[3]) - 12.0
+        total = jnp.where((sub == 3) | (sub == 4), 1.0, total)
+        here = d2_virtual[...] if t == tiles else d2_ref[t]
+        d[t] = jnp.concatenate([here, total], 0)
     for q in range(4):
         pi[q] = 1.0 / d_virtual[q]
 
@@ -581,45 +666,23 @@
         return jnp.concatenate([s_ref[q, t], hs[q, t]], 0)
 
     smooth(v, load_s, loader(i_ref, hi, pi, tiles), tiles, 16)
-    residuals(
-        v, load_s, loader(d_ref, hd, d_virtual, tiles), tiles, c0, c1, lambda t, r: None, 16
-    )
-    sub = row_ids(8)
-
-    def coarse(t, value):
-        diag = d2_virtual[...] if t == tiles else d2_ref[t]
-        s2_ref[t] = value
-        right = jnp.where(sub < 4, roll_rows(value[rows - 8 :], 4), diag[rows - 8 :])
-        left = jnp.where(sub < 4, value[:8], roll_rows(diag[:8], 4))
-        to_mate[t], to_other[t] = chosen(odd, left, right)
-
-    restrict(c0, c1, tiles, rows, coarse, 16)
-
-
-def last_kernel(
-    s_ref, d_ref, d_virtual, from_other, from_mate,
-    solution_ref, residual_ref,
-    s, d, inv, va, vb,
-):
-    tiles, own = d_ref.shape[0], d_ref.shape[1]
-    rows = own + 8
-    sub = row_ids(8)
     lane, row = lane_ids(rows), row_ids(rows)
+    valid = (row < own + 2) | (row >= own + 6)
+    load_d = loader(d_ref, hd, d_virtual, tiles)
+    residuals(v, load_s, load_d, tiles, c0, c1, lambda t, r: None, 16, valid)
+
     even = (lane + row) % 2 == 0
     odd = jnp.logical_not(even)
-    odd_band = is_odd()
-    for t in range(tiles + 1):
-        left, right = chosen(odd_band, from_mate[t], from_other[t])
-        diag = d_virtual[...] if t == tiles else d_ref[t]
-        source = jnp.concatenate(
-            [s_ref[t], jnp.where(sub < 4, right, roll_rows(left, 4))], 0
-        )
-        diag = jnp.concatenate([diag, jnp.where(sub < 4, roll_rows(right, 4), left)], 0)
-        inverse = 1.0 / diag
+
+    def start(t, value):
+        source = jnp.concatenate([value[:own], value[own:] + part[t]], 0)
+        inverse = 1.0 / d[t]
         s[t] = source
-        d[t] = diag
         inv[t] = inverse
-        va[t] = jnp.where(odd if t == tiles else even, source * inverse, 0.0)
+        virtual = isinstance(t, int) and t == tiles
+        va[t] = jnp.where(odd if virtual else even, source * inverse, 0.0)
+
+    restrict(c0, c1, tiles, rows, start, 16)
 
     def scan(v, use):
         up, down = roll_up(v[tiles]), roll_down(v[0])
@@ -717,38 +780,37 @@
     )
 
     def level_scratch(tiles, rows):
-        halo = (4, tiles + 1, 8, LANES)
-        return [(tiles + 1, rows + 8, LANES)] * 6 + [halo] * 3
-
-    pack1 = (2, tiles1 + 1, 8, LANES)
+        return [(tiles + 1, rows, LANES)] * 6
+
+    def halo_scratch(tiles):
+        return [(4, tiles + 1, 8, LANES)] * 3
+
+    pack1 = (4, tiles1 + 1, 8, LANES)
     r, s1, d1_virtual, d2_virtual, to_mate, to_other = call(
         fine_kernel,
         [quarters, (4, tiles1 + 1, rows1, LANES), (4, rows1, LANES), (rows1, LANES), pack1, pack1],
-        level_scratch(tiles, rows)
+        level_scratch(tiles, rows + 8)
+        + halo_scratch(tiles)
         + [(4, rows, LANES)] * 3
-        + [(tiles + 1, rows, LANES), (BATCH, 2, rows, LANES)],
-        s, d, inverse, d1, from_other, from_mate, polar, corner_near, corner_far,
+        + [(tiles + 1, rows, LANES), (BATCH, 2, rows, LANES)]
+        + level_scratch(tiles1, rows1)
+        + [(4, rows1, LANES)],
+        s, d, inverse, d1, i1, d2, from_other, from_mate, polar, corner_near, corner_far,
     )
     from_mate, from_other = swapped_edges(to_mate, to_other)
     (fine_residual,) = call(
         merge_kernel, [(columns, height)], [temp, (columns, height)], r,
         sems=(GROUPS,), far_out=1,
     )
-    pack2 = (tiles1 + 1, 8, LANES)
-    s2, to_mate, to_other = call(
-        middle_kernel,
-        [(tiles1 + 1, rows1, LANES), pack2, pack2],
-        level_scratch(tiles1, rows1) + [(4, rows1, LANES)],
-        pltpu.with_memory_space_constraint(fine_residual, pltpu.HBM),
+    wide = (tiles1 + 1, rows1 + 8, LANES)
+    solution_2, residual_2 = call(
+        coarse_kernel,
+        [(columns // 4, height // 4)] * 2,
+        level_scratch(tiles1, rows1 + 8)
+        + halo_scratch(tiles1)
+        + [(4, rows1, LANES), (tiles1 + 1, 8, LANES)]
+        + [wide] * 5,
         s1, d1, i1, d1_virtual, d2, d2_virtual, from_other, from_mate,
-        far_in=1,
-    )
-    from_mate, from_other = swapped_edges(to_mate, to_other)
-    solution_2, residual_2 = call(
-        last_kernel,
-        [(columns // 4, height // 4)] * 2,
-        [(tiles1 + 1, rows1 + 8, LANES)] * 5,
-        s2, d2, d2_virtual, from_other, from_mate,
     )
     return fine_residual, solution_2, residual_2
 

time: 34.9 us -> 31.2 us (0.89)
  the two profiles are of different devices: /device:TPU:0 before, /device:TPU:1 now
where the time goes in v10:
time: 31.2 us; the launch traced here: 31.1 us
  Pallas kernels  13.3 us (43%)
  starting transfers between devices  12.3 us (39%)
  waiting for transfers between devices  4.75 us (15%)
  between operations  0.7 us (2%)
    pallas_call x5, Pallas kernels, call(): pl.pallas_call(kernel, out_shape=[jax.ShapeDtypeStruct(shape, F32) for sh...  13.3 us
    ppermute x6, starting transfers between devices, swapped_with(): return lax.ppermute(x, 'lon', pairs + [(b, a) for a, b in pairs])  12.3 us
    ppermute x6, waiting for transfers between devices, swapped_with(): return lax.ppermute(x, 'lon', pairs + [(b, a) for a, b in pairs])  4.75 us
  transfers between devices with their start and end apart: 7, of which 3 were waited for; matrix products, arithmetic and copies ran while one was open for 0% of the time, Pallas kernels for 11%

profile of v10, /device:TPU:1, one launch (start us, length us, event | category | flops | bytes accessed | tf_op | source)
XLA Modules:
  0.0 31.1 jit_solution(17644715344208948764)
XLA Ops:
  0.6 0.0 copy-start.2
  0.6 0.0 copy-start.1
  0.7 0.0 copy-start
  0.7 2.5 %shard_map.58 = (f32[2,32,8,128]{3,2,1,0:T(8,128)S(1)}, f32[2,32,8,128]{3,2,1,0:T(8,128)S(1)}, f32[2,32,128]{2,1,0:T(8,128)S(1)}, f32[2,8,128]{2,1,0:T(8,128)S(1)}, f32[2,8,128]{2,1,0:T(8,128)S(1)}) custom-call(f32[64,8192]{1,0:T(8,128)} %right_ref.3, bf16[64,8192]{1,0:T(8,128)(2,1)} %weight_ref.3, s32[2,256]{1,0:T(2,128)} %flag_ref.3), custom_call_target="tpu_custom_call" | custom-call | tf_op jit(solution)/shard_map/pallas_call | solution.py:722
  3.2 2.7 %collective-permute-start = (f32[2,32,8,128]{3,2,1,0:T(8,128)S(1)}, f32[2,32,8,128]{3,2,1,0:T(8,128)S(1)}, u32[]{:S(2)}, u32[]{:S(2)}) collective-permute-start(f32[2,32,8,128]{3,2,1,0:T(8,128)S(1)} %get-tuple-element.29), channel_id=1, source_target_pairs={{0,15},{2,1},{4,3},{6,5},{8,7},{10,9},{12,11},{14,13},{15,0},{1,2}... | collective-permute-start | bytes 786440 | tf_op jit(solution)/shard_map/ppermute | solution.py:735
  5.8 2.9 %collective-permute-start.1 = (f32[2,32,8,128]{3,2,1,0:T(8,128)S(1)}, f32[2,32,8,128]{3,2,1,0:T(8,128)S(1)}, u32[]{:S(2)}, u32[]{:S(2)}) collective-permute-start(f32[2,32,8,128]{3,2,1,0:T(8,128)S(1)} %get-tuple-element.30), channel_id=1, source_target_pairs={{0,1},{2,3},{4,5},{6,7},{8,9},{10,11},{12,13},{14,15},{1,0},{3,2},... | collective-permute-start | bytes 786440 | tf_op jit(solution)/shard_map/ppermute | solution.py:735
  8.7 0.0 collective-permute-start.2
  8.7 1.2 %collective-permute-start.4 = (f32[2,8,128]{2,1,0:T(8,128)S(1)}, f32[2,8,128]{2,1,0:T(8,128)S(1)}, u32[]{:S(2)}, u32[]{:S(2)}) collective-permute-start(f32[2,8,128]{2,1,0:T(8,128)S(1)} %get-tuple-element.32), channel_id=1, source_target_pairs={{0,7},{2,9},{4,11},{6,13},{8,15},{10,1},{12,3},{14,5},{7,0},{9,2},... | collective-permute-start | bytes 24584 | tf_op jit(solution)/shard_map/ppermute | solution.py:735
  9.9 1.4 %collective-permute-start.3 = (f32[2,8,128]{2,1,0:T(8,128)S(1)}, f32[2,8,128]{2,1,0:T(8,128)S(1)}, u32[]{:S(2)}, u32[]{:S(2)}) collective-permute-start(f32[2,8,128]{2,1,0:T(8,128)S(1)} %get-tuple-element.22.edges_first), channel_id=1, source_target_pairs={{0,9},{2,11},{4,13},{6,15},{8,1},{10,3},{12,5},{14,7},{9,0},{11,2}... | collective-permute-start | bytes 24584 | tf_op jit(solution)/shard_map/ppermute | solution.py:735
  11.2 0.0 copy-done.2
  11.2 0.0 copy-done.1
  11.2 0.0 copy-done
  11.3 1.8 %shard_map.59 = (f32[4,32,32,128]{3,2,1,0:T(8,128)S(1)}, f32[4,32,32,128]{3,2,1,0:T(8,128)S(1)}, f32[4,32,32,128]{3,2,1,0:T(8,128)S(1)}, f32[4,16,16,128]{3,2,1,...) custom-call(f32[64,8192]{1,0:T(8,128)S(1)} %copy-done, bf16[64,8192]{1,0:T(8,128)(2,1)S(1)} %copy-done.1, ...), custom_call_target="tpu_custom_call" | custom-call | tf_op jit(solution)/shard_map/pallas_call | solution.py:722
  13.1 0.6 %collective-permute-done.4.corner_far = f32[2,8,128]{2,1,0:T(8,128)S(1)} collective-permute-done((f32[2,8,128]{2,1,0:T(8,128)S(1)}, f32[2,8,128]{2,1,0:T(8,128)S(1)}, u32[]{:S(2)}, u32[]{:S(2)}) %collective-permute-start.4) | collective-permute-done | bytes 8224 | tf_op jit(solution)/shard_map/ppermute | solution.py:735
  13.7 0.2 collective-permute-done.3.corner_near
  13.8 0.0 collective-permute-done.2.polar_ref
  13.8 0.0 collective-permute-done.from_other
  13.8 0.0 collective-permute-done.1.from_mate
  13.8 4.9 %shard_map.60 = (f32[4,32,32,128]{3,2,1,0:T(8,128)S(1)}, f32[4,17,16,128]{3,2,1,0:T(8,128)S(1)}, f32[4,16,128]{2,1,0:T(8,128)S(1)}, f32[16,128]{1,0:T(8,128)S(1)...) custom-call(f32[4,32,32,128]{3,2,1,0:T(8,128)S(1)} %get-tuple-element.23.s_ref, ...), custom_call_target="tpu_custom_call" | custom-call | tf_op jit(solution)/shard_map/pallas_call | solution.py:722
  18.7 2.7 %collective-permute-start.5 = (f32[4,17,8,128]{3,2,1,0:T(8,128)S(1)}, f32[4,17,8,128]{3,2,1,0:T(8,128)S(1)}, u32[]{:S(2)}, u32[]{:S(2)}) collective-permute-start(f32[4,17,8,128]{3,2,1,0:T(8,128)S(1)} %get-tuple-element.37), channel_id=1, source_target_pairs={{0,15},{2,1},{4,3},{6,5},{8,7},{10,9},{12,11},{14,13},{15,0},{1,2}... | collective-permute-start | bytes 835592 | tf_op jit(solution)/shard_map/ppermute | solution.py:735
  21.5 1.5 %collective-permute-start.6 = (f32[4,17,8,128]{3,2,1,0:T(8,128)S(1)}, f32[4,17,8,128]{3,2,1,0:T(8,128)S(1)}, u32[]{:S(2)}, u32[]{:S(2)}) collective-permute-start(f32[4,17,8,128]{3,2,1,0:T(8,128)S(1)} %get-tuple-element.38), channel_id=1, source_target_pairs={{0,1},{2,3},{4,5},{6,7},{8,9},{10,11},{12,13},{14,15},{1,0},{3,2},... | collective-permute-start | bytes 835592 | tf_op jit(solution)/shard_map/ppermute | solution.py:735
  22.9 1.8 %shard_map.61 = f32[64,8192]{1,0:T(8,128)} custom-call(f32[4,32,32,128]{3,2,1,0:T(8,128)S(1)} %get-tuple-element.33.r_ref), custom_call_target="tpu_custom_call" | custom-call | tf_op jit(solution)/shard_map/pallas_call | solution.py:722
  24.7 4.0 %collective-permute-done.5.from_other = f32[4,17,8,128]{3,2,1,0:T(8,128)S(1)} collective-permute-done((f32[4,17,8,128]{3,2,1,0:T(8,128)S(1)}, f32[4,17,8,128]{3,2,1,0:T(8,128)S(1)}, u32[]{:S(2)}, u32[]{:S(2)}) %collective-permute-start.5) | collective-permute-done | bytes 278560 | tf_op jit(solution)/shard_map/ppermute | solution.py:735
  28.7 0.0 collective-permute-done.6.from_mate
  28.7 2.4 %shard_map.62 = (f32[16,2048]{1,0:T(8,128)}, f32[16,2048]{1,0:T(8,128)}) custom-call(f32[4,17,16,128]{3,2,1,0:T(8,128)S(1)} %get-tuple-element.34.s_ref, f32[4,16,16,128]{3,2,1,0:T(8,128)S(1)} %get-tuple-element.26.d1_ref.d_ref, f32[4,16,16,128]{3,2,1,0:T(8,128)S(1)} %get-tuple-element.27.i1_ref.i_ref, f32[4,16,128]{2,1,0:T(8,128)S(1)} %get-tuple-element.35.d_virtual, ...), custom_call_target="tpu_custom_call" | custom-call | tf_op jit(solution)/shard_map/pallas_call | solution.py:722
Async XLA Ops:
  0.6 10.6 %copy-start.2 = (s32[2,256]{1,0:T(2,128)S(1)}, s32[2,256]{1,0:T(2,128)}, u32[]{:S(2)}) copy-start(s32[2,256]{1,0:T(2,128)} %flag_ref.3) | copy-start | bytes 6148
  0.6 10.6 %copy-start.1 = (bf16[64,8192]{1,0:T(8,128)(2,1)S(1)}, bf16[64,8192]{1,0:T(8,128)(2,1)}, u32[]{:S(2)}) copy-start(bf16[64,8192]{1,0:T(8,128)(2,1)} %weight_ref.3) | copy-start | bytes 3145732
  0.7 10.6 %copy-start = (f32[64,8192]{1,0:T(8,128)S(1)}, f32[64,8192]{1,0:T(8,128)}, u32[]{:S(2)}) copy-start(f32[64,8192]{1,0:T(8,128)} %right_ref.3) | copy-start | bytes 6291460
  3.2 10.7 %collective-permute-start = (f32[2,32,8,128]{3,2,1,0:T(8,128)S(1)}, f32[2,32,8,128]{3,2,1,0:T(8,128)S(1)}, u32[]{:S(2)}, u32[]{:S(2)}) collective-permute-start(f32[2,32,8,128]{3,2,1,0:T(8,128)S(1)} %get-tuple-element.29), channel_id=1, source_target_pairs={{0,15},{2,1},{4,3},{6,5},{8,7},{10,9},{12,11},{14,13},{15,0},{1,2}... | collective-permute-start | bytes 786440 | tf_op jit(solution)/shard_map/ppermute | solution.py:735
  5.8 8.0 %collective-permute-start.1 = (f32[2,32,8,128]{3,2,1,0:T(8,128)S(1)}, f32[2,32,8,128]{3,2,1,0:T(8,128)S(1)}, u32[]{:S(2)}, u32[]{:S(2)}) collective-permute-start(f32[2,32,8,128]{3,2,1,0:T(8,128)S(1)} %get-tuple-element.30), channel_id=1, source_target_pairs={{0,1},{2,3},{4,5},{6,7},{8,9},{10,11},{12,13},{14,15},{1,0},{3,2},... | collective-permute-start | bytes 786440 | tf_op jit(solution)/shard_map/ppermute | solution.py:735
  8.7 5.1 %collective-permute-start.2 = (f32[2,32,128]{2,1,0:T(8,128)S(1)}, f32[2,32,128]{2,1,0:T(8,128)S(1)}, u32[]{:S(2)}, u32[]{:S(2)}) collective-permute-start(f32[2,32,128]{2,1,0:T(8,128)S(1)} %get-tuple-element.31), channel_id=1, source_target_pairs={{0,8},{1,9},{2,10},{3,11},{4,12},{5,13},{6,14},{7,15},{8,0},{9,1},... | collective-permute-start | bytes 98312 | tf_op jit(solution)/shard_map/ppermute | solution.py:769
  8.7 4.9 %collective-permute-start.4 = (f32[2,8,128]{2,1,0:T(8,128)S(1)}, f32[2,8,128]{2,1,0:T(8,128)S(1)}, u32[]{:S(2)}, u32[]{:S(2)}) collective-permute-start(f32[2,8,128]{2,1,0:T(8,128)S(1)} %get-tuple-element.32), channel_id=1, source_target_pairs={{0,7},{2,9},{4,11},{6,13},{8,15},{10,1},{12,3},{14,5},{7,0},{9,2},... | collective-permute-start | bytes 24584 | tf_op jit(solution)/shard_map/ppermute | solution.py:735
  9.9 4.0 %collective-permute-start.3 = (f32[2,8,128]{2,1,0:T(8,128)S(1)}, f32[2,8,128]{2,1,0:T(8,128)S(1)}, u32[]{:S(2)}, u32[]{:S(2)}) collective-permute-start(f32[2,8,128]{2,1,0:T(8,128)S(1)} %get-tuple-element.22.edges_first), channel_id=1, source_target_pairs={{0,9},{2,11},{4,13},{6,15},{8,1},{10,3},{12,5},{14,7},{9,0},{11,2}... | collective-permute-start | bytes 24584 | tf_op jit(solution)/shard_map/ppermute | solution.py:735
  18.7 10.0 %collective-permute-start.5 = (f32[4,17,8,128]{3,2,1,0:T(8,128)S(1)}, f32[4,17,8,128]{3,2,1,0:T(8,128)S(1)}, u32[]{:S(2)}, u32[]{:S(2)}) collective-permute-start(f32[4,17,8,128]{3,2,1,0:T(8,128)S(1)} %get-tuple-element.37), channel_id=1, source_target_pairs={{0,15},{2,1},{4,3},{6,5},{8,7},{10,9},{12,11},{14,13},{15,0},{1,2}... | collective-permute-start | bytes 835592 | tf_op jit(solution)/shard_map/ppermute | solution.py:735
  21.5 7.2 %collective-permute-start.6 = (f32[4,17,8,128]{3,2,1,0:T(8,128)S(1)}, f32[4,17,8,128]{3,2,1,0:T(8,128)S(1)}, u32[]{:S(2)}, u32[]{:S(2)}) collective-permute-start(f32[4,17,8,128]{3,2,1,0:T(8,128)S(1)} %get-tuple-element.38), channel_id=1, source_target_pairs={{0,1},{2,3},{4,5},{6,7},{8,9},{10,11},{12,13},{14,15},{1,0},{3,2},... | collective-permute-start | bytes 835592 | tf_op jit(solution)/shard_map/ppermute | solution.py:735

commit v11 on v10

--- a/solution.py
+++ b/solution.py
@@ -182,56 +182,46 @@
         to_mate[i, t], to_other[i, t] = chosen(odd, left[i], right[i])
 
 
-def wide_packs(source, diag, partial, diag2, swapped):
+def placed(rows):
     sub = row_ids(8)
+    packed = roll_rows(rows[0][0], -rows[0][1])
+    for i, (x, at) in enumerate(rows):
+        if i:
+            packed = jnp.where(sub == i, roll_rows(x, i - at), packed)
+    return packed
+
+
+def sides(swapped):
     even, odd = reds(swapped)
+    return (even, even ^ 1, odd, odd ^ 1), (odd, odd ^ 1, even, even ^ 1)
+
+
+def state_packs(source, diag, last, first_black, residual, partial, diag2, swapped):
     rows = source[0].shape[0]
     packs = []
-    for here, far, near, row, step in (
-        (slice(rows - 8, rows), even, odd, 4, -1),
-        (slice(0, 8), odd, even, 3, 1),
+    for (a, ab, b, bb), here, near, far, ends in zip(
+        sides(swapped),
+        (slice(rows - 8, rows), slice(0, 8)),
+        (7, 0),
+        (6, 1),
+        ((4, 5, 6), (3, 2, 1)),
     ):
-        gs = [x[here] for x in source]
-        gd = [x[here] for x in diag]
-        part = partial[here]
-        at = sub == row
-        for q in (far, near):
-            gs[q] = jnp.where(at, gs[q] / gd[q], gs[q])
-        gd[far] = jnp.where(at, part / diag2[here], gd[far])
-        gs[far ^ 1] = jnp.where(at, roll_rows(part, step), gs[far ^ 1])
-        gd[far ^ 1] = jnp.where(at, roll_rows(part, 2 * step), gd[far ^ 1])
-        shift = 4 if row == 4 else 0
-        packs.append(
-            [
-                jnp.where(sub < 4, roll_rows(g[q], shift), roll_rows(g[q + 1], 4 - shift))
-                for g in (gs, gd)
-                for q in (0, 2)
-            ]
-        )
+        s, d, v = ([x[here] for x in group] for group in (source, diag, last))
+        part, d2 = partial[here], diag2[here]
+        pack0 = [(x, near) for x in s + d]
+        pack1 = [
+            (first_black[ab][here], near),
+            (s[bb] + v[a], far),
+            (d[bb], far),
+            (first_black[bb][here], far),
+            (v[b], far),
+            (s[b] - d[b] * v[b] + v[ab], far),
+            (residual[a][here] - v[bb], far),
+            (part / d2, ends[0]),
+        ]
+        pack2 = [(part, ends[1]), (part, ends[2]), (d2, ends[1]), (d2, ends[2])]
+        packs.append((placed(pack0), placed(pack1), placed(pack2)))
     return packs
-
-
-def wide_unpacked(left, right, swapped):
-    sub = row_ids(8)
-    even, odd = reds(swapped)
-    groups = []
-    for k in (0, 2):
-        group = []
-        for l, r in zip(left[k : k + 2], right[k : k + 2]):
-            group.append(jnp.where(sub < 4, r, roll_rows(l, 4)))
-            group.append(jnp.where(sub < 4, roll_rows(r, 4), l))
-        groups.append(group)
-    source, diag = groups
-    partial = jnp.zeros_like(sub, F32)
-    for far, near, row, step in ((even, odd, 4, 1), (odd, even, 3, -1)):
-        at = sub == row
-        for i, part in enumerate((diag[far], source[far ^ 1], diag[far ^ 1])):
-            partial = jnp.where(sub == row + i * step, roll_rows(part, i * step), partial)
-        source[far ^ 1] = jnp.where(at, 0.0, source[far ^ 1])
-        diag[far ^ 1] = jnp.where(at, 4.0, diag[far ^ 1])
-        for q in (far, near):
-            diag[q] = jnp.where(at, 1.0, diag[q])
-    return source, diag, partial
 
 
 def fill_halo(t, from_mate, from_other, odd, swapped, hs, hd, hi):
@@ -459,7 +449,7 @@
         v[q][tiles] = value
 
 
-def smooth(v, load_s, load_i, tiles, unroll):
+def smooth(v, load_s, load_i, tiles, unroll, after_sweep=None):
     zeros = jnp.zeros(v[0].shape[1:], F32)
 
     def first(t, _):
@@ -473,9 +463,10 @@
         v[q][tiles - 1] = zeros
         v[q][tiles] = load_s(q, tiles) * load_i(q, tiles)
         v[3 * (q - 1)][tiles] = zeros
-    half_sweep(v, load_s, load_i, tiles, False, unroll)
-    half_sweep(v, load_s, load_i, tiles, True, unroll)
-    half_sweep(v, load_s, load_i, tiles, False, unroll)
+    for sweep, red in enumerate((False, True, False)):
+        half_sweep(v, load_s, load_i, tiles, red, unroll)
+        if after_sweep is not None:
+            after_sweep(sweep)
 
 
 def residuals(v, load_s, load_d, tiles, c0, c1, keep, unroll, valid=None):
@@ -495,7 +486,8 @@
         r = [load_s(q, t) - (load_d(q, t) * x[q] - beside[q]) for q in range(4)]
         keep(t, r)
         if valid is not None:
-            r = [jnp.where(valid, x, 0.0) for x in r]
+            virtual = isinstance(t, int) and t == tiles
+            r = [jnp.where(valid(q, virtual), r[q], 0.0) for q in range(4)]
         c0[t] = (col_prev(r[2]) + col_next(r[0])) + 3.0 * (r[0] + r[2])
         c1[t] = (col_prev(r[3]) + col_next(r[1])) + 3.0 * (r[1] + r[3])
         return here1, here3, next0, next2
@@ -528,7 +520,7 @@
     from_other, from_mate, polar_ref, corner_near, corner_far,
     r_ref, s1_ref, d1_virtual, d2_virtual, to_mate, to_other,
     v0, v1, v2, v3, c0, c1, hs, hd, hi, ps, pd, pi, n1, temp,
-    w0, w1, w2, w3, e0, e1, pi1,
+    w0, w1, w2, w3, e0, e1, pi1, black_even, black_odd, red_even, red_odd,
 ):
     v = [v0, v1, v2, v3]
     tiles, rows = s_ref.shape[1], s_ref.shape[2]
@@ -594,18 +586,56 @@
     rows1 = rows // 2
     row = row_ids(rows1)
     load_s, load_d = own(s1_ref, s1_ref.at[:, tiles1]), own(d1_ref, d1_virtual)
-    smooth(w, load_s, own(i1_ref, pi1), tiles1, 16)
-    valid = (row >= 2) & (row < rows1 - 2)
-    residuals(w, load_s, load_d, tiles1, e0, e1, lambda t, r: None, 16, valid)
+
+    def after_sweep(sweep):
+        if sweep == 0:
+            for t in range(tiles1 + 1):
+                even, odd_red = reds(t == tiles1)
+                black_even[t] = w[even ^ 1][t]
+                black_odd[t] = w[odd_red ^ 1][t]
+
+    smooth(w, load_s, own(i1_ref, pi1), tiles1, 16, after_sweep)
+
+    def valid(q, virtual):
+        even, odd_red = reds(virtual)
+        first = 1 if q == odd_red ^ 1 else 2
+        last = rows1 - 2 if q == even ^ 1 else rows1 - 3
+        return (row >= first) & (row <= last)
+
+    def keep_red(t, r):
+        even, odd_red = reds(isinstance(t, int) and t == tiles1)
+        red_even[t] = r[even]
+        red_odd[t] = r[odd_red]
+
+    residuals(w, load_s, load_d, tiles1, e0, e1, keep_red, 16, valid)
+    shared = {}
 
     def edges(t, partial):
-        virtual = isinstance(t, int) and t == tiles1
-        source = [s1_ref[q, t] for q in range(4)]
-        diag = [load_d(q, t) for q in range(4)]
-        diag2 = d2_virtual[...] if virtual else d2_ref[t]
-        right, left = wide_packs(source, diag, partial, diag2, virtual)
-        for i in range(4):
-            to_mate[i, t], to_other[i, t] = chosen(odd, left[i], right[i])
+        virtual = t == tiles1
+        even, odd_red = reds(virtual)
+        packs = state_packs(
+            [s1_ref[q, t] for q in range(4)],
+            [load_d(q, t) for q in range(4)],
+            [w[q][t] for q in range(4)],
+            {even ^ 1: black_even[t], odd_red ^ 1: black_odd[t]},
+            {even: red_even[t], odd_red: red_odd[t]},
+            partial,
+            d2_virtual[...] if virtual else d2_ref[t],
+            virtual,
+        )
+        right, left = packs
+        count = tiles1 + 1
+        for i in (0, 1):
+            to_mate[i * count + t], to_other[i * count + t] = chosen(odd, left[i], right[i])
+        pair = chosen(odd, left[2], right[2])
+        if t % 2 == 0:
+            shared[0] = pair
+        if t % 2 == 1 or virtual:
+            if t % 2 == 1:
+                pair = [
+                    jnp.where(sub < 4, x, roll_rows(y, 4)) for x, y in zip(shared[0], pair)
+                ]
+            to_mate[2 * count + t // 2], to_other[2 * count + t // 2] = pair
 
     restrict(e0, e1, tiles1, rows1, edges, 16)
 
@@ -640,23 +670,59 @@
 def coarse_kernel(
     s_ref, d_ref, i_ref, d_virtual, d2_ref, d2_virtual, from_other, from_mate,
     solution_ref, residual_ref,
-    v0, v1, v2, v3, c0, c1, hs, hd, hi, pi, part, s, d, inv, va, vb,
+    v0, v1, v2, v3, c0, c1, hs, hd, hi, pi, part, fixes, s, d, inv, va, vb,
 ):
     v = [v0, v1, v2, v3]
     tiles, own = d_ref.shape[1], d_ref.shape[2]
     rows = own + 8
+    count = tiles + 1
     sub = row_ids(8)
     odd_band = is_odd()
-    for t in range(tiles + 1):
-        pairs = [chosen(odd_band, from_mate[i, t], from_other[i, t]) for i in range(4)]
-        left, right = zip(*pairs)
-        source, diag, part[t] = wide_unpacked(left, right, t == tiles)
+    for t in range(count):
+        places = t, count + t, 2 * count + t // 2
+        packs = [chosen(odd_band, from_mate[i], from_other[i]) for i in places]
+        source = [jnp.zeros((8, LANES), F32)] * 4
+        diag = [jnp.full((8, LANES), 4.0, F32)] * 4
+        inverse = [jnp.zeros((8, LANES), F32)] * 4
+        fixed = [jnp.zeros((8, LANES), F32)] * 4
+        more = jnp.zeros((8, LANES), F32)
+        total = jnp.ones((8, LANES), F32)
+        third = 4 * (t % 2)
+        for side, (a, ab, b, bb) in enumerate(sides(t == tiles)):
+            near, far, step = (7, 6, -1) if side == 0 else (0, 1, 1)
+            pack0, pack1, pack2 = (pair[side] for pair in packs)
+
+            def put(group, q, at, pack, row):
+                group[q] = jnp.where(sub == at, roll_rows(pack, at - row), group[q])
+
+            for q in range(4):
+                put(source, q, near, pack0, q)
+                put(diag, q, near, pack0, 4 + q)
+            put(source, bb, far, pack1, 1)
+            put(diag, bb, far, pack1, 2)
+            put(source, b, far, pack1, 5)
+            diag[b] = jnp.where(sub == far, 0.0, diag[b])
+            put(source, a, far, pack1, 6)
+            put(fixed, ab, near, pack1, 0)
+            put(fixed, bb, far, pack1, 3)
+            put(fixed, b, far, pack1, 4)
+            for at, pack, row in (
+                (far + 2 * step, pack1, 7), (far + step, pack2, third), (far, pack2, third + 1)
+            ):
+                more = jnp.where(sub == at, roll_rows(pack, at - row), more)
+            for at, row in ((far + step, third + 2), (far, third + 3)):
+                total = jnp.where(sub == at, roll_rows(pack2, at - row), total)
+            for q in range(4):
+                known = (sub == near) | (sub == far) if q == bb else sub == near
+                inverse[q] = jnp.where(known, 1.0 / diag[q], inverse[q])
         for q in range(4):
             hs[q, t] = source[q]
             hd[q, t] = diag[q]
-            hi[q, t] = 1.0 / diag[q]
-        total = (diag[0] + diag[1]) + (diag[2] + diag[3]) - 12.0
-        total = jnp.where((sub == 3) | (sub == 4), 1.0, total)
+            hi[q, t] = inverse[q]
+            fixes[q, t] = fixed[q]
+        part[t] = more
+        near_total = (diag[0] + diag[1]) + (diag[2] + diag[3]) - 12.0
+        total = jnp.where((sub == 0) | (sub == 7), near_total, total)
         here = d2_virtual[...] if t == tiles else d2_ref[t]
         d[t] = jnp.concatenate([here, total], 0)
     for q in range(4):
@@ -665,9 +731,28 @@
     def load_s(q, t):
         return jnp.concatenate([s_ref[q, t], hs[q, t]], 0)
 
-    smooth(v, load_s, loader(i_ref, hi, pi, tiles), tiles, 16)
+    def after_sweep(sweep):
+        if sweep == 2:
+            return
+        for t in range(count):
+            (a, ab, b, bb), (_, _, other_b, other_bb) = sides(t == tiles)
+            todo = {}
+            if sweep == 0:
+                todo = {ab: (sub == 7) | (sub == 1), bb: (sub == 6) | (sub == 0)}
+            else:
+                todo = {b: sub == 6, other_b: sub == 1}
+            for q, mask in todo.items():
+                v[q][t, own:] = jnp.where(mask, fixes[q, t], v[q][t, own:])
+
+    smooth(v, load_s, loader(i_ref, hi, pi, tiles), tiles, 16, after_sweep)
     lane, row = lane_ids(rows), row_ids(rows)
-    valid = (row < own + 2) | (row >= own + 6)
+
+    def valid(q, virtual):
+        even, odd_red = reds(virtual)
+        last = own if q == odd_red ^ 1 else own + 1
+        first = rows - 1 if q == even ^ 1 else rows - 2
+        return (row <= last) | (row >= first)
+
     load_d = loader(d_ref, hd, d_virtual, tiles)
     residuals(v, load_s, load_d, tiles, c0, c1, lambda t, r: None, 16, valid)
 
@@ -785,7 +870,7 @@
     def halo_scratch(tiles):
         return [(4, tiles + 1, 8, LANES)] * 3
 
-    pack1 = (4, tiles1 + 1, 8, LANES)
+    pack1 = (2 * (tiles1 + 1) + tiles1 // 2 + 1, 8, LANES)
     r, s1, d1_virtual, d2_virtual, to_mate, to_other = call(
         fine_kernel,
         [quarters, (4, tiles1 + 1, rows1, LANES), (4, rows1, LANES), (rows1, LANES), pack1, pack1],
@@ -794,7 +879,8 @@
         + [(4, rows, LANES)] * 3
         + [(tiles + 1, rows, LANES), (BATCH, 2, rows, LANES)]
         + level_scratch(tiles1, rows1)
-        + [(4, rows1, LANES)],
+        + [(4, rows1, LANES)]
+        + [(tiles1 + 1, rows1, LANES)] * 4,
         s, d, inverse, d1, i1, d2, from_other, from_mate, polar, corner_near, corner_far,
     )
     from_mate, from_other = swapped_edges(to_mate, to_other)
@@ -808,7 +894,7 @@
         [(columns // 4, height // 4)] * 2,
         level_scratch(tiles1, rows1 + 8)
         + halo_scratch(tiles1)
-        + [(4, rows1, LANES), (tiles1 + 1, 8, LANES)]
+        + [(4, rows1, LANES), (tiles1 + 1, 8, LANES), (4, tiles1 + 1, 8, LANES)]
         + [wide] * 5,
         s1, d1, i1, d1_virtual, d2, d2_virtual, from_other, from_mate,
     )

time: 31.2 us -> 29.7 us (0.952)
  the two profiles are of different devices: /device:TPU:1 before, /device:TPU:0 now
where the time goes in v11:
time: 29.7 us; the launch traced here: 29.5 us
  Pallas kernels  13.5 us (45%)
  starting transfers between devices  13 us (44%)
  waiting for transfers between devices  2.36 us (8%)
  between operations  0.73 us (2%)
    pallas_call x5, Pallas kernels, call(): pl.pallas_call(kernel, out_shape=[jax.ShapeDtypeStruct(shape, F32) for sh...  13.5 us
    ppermute x6, starting transfers between devices, swapped_with(): return lax.ppermute(x, 'lon', pairs + [(b, a) for a, b in pairs])  12.7 us
    ppermute x6, waiting for transfers between devices, swapped_with(): return lax.ppermute(x, 'lon', pairs + [(b, a) for a, b in pairs])  2.35 us
  transfers between devices with their start and end apart: 7, of which 1 were waited for; matrix products, arithmetic and copies ran while one was open for 0% of the time, Pallas kernels for 12%

profile of v11, /device:TPU:0, one launch (start us, length us, event | category | flops | bytes accessed | tf_op | source)
XLA Modules:
  0.0 29.5 jit_solution(543489633075869318)
XLA Ops:
  0.6 0.0 copy-start.2
  0.6 0.0 copy-start.1
  0.7 0.0 copy-start
  0.7 2.5 %shard_map.58 = (f32[2,32,8,128]{3,2,1,0:T(8,128)S(1)}, f32[2,32,8,128]{3,2,1,0:T(8,128)S(1)}, f32[2,32,128]{2,1,0:T(8,128)S(1)}, f32[2,8,128]{2,1,0:T(8,128)S(1)}, f32[2,8,128]{2,1,0:T(8,128)S(1)}) custom-call(f32[64,8192]{1,0:T(8,128)} %right_ref.3, bf16[64,8192]{1,0:T(8,128)(2,1)} %weight_ref.3, s32[2,256]{1,0:T(2,128)} %flag_ref.3), custom_call_target="tpu_custom_call" | custom-call | tf_op jit(solution)/shard_map/pallas_call | solution.py:807
  3.2 5.5 %collective-permute-start = (f32[2,32,8,128]{3,2,1,0:T(8,128)S(1)}, f32[2,32,8,128]{3,2,1,0:T(8,128)S(1)}, u32[]{:S(2)}, u32[]{:S(2)}) collective-permute-start(f32[2,32,8,128]{3,2,1,0:T(8,128)S(1)} %get-tuple-element.29), channel_id=1, source_target_pairs={{0,15},{2,1},{4,3},{6,5},{8,7},{10,9},{12,11},{14,13},{15,0},{1,2}... | collective-permute-start | bytes 786440 | tf_op jit(solution)/shard_map/ppermute | solution.py:820
  8.6 0.0 collective-permute-start.1
  8.7 0.2 collective-permute-start.2
  8.9 0.8 %collective-permute-start.4 = (f32[2,8,128]{2,1,0:T(8,128)S(1)}, f32[2,8,128]{2,1,0:T(8,128)S(1)}, u32[]{:S(2)}, u32[]{:S(2)}) collective-permute-start(f32[2,8,128]{2,1,0:T(8,128)S(1)} %get-tuple-element.32), channel_id=1, source_target_pairs={{0,7},{2,9},{4,11},{6,13},{8,15},{10,1},{12,3},{14,5},{7,0},{9,2},... | collective-permute-start | bytes 24584 | tf_op jit(solution)/shard_map/ppermute | solution.py:820
  9.7 2.8 %collective-permute-start.3 = (f32[2,8,128]{2,1,0:T(8,128)S(1)}, f32[2,8,128]{2,1,0:T(8,128)S(1)}, u32[]{:S(2)}, u32[]{:S(2)}) collective-permute-start(f32[2,8,128]{2,1,0:T(8,128)S(1)} %get-tuple-element.22.edges_first), channel_id=1, source_target_pairs={{0,9},{2,11},{4,13},{6,15},{8,1},{10,3},{12,5},{14,7},{9,0},{11,2}... | collective-permute-start | bytes 24584 | tf_op jit(solution)/shard_map/ppermute | solution.py:820
  12.5 0.0 copy-done.2
  12.5 0.0 copy-done.1
  12.5 0.0 copy-done
  12.5 1.8 %shard_map.59 = (f32[4,32,32,128]{3,2,1,0:T(8,128)S(1)}, f32[4,32,32,128]{3,2,1,0:T(8,128)S(1)}, f32[4,32,32,128]{3,2,1,0:T(8,128)S(1)}, f32[4,16,16,128]{3,2,1,...) custom-call(f32[64,8192]{1,0:T(8,128)S(1)} %copy-done, bf16[64,8192]{1,0:T(8,128)(2,1)S(1)} %copy-done.1, ...), custom_call_target="tpu_custom_call" | custom-call | tf_op jit(solution)/shard_map/pallas_call | solution.py:807
  14.3 0.0 collective-permute-done.4.corner_far
  14.3 0.0 collective-permute-done.3.corner_near
  14.3 0.0 collective-permute-done.2.polar_ref
  14.4 0.0 collective-permute-done.from_other
  14.4 0.0 collective-permute-done.1.from_mate
  14.4 4.9 %shard_map.60 = (f32[4,32,32,128]{3,2,1,0:T(8,128)S(1)}, f32[4,17,16,128]{3,2,1,0:T(8,128)S(1)}, f32[4,16,128]{2,1,0:T(8,128)S(1)}, f32[16,128]{1,0:T(8,128)S(1)...) custom-call(f32[4,32,32,128]{3,2,1,0:T(8,128)S(1)} %get-tuple-element.23.s_ref, ...), custom_call_target="tpu_custom_call" | custom-call | tf_op jit(solution)/shard_map/pallas_call | solution.py:807
  19.3 3.6 %collective-permute-start.5 = (f32[43,8,128]{2,1,0:T(8,128)S(1)}, f32[43,8,128]{2,1,0:T(8,128)S(1)}, u32[]{:S(2)}, u32[]{:S(2)}) collective-permute-start(f32[43,8,128]{2,1,0:T(8,128)S(1)} %get-tuple-element.37), channel_id=1, source_target_pairs={{0,15},{2,1},{4,3},{6,5},{8,7},{10,9},{12,11},{14,13},{15,0},{1,2}... | collective-permute-start | bytes 528392 | tf_op jit(solution)/shard_map/ppermute | solution.py:820
  22.9 0.0 collective-permute-start.6
  22.9 1.8 %shard_map.61 = f32[64,8192]{1,0:T(8,128)} custom-call(f32[4,32,32,128]{3,2,1,0:T(8,128)S(1)} %get-tuple-element.33.r_ref), custom_call_target="tpu_custom_call" | custom-call | tf_op jit(solution)/shard_map/pallas_call | solution.py:807
  24.7 2.3 %collective-permute-done.5.from_other = f32[43,8,128]{2,1,0:T(8,128)S(1)} collective-permute-done((f32[43,8,128]{2,1,0:T(8,128)S(1)}, f32[43,8,128]{2,1,0:T(8,128)S(1)}, u32[]{:S(2)}, u32[]{:S(2)}) %collective-permute-start.5) | collective-permute-done | bytes 176160 | tf_op jit(solution)/shard_map/ppermute | solution.py:820
  27.1 0.0 collective-permute-done.6.from_mate
  27.1 2.5 %shard_map.62 = (f32[16,2048]{1,0:T(8,128)}, f32[16,2048]{1,0:T(8,128)}) custom-call(f32[4,17,16,128]{3,2,1,0:T(8,128)S(1)} %get-tuple-element.34.s_ref, f32[4,16,16,128]{3,2,1,0:T(8,128)S(1)} %get-tuple-element.26.d1_ref.d_ref, f32[4,16,16,128]{3,2,1,0:T(8,128)S(1)} %get-tuple-element.27.i1_ref.i_ref, f32[4,16,128]{2,1,0:T(8,128)S(1)} %get-tuple-element.35.d_virtual, ...), custom_call_target="tpu_custom_call" | custom-call | tf_op jit(solution)/shard_map/pallas_call | solution.py:807
Async XLA Ops:
  0.6 11.9 %copy-start.2 = (s32[2,256]{1,0:T(2,128)S(1)}, s32[2,256]{1,0:T(2,128)}, u32[]{:S(2)}) copy-start(s32[2,256]{1,0:T(2,128)} %flag_ref.3) | copy-start | bytes 6148
  0.6 11.9 %copy-start.1 = (bf16[64,8192]{1,0:T(8,128)(2,1)S(1)}, bf16[64,8192]{1,0:T(8,128)(2,1)}, u32[]{:S(2)}) copy-start(bf16[64,8192]{1,0:T(8,128)(2,1)} %weight_ref.3) | copy-start | bytes 3145732
  0.7 11.9 %copy-start = (f32[64,8192]{1,0:T(8,128)S(1)}, f32[64,8192]{1,0:T(8,128)}, u32[]{:S(2)}) copy-start(f32[64,8192]{1,0:T(8,128)} %right_ref.3) | copy-start | bytes 6291460
  3.2 11.2 %collective-permute-start = (f32[2,32,8,128]{3,2,1,0:T(8,128)S(1)}, f32[2,32,8,128]{3,2,1,0:T(8,128)S(1)}, u32[]{:S(2)}, u32[]{:S(2)}) collective-permute-start(f32[2,32,8,128]{3,2,1,0:T(8,128)S(1)} %get-tuple-element.29), channel_id=1, source_target_pairs={{0,15},{2,1},{4,3},{6,5},{8,7},{10,9},{12,11},{14,13},{15,0},{1,2}... | collective-permute-start | bytes 786440 | tf_op jit(solution)/shard_map/ppermute | solution.py:820
  8.6 5.7 %collective-permute-start.1 = (f32[2,32,8,128]{3,2,1,0:T(8,128)S(1)}, f32[2,32,8,128]{3,2,1,0:T(8,128)S(1)}, u32[]{:S(2)}, u32[]{:S(2)}) collective-permute-start(f32[2,32,8,128]{3,2,1,0:T(8,128)S(1)} %get-tuple-element.30), channel_id=1, source_target_pairs={{0,1},{2,3},{4,5},{6,7},{8,9},{10,11},{12,13},{14,15},{1,0},{3,2},... | collective-permute-start | bytes 786440 | tf_op jit(solution)/shard_map/ppermute | solution.py:820
  8.7 5.7 %collective-permute-start.2 = (f32[2,32,128]{2,1,0:T(8,128)S(1)}, f32[2,32,128]{2,1,0:T(8,128)S(1)}, u32[]{:S(2)}, u32[]{:S(2)}) collective-permute-start(f32[2,32,128]{2,1,0:T(8,128)S(1)} %get-tuple-element.31), channel_id=1, source_target_pairs={{0,8},{1,9},{2,10},{3,11},{4,12},{5,13},{6,14},{7,15},{8,0},{9,1},... | collective-permute-start | bytes 98312 | tf_op jit(solution)/shard_map/ppermute | solution.py:854
  8.9 5.4 %collective-permute-start.4 = (f32[2,8,128]{2,1,0:T(8,128)S(1)}, f32[2,8,128]{2,1,0:T(8,128)S(1)}, u32[]{:S(2)}, u32[]{:S(2)}) collective-permute-start(f32[2,8,128]{2,1,0:T(8,128)S(1)} %get-tuple-element.32), channel_id=1, source_target_pairs={{0,7},{2,9},{4,11},{6,13},{8,15},{10,1},{12,3},{14,5},{7,0},{9,2},... | collective-permute-start | bytes 24584 | tf_op jit(solution)/shard_map/ppermute | solution.py:820
  9.7 4.6 %collective-permute-start.3 = (f32[2,8,128]{2,1,0:T(8,128)S(1)}, f32[2,8,128]{2,1,0:T(8,128)S(1)}, u32[]{:S(2)}, u32[]{:S(2)}) collective-permute-start(f32[2,8,128]{2,1,0:T(8,128)S(1)} %get-tuple-element.22.edges_first), channel_id=1, source_target_pairs={{0,9},{2,11},{4,13},{6,15},{8,1},{10,3},{12,5},{14,7},{9,0},{11,2}... | collective-permute-start | bytes 24584 | tf_op jit(solution)/shard_map/ppermute | solution.py:820
  19.3 7.7 %collective-permute-start.5 = (f32[43,8,128]{2,1,0:T(8,128)S(1)}, f32[43,8,128]{2,1,0:T(8,128)S(1)}, u32[]{:S(2)}, u32[]{:S(2)}) collective-permute-start(f32[43,8,128]{2,1,0:T(8,128)S(1)} %get-tuple-element.37), channel_id=1, source_target_pairs={{0,15},{2,1},{4,3},{6,5},{8,7},{10,9},{12,11},{14,13},{15,0},{1,2}... | collective-permute-start | bytes 528392 | tf_op jit(solution)/shard_map/ppermute | solution.py:820
  22.9 4.1 %collective-permute-start.6 = (f32[43,8,128]{2,1,0:T(8,128)S(1)}, f32[43,8,128]{2,1,0:T(8,128)S(1)}, u32[]{:S(2)}, u32[]{:S(2)}) collective-permute-start(f32[43,8,128]{2,1,0:T(8,128)S(1)} %get-tuple-element.38), channel_id=1, source_target_pairs={{0,1},{2,3},{4,5},{6,7},{8,9},{10,11},{12,13},{14,15},{1,0},{3,2},... | collective-permute-start | bytes 528392 | tf_op jit(solution)/shard_map/ppermute | solution.py:820

commit v12 on v11

--- a/solution.py
+++ b/solution.py
@@ -69,6 +69,11 @@
 
 def col_next(x):
     return pltpu.roll(x, x.shape[0] - 1, 0)
+
+
+def inverse_of(x):
+    y = pl.reciprocal(x, approx=True)
+    return y * (2.0 - x * y)
 
 
 def selector(shape, rule):
@@ -132,8 +137,8 @@
     ):
         gs = [x[here] for x in source]
         gd = [x[here] for x in diag]
-        near = gs[first] / gd[first]
-        far = roll_rows(gs[second] / gd[second], step)
+        near = gs[first] * inverse_of(gd[first])
+        far = roll_rows(gs[second] * inverse_of(gd[second]), step)
         gs[first] = jnp.where(sub == row, near, gs[first])
         gd[first] = jnp.where(sub == row, far, gd[first])
         offset = 2 if row == 6 else 0
@@ -217,7 +222,7 @@
             (v[b], far),
             (s[b] - d[b] * v[b] + v[ab], far),
             (residual[a][here] - v[bb], far),
-            (part / d2, ends[0]),
+            (part * inverse_of(d2), ends[0]),
         ]
         pack2 = [(part, ends[1]), (part, ends[2]), (d2, ends[1]), (d2, ends[2])]
         packs.append((placed(pack0), placed(pack1), placed(pack2)))
@@ -231,7 +236,7 @@
     for q in range(4):
         hs[q, t] = source[q]
         hd[q, t] = diag[q]
-        hi[q, t] = 1.0 / diag[q]
+        hi[q, t] = inverse_of(diag[q])
 
 
 def loader(own, halo, virtual, tiles):
@@ -391,12 +396,12 @@
             for q in range(4):
                 diag = 4.0 + screen[q]
                 d_ref[q, c] = diag
-                i_ref[q, c] = 1.0 / diag
+                i_ref[q, c] = inverse_of(diag)
 
     def use(c, screen):
         for q in range(4):
             d1_ref[q, c] = 4.0 + screen[q]
-            i1_ref[q, c] = 1.0 / (4.0 + screen[q])
+            i1_ref[q, c] = inverse_of(4.0 + screen[q])
         d2_ref[c] = 4.0 + ((screen[0] + screen[1]) + (screen[2] + screen[3]))
 
     split_tiles(lambda t: e_ref[t], tiles // 2, rows, matrix, temp_s, use)
@@ -518,7 +523,7 @@
 def fine_kernel(
     s_ref, d_ref, i_ref, d1_ref, i1_ref, d2_ref,
     from_other, from_mate, polar_ref, corner_near, corner_far,
-    r_ref, s1_ref, d1_virtual, d2_virtual, to_mate, to_other,
+    r_ref, s1_ref, d1_virtual, d2_virtual, s2_ref, to_mate, to_other,
     v0, v1, v2, v3, c0, c1, hs, hd, hi, ps, pd, pi, n1, temp,
     w0, w1, w2, w3, e0, e1, pi1, black_even, black_odd, red_even, red_odd,
 ):
@@ -542,12 +547,12 @@
         total = total + own_d
         ps[q] = own_s
         pd[q] = own_d
-        pi[q] = 1.0 / own_d
+        pi[q] = inverse_of(own_d)
         source = jnp.where(sub >= 5, left_s, jnp.where(sub <= 2, right_s, 0.0))
         diag = jnp.where(sub >= 5, left_d, jnp.where(sub <= 2, right_d, 4.0))
         hs[q, tiles] = source
         hd[q, tiles] = diag
-        hi[q, tiles] = 1.0 / diag
+        hi[q, tiles] = inverse_of(diag)
 
     load_s = loader(s_ref, hs, ps, tiles)
     smooth(v, load_s, loader(i_ref, hi, pi, tiles), tiles, 32)
@@ -576,7 +581,7 @@
     for q in range(4):
         s1_ref[q, tiles1] = source[q]
         d1_virtual[q] = 4.0 + screen[q]
-        pi1[q] = 1.0 / (4.0 + screen[q])
+        pi1[q] = inverse_of(4.0 + screen[q])
     d2_virtual[...] = 4.0 + ((screen[0] + screen[1]) + (screen[2] + screen[3]))
 
     def own(main, virtual):
@@ -613,6 +618,7 @@
     def edges(t, partial):
         virtual = t == tiles1
         even, odd_red = reds(virtual)
+        s2_ref[t] = partial
         packs = state_packs(
             [s1_ref[q, t] for q in range(4)],
             [load_d(q, t) for q in range(4)],
@@ -668,9 +674,9 @@
 
 
 def coarse_kernel(
-    s_ref, d_ref, i_ref, d_virtual, d2_ref, d2_virtual, from_other, from_mate,
+    s_ref, d_ref, i_ref, d_virtual, d2_ref, d2_virtual, s2_ref, from_other, from_mate,
     solution_ref, residual_ref,
-    v0, v1, v2, v3, c0, c1, hs, hd, hi, pi, part, fixes, s, d, inv, va, vb,
+    v0, v1, v2, v3, c0, c1, hs, hd, hi, part, fixes, s, d, inv, va, vb,
 ):
     v = [v0, v1, v2, v3]
     tiles, own = d_ref.shape[1], d_ref.shape[2]
@@ -678,6 +684,9 @@
     count = tiles + 1
     sub = row_ids(8)
     odd_band = is_odd()
+    def rim(x):
+        return jnp.where(sub < 4, x[:8], x[own - 8 :])
+
     for t in range(count):
         places = t, count + t, 2 * count + t // 2
         packs = [chosen(odd_band, from_mate[i], from_other[i]) for i in places]
@@ -714,23 +723,19 @@
                 total = jnp.where(sub == at, roll_rows(pack2, at - row), total)
             for q in range(4):
                 known = (sub == near) | (sub == far) if q == bb else sub == near
-                inverse[q] = jnp.where(known, 1.0 / diag[q], inverse[q])
+                inverse[q] = jnp.where(known, inverse_of(diag[q]), inverse[q])
         for q in range(4):
-            hs[q, t] = source[q]
-            hd[q, t] = diag[q]
-            hi[q, t] = inverse[q]
+            own_d = rim(d_virtual[q] if t == tiles else d_ref[q, t])
+            own_i = inverse_of(own_d) if t == tiles else rim(i_ref[q, t])
+            hs[q, t] = jnp.concatenate([source[q], rim(s_ref[q, t])], 0)
+            hd[q, t] = jnp.concatenate([diag[q], own_d], 0)
+            hi[q, t] = jnp.concatenate([inverse[q], own_i], 0)
             fixes[q, t] = fixed[q]
         part[t] = more
         near_total = (diag[0] + diag[1]) + (diag[2] + diag[3]) - 12.0
         total = jnp.where((sub == 0) | (sub == 7), near_total, total)
         here = d2_virtual[...] if t == tiles else d2_ref[t]
         d[t] = jnp.concatenate([here, total], 0)
-    for q in range(4):
-        pi[q] = 1.0 / d_virtual[q]
-
-    def load_s(q, t):
-        return jnp.concatenate([s_ref[q, t], hs[q, t]], 0)
-
     def after_sweep(sweep):
         if sweep == 2:
             return
@@ -742,32 +747,45 @@
             else:
                 todo = {b: sub == 6, other_b: sub == 1}
             for q, mask in todo.items():
-                v[q][t, own:] = jnp.where(mask, fixes[q, t], v[q][t, own:])
-
-    smooth(v, load_s, loader(i_ref, hi, pi, tiles), tiles, 16, after_sweep)
-    lane, row = lane_ids(rows), row_ids(rows)
+                v[q][t, :8] = jnp.where(mask, fixes[q, t], v[q][t, :8])
+
+    def of(ref):
+        return lambda q, t: ref[q, t]
+
+    smooth(v, of(hs), of(hi), tiles, 16, after_sweep)
+    row = row_ids(16)
 
     def valid(q, virtual):
         even, odd_red = reds(virtual)
-        last = own if q == odd_red ^ 1 else own + 1
-        first = rows - 1 if q == even ^ 1 else rows - 2
-        return (row <= last) | (row >= first)
-
-    load_d = loader(d_ref, hd, d_virtual, tiles)
-    residuals(v, load_s, load_d, tiles, c0, c1, lambda t, r: None, 16, valid)
-
+        after_band = 0 if q == odd_red ^ 1 else 1
+        before_band = 7 if q == even ^ 1 else 6
+        first = 8 if q == odd_red ^ 1 else 9
+        last = 15 if q == even ^ 1 else 14
+        return (row <= after_band) | ((row >= before_band) & (row <= first)) | (row >= last)
+
+    residuals(v, of(hs), of(hd), tiles, c0, c1, lambda t, r: None, 16, valid)
+
+    lane, row = lane_ids(rows), row_ids(rows)
     even = (lane + row) % 2 == 0
     odd = jnp.logical_not(even)
 
     def start(t, value):
-        source = jnp.concatenate([value[:own], value[own:] + part[t]], 0)
-        inverse = 1.0 / d[t]
+        ends = value[8:]
+        source = jnp.concatenate(
+            [
+                s2_ref[t, :8] + jnp.where(sub < 4, ends, 0.0),
+                s2_ref[t, own - 8 :] + jnp.where(sub >= 4, ends, 0.0),
+                value[:8] + part[t],
+            ],
+            0,
+        )
+        inverse = inverse_of(d[t])
         s[t] = source
         inv[t] = inverse
         virtual = isinstance(t, int) and t == tiles
         va[t] = jnp.where(odd if virtual else even, source * inverse, 0.0)
 
-    restrict(c0, c1, tiles, rows, start, 16)
+    restrict(c0, c1, tiles, 16, start, 16)
 
     def scan(v, use):
         up, down = roll_up(v[tiles]), roll_down(v[0])
@@ -871,9 +889,10 @@
         return [(4, tiles + 1, 8, LANES)] * 3
 
     pack1 = (2 * (tiles1 + 1) + tiles1 // 2 + 1, 8, LANES)
-    r, s1, d1_virtual, d2_virtual, to_mate, to_other = call(
+    r, s1, d1_virtual, d2_virtual, s2_own, to_mate, to_other = call(
         fine_kernel,
-        [quarters, (4, tiles1 + 1, rows1, LANES), (4, rows1, LANES), (rows1, LANES), pack1, pack1],
+        [quarters, (4, tiles1 + 1, rows1, LANES), (4, rows1, LANES), (rows1, LANES)]
+        + [(tiles1 + 1, rows1, LANES), pack1, pack1],
         level_scratch(tiles, rows + 8)
         + halo_scratch(tiles)
         + [(4, rows, LANES)] * 3
@@ -892,11 +911,11 @@
     solution_2, residual_2 = call(
         coarse_kernel,
         [(columns // 4, height // 4)] * 2,
-        level_scratch(tiles1, rows1 + 8)
-        + halo_scratch(tiles1)
-        + [(4, rows1, LANES), (tiles1 + 1, 8, LANES), (4, tiles1 + 1, 8, LANES)]
+        level_scratch(tiles1, 16)
+        + [(4, tiles1 + 1, 16, LANES)] * 3
+        + [(tiles1 + 1, 8, LANES), (4, tiles1 + 1, 8, LANES)]
         + [wide] * 5,
-        s1, d1, i1, d1_virtual, d2, d2_virtual, from_other, from_mate,
+        s1, d1, i1, d1_virtual, d2, d2_virtual, s2_own, from_other, from_mate,
     )
     return fine_residual, solution_2, residual_2
 

time: 29.7 us -> 29.7 us (level)
  no operation moved by 1% of the time
where the time goes in v12:
time: 29.7 us; the launch traced here: 29.5 us
  Pallas kernels  13.4 us (45%)
  starting transfers between devices  12.9 us (43%)
  waiting for transfers between devices  2.38 us (8%)
  between operations  0.73 us (2%)
    pallas_call x5, Pallas kernels, call(): pl.pallas_call(kernel, out_shape=[jax.ShapeDtypeStruct(shape, F32) for sh...  13.4 us
    ppermute x6, starting transfers between devices, swapped_with(): return lax.ppermute(x, 'lon', pairs + [(b, a) for a, b in pairs])  12.7 us
    ppermute x6, waiting for transfers between devices, swapped_with(): return lax.ppermute(x, 'lon', pairs + [(b, a) for a, b in pairs])  2.37 us
  transfers between devices with their start and end apart: 7, of which 1 were waited for; matrix products, arithmetic and copies ran while one was open for 0% of the time, Pallas kernels for 12%

profile of v12, /device:TPU:0, one launch (start us, length us, event | category | flops | bytes accessed | tf_op | source)
XLA Modules:
  0.0 29.5 jit_solution(11301888334678920421)
XLA Ops:
  0.6 0.0 copy-start.2
  0.6 0.0 copy-start.1
  0.7 0.0 copy-start
  0.7 2.5 %shard_map.58 = (f32[2,32,8,128]{3,2,1,0:T(8,128)S(1)}, f32[2,32,8,128]{3,2,1,0:T(8,128)S(1)}, f32[2,32,128]{2,1,0:T(8,128)S(1)}, f32[2,8,128]{2,1,0:T(8,128)S(1)}, f32[2,8,128]{2,1,0:T(8,128)S(1)}) custom-call(f32[64,8192]{1,0:T(8,128)} %right_ref.3, bf16[64,8192]{1,0:T(8,128)(2,1)} %weight_ref.3, s32[2,256]{1,0:T(2,128)} %flag_ref.3), custom_call_target="tpu_custom_call" | custom-call | tf_op jit(solution)/shard_map/pallas_call | solution.py:825
  3.2 5.5 %collective-permute-start = (f32[2,32,8,128]{3,2,1,0:T(8,128)S(1)}, f32[2,32,8,128]{3,2,1,0:T(8,128)S(1)}, u32[]{:S(2)}, u32[]{:S(2)}) collective-permute-start(f32[2,32,8,128]{3,2,1,0:T(8,128)S(1)} %get-tuple-element.30), channel_id=1, source_target_pairs={{0,15},{2,1},{4,3},{6,5},{8,7},{10,9},{12,11},{14,13},{15,0},{1,2}... | collective-permute-start | bytes 786440 | tf_op jit(solution)/shard_map/ppermute | solution.py:838
  8.7 0.0 collective-permute-start.1
  8.7 0.2 collective-permute-start.2
  8.9 0.8 %collective-permute-start.4 = (f32[2,8,128]{2,1,0:T(8,128)S(1)}, f32[2,8,128]{2,1,0:T(8,128)S(1)}, u32[]{:S(2)}, u32[]{:S(2)}) collective-permute-start(f32[2,8,128]{2,1,0:T(8,128)S(1)} %get-tuple-element.33), channel_id=1, source_target_pairs={{0,7},{2,9},{4,11},{6,13},{8,15},{10,1},{12,3},{14,5},{7,0},{9,2},... | collective-permute-start | bytes 24584 | tf_op jit(solution)/shard_map/ppermute | solution.py:838
  9.7 2.8 %collective-permute-start.3 = (f32[2,8,128]{2,1,0:T(8,128)S(1)}, f32[2,8,128]{2,1,0:T(8,128)S(1)}, u32[]{:S(2)}, u32[]{:S(2)}) collective-permute-start(f32[2,8,128]{2,1,0:T(8,128)S(1)} %get-tuple-element.23.edges_first), channel_id=1, source_target_pairs={{0,9},{2,11},{4,13},{6,15},{8,1},{10,3},{12,5},{14,7},{9,0},{11,2}... | collective-permute-start | bytes 24584 | tf_op jit(solution)/shard_map/ppermute | solution.py:838
  12.5 0.0 copy-done.2
  12.5 0.0 copy-done.1
  12.5 0.0 copy-done
  12.5 1.8 %shard_map.59 = (f32[4,32,32,128]{3,2,1,0:T(8,128)S(1)}, f32[4,32,32,128]{3,2,1,0:T(8,128)S(1)}, f32[4,32,32,128]{3,2,1,0:T(8,128)S(1)}, f32[4,16,16,128]{3,2,1,...) custom-call(f32[64,8192]{1,0:T(8,128)S(1)} %copy-done, bf16[64,8192]{1,0:T(8,128)(2,1)S(1)} %copy-done.1, ...), custom_call_target="tpu_custom_call" | custom-call | tf_op jit(solution)/shard_map/pallas_call | solution.py:825
  14.4 0.0 collective-permute-done.4.corner_far
  14.4 0.0 collective-permute-done.3.corner_near
  14.4 0.0 collective-permute-done.2.polar_ref
  14.4 0.0 collective-permute-done.from_other
  14.4 0.0 collective-permute-done.1.from_mate
  14.4 5.1 %shard_map.60 = (f32[4,32,32,128]{3,2,1,0:T(8,128)S(1)}, f32[4,17,16,128]{3,2,1,0:T(8,128)S(1)}, f32[4,16,128]{2,1,0:T(8,128)S(1)}, f32[16,128]{1,0:T(8,128)S(1)...) custom-call(f32[4,32,32,128]{3,2,1,0:T(8,128)S(1)} %get-tuple-element.24.s_ref, ...), custom_call_target="tpu_custom_call" | custom-call | tf_op jit(solution)/shard_map/pallas_call | solution.py:825
  19.5 3.6 %collective-permute-start.5 = (f32[43,8,128]{2,1,0:T(8,128)S(1)}, f32[43,8,128]{2,1,0:T(8,128)S(1)}, u32[]{:S(2)}, u32[]{:S(2)}) collective-permute-start(f32[43,8,128]{2,1,0:T(8,128)S(1)} %get-tuple-element.39), channel_id=1, source_target_pairs={{0,15},{2,1},{4,3},{6,5},{8,7},{10,9},{12,11},{14,13},{15,0},{1,2}... | collective-permute-start | bytes 528392 | tf_op jit(solution)/shard_map/ppermute | solution.py:838
  23.1 0.0 collective-permute-start.6
  23.1 1.8 %shard_map.61 = f32[64,8192]{1,0:T(8,128)} custom-call(f32[4,32,32,128]{3,2,1,0:T(8,128)S(1)} %get-tuple-element.34.r_ref), custom_call_target="tpu_custom_call" | custom-call | tf_op jit(solution)/shard_map/pallas_call | solution.py:825
  24.9 2.4 %collective-permute-done.5.from_other = f32[43,8,128]{2,1,0:T(8,128)S(1)} collective-permute-done((f32[43,8,128]{2,1,0:T(8,128)S(1)}, f32[43,8,128]{2,1,0:T(8,128)S(1)}, u32[]{:S(2)}, u32[]{:S(2)}) %collective-permute-start.5) | collective-permute-done | bytes 176160 | tf_op jit(solution)/shard_map/ppermute | solution.py:838
  27.2 0.0 collective-permute-done.6.from_mate
  27.2 2.3 %shard_map.62 = (f32[16,2048]{1,0:T(8,128)}, f32[16,2048]{1,0:T(8,128)}) custom-call(f32[4,17,16,128]{3,2,1,0:T(8,128)S(1)} %get-tuple-element.35.s_ref, f32[4,16,16,128]{3,2,1,0:T(8,128)S(1)} %get-tuple-element.27.d1_ref.d_ref, f32[4,16,16,128]{3,2,1,0:T(8,128)S(1)} %get-tuple-element.28.i1_ref.i_ref, f32[4,16,128]{2,1,0:T(8,128)S(1)} %get-tuple-element.36.d_virtual, ...), custom_call_target="tpu_custom_call" | custom-call | tf_op jit(solution)/shard_map/pallas_call | solution.py:825
Async XLA Ops:
  0.6 11.9 %copy-start.2 = (s32[2,256]{1,0:T(2,128)S(1)}, s32[2,256]{1,0:T(2,128)}, u32[]{:S(2)}) copy-start(s32[2,256]{1,0:T(2,128)} %flag_ref.3) | copy-start | bytes 6148
  0.6 11.9 %copy-start.1 = (bf16[64,8192]{1,0:T(8,128)(2,1)S(1)}, bf16[64,8192]{1,0:T(8,128)(2,1)}, u32[]{:S(2)}) copy-start(bf16[64,8192]{1,0:T(8,128)(2,1)} %weight_ref.3) | copy-start | bytes 3145732
  0.7 11.9 %copy-start = (f32[64,8192]{1,0:T(8,128)S(1)}, f32[64,8192]{1,0:T(8,128)}, u32[]{:S(2)}) copy-start(f32[64,8192]{1,0:T(8,128)} %right_ref.3) | copy-start | bytes 6291460
  3.2 11.2 %collective-permute-start = (f32[2,32,8,128]{3,2,1,0:T(8,128)S(1)}, f32[2,32,8,128]{3,2,1,0:T(8,128)S(1)}, u32[]{:S(2)}, u32[]{:S(2)}) collective-permute-start(f32[2,32,8,128]{3,2,1,0:T(8,128)S(1)} %get-tuple-element.30), channel_id=1, source_target_pairs={{0,15},{2,1},{4,3},{6,5},{8,7},{10,9},{12,11},{14,13},{15,0},{1,2}... | collective-permute-start | bytes 786440 | tf_op jit(solution)/shard_map/ppermute | solution.py:838
  8.7 5.7 %collective-permute-start.1 = (f32[2,32,8,128]{3,2,1,0:T(8,128)S(1)}, f32[2,32,8,128]{3,2,1,0:T(8,128)S(1)}, u32[]{:S(2)}, u32[]{:S(2)}) collective-permute-start(f32[2,32,8,128]{3,2,1,0:T(8,128)S(1)} %get-tuple-element.31), channel_id=1, source_target_pairs={{0,1},{2,3},{4,5},{6,7},{8,9},{10,11},{12,13},{14,15},{1,0},{3,2},... | collective-permute-start | bytes 786440 | tf_op jit(solution)/shard_map/ppermute | solution.py:838
  8.7 5.7 %collective-permute-start.2 = (f32[2,32,128]{2,1,0:T(8,128)S(1)}, f32[2,32,128]{2,1,0:T(8,128)S(1)}, u32[]{:S(2)}, u32[]{:S(2)}) collective-permute-start(f32[2,32,128]{2,1,0:T(8,128)S(1)} %get-tuple-element.32), channel_id=1, source_target_pairs={{0,8},{1,9},{2,10},{3,11},{4,12},{5,13},{6,14},{7,15},{8,0},{9,1},... | collective-permute-start | bytes 98312 | tf_op jit(solution)/shard_map/ppermute | solution.py:872
  8.9 5.5 %collective-permute-start.4 = (f32[2,8,128]{2,1,0:T(8,128)S(1)}, f32[2,8,128]{2,1,0:T(8,128)S(1)}, u32[]{:S(2)}, u32[]{:S(2)}) collective-permute-start(f32[2,8,128]{2,1,0:T(8,128)S(1)} %get-tuple-element.33), channel_id=1, source_target_pairs={{0,7},{2,9},{4,11},{6,13},{8,15},{10,1},{12,3},{14,5},{7,0},{9,2},... | collective-permute-start | bytes 24584 | tf_op jit(solution)/shard_map/ppermute | solution.py:838
  9.7 4.7 %collective-permute-start.3 = (f32[2,8,128]{2,1,0:T(8,128)S(1)}, f32[2,8,128]{2,1,0:T(8,128)S(1)}, u32[]{:S(2)}, u32[]{:S(2)}) collective-permute-start(f32[2,8,128]{2,1,0:T(8,128)S(1)} %get-tuple-element.23.edges_first), channel_id=1, source_target_pairs={{0,9},{2,11},{4,13},{6,15},{8,1},{10,3},{12,5},{14,7},{9,0},{11,2}... | collective-permute-start | bytes 24584 | tf_op jit(solution)/shard_map/ppermute | solution.py:838
  19.5 7.7 %collective-permute-start.5 = (f32[43,8,128]{2,1,0:T(8,128)S(1)}, f32[43,8,128]{2,1,0:T(8,128)S(1)}, u32[]{:S(2)}, u32[]{:S(2)}) collective-permute-start(f32[43,8,128]{2,1,0:T(8,128)S(1)} %get-tuple-element.39), channel_id=1, source_target_pairs={{0,15},{2,1},{4,3},{6,5},{8,7},{10,9},{12,11},{14,13},{15,0},{1,2}... | collective-permute-start | bytes 528392 | tf_op jit(solution)/shard_map/ppermute | solution.py:838
  23.1 4.1 %collective-permute-start.6 = (f32[43,8,128]{2,1,0:T(8,128)S(1)}, f32[43,8,128]{2,1,0:T(8,128)S(1)}, u32[]{:S(2)}, u32[]{:S(2)}) collective-permute-start(f32[43,8,128]{2,1,0:T(8,128)S(1)} %get-tuple-element.40), channel_id=1, source_target_pairs={{0,1},{2,3},{4,5},{6,7},{8,9},{10,11},{12,13},{14,15},{1,0},{3,2},... | collective-permute-start | bytes 528392 | tf_op jit(solution)/shard_map/ppermute | solution.py:838

commit v13 on v12

--- a/solution.py
+++ b/solution.py
@@ -72,8 +72,7 @@
 
 
 def inverse_of(x):
-    y = pl.reciprocal(x, approx=True)
-    return y * (2.0 - x * y)
+    return 1.0 / x
 
 
 def selector(shape, rule):
@@ -293,20 +292,17 @@
 
 def edge_kernel(
     right_ref, weight_ref, flag_ref,
-    to_mate, to_other, polar_ref, corner_near, corner_far,
-    edge_s, edge_w, end_s, end_w, flags, temp_s, temp_w, temp_p, temp_q, scale_ref, sems,
+    to_mate, to_other, corner_ref,
+    edge_s, edge_w, flags, temp_s, temp_w, scale_ref, sems,
 ):
     columns, height = right_ref.shape
-    rows, tiles = columns // 2, height // 256
+    tiles = height // 256
     pairs = [(flag_ref, flags)]
     for i, (src, dst, size) in enumerate(
         ((right_ref, edge_s, 8), (weight_ref, edge_w, 16))
     ):
         pairs.append((src.at[pl.ds(0, size)], dst.at[pl.ds(0, size)]))
         pairs.append((src.at[pl.ds(columns - size, size)], dst.at[pl.ds(size, size)]))
-    for src, dst in ((right_ref, end_s), (weight_ref, end_w)):
-        for end, start in enumerate((0, height - 256)):
-            pairs.append((src.at[:, pl.ds(start, 256)], dst.at[end]))
     copies = [
         pltpu.make_async_copy(src, dst, sems.at[i]) for i, (src, dst) in enumerate(pairs)
     ]
@@ -317,7 +313,7 @@
     flag_cols = flag_ref.shape[0]
     copies[0].wait()
     scale_ref[...] = seam_scales(flags[...], range(tiles))
-    for copy in copies[1:5]:
+    for copy in copies[1:]:
         copy.wait()
     sub = row_ids(8)
     lanes = [slice(c * 256, (c + 1) * 256) for c in range(tiles)]
@@ -330,47 +326,58 @@
     weight = jnp.concatenate([weight[:, :8], weight[:, 24:]], 1).reshape(tiles * 16, 256)
     source = quarters_of(source, temp_s)
     weight = quarters_of(weight, temp_w)
+    found = []
     for c in range(tiles):
         here = slice(c * 8, (c + 1) * 8)
         scales = scale_ref[c]
         scale = jnp.where(sub < 4, scales[:1], scales[flag_cols - 1 : flag_cols])
-        diag = [4.0 + w[here] * scale for w in weight]
-        store_edges(
-            c, edge_packs([x[here] for x in source], diag, False), odd, to_mate, to_other
-        )
-
-    for copy in copies[5:]:
-        copy.wait()
+        pair = [x[here] for x in source], [4.0 + w[here] * scale for w in weight]
+        store_edges(c, edge_packs(*pair, False), odd, to_mate, to_other)
+        if c in (0, tiles - 1):
+            found.append(pair)
+    both = mirrored_ends(*found)
+    for pc in (0, 1):
+        corner = both[8 * pc : 8 * (pc + 1)]
+        corner_ref[pc] = corner
+
+
+def mirrored_ends(first, last):
     mirror = selector((LANES, LANES), lambda a, b: a + b == LANES - 1)
-    lane = lane_ids(rows)
+    lane = lane_ids(first[0][0].shape[0])
+    ends = [
+        [jnp.where(lane >= 64, last[i][q ^ 1], first[i][q ^ 1]) for i in (0, 1)]
+        for q in range(4)
+    ]
+    return moved(jnp.concatenate(polar_packs(ends), 0), mirror)
+
+
+def polar_kernel(right_ref, weight_ref, flag_ref, edges_first, polar_ref, temp_s, temp_w):
+    columns, height = right_ref.shape
+    rows, tiles = columns // 2, height // 256
+    scales = seam_scales(flag_ref[...], (0, tiles - 1))
+    lanes = slice(0, 256), slice(height - 256, height)
     source, weight = moved(
-        jnp.concatenate([end_s[0], end_s[1]], 0),
-        matrix,
-        jnp.concatenate([end_w[0], end_w[1]], 0),
+        jnp.concatenate([right_ref[:, w] for w in lanes], 0),
+        splitter(),
+        jnp.concatenate([weight_ref[:, w] for w in lanes], 0),
     )
     found = []
-    for end, c in enumerate((0, tiles - 1)):
+    for end in (0, 1):
         here = slice(end * columns, (end + 1) * columns)
-        scale = seam_rows(scale_ref[c], flag_cols, rows)
+        scale = seam_rows(scales[end], flag_ref.shape[0], rows)
         found.append(
             (
-                quarters_of(source[here], temp_p.at[end]),
-                [4.0 + w * scale for w in quarters_of(weight[here], temp_q.at[end])],
+                quarters_of(source[here], temp_s.at[end]),
+                [4.0 + w * scale for w in quarters_of(weight[here], temp_w.at[end])],
             )
         )
-    ends = [
-        [jnp.where(lane >= 64, found[1][i][q ^ 1], found[0][i][q ^ 1]) for i in (0, 1)]
-        for q in range(4)
-    ]
-    both = moved(jnp.concatenate(polar_packs(ends), 0), mirror)
+    both = mirrored_ends(*found)
     for pc in (0, 1):
-        pack = both[pc * rows : (pc + 1) * rows]
-        polar_ref[pc] = pack
-        corner_near[pc], corner_far[pc] = chosen(odd, pack[:8], pack[rows - 8 :])
+        polar_ref[pc] = both[pc * rows : (pc + 1) * rows]
 
 
 def bulk_kernel(
-    right_ref, weight_ref, flag_ref, edges_first,
+    right_ref, weight_ref, flag_ref, polar_first,
     s_ref, d_ref, i_ref, d1_ref, i1_ref, d2_ref,
     temp_s, temp_d, scale_ref, e_ref,
 ):
@@ -418,7 +425,7 @@
             use(start + i, quarters_of(out[i * rows : (i + 1) * rows], temp.at[i, :, :rows]))
 
 
-def half_sweep(v, load_s, load_i, tiles, red, unroll):
+def half_sweep(v, load_s, load_i, tiles, red, unroll, left=None):
     rows = v[0].shape[1]
     lane = lane_ids(rows)
     y, z, qa, qb = (1, 2, 0, 3) if red else (3, 0, 2, 1)
@@ -445,8 +452,14 @@
         z_after = roll_down(v[z][t + 1])
         lat_a = vy + jnp.where(lane == 0, y_before, y_here)
         lat_b = vz + jnp.where(lane == LANES - 1, z_after, z_here)
-        v[qa][t] = (load_s(qa, t) + (lat_a + (vz + col_a(vz)))) * load_i(qa, t)
-        v[qb][t] = (load_s(qb, t) + (lat_b + (vy + col_b(vy)))) * load_i(qb, t)
+        all_a = load_s(qa, t) + (lat_a + (vz + col_a(vz)))
+        all_b = load_s(qb, t) + (lat_b + (vy + col_b(vy)))
+        new_a, new_b = all_a * load_i(qa, t), all_b * load_i(qb, t)
+        v[qa][t], v[qb][t] = new_a, new_b
+        if left is not None:
+            load_d, rest = left
+            rest[qa][t] = all_a - load_d(qa, t) * new_a
+            rest[qb][t] = all_b - load_d(qb, t) * new_b
         return y_here, z_after
 
     loop(tiles, body, (roll_up(v[y][tiles]), roll_down(v[z][0])), unroll)
@@ -454,7 +467,7 @@
         v[q][tiles] = value
 
 
-def smooth(v, load_s, load_i, tiles, unroll, after_sweep=None):
+def smooth(v, load_s, load_i, tiles, unroll, left, after_sweep=None):
     zeros = jnp.zeros(v[0].shape[1:], F32)
 
     def first(t, _):
@@ -469,38 +482,59 @@
         v[q][tiles] = load_s(q, tiles) * load_i(q, tiles)
         v[3 * (q - 1)][tiles] = zeros
     for sweep, red in enumerate((False, True, False)):
-        half_sweep(v, load_s, load_i, tiles, red, unroll)
+        half_sweep(v, load_s, load_i, tiles, red, unroll, left if sweep == 2 else None)
         if after_sweep is not None:
             after_sweep(sweep)
 
 
-def residuals(v, load_s, load_d, tiles, c0, c1, keep, unroll, valid=None):
+def residuals(v, load_s, left, tiles, c0, c1, keep, unroll, valid=None):
     lane = lane_ids(v[0].shape[1])
-
-    def body(t, carry):
-        up1, up3, down0, down2 = carry
-        x = [v[q][t] for q in range(4)]
-        here1, here3 = roll_up(x[1]), roll_up(x[3])
-        next0, next2 = (roll_down(v[q][after(t, tiles)]) for q in (0, 2))
-        beside = [
-            (x[1] + jnp.where(lane == 0, up1, here1)) + (x[2] + col_prev(x[2])),
-            (x[0] + jnp.where(lane == LANES - 1, next0, down0)) + (x[3] + col_prev(x[3])),
-            (x[3] + jnp.where(lane == 0, up3, here3)) + (x[0] + col_next(x[0])),
-            (x[2] + jnp.where(lane == LANES - 1, next2, down2)) + (x[1] + col_next(x[1])),
-        ]
-        r = [load_s(q, t) - (load_d(q, t) * x[q] - beside[q]) for q in range(4)]
+    load_d, rest = left
+
+    def use(t, r):
         keep(t, r)
         if valid is not None:
             virtual = isinstance(t, int) and t == tiles
             r = [jnp.where(valid(q, virtual), r[q], 0.0) for q in range(4)]
         c0[t] = (col_prev(r[2]) + col_next(r[0])) + 3.0 * (r[0] + r[2])
         c1[t] = (col_prev(r[3]) + col_next(r[1])) + 3.0 * (r[1] + r[3])
-        return here1, here3, next0, next2
-
-    start = (
-        roll_up(v[1][tiles]), roll_up(v[3][tiles]), roll_down(v[0][0]), roll_down(v[2][0])
-    )
-    body(tiles, loop(tiles, body, start, unroll))
+
+    def north(q, t):
+        return jnp.where(lane == 0, roll_up(v[q][before(t, tiles)]), roll_up(v[q][t]))
+
+    def south(q, t):
+        return jnp.where(
+            lane == LANES - 1, roll_down(v[q][after(t, tiles)]), roll_down(v[q][t])
+        )
+
+    def full(t):
+        x = [v[q][t] for q in range(4)]
+        beside = [
+            (x[1] + north(1, t)) + (x[2] + col_prev(x[2])),
+            (x[0] + south(0, t)) + (x[3] + col_prev(x[3])),
+            (x[3] + north(3, t)) + (x[0] + col_next(x[0])),
+            (x[2] + south(2, t)) + (x[1] + col_next(x[1])),
+        ]
+        use(t, [load_s(q, t) - (load_d(q, t) * x[q] - beside[q]) for q in range(4)])
+
+    def body(i, carry):
+        t = i + 1
+        up, down = carry
+        x = [v[q][t] for q in range(4)]
+        up_here, down_next = roll_up(x[1]), roll_down(v[2][t + 1])
+        beside0 = (x[1] + jnp.where(lane == 0, up, up_here)) + (x[2] + col_prev(x[2]))
+        beside3 = (x[2] + jnp.where(lane == LANES - 1, down_next, down)) + (
+            x[1] + col_next(x[1])
+        )
+        r0 = load_s(0, t) - (load_d(0, t) * x[0] - beside0)
+        r3 = load_s(3, t) - (load_d(3, t) * x[3] - beside3)
+        use(t, [r0, rest[1][t], rest[2][t], r3])
+        return up_here, down_next
+
+    full(0)
+    loop(tiles - 2, body, (roll_up(v[1][0]), roll_down(v[2][1])), unroll)
+    full(tiles - 1)
+    full(tiles)
 
 
 def restrict(c0, c1, tiles, rows, use, unroll):
@@ -526,6 +560,7 @@
     r_ref, s1_ref, d1_virtual, d2_virtual, s2_ref, to_mate, to_other,
     v0, v1, v2, v3, c0, c1, hs, hd, hi, ps, pd, pi, n1, temp,
     w0, w1, w2, w3, e0, e1, pi1, black_even, black_odd, red_even, red_odd,
+    rest1, rest2, part1, part2,
 ):
     v = [v0, v1, v2, v3]
     tiles, rows = s_ref.shape[1], s_ref.shape[2]
@@ -555,14 +590,15 @@
         hi[q, tiles] = inverse_of(diag)
 
     load_s = loader(s_ref, hs, ps, tiles)
-    smooth(v, load_s, loader(i_ref, hi, pi, tiles), tiles, 32)
+    left = loader(d_ref, hd, pd, tiles), {1: rest1, 2: rest2}
+    smooth(v, load_s, loader(i_ref, hi, pi, tiles), tiles, 32, left)
 
     def keep(t, r):
         if not (isinstance(t, int) and t == tiles):
             for q in range(4):
                 r_ref[q, t] = r[q][:rows]
 
-    residuals(v, load_s, loader(d_ref, hd, pd, tiles), tiles, c0, c1, keep, 16)
+    residuals(v, load_s, left, tiles, c0, c1, keep, 15)
 
     def coarse(t, value):
         n1[t] = value
@@ -599,7 +635,8 @@
                 black_even[t] = w[even ^ 1][t]
                 black_odd[t] = w[odd_red ^ 1][t]
 
-    smooth(w, load_s, own(i1_ref, pi1), tiles1, 16, after_sweep)
+    left = load_d, {1: part1, 2: part2}
+    smooth(w, load_s, own(i1_ref, pi1), tiles1, 16, left, after_sweep)
 
     def valid(q, virtual):
         even, odd_red = reds(virtual)
@@ -612,7 +649,7 @@
         red_even[t] = r[even]
         red_odd[t] = r[odd_red]
 
-    residuals(w, load_s, load_d, tiles1, e0, e1, keep_red, 16, valid)
+    residuals(w, load_s, left, tiles1, e0, e1, keep_red, 16, valid)
     shared = {}
 
     def edges(t, partial):
@@ -676,7 +713,7 @@
 def coarse_kernel(
     s_ref, d_ref, i_ref, d_virtual, d2_ref, d2_virtual, s2_ref, from_other, from_mate,
     solution_ref, residual_ref,
-    v0, v1, v2, v3, c0, c1, hs, hd, hi, part, fixes, s, d, inv, va, vb,
+    v0, v1, v2, v3, c0, c1, hs, hd, hi, part, fixes, rest1, rest2, s, d, inv, va, vb,
 ):
     v = [v0, v1, v2, v3]
     tiles, own = d_ref.shape[1], d_ref.shape[2]
@@ -752,7 +789,8 @@
     def of(ref):
         return lambda q, t: ref[q, t]
 
-    smooth(v, of(hs), of(hi), tiles, 16, after_sweep)
+    left = of(hd), {1: rest1, 2: rest2}
+    smooth(v, of(hs), of(hi), tiles, 16, left, after_sweep)
     row = row_ids(16)
 
     def valid(q, virtual):
@@ -763,7 +801,7 @@
         last = 15 if q == even ^ 1 else 14
         return (row <= after_band) | ((row >= before_band) & (row <= first)) | (row >= last)
 
-    residuals(v, of(hs), of(hd), tiles, c0, c1, lambda t, r: None, 16, valid)
+    residuals(v, of(hs), left, tiles, c0, c1, lambda t, r: None, 16, valid)
 
     lane, row = lane_ids(rows), row_ids(rows)
     even = (lane + row) % 2 == 0
@@ -851,35 +889,34 @@
     temp = (BATCH, 2, columns, LANES)
     quarters = (4, tiles, rows, LANES)
     quarters1 = (4, tiles1, rows1, LANES)
-    pack = (2, tiles, 8, LANES)
-    corner = (2, 8, LANES)
     split = (2, 16 * tiles, LANES)
-    to_mate, to_other, polar, corner_near, corner_far = call(
+    to_mate, to_other, corner = call(
         edge_kernel,
-        [pack, pack, (2, rows, LANES), corner, corner],
+        [(2, tiles, 8, LANES), (2, tiles, 8, LANES), (2, 8, LANES)],
         [(16, height), pltpu.VMEM((32, height), BF16)]
-        + [(2, columns, 256), pltpu.VMEM((2, columns, 256), BF16)]
-        + [pltpu.VMEM(seam_flags.shape, jnp.int32), split, split]
-        + [(2, 2, columns, LANES)] * 2
-        + [(tiles, 8, LANES)],
+        + [pltpu.VMEM(seam_flags.shape, jnp.int32), split, split, (tiles, 8, LANES)],
         *[
             pltpu.with_memory_space_constraint(x, pltpu.HBM)
             for x in (right_side, texel_weight, seam_flags)
         ],
-        sems=(9,), far_in=3,
+        sems=(5,), far_in=3,
     )
     from_mate, from_other = swapped_edges(to_mate, to_other)
+    corner_far = swapped_with(corner, half_turn - 1)
+    corner_near = swapped_with(corner, half_turn + 1)
+    ends = (2, 2, columns, LANES)
+    (polar_own,) = call(
+        polar_kernel, [(2, rows, LANES)], [ends, ends],
+        right_side, texel_weight, seam_flags, corner,
+    )
     polar = lax.ppermute(
-        polar, "lon", [(i, (i + half_turn) % (2 * half_turn)) for i in range(2 * half_turn)]
-    )
-    corner_near_own = corner_near
-    corner_far = swapped_with(corner_far, half_turn - 1)
-    corner_near = swapped_with(corner_near, half_turn + 1)
+        polar_own, "lon", [(i, (i + half_turn) % (2 * half_turn)) for i in range(2 * half_turn)]
+    )
     s, d, inverse, d1, i1, d2 = call(
         bulk_kernel,
         [quarters] * 3 + [quarters1, quarters1, quarters1[1:]],
         [temp, temp, (tiles, 8, LANES), quarters[1:]],
-        right_side, texel_weight, seam_flags, corner_near_own,
+        right_side, texel_weight, seam_flags, polar_own,
     )
 
     def level_scratch(tiles, rows):
@@ -899,7 +936,9 @@
         + [(tiles + 1, rows, LANES), (BATCH, 2, rows, LANES)]
         + level_scratch(tiles1, rows1)
         + [(4, rows1, LANES)]
-        + [(tiles1 + 1, rows1, LANES)] * 4,
+        + [(tiles1 + 1, rows1, LANES)] * 4
+        + [(tiles, rows + 8, LANES)] * 2
+        + [(tiles1, rows1, LANES)] * 2,
         s, d, inverse, d1, i1, d2, from_other, from_mate, polar, corner_near, corner_far,
     )
     from_mate, from_other = swapped_edges(to_mate, to_other)
@@ -914,6 +953,7 @@
         level_scratch(tiles1, 16)
         + [(4, tiles1 + 1, 16, LANES)] * 3
         + [(tiles1 + 1, 8, LANES), (4, tiles1 + 1, 8, LANES)]
+        + [(tiles1, 16, LANES)] * 2
         + [wide] * 5,
         s1, d1, i1, d1_virtual, d2, d2_virtual, s2_own, from_other, from_mate,
     )

time: 29.7 us -> 29.4 us (0.990)
    pallas_call x5 -> x6, Pallas kernels: 13.4 us -> 13.2 us  [call(): pl.pallas_call(kernel, out_shape=[jax.ShapeDtypeStruct(shape, F32) for sh...]
  transfers between devices with their start and end apart: 7 -> 7, of which waited for: 1 -> 1; matrix products, arithmetic and copies ran while one was open for 0% -> 0% of each run, Pallas kernels for 12% -> 14%
where the time goes in v13:
time: 29.4 us; the launch traced here: 29.2 us
  Pallas kernels  13.2 us (45%)
  starting transfers between devices  13 us (44%)
  waiting for transfers between devices  2.31 us (8%)
  between operations  0.74 us (3%)
    pallas_call x6, Pallas kernels, call(): pl.pallas_call(kernel, out_shape=[jax.ShapeDtypeStruct(shape, F32) for sh...  13.2 us
    ppermute x6, starting transfers between devices, swapped_with(): return lax.ppermute(x, 'lon', pairs + [(b, a) for a, b in pairs])  12.8 us
    ppermute x6, waiting for transfers between devices, swapped_with(): return lax.ppermute(x, 'lon', pairs + [(b, a) for a, b in pairs])  2.31 us
  transfers between devices with their start and end apart: 7, of which 1 were waited for; matrix products, arithmetic and copies ran while one was open for 0% of the time, Pallas kernels for 14%

profile of v13, /device:TPU:0, one launch (start us, length us, event | category | flops | bytes accessed | tf_op | source)
XLA Modules:
  0.0 29.2 jit_solution(1479764751760600699)
XLA Ops:
  0.6 0.0 copy-start.2
  0.6 0.0 copy-start.1
  0.7 0.0 copy-start
  0.7 2.1 %shard_map.58 = (f32[2,32,8,128]{3,2,1,0:T(8,128)S(1)}, f32[2,32,8,128]{3,2,1,0:T(8,128)S(1)}, f32[2,8,128]{2,1,0:T(8,128)S(1)}) custom-call(f32[64,8192]{1,0:T(8,128)} %right_ref.5, bf16[64,8192]{1,0:T(8,128)(2,1)} %weight_ref.5, s32[2,256]{1,0:T(2,128)} %flag_ref.5), custom_call_target="tpu_custom_call" | custom-call | tf_op jit(solution)/shard_map/pallas_call | solution.py:863
  2.8 5.5 %collective-permute-start = (f32[2,32,8,128]{3,2,1,0:T(8,128)S(1)}, f32[2,32,8,128]{3,2,1,0:T(8,128)S(1)}, u32[]{:S(2)}, u32[]{:S(2)}) collective-permute-start(f32[2,32,8,128]{3,2,1,0:T(8,128)S(1)} %get-tuple-element.28), channel_id=1, source_target_pairs={{0,15},{2,1},{4,3},{6,5},{8,7},{10,9},{12,11},{14,13},{15,0},{1,2}... | collective-permute-start | bytes 786440 | tf_op jit(solution)/shard_map/ppermute | solution.py:876
  8.3 0.0 collective-permute-start.1
  8.3 0.0 copy-done.2
  8.3 0.0 copy-done.1
  8.3 0.0 copy-done
  8.3 0.4 %shard_map.59.polar_first = f32[2,32,128]{2,1,0:T(8,128)S(1)} custom-call(f32[64,8192]{1,0:T(8,128)S(1)} %copy-done, bf16[64,8192]{1,0:T(8,128)(2,1)S(1)} %copy-done.1, s32[2,256]{1,0:T(2,128)S(1)} %copy-done.2, f32[2,8,128]{2,1,0:T(8,128)S(1)} %get-tuple-element.21.edges_first), custom_call_target="tpu_custom_call" | custom-call | tf_op jit(solution)/shard_map/pallas_call | solution.py:863
  8.7 0.2 collective-permute-start.2
  8.9 0.8 %collective-permute-start.4 = (f32[2,8,128]{2,1,0:T(8,128)S(1)}, f32[2,8,128]{2,1,0:T(8,128)S(1)}, u32[]{:S(2)}, u32[]{:S(2)}) collective-permute-start(f32[2,8,128]{2,1,0:T(8,128)S(1)} %get-tuple-element.21.edges_first), channel_id=1, source_target_pairs={{0,7},{2,9},{4,11},{6,13},{8,15},{10,1},{12,3},{14,5},{7,0},{9,2},... | collective-permute-start | bytes 24584 | tf_op jit(solution)/shard_map/ppermute | solution.py:876
  9.7 2.8 %collective-permute-start.3 = (f32[2,8,128]{2,1,0:T(8,128)S(1)}, f32[2,8,128]{2,1,0:T(8,128)S(1)}, u32[]{:S(2)}, u32[]{:S(2)}) collective-permute-start(f32[2,8,128]{2,1,0:T(8,128)S(1)} %get-tuple-element.21.edges_first), channel_id=1, source_target_pairs={{0,9},{2,11},{4,13},{6,15},{8,1},{10,3},{12,5},{14,7},{9,0},{11,2}... | collective-permute-start | bytes 24584 | tf_op jit(solution)/shard_map/ppermute | solution.py:876
  12.6 1.8 %shard_map.60 = (f32[4,32,32,128]{3,2,1,0:T(8,128)S(1)}, f32[4,32,32,128]{3,2,1,0:T(8,128)S(1)}, f32[4,32,32,128]{3,2,1,0:T(8,128)S(1)}, f32[4,16,16,128]{3,2,1,...) custom-call(f32[64,8192]{1,0:T(8,128)S(1)} %copy-done, bf16[64,8192]{1,0:T(8,128)(2,1)S(1)} %copy-done.1, ...), custom_call_target="tpu_custom_call" | custom-call | tf_op jit(solution)/shard_map/pallas_call | solution.py:863
  14.4 0.0 collective-permute-done.4.corner_far
  14.4 0.0 collective-permute-done.3.corner_near
  14.4 0.0 collective-permute-done.2.polar_ref
  14.4 0.0 collective-permute-done.from_other
  14.4 0.0 collective-permute-done.1.from_mate
  14.4 4.9 %shard_map.61 = (f32[4,32,32,128]{3,2,1,0:T(8,128)S(1)}, f32[4,17,16,128]{3,2,1,0:T(8,128)S(1)}, f32[4,16,128]{2,1,0:T(8,128)S(1)}, f32[16,128]{1,0:T(8,128)S(1)...) custom-call(f32[4,32,32,128]{3,2,1,0:T(8,128)S(1)} %get-tuple-element.22.s_ref, ...), custom_call_target="tpu_custom_call" | custom-call | tf_op jit(solution)/shard_map/pallas_call | solution.py:863
  19.3 3.7 %collective-permute-start.5 = (f32[43,8,128]{2,1,0:T(8,128)S(1)}, f32[43,8,128]{2,1,0:T(8,128)S(1)}, u32[]{:S(2)}, u32[]{:S(2)}) collective-permute-start(f32[43,8,128]{2,1,0:T(8,128)S(1)} %get-tuple-element.35), channel_id=1, source_target_pairs={{0,15},{2,1},{4,3},{6,5},{8,7},{10,9},{12,11},{14,13},{15,0},{1,2}... | collective-permute-start | bytes 528392 | tf_op jit(solution)/shard_map/ppermute | solution.py:876
  23.0 0.0 collective-permute-start.6
  23.0 1.8 %shard_map.62 = f32[64,8192]{1,0:T(8,128)} custom-call(f32[4,32,32,128]{3,2,1,0:T(8,128)S(1)} %get-tuple-element.30.r_ref), custom_call_target="tpu_custom_call" | custom-call | tf_op jit(solution)/shard_map/pallas_call | solution.py:863
  24.8 2.3 %collective-permute-done.5.from_other = f32[43,8,128]{2,1,0:T(8,128)S(1)} collective-permute-done((f32[43,8,128]{2,1,0:T(8,128)S(1)}, f32[43,8,128]{2,1,0:T(8,128)S(1)}, u32[]{:S(2)}, u32[]{:S(2)}) %collective-permute-start.5) | collective-permute-done | bytes 176160 | tf_op jit(solution)/shard_map/ppermute | solution.py:876
  27.1 0.0 collective-permute-done.6.from_mate
  27.1 2.2 %shard_map.63 = (f32[16,2048]{1,0:T(8,128)}, f32[16,2048]{1,0:T(8,128)}) custom-call(f32[4,17,16,128]{3,2,1,0:T(8,128)S(1)} %get-tuple-element.31.s_ref, f32[4,16,16,128]{3,2,1,0:T(8,128)S(1)} %get-tuple-element.25.d1_ref.d_ref, f32[4,16,16,128]{3,2,1,0:T(8,128)S(1)} %get-tuple-element.26.i1_ref.i_ref, f32[4,16,128]{2,1,0:T(8,128)S(1)} %get-tuple-element.32.d_virtual, ...), custom_call_target="tpu_custom_call" | custom-call | tf_op jit(solution)/shard_map/pallas_call | solution.py:863
Async XLA Ops:
  0.6 7.6 %copy-start.2 = (s32[2,256]{1,0:T(2,128)S(1)}, s32[2,256]{1,0:T(2,128)}, u32[]{:S(2)}) copy-start(s32[2,256]{1,0:T(2,128)} %flag_ref.5) | copy-start | bytes 6148
  0.6 7.6 %copy-start.1 = (bf16[64,8192]{1,0:T(8,128)(2,1)S(1)}, bf16[64,8192]{1,0:T(8,128)(2,1)}, u32[]{:S(2)}) copy-start(bf16[64,8192]{1,0:T(8,128)(2,1)} %weight_ref.5) | copy-start | bytes 3145732
  0.7 7.6 %copy-start = (f32[64,8192]{1,0:T(8,128)S(1)}, f32[64,8192]{1,0:T(8,128)}, u32[]{:S(2)}) copy-start(f32[64,8192]{1,0:T(8,128)} %right_ref.5) | copy-start | bytes 6291460
  2.8 11.7 %collective-permute-start = (f32[2,32,8,128]{3,2,1,0:T(8,128)S(1)}, f32[2,32,8,128]{3,2,1,0:T(8,128)S(1)}, u32[]{:S(2)}, u32[]{:S(2)}) collective-permute-start(f32[2,32,8,128]{3,2,1,0:T(8,128)S(1)} %get-tuple-element.28), channel_id=1, source_target_pairs={{0,15},{2,1},{4,3},{6,5},{8,7},{10,9},{12,11},{14,13},{15,0},{1,2}... | collective-permute-start | bytes 786440 | tf_op jit(solution)/shard_map/ppermute | solution.py:876
  8.3 6.2 %collective-permute-start.1 = (f32[2,32,8,128]{3,2,1,0:T(8,128)S(1)}, f32[2,32,8,128]{3,2,1,0:T(8,128)S(1)}, u32[]{:S(2)}, u32[]{:S(2)}) collective-permute-start(f32[2,32,8,128]{3,2,1,0:T(8,128)S(1)} %get-tuple-element.29), channel_id=1, source_target_pairs={{0,1},{2,3},{4,5},{6,7},{8,9},{10,11},{12,13},{14,15},{1,0},{3,2},... | collective-permute-start | bytes 786440 | tf_op jit(solution)/shard_map/ppermute | solution.py:876
  8.7 5.7 %collective-permute-start.2 = (f32[2,32,128]{2,1,0:T(8,128)S(1)}, f32[2,32,128]{2,1,0:T(8,128)S(1)}, u32[]{:S(2)}, u32[]{:S(2)}) collective-permute-start(f32[2,32,128]{2,1,0:T(8,128)S(1)} %shard_map.59.polar_first), channel_id=1, source_target_pairs={{0,8},{1,9},{2,10},{3,11},{4,12},{5,13},{6,14},{7,15},{8,0},{9,1},... | collective-permute-start | bytes 98312 | tf_op jit(solution)/shard_map/ppermute | solution.py:912
  8.9 5.5 %collective-permute-start.4 = (f32[2,8,128]{2,1,0:T(8,128)S(1)}, f32[2,8,128]{2,1,0:T(8,128)S(1)}, u32[]{:S(2)}, u32[]{:S(2)}) collective-permute-start(f32[2,8,128]{2,1,0:T(8,128)S(1)} %get-tuple-element.21.edges_first), channel_id=1, source_target_pairs={{0,7},{2,9},{4,11},{6,13},{8,15},{10,1},{12,3},{14,5},{7,0},{9,2},... | collective-permute-start | bytes 24584 | tf_op jit(solution)/shard_map/ppermute | solution.py:876
  9.7 4.6 %collective-permute-start.3 = (f32[2,8,128]{2,1,0:T(8,128)S(1)}, f32[2,8,128]{2,1,0:T(8,128)S(1)}, u32[]{:S(2)}, u32[]{:S(2)}) collective-permute-start(f32[2,8,128]{2,1,0:T(8,128)S(1)} %get-tuple-element.21.edges_first), channel_id=1, source_target_pairs={{0,9},{2,11},{4,13},{6,15},{8,1},{10,3},{12,5},{14,7},{9,0},{11,2}... | collective-permute-start | bytes 24584 | tf_op jit(solution)/shard_map/ppermute | solution.py:876
  19.3 7.7 %collective-permute-start.5 = (f32[43,8,128]{2,1,0:T(8,128)S(1)}, f32[43,8,128]{2,1,0:T(8,128)S(1)}, u32[]{:S(2)}, u32[]{:S(2)}) collective-permute-start(f32[43,8,128]{2,1,0:T(8,128)S(1)} %get-tuple-element.35), channel_id=1, source_target_pairs={{0,15},{2,1},{4,3},{6,5},{8,7},{10,9},{12,11},{14,13},{15,0},{1,2}... | collective-permute-start | bytes 528392 | tf_op jit(solution)/shard_map/ppermute | solution.py:876
  23.0 4.1 %collective-permute-start.6 = (f32[43,8,128]{2,1,0:T(8,128)S(1)}, f32[43,8,128]{2,1,0:T(8,128)S(1)}, u32[]{:S(2)}, u32[]{:S(2)}) collective-permute-start(f32[43,8,128]{2,1,0:T(8,128)S(1)} %get-tuple-element.36), channel_id=1, source_target_pairs={{0,1},{2,3},{4,5},{6,7},{8,9},{10,11},{12,13},{14,15},{1,0},{3,2},... | collective-permute-start | bytes 528392 | tf_op jit(solution)/shard_map/ppermute | solution.py:876

commit v14 on v13

--- a/solution.py
+++ b/solution.py
@@ -379,10 +379,10 @@
 def bulk_kernel(
     right_ref, weight_ref, flag_ref, polar_first,
     s_ref, d_ref, i_ref, d1_ref, i1_ref, d2_ref,
-    temp_s, temp_d, scale_ref, e_ref,
+    temp, scale_ref, e_ref, split_temp,
 ):
-    tiles, rows = s_ref.shape[1], s_ref.shape[2]
-    columns = 2 * rows
+    tiles, columns = s_ref.shape[1], s_ref.shape[2]
+    rows = columns // 2
     matrix = splitter()
     scale_ref[...] = seam_scales(flag_ref[...], range(tiles))
     for start in range(0, tiles, BATCH):
@@ -395,15 +395,18 @@
         for i in range(BATCH):
             c = start + i
             here = slice(i * columns, (i + 1) * columns)
-            scale = seam_rows(scale_ref[c], flag_ref.shape[0], rows)
-            for q, value in enumerate(quarters_of(source[here], temp_s.at[i])):
-                s_ref[q, c] = value
-            screen = [w * scale for w in quarters_of(weight[here], temp_d.at[i])]
-            e_ref[c] = (screen[0] + screen[1]) + (screen[2] + screen[3])
-            for q in range(4):
-                diag = 4.0 + screen[q]
-                d_ref[q, c] = diag
-                i_ref[q, c] = inverse_of(diag)
+            scale = seam_rows(scale_ref[c], flag_ref.shape[0], columns)
+            screens = []
+            for pr in (0, 1):
+                half = slice(pr * LANES, (pr + 1) * LANES)
+                screen = weight[here, half] * scale
+                diag = 4.0 + screen
+                s_ref[pr, c] = source[here, half]
+                d_ref[pr, c] = diag
+                i_ref[pr, c] = 1.0 / diag
+                screens.append(screen)
+            temp[i] = screens[0] + screens[1]
+            e_ref[c] = temp[i, pl.ds(0, rows, 2), :] + temp[i, pl.ds(1, rows, 2), :]
 
     def use(c, screen):
         for q in range(4):
@@ -411,7 +414,7 @@
             i1_ref[q, c] = inverse_of(4.0 + screen[q])
         d2_ref[c] = 4.0 + ((screen[0] + screen[1]) + (screen[2] + screen[3]))
 
-    split_tiles(lambda t: e_ref[t], tiles // 2, rows, matrix, temp_s, use)
+    split_tiles(lambda t: e_ref[t], tiles // 2, rows, matrix, split_temp, use)
 
 
 def split_tiles(load, tiles, rows, matrix, temp, use):
@@ -554,16 +557,169 @@
     body(tiles, loop(tiles, body, start, unroll))
 
 
+class Fine:
+    def __init__(self, own, halo, virtual, tiles, columns):
+        self.own, self.halo, self.virtual = own, halo, virtual
+        self.tiles, self.columns = tiles, columns
+
+    def part(self, parity, t, start):
+        return self.own[parity][t, pl.ds(8 + start, self.columns // 2, 2), :]
+
+    def rows(self, q, t):
+        return self.part(q % 2, t, q // 2)
+
+    def whole(self, q, t):
+        if t == self.tiles:
+            return self.virtual[q][...]
+        return jnp.concatenate([self.rows(q, t), self.halo[q][t]], 0)
+
+    def ends(self, q, t):
+        if t == self.tiles:
+            whole = self.virtual[q][...]
+            return whole[: self.columns // 2], whole[self.columns // 2 :]
+        return self.rows(q, t), self.halo[q][t]
+
+    def line(self, parity, t, column):
+        row = self.own[parity][t, 8 + column : 9 + column]
+        return jnp.broadcast_to(row, (8, LANES))
+
+    def put(self, q, t, own, halo):
+        pr, pc = q % 2, q // 2
+        self.own[pr][t, pl.ds(8 + pc, self.columns // 2, 2), :] = own
+        self.halo[q][t] = halo
+        if pc == 1:
+            self.own[pr][t, 7:8] = halo[7:8]
+        else:
+            at = 8 + self.columns
+            self.own[pr][t, at : at + 1] = halo[0:1]
+
+    def beside_columns(self, q, t, halo):
+        sub = row_ids(8)
+        pr, pc = q % 2, q // 2
+        own = self.part(pr, t, pc - 1) + self.part(pr, t, pc + 1)
+        if pc == 0:
+            other = jnp.where(sub == 0, self.line(pr, t, self.columns - 1), col_prev(halo))
+        else:
+            other = jnp.where(sub == 7, self.line(pr, t, 0), col_next(halo))
+        return own, halo + other
+
+
+def fine_sweep(v, load_s, load_i, whole_s, whole_i, red, left):
+    tiles = v.tiles
+    y, z, qa, qb = (1, 2, 0, 3) if red else (3, 0, 2, 1)
+
+    def lane_sum(parts, rolled, edge, lane_at):
+        return [
+            x + jnp.where(lane_ids(x.shape[0]) == lane_at, e, r)
+            for x, r, e in zip(parts, rolled, edge)
+        ]
+
+    def beside_virtual(q):
+        here, cols = v.whole(q ^ 1, tiles), v.whole(q ^ 2, tiles)
+        lane = lane_ids(here.shape[0])
+        if q % 2 == 0:
+            lat = jnp.where(lane == 0, roll_up(v.whole(q ^ 1, tiles - 1)), roll_up(here))
+        else:
+            lat = jnp.where(lane == LANES - 1, roll_down(v.whole(q ^ 1, 0)), roll_down(here))
+        return (here + lat) + (cols + (col_prev if q < 2 else col_next)(cols))
+
+    held = [
+        (q, (whole_s(q, tiles) + beside_virtual(q)) * whole_i(q, tiles)) for q in (y, z)
+    ]
+    y_before = [roll_up(x) for x in v.ends(y, tiles)]
+    z_here = [roll_down(x) for x in v.ends(z, 0)]
+    for t in range(tiles):
+        vy, vz = v.ends(y, t), v.ends(z, t)
+        y_here = [roll_up(x) for x in vy]
+        z_after = [roll_down(x) for x in v.ends(z, t + 1)]
+        lat_a = lane_sum(vy, y_here, y_before, 0)
+        lat_b = lane_sum(vz, z_here, z_after, LANES - 1)
+        new = []
+        for q, lat, halo in ((qa, lat_a, vz[1]), (qb, lat_b, vy[1])):
+            cols = v.beside_columns(q, t, halo)
+            total = [x + (l + c) for x, l, c in zip(load_s(q, t), lat, cols)]
+            value = [x * i for x, i in zip(total, load_i(q, t))]
+            new.append((q, value))
+            if left is not None:
+                load_d, rest = left
+                rest.put(q, t, *[x - d * u for x, d, u in zip(total, load_d(q, t), value)])
+        for q, value in new:
+            v.put(q, t, *value)
+        y_before, z_here = y_here, z_after
+    for q, value in held:
+        v.virtual[q][...] = value
+
+
+def fine_residuals(v, load_s, load_d, whole_s, whole_d, rest, c0, c1):
+    tiles = v.tiles
+    rows = v.columns // 2
+
+    def columns_summed(t):
+        for pr, ref in ((0, c0), (1, c1)):
+            outer = rest.part(pr, t, -1) + rest.part(pr, t, 2)
+            inner = rest.part(pr, t, 0) + rest.part(pr, t, 1)
+            ref[t] = outer + 3.0 * inner
+
+    def full(t):
+        x = [v.whole(q, t) for q in range(4)]
+        lane = lane_ids(x[0].shape[0])
+
+        def north(q):
+            return jnp.where(lane == 0, roll_up(v.whole(q, before(t, tiles))), roll_up(x[q]))
+
+        def south(q):
+            return jnp.where(
+                lane == LANES - 1, roll_down(v.whole(q, after(t, tiles))), roll_down(x[q])
+            )
+
+        beside = [
+            (x[1] + north(1)) + (x[2] + col_prev(x[2])),
+            (x[0] + south(0)) + (x[3] + col_prev(x[3])),
+            (x[3] + north(3)) + (x[0] + col_next(x[0])),
+            (x[2] + south(2)) + (x[1] + col_next(x[1])),
+        ]
+        r = [whole_s(q, t) - (whole_d(q, t) * x[q] - beside[q]) for q in range(4)]
+        if t == tiles:
+            c0[t] = ((col_prev(r[2]) + col_next(r[0])) + 3.0 * (r[0] + r[2]))[:rows]
+            c1[t] = ((col_prev(r[3]) + col_next(r[1])) + 3.0 * (r[1] + r[3]))[:rows]
+        else:
+            for q in range(4):
+                rest.put(q, t, r[q][:rows], r[q][rows:])
+            columns_summed(t)
+
+    full(0)
+    up = [roll_up(x) for x in v.ends(1, 0)]
+    down = [roll_down(x) for x in v.ends(2, 1)]
+    for t in range(1, tiles - 1):
+        x = [v.ends(q, t) for q in range(4)]
+        up_here = [roll_up(part) for part in x[1]]
+        down_next = [roll_down(part) for part in v.ends(2, t + 1)]
+        for q, ns, near, edge, lane_at in (
+            (0, 1, up_here, up, 0), (3, 2, down, down_next, LANES - 1)
+        ):
+            cols = v.beside_columns(q, t, x[q ^ 2][1])
+            r = []
+            for i, (s, d) in enumerate(zip(load_s(q, t), load_d(q, t))):
+                lane = lane_ids(s.shape[0])
+                beside = x[ns][i] + jnp.where(lane == lane_at, edge[i], near[i]) + cols[i]
+                r.append(s - (d * x[q][i] - beside))
+            rest.put(q, t, *r)
+        columns_summed(t)
+        up, down = up_here, down_next
+    full(tiles - 1)
+    full(tiles)
+
+
 def fine_kernel(
     s_ref, d_ref, i_ref, d1_ref, i1_ref, d2_ref,
     from_other, from_mate, polar_ref, corner_near, corner_far,
     r_ref, s1_ref, d1_virtual, d2_virtual, s2_ref, to_mate, to_other,
-    v0, v1, v2, v3, c0, c1, hs, hd, hi, ps, pd, pi, n1, temp,
+    v_ref, hv, pv, hr, c0, c1, hs, hd, hi, ps, pd, pi, n1, temp,
     w0, w1, w2, w3, e0, e1, pi1, black_even, black_odd, red_even, red_odd,
-    rest1, rest2, part1, part2,
+    part1, part2,
 ):
-    v = [v0, v1, v2, v3]
-    tiles, rows = s_ref.shape[1], s_ref.shape[2]
+    tiles, columns = s_ref.shape[1], s_ref.shape[2]
+    rows = columns // 2
     sub = row_ids(8)
     odd = is_odd()
 
@@ -589,21 +745,47 @@
         hd[q, tiles] = diag
         hi[q, tiles] = inverse_of(diag)
 
-    load_s = loader(s_ref, hs, ps, tiles)
-    left = loader(d_ref, hd, pd, tiles), {1: rest1, 2: rest2}
-    smooth(v, load_s, loader(i_ref, hi, pi, tiles), tiles, 32, left)
-
-    def keep(t, r):
-        if not (isinstance(t, int) and t == tiles):
-            for q in range(4):
-                r_ref[q, t] = r[q][:rows]
-
-    residuals(v, load_s, left, tiles, c0, c1, keep, 15)
+    def loaders(ref, halo, virtual):
+        def split(q, t):
+            return ref[q % 2, t, pl.ds(q // 2, rows, 2), :], halo[q, t]
+
+        def whole(q, t):
+            if t == tiles:
+                return jnp.concatenate([virtual[q], halo[q, t]], 0)
+            return jnp.concatenate(split(q, t), 0)
+
+        return split, whole
+
+    load_s, whole_s = loaders(s_ref, hs, ps)
+    load_d, whole_d = loaders(d_ref, hd, pd)
+    load_i, whole_i = loaders(i_ref, hi, pi)
+
+    def held(own_ref, halo_ref):
+        return Fine(
+            [own_ref.at[p] for p in (0, 1)],
+            [halo_ref.at[q] for q in range(4)],
+            [pv.at[q] for q in range(4)],
+            tiles,
+            columns,
+        )
+
+    v, rest = held(v_ref, hv), held(r_ref, hr)
+    for t in range(tiles):
+        for q in (0, 3):
+            v.put(q, t, *[x * i for x, i in zip(load_s(q, t), load_i(q, t))])
+    for q in (1, 2):
+        for t in (0, tiles - 1):
+            v.put(q, t, jnp.zeros((rows, LANES), F32), jnp.zeros((8, LANES), F32))
+        pv[q] = whole_s(q, tiles) * whole_i(q, tiles)
+        pv[3 * (q - 1)] = jnp.zeros((rows + 8, LANES), F32)
+    for red, left in ((False, None), (True, None), (False, (load_d, rest))):
+        fine_sweep(v, load_s, load_i, whole_s, whole_i, red, left)
+    fine_residuals(v, load_s, load_d, whole_s, whole_d, rest, c0, c1)
 
     def coarse(t, value):
         n1[t] = value
 
-    restrict(c0, c1, tiles, rows, coarse, 16)
+    restrict(c0, c1, tiles, rows, coarse, tiles)
 
     def use(c, source):
         for q in range(4):
@@ -683,25 +865,24 @@
     restrict(e0, e1, tiles1, rows1, edges, 16)
 
 
-def merge_kernel(r_ref, out_ref, temp, out_buf, sems):
+def merge_kernel(r_ref, out_ref, out_buf, sems):
     tiles = r_ref.shape[1]
-    rows = r_ref.shape[2]
+    columns = out_ref.shape[0]
     matrix = merger()
     chunk = out_ref.shape[1] // GROUPS
     copies = []
     for group in range(GROUPS):
         for batch in range(tiles // GROUPS // BATCH):
             start = group * (tiles // GROUPS) + batch * BATCH
-            both = []
-            for i in range(BATCH):
-                for pr in (0, 1):
-                    for pc in (0, 1):
-                        temp[i, pr, pl.ds(pc, rows, 2), :] = r_ref[2 * pc + pr, start + i]
-                both.append(jnp.concatenate([temp[i, 0], temp[i, 1]], 1))
+            own = slice(8, 8 + columns)
+            both = [
+                jnp.concatenate([r_ref[0, start + i, own], r_ref[1, start + i, own]], 1)
+                for i in range(BATCH)
+            ]
             out = moved(jnp.concatenate(both, 0), matrix)
             for i in range(BATCH):
                 where = slice((start + i) * 256, (start + i + 1) * 256)
-                out_buf[:, where] = out[2 * rows * i : 2 * rows * (i + 1)]
+                out_buf[:, where] = out[columns * i : columns * (i + 1)]
         part = pl.ds(group * chunk, chunk)
         copy = pltpu.make_async_copy(out_buf.at[:, part], out_ref.at[:, part], sems.at[group])
         copy.start()
@@ -887,7 +1068,8 @@
     tiles, rows = height // 256, columns // 2
     tiles1, rows1 = tiles // 2, rows // 2
     temp = (BATCH, 2, columns, LANES)
-    quarters = (4, tiles, rows, LANES)
+    natural = (2, tiles, columns, LANES)
+    padded = (2, tiles, columns + 16, LANES)
     quarters1 = (4, tiles1, rows1, LANES)
     split = (2, 16 * tiles, LANES)
     to_mate, to_other, corner = call(
@@ -914,8 +1096,8 @@
     )
     s, d, inverse, d1, i1, d2 = call(
         bulk_kernel,
-        [quarters] * 3 + [quarters1, quarters1, quarters1[1:]],
-        [temp, temp, (tiles, 8, LANES), quarters[1:]],
+        [natural] * 3 + [quarters1, quarters1, quarters1[1:]],
+        [(BATCH, columns, LANES), (tiles, 8, LANES), (tiles, rows, LANES), (BATCH, 2, rows, LANES)],
         right_side, texel_weight, seam_flags, polar_own,
     )
 
@@ -928,22 +1110,22 @@
     pack1 = (2 * (tiles1 + 1) + tiles1 // 2 + 1, 8, LANES)
     r, s1, d1_virtual, d2_virtual, s2_own, to_mate, to_other = call(
         fine_kernel,
-        [quarters, (4, tiles1 + 1, rows1, LANES), (4, rows1, LANES), (rows1, LANES)]
+        [padded, (4, tiles1 + 1, rows1, LANES), (4, rows1, LANES), (rows1, LANES)]
         + [(tiles1 + 1, rows1, LANES), pack1, pack1],
-        level_scratch(tiles, rows + 8)
+        [padded, (4, tiles, 8, LANES), (4, rows + 8, LANES), (4, tiles, 8, LANES)]
+        + [(tiles + 1, rows, LANES)] * 2
         + halo_scratch(tiles)
         + [(4, rows, LANES)] * 3
         + [(tiles + 1, rows, LANES), (BATCH, 2, rows, LANES)]
         + level_scratch(tiles1, rows1)
         + [(4, rows1, LANES)]
         + [(tiles1 + 1, rows1, LANES)] * 4
-        + [(tiles, rows + 8, LANES)] * 2
         + [(tiles1, rows1, LANES)] * 2,
         s, d, inverse, d1, i1, d2, from_other, from_mate, polar, corner_near, corner_far,
     )
     from_mate, from_other = swapped_edges(to_mate, to_other)
     (fine_residual,) = call(
-        merge_kernel, [(columns, height)], [temp, (columns, height)], r,
+        merge_kernel, [(columns, height)], [(columns, height)], r,
         sems=(GROUPS,), far_out=1,
     )
     wide = (tiles1 + 1, rows1 + 8, LANES)

time: 29.4 us -> 28.3 us (0.963)
  Pallas kernels: 13.2 us -> 11.8 us
    pallas_call x6, Pallas kernels: 13.2 us -> 11.8 us  [call(): pl.pallas_call(kernel, out_shape=[jax.ShapeDtypeStruct(shape, F32) for sh...]
  transfers between devices with their start and end apart: 7 -> 7, of which waited for: 1 -> 2; matrix products, arithmetic and copies ran while one was open for 0% -> 0% of each run, Pallas kernels for 14% -> 13%
where the time goes in v14:
time: 28.3 us; the launch traced here: 28.2 us
  starting transfers between devices  13.2 us (47%)
  Pallas kernels  11.8 us (42%)
  waiting for transfers between devices  2.46 us (9%)
  between operations  0.72 us (3%)
    ppermute x6, starting transfers between devices, swapped_with(): return lax.ppermute(x, 'lon', pairs + [(b, a) for a, b in pairs])  13 us
    pallas_call x6, Pallas kernels, call(): pl.pallas_call(kernel, out_shape=[jax.ShapeDtypeStruct(shape, F32) for sh...  11.8 us
    ppermute x6, waiting for transfers between devices, swapped_with(): return lax.ppermute(x, 'lon', pairs + [(b, a) for a, b in pairs])  2.46 us
  transfers between devices with their start and end apart: 7, of which 2 were waited for; matrix products, arithmetic and copies ran while one was open for 0% of the time, Pallas kernels for 13%

profile of v14, /device:TPU:0, one launch (start us, length us, event | category | flops | bytes accessed | tf_op | source)
XLA Modules:
  0.0 28.2 jit_solution(8698373361904871370)
XLA Ops:
  0.6 0.0 copy-start.2
  0.6 0.0 copy-start.1
  0.7 0.0 copy-start
  0.7 2.1 %shard_map.58 = (f32[2,32,8,128]{3,2,1,0:T(8,128)S(1)}, f32[2,32,8,128]{3,2,1,0:T(8,128)S(1)}, f32[2,8,128]{2,1,0:T(8,128)S(1)}) custom-call(f32[64,8192]{1,0:T(8,128)} %right_ref.5, bf16[64,8192]{1,0:T(8,128)(2,1)} %weight_ref.5, s32[2,256]{1,0:T(2,128)} %flag_ref.5), custom_call_target="tpu_custom_call" | custom-call | tf_op jit(solution)/shard_map/pallas_call | solution.py:1044
  2.8 5.5 %collective-permute-start = (f32[2,32,8,128]{3,2,1,0:T(8,128)S(1)}, f32[2,32,8,128]{3,2,1,0:T(8,128)S(1)}, u32[]{:S(2)}, u32[]{:S(2)}) collective-permute-start(f32[2,32,8,128]{3,2,1,0:T(8,128)S(1)} %get-tuple-element.28), channel_id=1, source_target_pairs={{0,15},{2,1},{4,3},{6,5},{8,7},{10,9},{12,11},{14,13},{15,0},{1,2}... | collective-permute-start | bytes 786440 | tf_op jit(solution)/shard_map/ppermute | solution.py:1057
  8.3 0.0 collective-permute-start.1
  8.3 0.0 copy-done.2
  8.3 0.0 copy-done.1
  8.3 0.0 copy-done
  8.3 0.4 %shard_map.59.polar_first = f32[2,32,128]{2,1,0:T(8,128)S(1)} custom-call(f32[64,8192]{1,0:T(8,128)S(1)} %copy-done, bf16[64,8192]{1,0:T(8,128)(2,1)S(1)} %copy-done.1, s32[2,256]{1,0:T(2,128)S(1)} %copy-done.2, f32[2,8,128]{2,1,0:T(8,128)S(1)} %get-tuple-element.21.edges_first), custom_call_target="tpu_custom_call" | custom-call | tf_op jit(solution)/shard_map/pallas_call | solution.py:1044
  8.7 0.2 collective-permute-start.2
  8.9 0.8 %collective-permute-start.4 = (f32[2,8,128]{2,1,0:T(8,128)S(1)}, f32[2,8,128]{2,1,0:T(8,128)S(1)}, u32[]{:S(2)}, u32[]{:S(2)}) collective-permute-start(f32[2,8,128]{2,1,0:T(8,128)S(1)} %get-tuple-element.21.edges_first), channel_id=1, source_target_pairs={{0,7},{2,9},{4,11},{6,13},{8,15},{10,1},{12,3},{14,5},{7,0},{9,2},... | collective-permute-start | bytes 24584 | tf_op jit(solution)/shard_map/ppermute | solution.py:1057
  9.7 2.8 %collective-permute-start.3 = (f32[2,8,128]{2,1,0:T(8,128)S(1)}, f32[2,8,128]{2,1,0:T(8,128)S(1)}, u32[]{:S(2)}, u32[]{:S(2)}) collective-permute-start(f32[2,8,128]{2,1,0:T(8,128)S(1)} %get-tuple-element.21.edges_first), channel_id=1, source_target_pairs={{0,9},{2,11},{4,13},{6,15},{8,1},{10,3},{12,5},{14,7},{9,0},{11,2}... | collective-permute-start | bytes 24584 | tf_op jit(solution)/shard_map/ppermute | solution.py:1057
  12.6 1.5 %shard_map.60 = (f32[2,32,64,128]{3,2,1,0:T(8,128)S(1)}, f32[2,32,64,128]{3,2,1,0:T(8,128)S(1)}, f32[2,32,64,128]{3,2,1,0:T(8,128)S(1)}, f32[4,16,16,128]{3,2,1,...) custom-call(f32[64,8192]{1,0:T(8,128)S(1)} %copy-done, bf16[64,8192]{1,0:T(8,128)(2,1)S(1)} %copy-done.1, ...), custom_call_target="tpu_custom_call" | custom-call | tf_op jit(solution)/shard_map/pallas_call | solution.py:1044
  14.1 0.0 collective-permute-done.4.corner_far
  14.1 0.2 collective-permute-done.3.corner_near
  14.3 0.0 collective-permute-done.2.polar_ref
  14.3 0.0 collective-permute-done.from_other
  14.3 0.0 collective-permute-done.1.from_mate
  14.3 4.0 %shard_map.61 = (f32[2,32,80,128]{3,2,1,0:T(8,128)S(1)}, f32[4,17,16,128]{3,2,1,0:T(8,128)S(1)}, f32[4,16,128]{2,1,0:T(8,128)S(1)}, f32[16,128]{1,0:T(8,128)S(1)...) custom-call(f32[2,32,64,128]{3,2,1,0:T(8,128)S(1)} %get-tuple-element.22.s_ref, ...), custom_call_target="tpu_custom_call" | custom-call | tf_op jit(solution)/shard_map/pallas_call | solution.py:1044
  18.3 3.8 %collective-permute-start.5 = (f32[43,8,128]{2,1,0:T(8,128)S(1)}, f32[43,8,128]{2,1,0:T(8,128)S(1)}, u32[]{:S(2)}, u32[]{:S(2)}) collective-permute-start(f32[43,8,128]{2,1,0:T(8,128)S(1)} %get-tuple-element.35), channel_id=1, source_target_pairs={{0,15},{2,1},{4,3},{6,5},{8,7},{10,9},{12,11},{14,13},{15,0},{1,2}... | collective-permute-start | bytes 528392 | tf_op jit(solution)/shard_map/ppermute | solution.py:1057
  22.1 0.0 collective-permute-start.6
  22.1 1.7 %shard_map.62 = f32[64,8192]{1,0:T(8,128)} custom-call(f32[2,32,80,128]{3,2,1,0:T(8,128)S(1)} %get-tuple-element.30.r_ref), custom_call_target="tpu_custom_call" | custom-call | tf_op jit(solution)/shard_map/pallas_call | solution.py:1044
  23.8 2.3 %collective-permute-done.5.from_other = f32[43,8,128]{2,1,0:T(8,128)S(1)} collective-permute-done((f32[43,8,128]{2,1,0:T(8,128)S(1)}, f32[43,8,128]{2,1,0:T(8,128)S(1)}, u32[]{:S(2)}, u32[]{:S(2)}) %collective-permute-start.5) | collective-permute-done | bytes 176160 | tf_op jit(solution)/shard_map/ppermute | solution.py:1057
  26.0 0.0 collective-permute-done.6.from_mate
  26.0 2.2 %shard_map.63 = (f32[16,2048]{1,0:T(8,128)}, f32[16,2048]{1,0:T(8,128)}) custom-call(f32[4,17,16,128]{3,2,1,0:T(8,128)S(1)} %get-tuple-element.31.s_ref, f32[4,16,16,128]{3,2,1,0:T(8,128)S(1)} %get-tuple-element.25.d1_ref.d_ref, f32[4,16,16,128]{3,2,1,0:T(8,128)S(1)} %get-tuple-element.26.i1_ref.i_ref, f32[4,16,128]{2,1,0:T(8,128)S(1)} %get-tuple-element.32.d_virtual, ...), custom_call_target="tpu_custom_call" | custom-call | tf_op jit(solution)/shard_map/pallas_call | solution.py:1044
Async XLA Ops:
  0.6 7.6 %copy-start.2 = (s32[2,256]{1,0:T(2,128)S(1)}, s32[2,256]{1,0:T(2,128)}, u32[]{:S(2)}) copy-start(s32[2,256]{1,0:T(2,128)} %flag_ref.5) | copy-start | bytes 6148
  0.6 7.6 %copy-start.1 = (bf16[64,8192]{1,0:T(8,128)(2,1)S(1)}, bf16[64,8192]{1,0:T(8,128)(2,1)}, u32[]{:S(2)}) copy-start(bf16[64,8192]{1,0:T(8,128)(2,1)} %weight_ref.5) | copy-start | bytes 3145732
  0.7 7.6 %copy-start = (f32[64,8192]{1,0:T(8,128)S(1)}, f32[64,8192]{1,0:T(8,128)}, u32[]{:S(2)}) copy-start(f32[64,8192]{1,0:T(8,128)} %right_ref.5) | copy-start | bytes 6291460
  2.8 11.5 %collective-permute-start = (f32[2,32,8,128]{3,2,1,0:T(8,128)S(1)}, f32[2,32,8,128]{3,2,1,0:T(8,128)S(1)}, u32[]{:S(2)}, u32[]{:S(2)}) collective-permute-start(f32[2,32,8,128]{3,2,1,0:T(8,128)S(1)} %get-tuple-element.28), channel_id=1, source_target_pairs={{0,15},{2,1},{4,3},{6,5},{8,7},{10,9},{12,11},{14,13},{15,0},{1,2}... | collective-permute-start | bytes 786440 | tf_op jit(solution)/shard_map/ppermute | solution.py:1057
  8.3 6.0 %collective-permute-start.1 = (f32[2,32,8,128]{3,2,1,0:T(8,128)S(1)}, f32[2,32,8,128]{3,2,1,0:T(8,128)S(1)}, u32[]{:S(2)}, u32[]{:S(2)}) collective-permute-start(f32[2,32,8,128]{3,2,1,0:T(8,128)S(1)} %get-tuple-element.29), channel_id=1, source_target_pairs={{0,1},{2,3},{4,5},{6,7},{8,9},{10,11},{12,13},{14,15},{1,0},{3,2},... | collective-permute-start | bytes 786440 | tf_op jit(solution)/shard_map/ppermute | solution.py:1057
  8.7 5.5 %collective-permute-start.2 = (f32[2,32,128]{2,1,0:T(8,128)S(1)}, f32[2,32,128]{2,1,0:T(8,128)S(1)}, u32[]{:S(2)}, u32[]{:S(2)}) collective-permute-start(f32[2,32,128]{2,1,0:T(8,128)S(1)} %shard_map.59.polar_first), channel_id=1, source_target_pairs={{0,8},{1,9},{2,10},{3,11},{4,12},{5,13},{6,14},{7,15},{8,0},{9,1},... | collective-permute-start | bytes 98312 | tf_op jit(solution)/shard_map/ppermute | solution.py:1094
  8.9 5.1 %collective-permute-start.4 = (f32[2,8,128]{2,1,0:T(8,128)S(1)}, f32[2,8,128]{2,1,0:T(8,128)S(1)}, u32[]{:S(2)}, u32[]{:S(2)}) collective-permute-start(f32[2,8,128]{2,1,0:T(8,128)S(1)} %get-tuple-element.21.edges_first), channel_id=1, source_target_pairs={{0,7},{2,9},{4,11},{6,13},{8,15},{10,1},{12,3},{14,5},{7,0},{9,2},... | collective-permute-start | bytes 24584 | tf_op jit(solution)/shard_map/ppermute | solution.py:1057
  9.7 4.5 %collective-permute-start.3 = (f32[2,8,128]{2,1,0:T(8,128)S(1)}, f32[2,8,128]{2,1,0:T(8,128)S(1)}, u32[]{:S(2)}, u32[]{:S(2)}) collective-permute-start(f32[2,8,128]{2,1,0:T(8,128)S(1)} %get-tuple-element.21.edges_first), channel_id=1, source_target_pairs={{0,9},{2,11},{4,13},{6,15},{8,1},{10,3},{12,5},{14,7},{9,0},{11,2}... | collective-permute-start | bytes 24584 | tf_op jit(solution)/shard_map/ppermute | solution.py:1057
  18.3 7.7 %collective-permute-start.5 = (f32[43,8,128]{2,1,0:T(8,128)S(1)}, f32[43,8,128]{2,1,0:T(8,128)S(1)}, u32[]{:S(2)}, u32[]{:S(2)}) collective-permute-start(f32[43,8,128]{2,1,0:T(8,128)S(1)} %get-tuple-element.35), channel_id=1, source_target_pairs={{0,15},{2,1},{4,3},{6,5},{8,7},{10,9},{12,11},{14,13},{15,0},{1,2}... | collective-permute-start | bytes 528392 | tf_op jit(solution)/shard_map/ppermute | solution.py:1057
  22.1 3.9 %collective-permute-start.6 = (f32[43,8,128]{2,1,0:T(8,128)S(1)}, f32[43,8,128]{2,1,0:T(8,128)S(1)}, u32[]{:S(2)}, u32[]{:S(2)}) collective-permute-start(f32[43,8,128]{2,1,0:T(8,128)S(1)} %get-tuple-element.36), channel_id=1, source_target_pairs={{0,1},{2,3},{4,5},{6,7},{8,9},{10,11},{12,13},{14,15},{1,0},{3,2},... | collective-permute-start | bytes 528392 | tf_op jit(solution)/shard_map/ppermute | solution.py:1057

commit v15 on v14

--- a/solution.py
+++ b/solution.py
@@ -186,45 +186,44 @@
         to_mate[i, t], to_other[i, t] = chosen(odd, left[i], right[i])
 
 
-def placed(rows):
-    sub = row_ids(8)
-    packed = roll_rows(rows[0][0], -rows[0][1])
-    for i, (x, at) in enumerate(rows):
-        if i:
-            packed = jnp.where(sub == i, roll_rows(x, i - at), packed)
-    return packed
-
-
 def sides(swapped):
     even, odd = reds(swapped)
     return (even, even ^ 1, odd, odd ^ 1), (odd, odd ^ 1, even, even ^ 1)
 
 
+def paired(groups, shift):
+    sub = row_ids(8)
+    packed = roll_rows(groups[0], shift)
+    for g in (1, 2, 3):
+        packed = jnp.where(sub // 2 == g, roll_rows(groups[g], 2 * g + shift), packed)
+    return packed
+
+
 def state_packs(source, diag, last, first_black, residual, partial, diag2, swapped):
+    sub = row_ids(8)
     rows = source[0].shape[0]
     packs = []
-    for (a, ab, b, bb), here, near, far, ends in zip(
-        sides(swapped),
-        (slice(rows - 8, rows), slice(0, 8)),
-        (7, 0),
-        (6, 1),
-        ((4, 5, 6), (3, 2, 1)),
+    for (a, ab, b, bb), here, near, far, step in zip(
+        sides(swapped), (slice(rows - 8, rows), slice(0, 8)), (7, 0), (6, 1), (-1, 1)
     ):
         s, d, v = ([x[here] for x in group] for group in (source, diag, last))
         part, d2 = partial[here], diag2[here]
-        pack0 = [(x, near) for x in s + d]
-        pack1 = [
-            (first_black[ab][here], near),
-            (s[bb] + v[a], far),
-            (d[bb], far),
-            (first_black[bb][here], far),
-            (v[b], far),
-            (s[b] - d[b] * v[b] + v[ab], far),
-            (residual[a][here] - v[bb], far),
-            (part * inverse_of(d2), ends[0]),
+        beside = [
+            s[bb] + v[a],
+            d[bb],
+            first_black[bb][here],
+            v[b],
+            s[b] - d[b] * v[b] + v[ab],
+            residual[a][here] - v[bb],
+            part,
+            roll_rows(d2, -step),
         ]
-        pack2 = [(part, ends[1]), (part, ends[2]), (d2, ends[1]), (d2, ends[2])]
-        packs.append((placed(pack0), placed(pack1), placed(pack2)))
+        groups = [jnp.where(sub == far, y, x) for x, y in zip(s + d, beside)]
+        shift = 2 if near == 7 else 0
+        more = jnp.where(sub == far, d2, first_black[ab][here])
+        more = jnp.where(sub == far + step, part, more)
+        more = jnp.where(sub == far + 2 * step, part * inverse_of(d2), more)
+        packs.append((paired(groups[:4], shift), paired(groups[4:], shift), more))
     return packs
 
 
@@ -428,114 +427,124 @@
             use(start + i, quarters_of(out[i * rows : (i + 1) * rows], temp.at[i, :, :rows]))
 
 
-def half_sweep(v, load_s, load_i, tiles, red, unroll, left=None):
-    rows = v[0].shape[1]
-    lane = lane_ids(rows)
+class Ring:
+    def __init__(self, own, virtual, tiles, rows):
+        self.own, self.virtual, self.tiles, self.rows = own, virtual, tiles, rows
+
+    def part(self, parity, t, start):
+        return self.own[parity, t, pl.ds(8 + start, self.rows, 2), :]
+
+    def whole(self, q, t):
+        return self.virtual[q] if t == self.tiles else self.part(q % 2, t, q // 2)
+
+    def put(self, q, t, x):
+        if t == self.tiles:
+            self.virtual[q] = x
+            return
+        pr, pc = q % 2, q // 2
+        self.own[pr, t, pl.ds(8 + pc, self.rows, 2), :] = x
+        if pc == 1:
+            self.own[pr, t, 7:8] = x[self.rows - 1 :]
+        else:
+            end = 8 + 2 * self.rows
+            self.own[pr, t, end : end + 1] = x[:1]
+
+    def beside_columns(self, q, t):
+        pr, pc = q % 2, q // 2
+        if t == self.tiles:
+            x = self.virtual[q ^ 2]
+            return x + (col_next if pc else col_prev)(x)
+        return self.part(pr, t, pc - 1) + self.part(pr, t, pc + 1)
+
+    def beside(self, q, t):
+        x = self.whole(q ^ 1, t)
+        lane = lane_ids(self.rows)
+        if q % 2 == 0:
+            other = roll_up(self.whole(q ^ 1, before(t, self.tiles)))
+            lat = jnp.where(lane == 0, other, roll_up(x))
+        else:
+            other = roll_down(self.whole(q ^ 1, after(t, self.tiles)))
+            lat = jnp.where(lane == LANES - 1, other, roll_down(x))
+        return (x + lat) + self.beside_columns(q, t)
+
+
+def ring_sweep(v, load_s, load_i, red, left):
+    tiles = v.tiles
+    lane = lane_ids(v.rows)
     y, z, qa, qb = (1, 2, 0, 3) if red else (3, 0, 2, 1)
-    col_a, col_b = (col_prev, col_next) if red else (col_next, col_prev)
-
-    def beside_virtual(q):
-        ns, we = q ^ 1, q ^ 2
-        here = v[ns][tiles]
-        if q % 2 == 0:
-            lat = jnp.where(lane == 0, roll_up(v[ns][tiles - 1]), roll_up(here))
-        else:
-            lat = jnp.where(lane == LANES - 1, roll_down(v[ns][0]), roll_down(here))
-        cols = v[we][tiles]
-        return (here + lat) + (cols + (col_prev if q < 2 else col_next)(cols))
-
-    held = [
-        (q, (load_s(q, tiles) + beside_virtual(q)) * load_i(q, tiles)) for q in (y, z)
-    ]
-
-    def body(t, carry):
-        y_before, z_here = carry
-        vy, vz = v[y][t], v[z][t]
-        y_here = roll_up(vy)
-        z_after = roll_down(v[z][t + 1])
+    held = [(q, (load_s(q, tiles) + v.beside(q, tiles)) * load_i(q, tiles)) for q in (y, z)]
+    y_before, vz = roll_up(v.whole(y, tiles)), v.whole(z, 0)
+    z_here = roll_down(vz)
+    for t in range(tiles):
+        vy, z_next = v.whole(y, t), v.whole(z, t + 1)
+        y_here, z_after = roll_up(vy), roll_down(z_next)
         lat_a = vy + jnp.where(lane == 0, y_before, y_here)
         lat_b = vz + jnp.where(lane == LANES - 1, z_after, z_here)
-        all_a = load_s(qa, t) + (lat_a + (vz + col_a(vz)))
-        all_b = load_s(qb, t) + (lat_b + (vy + col_b(vy)))
-        new_a, new_b = all_a * load_i(qa, t), all_b * load_i(qb, t)
-        v[qa][t], v[qb][t] = new_a, new_b
-        if left is not None:
-            load_d, rest = left
-            rest[qa][t] = all_a - load_d(qa, t) * new_a
-            rest[qb][t] = all_b - load_d(qb, t) * new_b
-        return y_here, z_after
-
-    loop(tiles, body, (roll_up(v[y][tiles]), roll_down(v[z][0])), unroll)
+        new = []
+        for q, lat in ((qa, lat_a), (qb, lat_b)):
+            total = load_s(q, t) + (lat + v.beside_columns(q, t))
+            value = total * load_i(q, t)
+            new.append((q, value))
+            if left is not None:
+                load_d, rest = left
+                rest.put(q, t, total - load_d(q, t) * value)
+        for q, value in new:
+            v.put(q, t, value)
+        y_before, z_here, vz = y_here, z_after, z_next
     for q, value in held:
-        v[q][tiles] = value
-
-
-def smooth(v, load_s, load_i, tiles, unroll, left, after_sweep=None):
-    zeros = jnp.zeros(v[0].shape[1:], F32)
-
-    def first(t, _):
-        for q in (0, 3):
-            v[q][t] = load_s(q, t) * load_i(q, t)
-        return 0
-
-    loop(tiles, first, 0, unroll)
-    for q in (1, 2):
-        v[q][0] = zeros
-        v[q][tiles - 1] = zeros
-        v[q][tiles] = load_s(q, tiles) * load_i(q, tiles)
-        v[3 * (q - 1)][tiles] = zeros
+        v.put(q, tiles, value)
+
+
+def ring_smooth(v, load_s, load_i, load_d, rest, after_sweep):
+    tiles = v.tiles
+    zeros = jnp.zeros((v.rows, LANES), F32)
+    for t in range(tiles + 1):
+        reds_here = (1, 2) if t == tiles else (0, 3)
+        for q in reds_here:
+            v.put(q, t, load_s(q, t) * load_i(q, t))
+        if t in (0, tiles - 1, tiles):
+            for q in reds_here:
+                v.put(q ^ 1, t, zeros)
     for sweep, red in enumerate((False, True, False)):
-        half_sweep(v, load_s, load_i, tiles, red, unroll, left if sweep == 2 else None)
-        if after_sweep is not None:
-            after_sweep(sweep)
-
-
-def residuals(v, load_s, left, tiles, c0, c1, keep, unroll, valid=None):
-    lane = lane_ids(v[0].shape[1])
-    load_d, rest = left
+        ring_sweep(v, load_s, load_i, red, (load_d, rest) if sweep == 2 else None)
+        after_sweep(sweep)
+
+
+def ring_residuals(v, load_s, load_d, rest, c0, c1, keep, valid):
+    tiles = v.tiles
+    lane = lane_ids(v.rows)
 
     def use(t, r):
         keep(t, r)
-        if valid is not None:
-            virtual = isinstance(t, int) and t == tiles
-            r = [jnp.where(valid(q, virtual), r[q], 0.0) for q in range(4)]
-        c0[t] = (col_prev(r[2]) + col_next(r[0])) + 3.0 * (r[0] + r[2])
-        c1[t] = (col_prev(r[3]) + col_next(r[1])) + 3.0 * (r[1] + r[3])
-
-    def north(q, t):
-        return jnp.where(lane == 0, roll_up(v[q][before(t, tiles)]), roll_up(v[q][t]))
-
-    def south(q, t):
-        return jnp.where(
-            lane == LANES - 1, roll_down(v[q][after(t, tiles)]), roll_down(v[q][t])
-        )
+        r = [jnp.where(valid(q, t == tiles), r[q], 0.0) for q in range(4)]
+        if t == tiles:
+            c0[t] = (col_prev(r[2]) + col_next(r[0])) + 3.0 * (r[0] + r[2])
+            c1[t] = (col_prev(r[3]) + col_next(r[1])) + 3.0 * (r[1] + r[3])
+            return
+        for q in range(4):
+            rest.put(q, t, r[q])
+        for pr, ref in ((0, c0), (1, c1)):
+            outer = rest.part(pr, t, -1) + rest.part(pr, t, 2)
+            ref[t] = outer + 3.0 * (rest.part(pr, t, 0) + rest.part(pr, t, 1))
+
+    def residual(q, t, beside):
+        return load_s(q, t) - (load_d(q, t) * v.whole(q, t) - beside)
 
     def full(t):
-        x = [v[q][t] for q in range(4)]
-        beside = [
-            (x[1] + north(1, t)) + (x[2] + col_prev(x[2])),
-            (x[0] + south(0, t)) + (x[3] + col_prev(x[3])),
-            (x[3] + north(3, t)) + (x[0] + col_next(x[0])),
-            (x[2] + south(2, t)) + (x[1] + col_next(x[1])),
-        ]
-        use(t, [load_s(q, t) - (load_d(q, t) * x[q] - beside[q]) for q in range(4)])
-
-    def body(i, carry):
-        t = i + 1
-        up, down = carry
-        x = [v[q][t] for q in range(4)]
-        up_here, down_next = roll_up(x[1]), roll_down(v[2][t + 1])
-        beside0 = (x[1] + jnp.where(lane == 0, up, up_here)) + (x[2] + col_prev(x[2]))
-        beside3 = (x[2] + jnp.where(lane == LANES - 1, down_next, down)) + (
-            x[1] + col_next(x[1])
-        )
-        r0 = load_s(0, t) - (load_d(0, t) * x[0] - beside0)
-        r3 = load_s(3, t) - (load_d(3, t) * x[3] - beside3)
-        use(t, [r0, rest[1][t], rest[2][t], r3])
-        return up_here, down_next
+        use(t, [residual(q, t, v.beside(q, t)) for q in range(4)])
 
     full(0)
-    loop(tiles - 2, body, (roll_up(v[1][0]), roll_down(v[2][1])), unroll)
+    up, x2 = roll_up(v.whole(1, 0)), v.whole(2, 1)
+    down = roll_down(x2)
+    for t in range(1, tiles - 1):
+        x1, next2 = v.whole(1, t), v.whole(2, t + 1)
+        up_here, down_next = roll_up(x1), roll_down(next2)
+        lat0 = x1 + jnp.where(lane == 0, up, up_here)
+        lat3 = x2 + jnp.where(lane == LANES - 1, down_next, down)
+        r0 = residual(0, t, lat0 + v.beside_columns(0, t))
+        r3 = residual(3, t, lat3 + v.beside_columns(3, t))
+        use(t, [r0, rest.whole(1, t), rest.whole(2, t), r3])
+        up, down, x2 = up_here, down_next, next2
     full(tiles - 1)
     full(tiles)
 
@@ -715,8 +724,7 @@
     from_other, from_mate, polar_ref, corner_near, corner_far,
     r_ref, s1_ref, d1_virtual, d2_virtual, s2_ref, to_mate, to_other,
     v_ref, hv, pv, hr, c0, c1, hs, hd, hi, ps, pd, pi, n1, temp,
-    w0, w1, w2, w3, e0, e1, pi1, black_even, black_odd, red_even, red_odd,
-    part1, part2,
+    w_ref, wv, rest1, e0, e1, pi1, black_even, black_odd, red_even, red_odd,
 ):
     tiles, columns = s_ref.shape[1], s_ref.shape[2]
     rows = columns // 2
@@ -805,8 +813,8 @@
     def own(main, virtual):
         return lambda q, t: virtual[q] if isinstance(t, int) and t == tiles1 else main[q, t]
 
-    w = [w0, w1, w2, w3]
     rows1 = rows // 2
+    w, rest1 = Ring(w_ref, wv, tiles1, rows1), Ring(rest1, wv, tiles1, rows1)
     row = row_ids(rows1)
     load_s, load_d = own(s1_ref, s1_ref.at[:, tiles1]), own(d1_ref, d1_virtual)
 
@@ -814,11 +822,10 @@
         if sweep == 0:
             for t in range(tiles1 + 1):
                 even, odd_red = reds(t == tiles1)
-                black_even[t] = w[even ^ 1][t]
-                black_odd[t] = w[odd_red ^ 1][t]
-
-    left = load_d, {1: part1, 2: part2}
-    smooth(w, load_s, own(i1_ref, pi1), tiles1, 16, left, after_sweep)
+                black_even[t] = w.whole(even ^ 1, t)
+                black_odd[t] = w.whole(odd_red ^ 1, t)
+
+    ring_smooth(w, load_s, own(i1_ref, pi1), load_d, rest1, after_sweep)
 
     def valid(q, virtual):
         even, odd_red = reds(virtual)
@@ -831,7 +838,7 @@
         red_even[t] = r[even]
         red_odd[t] = r[odd_red]
 
-    residuals(w, load_s, left, tiles1, e0, e1, keep_red, 16, valid)
+    ring_residuals(w, load_s, load_d, rest1, e0, e1, keep_red, valid)
     shared = {}
 
     def edges(t, partial):
@@ -841,7 +848,7 @@
         packs = state_packs(
             [s1_ref[q, t] for q in range(4)],
             [load_d(q, t) for q in range(4)],
-            [w[q][t] for q in range(4)],
+            [w.whole(q, t) for q in range(4)],
             {even ^ 1: black_even[t], odd_red ^ 1: black_odd[t]},
             {even: red_even[t], odd_red: red_odd[t]},
             partial,
@@ -852,14 +859,13 @@
         count = tiles1 + 1
         for i in (0, 1):
             to_mate[i * count + t], to_other[i * count + t] = chosen(odd, left[i], right[i])
-        pair = chosen(odd, left[2], right[2])
         if t % 2 == 0:
+            pair = chosen(odd, left[2], roll_rows(right[2], 4))
             shared[0] = pair
+        else:
+            pair = chosen(odd, roll_rows(left[2], 4), right[2])
+            pair = [jnp.where(sub < 4, x, y) for x, y in zip(shared[0], pair)]
         if t % 2 == 1 or virtual:
-            if t % 2 == 1:
-                pair = [
-                    jnp.where(sub < 4, x, roll_rows(y, 4)) for x, y in zip(shared[0], pair)
-                ]
             to_mate[2 * count + t // 2], to_other[2 * count + t // 2] = pair
 
     restrict(e0, e1, tiles1, rows1, edges, 16)
@@ -894,10 +900,10 @@
 def coarse_kernel(
     s_ref, d_ref, i_ref, d_virtual, d2_ref, d2_virtual, s2_ref, from_other, from_mate,
     solution_ref, residual_ref,
-    v0, v1, v2, v3, c0, c1, hs, hd, hi, part, fixes, rest1, rest2, s, d, inv, va, vb,
+    v_ref, vv, rest, c0, c1, hs, hd, hi, part, fixes, s, d, inv, va, vb,
 ):
-    v = [v0, v1, v2, v3]
     tiles, own = d_ref.shape[1], d_ref.shape[2]
+    v, rest = Ring(v_ref, vv, tiles, 16), Ring(rest, vv, tiles, 16)
     rows = own + 8
     count = tiles + 1
     sub = row_ids(8)
@@ -914,31 +920,33 @@
         fixed = [jnp.zeros((8, LANES), F32)] * 4
         more = jnp.zeros((8, LANES), F32)
         total = jnp.ones((8, LANES), F32)
-        third = 4 * (t % 2)
         for side, (a, ab, b, bb) in enumerate(sides(t == tiles)):
             near, far, step = (7, 6, -1) if side == 0 else (0, 1, 1)
+            first = 6 if side == 0 else 0
             pack0, pack1, pack2 = (pair[side] for pair in packs)
-
-            def put(group, q, at, pack, row):
-                group[q] = jnp.where(sub == at, roll_rows(pack, at - row), group[q])
+            groups = [
+                roll_rows(pack, first - 2 * g) for pack in (pack0, pack1) for g in range(4)
+            ]
+            pack2 = roll_rows(pack2, 4 * (t % 2) + (4 if side == 0 else 0))
+
+            def put(group, q, at, x):
+                group[q] = jnp.where(sub == at, x, group[q])
 
             for q in range(4):
-                put(source, q, near, pack0, q)
-                put(diag, q, near, pack0, 4 + q)
-            put(source, bb, far, pack1, 1)
-            put(diag, bb, far, pack1, 2)
-            put(source, b, far, pack1, 5)
-            diag[b] = jnp.where(sub == far, 0.0, diag[b])
-            put(source, a, far, pack1, 6)
-            put(fixed, ab, near, pack1, 0)
-            put(fixed, bb, far, pack1, 3)
-            put(fixed, b, far, pack1, 4)
-            for at, pack, row in (
-                (far + 2 * step, pack1, 7), (far + step, pack2, third), (far, pack2, third + 1)
-            ):
-                more = jnp.where(sub == at, roll_rows(pack, at - row), more)
-            for at, row in ((far + step, third + 2), (far, third + 3)):
-                total = jnp.where(sub == at, roll_rows(pack2, at - row), total)
+                put(source, q, near, groups[q])
+                put(diag, q, near, groups[4 + q])
+            put(source, bb, far, groups[0])
+            put(diag, bb, far, groups[1])
+            put(fixed, bb, far, groups[2])
+            put(fixed, b, far, groups[3])
+            put(source, b, far, groups[4])
+            put(diag, b, far, 0.0)
+            put(source, a, far, groups[5])
+            put(fixed, ab, near, pack2)
+            more = jnp.where(sub == far, groups[6], more)
+            more = jnp.where((sub == far + step) | (sub == far + 2 * step), pack2, more)
+            total = jnp.where(sub == far, pack2, total)
+            total = jnp.where(sub == far + step, roll_rows(groups[7], step), total)
             for q in range(4):
                 known = (sub == near) | (sub == far) if q == bb else sub == near
                 inverse[q] = jnp.where(known, inverse_of(diag[q]), inverse[q])
@@ -954,6 +962,7 @@
         total = jnp.where((sub == 0) | (sub == 7), near_total, total)
         here = d2_virtual[...] if t == tiles else d2_ref[t]
         d[t] = jnp.concatenate([here, total], 0)
+
     def after_sweep(sweep):
         if sweep == 2:
             return
@@ -965,13 +974,17 @@
             else:
                 todo = {b: sub == 6, other_b: sub == 1}
             for q, mask in todo.items():
-                v[q][t, :8] = jnp.where(mask, fixes[q, t], v[q][t, :8])
+                if t == tiles:
+                    vv[q, :8] = jnp.where(mask, fixes[q, t], vv[q, :8])
+                else:
+                    place = pl.ds(8 + q // 2, 8, 2)
+                    x = v_ref[q % 2, t, place, :]
+                    v_ref[q % 2, t, place, :] = jnp.where(mask, fixes[q, t], x)
 
     def of(ref):
         return lambda q, t: ref[q, t]
 
-    left = of(hd), {1: rest1, 2: rest2}
-    smooth(v, of(hs), of(hi), tiles, 16, left, after_sweep)
+    ring_smooth(v, of(hs), of(hi), of(hd), rest, after_sweep)
     row = row_ids(16)
 
     def valid(q, virtual):
@@ -982,7 +995,7 @@
         last = 15 if q == even ^ 1 else 14
         return (row <= after_band) | ((row >= before_band) & (row <= first)) | (row >= last)
 
-    residuals(v, of(hs), left, tiles, c0, c1, lambda t, r: None, 16, valid)
+    ring_residuals(v, of(hs), of(hd), rest, c0, c1, lambda t, r: None, valid)
 
     lane, row = lane_ids(rows), row_ids(rows)
     even = (lane + row) % 2 == 0
@@ -1101,8 +1114,8 @@
         right_side, texel_weight, seam_flags, polar_own,
     )
 
-    def level_scratch(tiles, rows):
-        return [(tiles + 1, rows, LANES)] * 6
+    ring = [(2, tiles1, 2 * rows1 + 16, LANES), (4, rows1, LANES)]
+    ring += [ring[0], (tiles1 + 1, rows1, LANES), (tiles1 + 1, rows1, LANES)]
 
     def halo_scratch(tiles):
         return [(4, tiles + 1, 8, LANES)] * 3
@@ -1117,10 +1130,9 @@
         + halo_scratch(tiles)
         + [(4, rows, LANES)] * 3
         + [(tiles + 1, rows, LANES), (BATCH, 2, rows, LANES)]
-        + level_scratch(tiles1, rows1)
+        + ring
         + [(4, rows1, LANES)]
-        + [(tiles1 + 1, rows1, LANES)] * 4
-        + [(tiles1, rows1, LANES)] * 2,
+        + [(tiles1 + 1, rows1, LANES)] * 4,
         s, d, inverse, d1, i1, d2, from_other, from_mate, polar, corner_near, corner_far,
     )
     from_mate, from_other = swapped_edges(to_mate, to_other)
@@ -1132,10 +1144,9 @@
     solution_2, residual_2 = call(
         coarse_kernel,
         [(columns // 4, height // 4)] * 2,
-        level_scratch(tiles1, 16)
+        ring
         + [(4, tiles1 + 1, 16, LANES)] * 3
         + [(tiles1 + 1, 8, LANES), (4, tiles1 + 1, 8, LANES)]
-        + [(tiles1, 16, LANES)] * 2
         + [wide] * 5,
         s1, d1, i1, d1_virtual, d2, d2_virtual, s2_own, from_other, from_mate,
     )

time: 28.3 us -> 28.6 us (1.011)
  Pallas kernels: 11.8 us -> 12.1 us
where the time goes in v15:
time: 28.6 us; the launch traced here: 28.4 us
  starting transfers between devices  13.2 us (46%)
  Pallas kernels  12.1 us (42%)
  waiting for transfers between devices  2.46 us (9%)
  between operations  0.71 us (2%)
    ppermute x6, starting transfers between devices, swapped_with(): return lax.ppermute(x, 'lon', pairs + [(b, a) for a, b in pairs])  13 us
    pallas_call x6, Pallas kernels, call(): pl.pallas_call(kernel, out_shape=[jax.ShapeDtypeStruct(shape, F32) for sh...  12.1 us
    ppermute x6, waiting for transfers between devices, swapped_with(): return lax.ppermute(x, 'lon', pairs + [(b, a) for a, b in pairs])  2.46 us
  transfers between devices with their start and end apart: 7, of which 2 were waited for; matrix products, arithmetic and copies ran while one was open for 0% of the time, Pallas kernels for 13%

profile of v15, /device:TPU:0, one launch (start us, length us, event | category | flops | bytes accessed | tf_op | source)
XLA Modules:
  0.0 28.4 jit_solution(8745170241725739200)
XLA Ops:
  0.6 0.0 copy-start.2
  0.6 0.0 copy-start.1
  0.7 0.0 copy-start
  0.7 2.1 %shard_map.58 = (f32[2,32,8,128]{3,2,1,0:T(8,128)S(1)}, f32[2,32,8,128]{3,2,1,0:T(8,128)S(1)}, f32[2,8,128]{2,1,0:T(8,128)S(1)}) custom-call(f32[64,8192]{1,0:T(8,128)} %right_ref.5, bf16[64,8192]{1,0:T(8,128)(2,1)} %weight_ref.5, s32[2,256]{1,0:T(2,128)} %flag_ref.5), custom_call_target="tpu_custom_call" | custom-call | tf_op jit(solution)/shard_map/pallas_call | solution.py:1057
  2.8 5.5 %collective-permute-start = (f32[2,32,8,128]{3,2,1,0:T(8,128)S(1)}, f32[2,32,8,128]{3,2,1,0:T(8,128)S(1)}, u32[]{:S(2)}, u32[]{:S(2)}) collective-permute-start(f32[2,32,8,128]{3,2,1,0:T(8,128)S(1)} %get-tuple-element.28), channel_id=1, source_target_pairs={{0,15},{2,1},{4,3},{6,5},{8,7},{10,9},{12,11},{14,13},{15,0},{1,2}... | collective-permute-start | bytes 786440 | tf_op jit(solution)/shard_map/ppermute | solution.py:1070
  8.3 0.0 collective-permute-start.1
  8.3 0.0 copy-done.2
  8.3 0.0 copy-done.1
  8.3 0.0 copy-done
  8.3 0.4 %shard_map.59.polar_first = f32[2,32,128]{2,1,0:T(8,128)S(1)} custom-call(f32[64,8192]{1,0:T(8,128)S(1)} %copy-done, bf16[64,8192]{1,0:T(8,128)(2,1)S(1)} %copy-done.1, s32[2,256]{1,0:T(2,128)S(1)} %copy-done.2, f32[2,8,128]{2,1,0:T(8,128)S(1)} %get-tuple-element.21.edges_first), custom_call_target="tpu_custom_call" | custom-call | tf_op jit(solution)/shard_map/pallas_call | solution.py:1057
  8.7 0.2 collective-permute-start.2
  8.9 0.8 %collective-permute-start.4 = (f32[2,8,128]{2,1,0:T(8,128)S(1)}, f32[2,8,128]{2,1,0:T(8,128)S(1)}, u32[]{:S(2)}, u32[]{:S(2)}) collective-permute-start(f32[2,8,128]{2,1,0:T(8,128)S(1)} %get-tuple-element.21.edges_first), channel_id=1, source_target_pairs={{0,7},{2,9},{4,11},{6,13},{8,15},{10,1},{12,3},{14,5},{7,0},{9,2},... | collective-permute-start | bytes 24584 | tf_op jit(solution)/shard_map/ppermute | solution.py:1070
  9.7 2.8 %collective-permute-start.3 = (f32[2,8,128]{2,1,0:T(8,128)S(1)}, f32[2,8,128]{2,1,0:T(8,128)S(1)}, u32[]{:S(2)}, u32[]{:S(2)}) collective-permute-start(f32[2,8,128]{2,1,0:T(8,128)S(1)} %get-tuple-element.21.edges_first), channel_id=1, source_target_pairs={{0,9},{2,11},{4,13},{6,15},{8,1},{10,3},{12,5},{14,7},{9,0},{11,2}... | collective-permute-start | bytes 24584 | tf_op jit(solution)/shard_map/ppermute | solution.py:1070
  12.6 1.5 %shard_map.60 = (f32[2,32,64,128]{3,2,1,0:T(8,128)S(1)}, f32[2,32,64,128]{3,2,1,0:T(8,128)S(1)}, f32[2,32,64,128]{3,2,1,0:T(8,128)S(1)}, f32[4,16,16,128]{3,2,1,...) custom-call(f32[64,8192]{1,0:T(8,128)S(1)} %copy-done, bf16[64,8192]{1,0:T(8,128)(2,1)S(1)} %copy-done.1, ...), custom_call_target="tpu_custom_call" | custom-call | tf_op jit(solution)/shard_map/pallas_call | solution.py:1057
  14.1 0.0 collective-permute-done.4.corner_far
  14.1 0.2 collective-permute-done.3.corner_near
  14.3 0.0 collective-permute-done.2.polar_ref
  14.3 0.0 collective-permute-done.from_other
  14.3 0.0 collective-permute-done.1.from_mate
  14.3 4.0 %shard_map.61 = (f32[2,32,80,128]{3,2,1,0:T(8,128)S(1)}, f32[4,17,16,128]{3,2,1,0:T(8,128)S(1)}, f32[4,16,128]{2,1,0:T(8,128)S(1)}, f32[16,128]{1,0:T(8,128)S(1)...) custom-call(f32[2,32,64,128]{3,2,1,0:T(8,128)S(1)} %get-tuple-element.22.s_ref, ...), custom_call_target="tpu_custom_call" | custom-call | tf_op jit(solution)/shard_map/pallas_call | solution.py:1057
  18.3 3.8 %collective-permute-start.5 = (f32[43,8,128]{2,1,0:T(8,128)S(1)}, f32[43,8,128]{2,1,0:T(8,128)S(1)}, u32[]{:S(2)}, u32[]{:S(2)}) collective-permute-start(f32[43,8,128]{2,1,0:T(8,128)S(1)} %get-tuple-element.35), channel_id=1, source_target_pairs={{0,15},{2,1},{4,3},{6,5},{8,7},{10,9},{12,11},{14,13},{15,0},{1,2}... | collective-permute-start | bytes 528392 | tf_op jit(solution)/shard_map/ppermute | solution.py:1070
  22.1 0.0 collective-permute-start.6
  22.2 1.7 %shard_map.62 = f32[64,8192]{1,0:T(8,128)} custom-call(f32[2,32,80,128]{3,2,1,0:T(8,128)S(1)} %get-tuple-element.30.r_ref), custom_call_target="tpu_custom_call" | custom-call | tf_op jit(solution)/shard_map/pallas_call | solution.py:1057
  23.8 2.2 %collective-permute-done.5.from_other = f32[43,8,128]{2,1,0:T(8,128)S(1)} collective-permute-done((f32[43,8,128]{2,1,0:T(8,128)S(1)}, f32[43,8,128]{2,1,0:T(8,128)S(1)}, u32[]{:S(2)}, u32[]{:S(2)}) %collective-permute-start.5) | collective-permute-done | bytes 176160 | tf_op jit(solution)/shard_map/ppermute | solution.py:1070
  26.1 0.0 collective-permute-done.6.from_mate
  26.1 2.4 %shard_map.63 = (f32[16,2048]{1,0:T(8,128)}, f32[16,2048]{1,0:T(8,128)}) custom-call(f32[4,17,16,128]{3,2,1,0:T(8,128)S(1)} %get-tuple-element.31.s_ref, f32[4,16,16,128]{3,2,1,0:T(8,128)S(1)} %get-tuple-element.25.d1_ref.d_ref, f32[4,16,16,128]{3,2,1,0:T(8,128)S(1)} %get-tuple-element.26.i1_ref.i_ref, f32[4,16,128]{2,1,0:T(8,128)S(1)} %get-tuple-element.32.d_virtual, ...), custom_call_target="tpu_custom_call" | custom-call | tf_op jit(solution)/shard_map/pallas_call | solution.py:1057
Async XLA Ops:
  0.6 7.6 %copy-start.2 = (s32[2,256]{1,0:T(2,128)S(1)}, s32[2,256]{1,0:T(2,128)}, u32[]{:S(2)}) copy-start(s32[2,256]{1,0:T(2,128)} %flag_ref.5) | copy-start | bytes 6148
  0.6 7.6 %copy-start.1 = (bf16[64,8192]{1,0:T(8,128)(2,1)S(1)}, bf16[64,8192]{1,0:T(8,128)(2,1)}, u32[]{:S(2)}) copy-start(bf16[64,8192]{1,0:T(8,128)(2,1)} %weight_ref.5) | copy-start | bytes 3145732
  0.7 7.6 %copy-start = (f32[64,8192]{1,0:T(8,128)S(1)}, f32[64,8192]{1,0:T(8,128)}, u32[]{:S(2)}) copy-start(f32[64,8192]{1,0:T(8,128)} %right_ref.5) | copy-start | bytes 6291460
  2.8 11.5 %collective-permute-start = (f32[2,32,8,128]{3,2,1,0:T(8,128)S(1)}, f32[2,32,8,128]{3,2,1,0:T(8,128)S(1)}, u32[]{:S(2)}, u32[]{:S(2)}) collective-permute-start(f32[2,32,8,128]{3,2,1,0:T(8,128)S(1)} %get-tuple-element.28), channel_id=1, source_target_pairs={{0,15},{2,1},{4,3},{6,5},{8,7},{10,9},{12,11},{14,13},{15,0},{1,2}... | collective-permute-start | bytes 786440 | tf_op jit(solution)/shard_map/ppermute | solution.py:1070
  8.3 6.0 %collective-permute-start.1 = (f32[2,32,8,128]{3,2,1,0:T(8,128)S(1)}, f32[2,32,8,128]{3,2,1,0:T(8,128)S(1)}, u32[]{:S(2)}, u32[]{:S(2)}) collective-permute-start(f32[2,32,8,128]{3,2,1,0:T(8,128)S(1)} %get-tuple-element.29), channel_id=1, source_target_pairs={{0,1},{2,3},{4,5},{6,7},{8,9},{10,11},{12,13},{14,15},{1,0},{3,2},... | collective-permute-start | bytes 786440 | tf_op jit(solution)/shard_map/ppermute | solution.py:1070
  8.7 5.5 %collective-permute-start.2 = (f32[2,32,128]{2,1,0:T(8,128)S(1)}, f32[2,32,128]{2,1,0:T(8,128)S(1)}, u32[]{:S(2)}, u32[]{:S(2)}) collective-permute-start(f32[2,32,128]{2,1,0:T(8,128)S(1)} %shard_map.59.polar_first), channel_id=1, source_target_pairs={{0,8},{1,9},{2,10},{3,11},{4,12},{5,13},{6,14},{7,15},{8,0},{9,1},... | collective-permute-start | bytes 98312 | tf_op jit(solution)/shard_map/ppermute | solution.py:1107
  8.9 5.1 %collective-permute-start.4 = (f32[2,8,128]{2,1,0:T(8,128)S(1)}, f32[2,8,128]{2,1,0:T(8,128)S(1)}, u32[]{:S(2)}, u32[]{:S(2)}) collective-permute-start(f32[2,8,128]{2,1,0:T(8,128)S(1)} %get-tuple-element.21.edges_first), channel_id=1, source_target_pairs={{0,7},{2,9},{4,11},{6,13},{8,15},{10,1},{12,3},{14,5},{7,0},{9,2},... | collective-permute-start | bytes 24584 | tf_op jit(solution)/shard_map/ppermute | solution.py:1070
  9.7 4.5 %collective-permute-start.3 = (f32[2,8,128]{2,1,0:T(8,128)S(1)}, f32[2,8,128]{2,1,0:T(8,128)S(1)}, u32[]{:S(2)}, u32[]{:S(2)}) collective-permute-start(f32[2,8,128]{2,1,0:T(8,128)S(1)} %get-tuple-element.21.edges_first), channel_id=1, source_target_pairs={{0,9},{2,11},{4,13},{6,15},{8,1},{10,3},{12,5},{14,7},{9,0},{11,2}... | collective-permute-start | bytes 24584 | tf_op jit(solution)/shard_map/ppermute | solution.py:1070
  18.3 7.7 %collective-permute-start.5 = (f32[43,8,128]{2,1,0:T(8,128)S(1)}, f32[43,8,128]{2,1,0:T(8,128)S(1)}, u32[]{:S(2)}, u32[]{:S(2)}) collective-permute-start(f32[43,8,128]{2,1,0:T(8,128)S(1)} %get-tuple-element.35), channel_id=1, source_target_pairs={{0,15},{2,1},{4,3},{6,5},{8,7},{10,9},{12,11},{14,13},{15,0},{1,2}... | collective-permute-start | bytes 528392 | tf_op jit(solution)/shard_map/ppermute | solution.py:1070
  22.1 3.9 %collective-permute-start.6 = (f32[43,8,128]{2,1,0:T(8,128)S(1)}, f32[43,8,128]{2,1,0:T(8,128)S(1)}, u32[]{:S(2)}, u32[]{:S(2)}) collective-permute-start(f32[43,8,128]{2,1,0:T(8,128)S(1)} %get-tuple-element.36), channel_id=1, source_target_pairs={{0,1},{2,3},{4,5},{6,7},{8,9},{10,11},{12,13},{14,15},{1,0},{3,2},... | collective-permute-start | bytes 528392 | tf_op jit(solution)/shard_map/ppermute | solution.py:1070

commit v16 on v14

--- a/solution.py
+++ b/solution.py
@@ -186,45 +186,44 @@
         to_mate[i, t], to_other[i, t] = chosen(odd, left[i], right[i])
 
 
-def placed(rows):
-    sub = row_ids(8)
-    packed = roll_rows(rows[0][0], -rows[0][1])
-    for i, (x, at) in enumerate(rows):
-        if i:
-            packed = jnp.where(sub == i, roll_rows(x, i - at), packed)
-    return packed
-
-
 def sides(swapped):
     even, odd = reds(swapped)
     return (even, even ^ 1, odd, odd ^ 1), (odd, odd ^ 1, even, even ^ 1)
 
 
+def paired(groups, shift):
+    sub = row_ids(8)
+    packed = roll_rows(groups[0], shift)
+    for g in (1, 2, 3):
+        packed = jnp.where(sub // 2 == g, roll_rows(groups[g], 2 * g + shift), packed)
+    return packed
+
+
 def state_packs(source, diag, last, first_black, residual, partial, diag2, swapped):
+    sub = row_ids(8)
     rows = source[0].shape[0]
     packs = []
-    for (a, ab, b, bb), here, near, far, ends in zip(
-        sides(swapped),
-        (slice(rows - 8, rows), slice(0, 8)),
-        (7, 0),
-        (6, 1),
-        ((4, 5, 6), (3, 2, 1)),
+    for (a, ab, b, bb), here, near, far, step in zip(
+        sides(swapped), (slice(rows - 8, rows), slice(0, 8)), (7, 0), (6, 1), (-1, 1)
     ):
         s, d, v = ([x[here] for x in group] for group in (source, diag, last))
         part, d2 = partial[here], diag2[here]
-        pack0 = [(x, near) for x in s + d]
-        pack1 = [
-            (first_black[ab][here], near),
-            (s[bb] + v[a], far),
-            (d[bb], far),
-            (first_black[bb][here], far),
-            (v[b], far),
-            (s[b] - d[b] * v[b] + v[ab], far),
-            (residual[a][here] - v[bb], far),
-            (part * inverse_of(d2), ends[0]),
+        beside = [
+            s[bb] + v[a],
+            d[bb],
+            first_black[bb][here],
+            v[b],
+            s[b] - d[b] * v[b] + v[ab],
+            residual[a][here] - v[bb],
+            part,
+            roll_rows(d2, -step),
         ]
-        pack2 = [(part, ends[1]), (part, ends[2]), (d2, ends[1]), (d2, ends[2])]
-        packs.append((placed(pack0), placed(pack1), placed(pack2)))
+        groups = [jnp.where(sub == far, y, x) for x, y in zip(s + d, beside)]
+        shift = 2 if near == 7 else 0
+        more = jnp.where(sub == far, d2, first_black[ab][here])
+        more = jnp.where(sub == far + step, part, more)
+        more = jnp.where(sub == far + 2 * step, part * inverse_of(d2), more)
+        packs.append((paired(groups[:4], shift), paired(groups[4:], shift), more))
     return packs
 
 
@@ -852,14 +851,13 @@
         count = tiles1 + 1
         for i in (0, 1):
             to_mate[i * count + t], to_other[i * count + t] = chosen(odd, left[i], right[i])
-        pair = chosen(odd, left[2], right[2])
         if t % 2 == 0:
+            pair = chosen(odd, left[2], roll_rows(right[2], 4))
             shared[0] = pair
+        else:
+            pair = chosen(odd, roll_rows(left[2], 4), right[2])
+            pair = [jnp.where(sub < 4, x, y) for x, y in zip(shared[0], pair)]
         if t % 2 == 1 or virtual:
-            if t % 2 == 1:
-                pair = [
-                    jnp.where(sub < 4, x, roll_rows(y, 4)) for x, y in zip(shared[0], pair)
-                ]
             to_mate[2 * count + t // 2], to_other[2 * count + t // 2] = pair
 
     restrict(e0, e1, tiles1, rows1, edges, 16)
@@ -914,31 +912,33 @@
         fixed = [jnp.zeros((8, LANES), F32)] * 4
         more = jnp.zeros((8, LANES), F32)
         total = jnp.ones((8, LANES), F32)
-        third = 4 * (t % 2)
         for side, (a, ab, b, bb) in enumerate(sides(t == tiles)):
             near, far, step = (7, 6, -1) if side == 0 else (0, 1, 1)
+            first = 6 if side == 0 else 0
             pack0, pack1, pack2 = (pair[side] for pair in packs)
-
-            def put(group, q, at, pack, row):
-                group[q] = jnp.where(sub == at, roll_rows(pack, at - row), group[q])
+            groups = [
+                roll_rows(pack, first - 2 * g) for pack in (pack0, pack1) for g in range(4)
+            ]
+            pack2 = roll_rows(pack2, 4 * (t % 2) + (4 if side == 0 else 0))
+
+            def put(group, q, at, x):
+                group[q] = jnp.where(sub == at, x, group[q])
 
             for q in range(4):
-                put(source, q, near, pack0, q)
-                put(diag, q, near, pack0, 4 + q)
-            put(source, bb, far, pack1, 1)
-            put(diag, bb, far, pack1, 2)
-            put(source, b, far, pack1, 5)
-            diag[b] = jnp.where(sub == far, 0.0, diag[b])
-            put(source, a, far, pack1, 6)
-            put(fixed, ab, near, pack1, 0)
-            put(fixed, bb, far, pack1, 3)
-            put(fixed, b, far, pack1, 4)
-            for at, pack, row in (
-                (far + 2 * step, pack1, 7), (far + step, pack2, third), (far, pack2, third + 1)
-            ):
-                more = jnp.where(sub == at, roll_rows(pack, at - row), more)
-            for at, row in ((far + step, third + 2), (far, third + 3)):
-                total = jnp.where(sub == at, roll_rows(pack2, at - row), total)
+                put(source, q, near, groups[q])
+                put(diag, q, near, groups[4 + q])
+            put(source, bb, far, groups[0])
+            put(diag, bb, far, groups[1])
+            put(fixed, bb, far, groups[2])
+            put(fixed, b, far, groups[3])
+            put(source, b, far, groups[4])
+            put(diag, b, far, 0.0)
+            put(source, a, far, groups[5])
+            put(fixed, ab, near, pack2)
+            more = jnp.where(sub == far, groups[6], more)
+            more = jnp.where((sub == far + step) | (sub == far + 2 * step), pack2, more)
+            total = jnp.where(sub == far, pack2, total)
+            total = jnp.where(sub == far + step, roll_rows(groups[7], step), total)
             for q in range(4):
                 known = (sub == near) | (sub == far) if q == bb else sub == near
                 inverse[q] = jnp.where(known, inverse_of(diag[q]), inverse[q])

time: 28.3 us -> 28.3 us (level)
  no operation moved by 1% of the time
where the time goes in v16:
time: 28.3 us; the launch traced here: 28.1 us
  starting transfers between devices  13.2 us (47%)
  Pallas kernels  11.8 us (42%)
  waiting for transfers between devices  2.46 us (9%)
  between operations  0.72 us (3%)
    ppermute x6, starting transfers between devices, swapped_with(): return lax.ppermute(x, 'lon', pairs + [(b, a) for a, b in pairs])  13 us
    pallas_call x6, Pallas kernels, call(): pl.pallas_call(kernel, out_shape=[jax.ShapeDtypeStruct(shape, F32) for sh...  11.8 us
    ppermute x6, waiting for transfers between devices, swapped_with(): return lax.ppermute(x, 'lon', pairs + [(b, a) for a, b in pairs])  2.46 us
  transfers between devices with their start and end apart: 7, of which 2 were waited for; matrix products, arithmetic and copies ran while one was open for 0% of the time, Pallas kernels for 13%

profile of v16, /device:TPU:0, one launch (start us, length us, event | category | flops | bytes accessed | tf_op | source)
XLA Modules:
  0.0 28.1 jit_solution(8404201862529568476)
XLA Ops:
  0.6 0.0 copy-start.2
  0.6 0.0 copy-start.1
  0.7 0.0 copy-start
  0.7 2.1 %shard_map.58 = (f32[2,32,8,128]{3,2,1,0:T(8,128)S(1)}, f32[2,32,8,128]{3,2,1,0:T(8,128)S(1)}, f32[2,8,128]{2,1,0:T(8,128)S(1)}) custom-call(f32[64,8192]{1,0:T(8,128)} %right_ref.5, bf16[64,8192]{1,0:T(8,128)(2,1)} %weight_ref.5, s32[2,256]{1,0:T(2,128)} %flag_ref.5), custom_call_target="tpu_custom_call" | custom-call | tf_op jit(solution)/shard_map/pallas_call | solution.py:1044
  2.8 5.5 %collective-permute-start = (f32[2,32,8,128]{3,2,1,0:T(8,128)S(1)}, f32[2,32,8,128]{3,2,1,0:T(8,128)S(1)}, u32[]{:S(2)}, u32[]{:S(2)}) collective-permute-start(f32[2,32,8,128]{3,2,1,0:T(8,128)S(1)} %get-tuple-element.28), channel_id=1, source_target_pairs={{0,15},{2,1},{4,3},{6,5},{8,7},{10,9},{12,11},{14,13},{15,0},{1,2}... | collective-permute-start | bytes 786440 | tf_op jit(solution)/shard_map/ppermute | solution.py:1057
  8.3 0.0 collective-permute-start.1
  8.3 0.0 copy-done.2
  8.3 0.0 copy-done.1
  8.3 0.0 copy-done
  8.3 0.4 %shard_map.59.polar_first = f32[2,32,128]{2,1,0:T(8,128)S(1)} custom-call(f32[64,8192]{1,0:T(8,128)S(1)} %copy-done, bf16[64,8192]{1,0:T(8,128)(2,1)S(1)} %copy-done.1, s32[2,256]{1,0:T(2,128)S(1)} %copy-done.2, f32[2,8,128]{2,1,0:T(8,128)S(1)} %get-tuple-element.21.edges_first), custom_call_target="tpu_custom_call" | custom-call | tf_op jit(solution)/shard_map/pallas_call | solution.py:1044
  8.7 0.2 collective-permute-start.2
  8.9 0.8 %collective-permute-start.4 = (f32[2,8,128]{2,1,0:T(8,128)S(1)}, f32[2,8,128]{2,1,0:T(8,128)S(1)}, u32[]{:S(2)}, u32[]{:S(2)}) collective-permute-start(f32[2,8,128]{2,1,0:T(8,128)S(1)} %get-tuple-element.21.edges_first), channel_id=1, source_target_pairs={{0,7},{2,9},{4,11},{6,13},{8,15},{10,1},{12,3},{14,5},{7,0},{9,2},... | collective-permute-start | bytes 24584 | tf_op jit(solution)/shard_map/ppermute | solution.py:1057
  9.7 2.8 %collective-permute-start.3 = (f32[2,8,128]{2,1,0:T(8,128)S(1)}, f32[2,8,128]{2,1,0:T(8,128)S(1)}, u32[]{:S(2)}, u32[]{:S(2)}) collective-permute-start(f32[2,8,128]{2,1,0:T(8,128)S(1)} %get-tuple-element.21.edges_first), channel_id=1, source_target_pairs={{0,9},{2,11},{4,13},{6,15},{8,1},{10,3},{12,5},{14,7},{9,0},{11,2}... | collective-permute-start | bytes 24584 | tf_op jit(solution)/shard_map/ppermute | solution.py:1057
  12.6 1.5 %shard_map.60 = (f32[2,32,64,128]{3,2,1,0:T(8,128)S(1)}, f32[2,32,64,128]{3,2,1,0:T(8,128)S(1)}, f32[2,32,64,128]{3,2,1,0:T(8,128)S(1)}, f32[4,16,16,128]{3,2,1,...) custom-call(f32[64,8192]{1,0:T(8,128)S(1)} %copy-done, bf16[64,8192]{1,0:T(8,128)(2,1)S(1)} %copy-done.1, ...), custom_call_target="tpu_custom_call" | custom-call | tf_op jit(solution)/shard_map/pallas_call | solution.py:1044
  14.1 0.0 collective-permute-done.4.corner_far
  14.1 0.2 collective-permute-done.3.corner_near
  14.3 0.0 collective-permute-done.2.polar_ref
  14.3 0.0 collective-permute-done.from_other
  14.3 0.0 collective-permute-done.1.from_mate
  14.3 3.9 %shard_map.61 = (f32[2,32,80,128]{3,2,1,0:T(8,128)S(1)}, f32[4,17,16,128]{3,2,1,0:T(8,128)S(1)}, f32[4,16,128]{2,1,0:T(8,128)S(1)}, f32[16,128]{1,0:T(8,128)S(1)...) custom-call(f32[2,32,64,128]{3,2,1,0:T(8,128)S(1)} %get-tuple-element.22.s_ref, ...), custom_call_target="tpu_custom_call" | custom-call | tf_op jit(solution)/shard_map/pallas_call | solution.py:1044
  18.2 3.8 %collective-permute-start.5 = (f32[43,8,128]{2,1,0:T(8,128)S(1)}, f32[43,8,128]{2,1,0:T(8,128)S(1)}, u32[]{:S(2)}, u32[]{:S(2)}) collective-permute-start(f32[43,8,128]{2,1,0:T(8,128)S(1)} %get-tuple-element.35), channel_id=1, source_target_pairs={{0,15},{2,1},{4,3},{6,5},{8,7},{10,9},{12,11},{14,13},{15,0},{1,2}... | collective-permute-start | bytes 528392 | tf_op jit(solution)/shard_map/ppermute | solution.py:1057
  22.0 0.0 collective-permute-start.6
  22.0 1.7 %shard_map.62 = f32[64,8192]{1,0:T(8,128)} custom-call(f32[2,32,80,128]{3,2,1,0:T(8,128)S(1)} %get-tuple-element.30.r_ref), custom_call_target="tpu_custom_call" | custom-call | tf_op jit(solution)/shard_map/pallas_call | solution.py:1044
  23.7 2.3 %collective-permute-done.5.from_other = f32[43,8,128]{2,1,0:T(8,128)S(1)} collective-permute-done((f32[43,8,128]{2,1,0:T(8,128)S(1)}, f32[43,8,128]{2,1,0:T(8,128)S(1)}, u32[]{:S(2)}, u32[]{:S(2)}) %collective-permute-start.5) | collective-permute-done | bytes 176160 | tf_op jit(solution)/shard_map/ppermute | solution.py:1057
  26.0 0.0 collective-permute-done.6.from_mate
  26.0 2.2 %shard_map.63 = (f32[16,2048]{1,0:T(8,128)}, f32[16,2048]{1,0:T(8,128)}) custom-call(f32[4,17,16,128]{3,2,1,0:T(8,128)S(1)} %get-tuple-element.31.s_ref, f32[4,16,16,128]{3,2,1,0:T(8,128)S(1)} %get-tuple-element.25.d1_ref.d_ref, f32[4,16,16,128]{3,2,1,0:T(8,128)S(1)} %get-tuple-element.26.i1_ref.i_ref, f32[4,16,128]{2,1,0:T(8,128)S(1)} %get-tuple-element.32.d_virtual, ...), custom_call_target="tpu_custom_call" | custom-call | tf_op jit(solution)/shard_map/pallas_call | solution.py:1044
Async XLA Ops:
  0.6 7.6 %copy-start.2 = (s32[2,256]{1,0:T(2,128)S(1)}, s32[2,256]{1,0:T(2,128)}, u32[]{:S(2)}) copy-start(s32[2,256]{1,0:T(2,128)} %flag_ref.5) | copy-start | bytes 6148
  0.6 7.6 %copy-start.1 = (bf16[64,8192]{1,0:T(8,128)(2,1)S(1)}, bf16[64,8192]{1,0:T(8,128)(2,1)}, u32[]{:S(2)}) copy-start(bf16[64,8192]{1,0:T(8,128)(2,1)} %weight_ref.5) | copy-start | bytes 3145732
  0.7 7.6 %copy-start = (f32[64,8192]{1,0:T(8,128)S(1)}, f32[64,8192]{1,0:T(8,128)}, u32[]{:S(2)}) copy-start(f32[64,8192]{1,0:T(8,128)} %right_ref.5) | copy-start | bytes 6291460
  2.8 11.5 %collective-permute-start = (f32[2,32,8,128]{3,2,1,0:T(8,128)S(1)}, f32[2,32,8,128]{3,2,1,0:T(8,128)S(1)}, u32[]{:S(2)}, u32[]{:S(2)}) collective-permute-start(f32[2,32,8,128]{3,2,1,0:T(8,128)S(1)} %get-tuple-element.28), channel_id=1, source_target_pairs={{0,15},{2,1},{4,3},{6,5},{8,7},{10,9},{12,11},{14,13},{15,0},{1,2}... | collective-permute-start | bytes 786440 | tf_op jit(solution)/shard_map/ppermute | solution.py:1057
  8.3 6.0 %collective-permute-start.1 = (f32[2,32,8,128]{3,2,1,0:T(8,128)S(1)}, f32[2,32,8,128]{3,2,1,0:T(8,128)S(1)}, u32[]{:S(2)}, u32[]{:S(2)}) collective-permute-start(f32[2,32,8,128]{3,2,1,0:T(8,128)S(1)} %get-tuple-element.29), channel_id=1, source_target_pairs={{0,1},{2,3},{4,5},{6,7},{8,9},{10,11},{12,13},{14,15},{1,0},{3,2},... | collective-permute-start | bytes 786440 | tf_op jit(solution)/shard_map/ppermute | solution.py:1057
  8.7 5.5 %collective-permute-start.2 = (f32[2,32,128]{2,1,0:T(8,128)S(1)}, f32[2,32,128]{2,1,0:T(8,128)S(1)}, u32[]{:S(2)}, u32[]{:S(2)}) collective-permute-start(f32[2,32,128]{2,1,0:T(8,128)S(1)} %shard_map.59.polar_first), channel_id=1, source_target_pairs={{0,8},{1,9},{2,10},{3,11},{4,12},{5,13},{6,14},{7,15},{8,0},{9,1},... | collective-permute-start | bytes 98312 | tf_op jit(solution)/shard_map/ppermute | solution.py:1094
  8.9 5.1 %collective-permute-start.4 = (f32[2,8,128]{2,1,0:T(8,128)S(1)}, f32[2,8,128]{2,1,0:T(8,128)S(1)}, u32[]{:S(2)}, u32[]{:S(2)}) collective-permute-start(f32[2,8,128]{2,1,0:T(8,128)S(1)} %get-tuple-element.21.edges_first), channel_id=1, source_target_pairs={{0,7},{2,9},{4,11},{6,13},{8,15},{10,1},{12,3},{14,5},{7,0},{9,2},... | collective-permute-start | bytes 24584 | tf_op jit(solution)/shard_map/ppermute | solution.py:1057
  9.7 4.5 %collective-permute-start.3 = (f32[2,8,128]{2,1,0:T(8,128)S(1)}, f32[2,8,128]{2,1,0:T(8,128)S(1)}, u32[]{:S(2)}, u32[]{:S(2)}) collective-permute-start(f32[2,8,128]{2,1,0:T(8,128)S(1)} %get-tuple-element.21.edges_first), channel_id=1, source_target_pairs={{0,9},{2,11},{4,13},{6,15},{8,1},{10,3},{12,5},{14,7},{9,0},{11,2}... | collective-permute-start | bytes 24584 | tf_op jit(solution)/shard_map/ppermute | solution.py:1057
  18.2 7.7 %collective-permute-start.5 = (f32[43,8,128]{2,1,0:T(8,128)S(1)}, f32[43,8,128]{2,1,0:T(8,128)S(1)}, u32[]{:S(2)}, u32[]{:S(2)}) collective-permute-start(f32[43,8,128]{2,1,0:T(8,128)S(1)} %get-tuple-element.35), channel_id=1, source_target_pairs={{0,15},{2,1},{4,3},{6,5},{8,7},{10,9},{12,11},{14,13},{15,0},{1,2}... | collective-permute-start | bytes 528392 | tf_op jit(solution)/shard_map/ppermute | solution.py:1057
  22.0 3.9 %collective-permute-start.6 = (f32[43,8,128]{2,1,0:T(8,128)S(1)}, f32[43,8,128]{2,1,0:T(8,128)S(1)}, u32[]{:S(2)}, u32[]{:S(2)}) collective-permute-start(f32[43,8,128]{2,1,0:T(8,128)S(1)} %get-tuple-element.36), channel_id=1, source_target_pairs={{0,1},{2,3},{4,5},{6,7},{8,9},{10,11},{12,13},{14,15},{1,0},{3,2},... | collective-permute-start | bytes 528392 | tf_op jit(solution)/shard_map/ppermute | solution.py:1057

commit v17 on v16

--- a/solution.py
+++ b/solution.py
@@ -296,12 +296,13 @@
 ):
     columns, height = right_ref.shape
     tiles = height // 256
+    half = height // 2
     pairs = [(flag_ref, flags)]
-    for i, (src, dst, size) in enumerate(
-        ((right_ref, edge_s, 8), (weight_ref, edge_w, 16))
-    ):
-        pairs.append((src.at[pl.ds(0, size)], dst.at[pl.ds(0, size)]))
-        pairs.append((src.at[pl.ds(columns - size, size)], dst.at[pl.ds(size, size)]))
+    for start in (0, half):
+        part = pl.ds(start, half)
+        for src, dst, size in ((right_ref, edge_s, 8), (weight_ref, edge_w, 16)):
+            for at, to in ((0, 0), (columns - size, size)):
+                pairs.append((src.at[pl.ds(at, size), part], dst.at[pl.ds(to, size), part]))
     copies = [
         pltpu.make_async_copy(src, dst, sems.at[i]) for i, (src, dst) in enumerate(pairs)
     ]
@@ -312,28 +313,31 @@
     flag_cols = flag_ref.shape[0]
     copies[0].wait()
     scale_ref[...] = seam_scales(flags[...], range(tiles))
-    for copy in copies[1:]:
-        copy.wait()
     sub = row_ids(8)
-    lanes = [slice(c * 256, (c + 1) * 256) for c in range(tiles)]
-    source, weight = moved(
-        jnp.concatenate([edge_s[:, w] for w in lanes], 0),
-        matrix,
-        jnp.concatenate([edge_w[:, w] for w in lanes], 0),
-    )
-    weight = weight.reshape(tiles, 32, 256)
-    weight = jnp.concatenate([weight[:, :8], weight[:, 24:]], 1).reshape(tiles * 16, 256)
-    source = quarters_of(source, temp_s)
-    weight = quarters_of(weight, temp_w)
+    count = tiles // 2
     found = []
-    for c in range(tiles):
-        here = slice(c * 8, (c + 1) * 8)
-        scales = scale_ref[c]
-        scale = jnp.where(sub < 4, scales[:1], scales[flag_cols - 1 : flag_cols])
-        pair = [x[here] for x in source], [4.0 + w[here] * scale for w in weight]
-        store_edges(c, edge_packs(*pair, False), odd, to_mate, to_other)
-        if c in (0, tiles - 1):
-            found.append(pair)
+    for part in (0, 1):
+        for copy in copies[1 + 4 * part : 5 + 4 * part]:
+            copy.wait()
+        chunks = range(part * count, (part + 1) * count)
+        lanes = [slice(c * 256, (c + 1) * 256) for c in chunks]
+        source, weight = moved(
+            jnp.concatenate([edge_s[:, w] for w in lanes], 0),
+            matrix,
+            jnp.concatenate([edge_w[:, w] for w in lanes], 0),
+        )
+        weight = weight.reshape(count, 32, 256)
+        weight = jnp.concatenate([weight[:, :8], weight[:, 24:]], 1).reshape(count * 16, 256)
+        source = quarters_of(source, temp_s.at[part])
+        weight = quarters_of(weight, temp_w.at[part])
+        for i, c in enumerate(chunks):
+            here = slice(i * 8, (i + 1) * 8)
+            scales = scale_ref[c]
+            scale = jnp.where(sub < 4, scales[:1], scales[flag_cols - 1 : flag_cols])
+            pair = [x[here] for x in source], [4.0 + w[here] * scale for w in weight]
+            store_edges(c, edge_packs(*pair, False), odd, to_mate, to_other)
+            if c in (0, tiles - 1):
+                found.append(pair)
     both = mirrored_ends(*found)
     for pc in (0, 1):
         corner = both[8 * pc : 8 * (pc + 1)]
@@ -893,6 +897,7 @@
     s_ref, d_ref, i_ref, d_virtual, d2_ref, d2_virtual, s2_ref, from_other, from_mate,
     solution_ref, residual_ref,
     v0, v1, v2, v3, c0, c1, hs, hd, hi, part, fixes, rest1, rest2, s, d, inv, va, vb,
+    solution_buf, residual_buf, sems,
 ):
     v = [v0, v1, v2, v3]
     tiles, own = d_ref.shape[1], d_ref.shape[2]
@@ -1024,13 +1029,25 @@
 
         scan(old, relax)
 
+    for t in range(tiles):
+        solution_buf[:, t * LANES : (t + 1) * LANES] = vb[t, :own]
+    copies = [
+        pltpu.make_async_copy(src, dst, sems.at[i])
+        for i, (src, dst) in enumerate(
+            ((solution_buf, solution_ref), (residual_buf, residual_ref))
+        )
+    ]
+    copies[0].start()
+
     def finish(t, x, beside):
         if t < tiles:
             where = slice(t * LANES, (t + 1) * LANES)
-            solution_ref[:, where] = x[:own]
-            residual_ref[:, where] = (s[t] - (d[t] * x - beside))[:own]
+            residual_buf[:, where] = (s[t] - (d[t] * x - beside))[:own]
 
     scan(vb, finish)
+    copies[1].start()
+    for copy in copies:
+        copy.wait()
 
 
 VMEM = pl.BlockSpec(memory_space=pltpu.VMEM)
@@ -1071,7 +1088,7 @@
     natural = (2, tiles, columns, LANES)
     padded = (2, tiles, columns + 16, LANES)
     quarters1 = (4, tiles1, rows1, LANES)
-    split = (2, 16 * tiles, LANES)
+    split = (2, 2, 8 * tiles, LANES)
     to_mate, to_other, corner = call(
         edge_kernel,
         [(2, tiles, 8, LANES), (2, tiles, 8, LANES), (2, 8, LANES)],
@@ -1081,7 +1098,7 @@
             pltpu.with_memory_space_constraint(x, pltpu.HBM)
             for x in (right_side, texel_weight, seam_flags)
         ],
-        sems=(5,), far_in=3,
+        sems=(9,), far_in=3,
     )
     from_mate, from_other = swapped_edges(to_mate, to_other)
     corner_far = swapped_with(corner, half_turn - 1)
@@ -1136,8 +1153,10 @@
         + [(4, tiles1 + 1, 16, LANES)] * 3
         + [(tiles1 + 1, 8, LANES), (4, tiles1 + 1, 8, LANES)]
         + [(tiles1, 16, LANES)] * 2
-        + [wide] * 5,
+        + [wide] * 5
+        + [(columns // 4, height // 4)] * 2,
         s1, d1, i1, d1_virtual, d2, d2_virtual, s2_own, from_other, from_mate,
+        sems=(2,), far_out=2,
     )
     return fine_residual, solution_2, residual_2
 

time: 28.3 us -> 28.6 us (1.011)
  Pallas kernels: 11.8 us -> 12.1 us
    pallas_call x6, Pallas kernels: 11.8 us -> 12.1 us  [call(): pl.pallas_call(kernel, out_shape=[jax.ShapeDtypeStruct(shape, F32) for sh...]
where the time goes in v17:
time: 28.6 us; the launch traced here: 28.5 us
  starting transfers between devices  13.2 us (46%)
  Pallas kernels  12.1 us (42%)
  waiting for transfers between devices  2.43 us (8%)
  between operations  0.72 us (3%)
    ppermute x6, starting transfers between devices, swapped_with(): return lax.ppermute(x, 'lon', pairs + [(b, a) for a, b in pairs])  12.9 us
    pallas_call x6, Pallas kernels, call(): pl.pallas_call(kernel, out_shape=[jax.ShapeDtypeStruct(shape, F32) for sh...  12.1 us
    ppermute x6, waiting for transfers between devices, swapped_with(): return lax.ppermute(x, 'lon', pairs + [(b, a) for a, b in pairs])  2.43 us
  transfers between devices with their start and end apart: 7, of which 2 were waited for; matrix products, arithmetic and copies ran while one was open for 0% of the time, Pallas kernels for 13%

profile of v17, /device:TPU:0, one launch (start us, length us, event | category | flops | bytes accessed | tf_op | source)
XLA Modules:
  0.0 28.5 jit_solution(17815970626163953945)
XLA Ops:
  0.6 0.0 copy-start.2
  0.6 0.0 copy-start.1
  0.7 0.0 copy-start
  0.7 2.4 %shard_map.58 = (f32[2,32,8,128]{3,2,1,0:T(8,128)S(1)}, f32[2,32,8,128]{3,2,1,0:T(8,128)S(1)}, f32[2,8,128]{2,1,0:T(8,128)S(1)}) custom-call(f32[64,8192]{1,0:T(8,128)} %right_ref.5, bf16[64,8192]{1,0:T(8,128)(2,1)} %weight_ref.5, s32[2,256]{1,0:T(2,128)} %flag_ref.5), custom_call_target="tpu_custom_call" | custom-call | tf_op jit(solution)/shard_map/pallas_call | solution.py:1061
  3.1 5.5 %collective-permute-start = (f32[2,32,8,128]{3,2,1,0:T(8,128)S(1)}, f32[2,32,8,128]{3,2,1,0:T(8,128)S(1)}, u32[]{:S(2)}, u32[]{:S(2)}) collective-permute-start(f32[2,32,8,128]{3,2,1,0:T(8,128)S(1)} %get-tuple-element.28), channel_id=1, source_target_pairs={{0,15},{2,1},{4,3},{6,5},{8,7},{10,9},{12,11},{14,13},{15,0},{1,2}... | collective-permute-start | bytes 786440 | tf_op jit(solution)/shard_map/ppermute | solution.py:1074
  8.6 0.0 collective-permute-start.1
  8.6 0.0 copy-done.2
  8.6 0.0 copy-done.1
  8.6 0.0 copy-done
  8.6 0.4 %shard_map.59.polar_first = f32[2,32,128]{2,1,0:T(8,128)S(1)} custom-call(f32[64,8192]{1,0:T(8,128)S(1)} %copy-done, bf16[64,8192]{1,0:T(8,128)(2,1)S(1)} %copy-done.1, s32[2,256]{1,0:T(2,128)S(1)} %copy-done.2, f32[2,8,128]{2,1,0:T(8,128)S(1)} %get-tuple-element.21.edges_first), custom_call_target="tpu_custom_call" | custom-call | tf_op jit(solution)/shard_map/pallas_call | solution.py:1061
  9.1 0.2 collective-permute-start.2
  9.3 0.8 %collective-permute-start.4 = (f32[2,8,128]{2,1,0:T(8,128)S(1)}, f32[2,8,128]{2,1,0:T(8,128)S(1)}, u32[]{:S(2)}, u32[]{:S(2)}) collective-permute-start(f32[2,8,128]{2,1,0:T(8,128)S(1)} %get-tuple-element.21.edges_first), channel_id=1, source_target_pairs={{0,7},{2,9},{4,11},{6,13},{8,15},{10,1},{12,3},{14,5},{7,0},{9,2},... | collective-permute-start | bytes 24584 | tf_op jit(solution)/shard_map/ppermute | solution.py:1074
  10.1 2.8 %collective-permute-start.3 = (f32[2,8,128]{2,1,0:T(8,128)S(1)}, f32[2,8,128]{2,1,0:T(8,128)S(1)}, u32[]{:S(2)}, u32[]{:S(2)}) collective-permute-start(f32[2,8,128]{2,1,0:T(8,128)S(1)} %get-tuple-element.21.edges_first), channel_id=1, source_target_pairs={{0,9},{2,11},{4,13},{6,15},{8,1},{10,3},{12,5},{14,7},{9,0},{11,2}... | collective-permute-start | bytes 24584 | tf_op jit(solution)/shard_map/ppermute | solution.py:1074
  12.9 1.5 %shard_map.60 = (f32[2,32,64,128]{3,2,1,0:T(8,128)S(1)}, f32[2,32,64,128]{3,2,1,0:T(8,128)S(1)}, f32[2,32,64,128]{3,2,1,0:T(8,128)S(1)}, f32[4,16,16,128]{3,2,1,...) custom-call(f32[64,8192]{1,0:T(8,128)S(1)} %copy-done, bf16[64,8192]{1,0:T(8,128)(2,1)S(1)} %copy-done.1, ...), custom_call_target="tpu_custom_call" | custom-call | tf_op jit(solution)/shard_map/pallas_call | solution.py:1061
  14.4 0.0 collective-permute-done.4.corner_far
  14.4 0.2 collective-permute-done.3.corner_near
  14.6 0.0 collective-permute-done.2.polar_ref
  14.6 0.0 collective-permute-done.from_other
  14.6 0.0 collective-permute-done.1.from_mate
  14.6 3.9 %shard_map.61 = (f32[2,32,80,128]{3,2,1,0:T(8,128)S(1)}, f32[4,17,16,128]{3,2,1,0:T(8,128)S(1)}, f32[4,16,128]{2,1,0:T(8,128)S(1)}, f32[16,128]{1,0:T(8,128)S(1)...) custom-call(f32[2,32,64,128]{3,2,1,0:T(8,128)S(1)} %get-tuple-element.22.s_ref, ...), custom_call_target="tpu_custom_call" | custom-call | tf_op jit(solution)/shard_map/pallas_call | solution.py:1061
  18.5 3.8 %collective-permute-start.5 = (f32[43,8,128]{2,1,0:T(8,128)S(1)}, f32[43,8,128]{2,1,0:T(8,128)S(1)}, u32[]{:S(2)}, u32[]{:S(2)}) collective-permute-start(f32[43,8,128]{2,1,0:T(8,128)S(1)} %get-tuple-element.35), channel_id=1, source_target_pairs={{0,15},{2,1},{4,3},{6,5},{8,7},{10,9},{12,11},{14,13},{15,0},{1,2}... | collective-permute-start | bytes 528392 | tf_op jit(solution)/shard_map/ppermute | solution.py:1074
  22.4 0.0 collective-permute-start.6
  22.4 1.7 %shard_map.62 = f32[64,8192]{1,0:T(8,128)} custom-call(f32[2,32,80,128]{3,2,1,0:T(8,128)S(1)} %get-tuple-element.30.r_ref), custom_call_target="tpu_custom_call" | custom-call | tf_op jit(solution)/shard_map/pallas_call | solution.py:1061
  24.0 2.2 %collective-permute-done.5.from_other = f32[43,8,128]{2,1,0:T(8,128)S(1)} collective-permute-done((f32[43,8,128]{2,1,0:T(8,128)S(1)}, f32[43,8,128]{2,1,0:T(8,128)S(1)}, u32[]{:S(2)}, u32[]{:S(2)}) %collective-permute-start.5) | collective-permute-done | bytes 176160 | tf_op jit(solution)/shard_map/ppermute | solution.py:1074
  26.3 0.0 collective-permute-done.6.from_mate
  26.3 2.2 %shard_map.63 = (f32[16,2048]{1,0:T(8,128)}, f32[16,2048]{1,0:T(8,128)}) custom-call(f32[4,17,16,128]{3,2,1,0:T(8,128)S(1)} %get-tuple-element.31.s_ref, f32[4,16,16,128]{3,2,1,0:T(8,128)S(1)} %get-tuple-element.25.d1_ref.d_ref, f32[4,16,16,128]{3,2,1,0:T(8,128)S(1)} %get-tuple-element.26.i1_ref.i_ref, f32[4,16,128]{2,1,0:T(8,128)S(1)} %get-tuple-element.32.d_virtual, ...), custom_call_target="tpu_custom_call" | custom-call | tf_op jit(solution)/shard_map/pallas_call | solution.py:1061
Async XLA Ops:
  0.6 8.0 %copy-start.2 = (s32[2,256]{1,0:T(2,128)S(1)}, s32[2,256]{1,0:T(2,128)}, u32[]{:S(2)}) copy-start(s32[2,256]{1,0:T(2,128)} %flag_ref.5) | copy-start | bytes 6148
  0.6 8.0 %copy-start.1 = (bf16[64,8192]{1,0:T(8,128)(2,1)S(1)}, bf16[64,8192]{1,0:T(8,128)(2,1)}, u32[]{:S(2)}) copy-start(bf16[64,8192]{1,0:T(8,128)(2,1)} %weight_ref.5) | copy-start | bytes 3145732
  0.7 8.0 %copy-start = (f32[64,8192]{1,0:T(8,128)S(1)}, f32[64,8192]{1,0:T(8,128)}, u32[]{:S(2)}) copy-start(f32[64,8192]{1,0:T(8,128)} %right_ref.5) | copy-start | bytes 6291460
  3.1 11.5 %collective-permute-start = (f32[2,32,8,128]{3,2,1,0:T(8,128)S(1)}, f32[2,32,8,128]{3,2,1,0:T(8,128)S(1)}, u32[]{:S(2)}, u32[]{:S(2)}) collective-permute-start(f32[2,32,8,128]{3,2,1,0:T(8,128)S(1)} %get-tuple-element.28), channel_id=1, source_target_pairs={{0,15},{2,1},{4,3},{6,5},{8,7},{10,9},{12,11},{14,13},{15,0},{1,2}... | collective-permute-start | bytes 786440 | tf_op jit(solution)/shard_map/ppermute | solution.py:1074
  8.6 6.0 %collective-permute-start.1 = (f32[2,32,8,128]{3,2,1,0:T(8,128)S(1)}, f32[2,32,8,128]{3,2,1,0:T(8,128)S(1)}, u32[]{:S(2)}, u32[]{:S(2)}) collective-permute-start(f32[2,32,8,128]{3,2,1,0:T(8,128)S(1)} %get-tuple-element.29), channel_id=1, source_target_pairs={{0,1},{2,3},{4,5},{6,7},{8,9},{10,11},{12,13},{14,15},{1,0},{3,2},... | collective-permute-start | bytes 786440 | tf_op jit(solution)/shard_map/ppermute | solution.py:1074
  9.1 5.5 %collective-permute-start.2 = (f32[2,32,128]{2,1,0:T(8,128)S(1)}, f32[2,32,128]{2,1,0:T(8,128)S(1)}, u32[]{:S(2)}, u32[]{:S(2)}) collective-permute-start(f32[2,32,128]{2,1,0:T(8,128)S(1)} %shard_map.59.polar_first), channel_id=1, source_target_pairs={{0,8},{1,9},{2,10},{3,11},{4,12},{5,13},{6,14},{7,15},{8,0},{9,1},... | collective-permute-start | bytes 98312 | tf_op jit(solution)/shard_map/ppermute | solution.py:1111
  9.3 5.1 %collective-permute-start.4 = (f32[2,8,128]{2,1,0:T(8,128)S(1)}, f32[2,8,128]{2,1,0:T(8,128)S(1)}, u32[]{:S(2)}, u32[]{:S(2)}) collective-permute-start(f32[2,8,128]{2,1,0:T(8,128)S(1)} %get-tuple-element.21.edges_first), channel_id=1, source_target_pairs={{0,7},{2,9},{4,11},{6,13},{8,15},{10,1},{12,3},{14,5},{7,0},{9,2},... | collective-permute-start | bytes 24584 | tf_op jit(solution)/shard_map/ppermute | solution.py:1074
  10.1 4.5 %collective-permute-start.3 = (f32[2,8,128]{2,1,0:T(8,128)S(1)}, f32[2,8,128]{2,1,0:T(8,128)S(1)}, u32[]{:S(2)}, u32[]{:S(2)}) collective-permute-start(f32[2,8,128]{2,1,0:T(8,128)S(1)} %get-tuple-element.21.edges_first), channel_id=1, source_target_pairs={{0,9},{2,11},{4,13},{6,15},{8,1},{10,3},{12,5},{14,7},{9,0},{11,2}... | collective-permute-start | bytes 24584 | tf_op jit(solution)/shard_map/ppermute | solution.py:1074
  18.5 7.7 %collective-permute-start.5 = (f32[43,8,128]{2,1,0:T(8,128)S(1)}, f32[43,8,128]{2,1,0:T(8,128)S(1)}, u32[]{:S(2)}, u32[]{:S(2)}) collective-permute-start(f32[43,8,128]{2,1,0:T(8,128)S(1)} %get-tuple-element.35), channel_id=1, source_target_pairs={{0,15},{2,1},{4,3},{6,5},{8,7},{10,9},{12,11},{14,13},{15,0},{1,2}... | collective-permute-start | bytes 528392 | tf_op jit(solution)/shard_map/ppermute | solution.py:1074
  22.4 3.9 %collective-permute-start.6 = (f32[43,8,128]{2,1,0:T(8,128)S(1)}, f32[43,8,128]{2,1,0:T(8,128)S(1)}, u32[]{:S(2)}, u32[]{:S(2)}) collective-permute-start(f32[43,8,128]{2,1,0:T(8,128)S(1)} %get-tuple-element.36), channel_id=1, source_target_pairs={{0,1},{2,3},{4,5},{6,7},{8,9},{10,11},{12,13},{14,15},{1,0},{3,2},... | collective-permute-start | bytes 528392 | tf_op jit(solution)/shard_map/ppermute | solution.py:1074

commit v18 on v16

--- a/solution.py
+++ b/solution.py
@@ -291,17 +291,20 @@
 
 def edge_kernel(
     right_ref, weight_ref, flag_ref,
-    to_mate, to_other, corner_ref,
-    edge_s, edge_w, flags, temp_s, temp_w, scale_ref, sems,
+    right_here, weight_here, to_mate, to_other, corner_ref,
+    flags, temp_s, temp_w, scale_ref, sems,
 ):
     columns, height = right_ref.shape
     tiles = height // 256
     pairs = [(flag_ref, flags)]
-    for i, (src, dst, size) in enumerate(
-        ((right_ref, edge_s, 8), (weight_ref, edge_w, 16))
-    ):
-        pairs.append((src.at[pl.ds(0, size)], dst.at[pl.ds(0, size)]))
-        pairs.append((src.at[pl.ds(columns - size, size)], dst.at[pl.ds(size, size)]))
+    inputs = (right_ref, right_here, 8), (weight_ref, weight_here, 16)
+    for src, dst, size in inputs:
+        for start in (0, columns - size):
+            part = pl.ds(start, size)
+            pairs.append((src.at[part], dst.at[part]))
+    for src, dst, size in inputs:
+        part = pl.ds(size, columns - 2 * size)
+        pairs.append((src.at[part], dst.at[part]))
     copies = [
         pltpu.make_async_copy(src, dst, sems.at[i]) for i, (src, dst) in enumerate(pairs)
     ]
@@ -312,14 +315,18 @@
     flag_cols = flag_ref.shape[0]
     copies[0].wait()
     scale_ref[...] = seam_scales(flags[...], range(tiles))
-    for copy in copies[1:]:
+    for copy in copies[1:5]:
         copy.wait()
     sub = row_ids(8)
     lanes = [slice(c * 256, (c + 1) * 256) for c in range(tiles)]
+
+    def ends(size):
+        return slice(0, size), slice(columns - size, columns)
+
     source, weight = moved(
-        jnp.concatenate([edge_s[:, w] for w in lanes], 0),
+        jnp.concatenate([right_here[at, w] for w in lanes for at in ends(8)], 0),
         matrix,
-        jnp.concatenate([edge_w[:, w] for w in lanes], 0),
+        jnp.concatenate([weight_here[at, w] for w in lanes for at in ends(16)], 0),
     )
     weight = weight.reshape(tiles, 32, 256)
     weight = jnp.concatenate([weight[:, :8], weight[:, 24:]], 1).reshape(tiles * 16, 256)
@@ -336,8 +343,9 @@
             found.append(pair)
     both = mirrored_ends(*found)
     for pc in (0, 1):
-        corner = both[8 * pc : 8 * (pc + 1)]
-        corner_ref[pc] = corner
+        corner_ref[pc] = both[8 * pc : 8 * (pc + 1)]
+    for copy in copies[5:]:
+        copy.wait()
 
 
 def mirrored_ends(first, last):
@@ -1043,7 +1051,9 @@
         scratch.append(pltpu.SemaphoreType.DMA(sems))
     return pl.pallas_call(
         kernel,
-        out_shape=[jax.ShapeDtypeStruct(shape, F32) for shape in out_shapes],
+        out_shape=[
+            jax.ShapeDtypeStruct(x, F32) if isinstance(x, tuple) else x for x in out_shapes
+        ],
         in_specs=[HBM] * far_in + [VMEM] * (len(args) - far_in),
         out_specs=[HBM] * far_out + [VMEM] * (len(out_shapes) - far_out),
         scratch_shapes=scratch,
@@ -1072,16 +1082,16 @@
     padded = (2, tiles, columns + 16, LANES)
     quarters1 = (4, tiles1, rows1, LANES)
     split = (2, 16 * tiles, LANES)
-    to_mate, to_other, corner = call(
+    right_here, weight_here, to_mate, to_other, corner = call(
         edge_kernel,
-        [(2, tiles, 8, LANES), (2, tiles, 8, LANES), (2, 8, LANES)],
-        [(16, height), pltpu.VMEM((32, height), BF16)]
-        + [pltpu.VMEM(seam_flags.shape, jnp.int32), split, split, (tiles, 8, LANES)],
+        [(columns, height), jax.ShapeDtypeStruct((columns, height), BF16)]
+        + [(2, tiles, 8, LANES), (2, tiles, 8, LANES), (2, 8, LANES)],
+        [pltpu.VMEM(seam_flags.shape, jnp.int32), split, split, (tiles, 8, LANES)],
         *[
             pltpu.with_memory_space_constraint(x, pltpu.HBM)
             for x in (right_side, texel_weight, seam_flags)
         ],
-        sems=(5,), far_in=3,
+        sems=(7,), far_in=3,
     )
     from_mate, from_other = swapped_edges(to_mate, to_other)
     corner_far = swapped_with(corner, half_turn - 1)
@@ -1089,7 +1099,7 @@
     ends = (2, 2, columns, LANES)
     (polar_own,) = call(
         polar_kernel, [(2, rows, LANES)], [ends, ends],
-        right_side, texel_weight, seam_flags, corner,
+        right_here, weight_here, seam_flags, corner,
     )
     polar = lax.ppermute(
         polar_own, "lon", [(i, (i + half_turn) % (2 * half_turn)) for i in range(2 * half_turn)]
@@ -1098,7 +1108,7 @@
         bulk_kernel,
         [natural] * 3 + [quarters1, quarters1, quarters1[1:]],
         [(BATCH, columns, LANES), (tiles, 8, LANES), (tiles, rows, LANES), (BATCH, 2, rows, LANES)],
-        right_side, texel_weight, seam_flags, polar_own,
+        right_here, weight_here, seam_flags, polar_own,
     )
 
     def level_scratch(tiles, rows):

time: 28.3 us -> 28.1 us (level)
  no operation moved by 1% of the time
where the time goes in v18:
time: 28.1 us; the launch traced here: 28 us
  starting transfers between devices  13.2 us (47%)
  Pallas kernels  11.7 us (42%)
  waiting for transfers between devices  2.42 us (9%)
  between operations  0.69 us (2%)
    ppermute x6, starting transfers between devices, swapped_with(): return lax.ppermute(x, 'lon', pairs + [(b, a) for a, b in pairs])  12.9 us
    pallas_call x6, Pallas kernels, call(): pl.pallas_call(kernel, out_shape=[jax.ShapeDtypeStruct(x, F32) if isinsta...  11.7 us
    ppermute x6, waiting for transfers between devices, swapped_with(): return lax.ppermute(x, 'lon', pairs + [(b, a) for a, b in pairs])  2.42 us
  transfers between devices with their start and end apart: 7, of which 2 were waited for; matrix products, arithmetic and copies ran while one was open for 0% of the time, Pallas kernels for 13%

profile of v18, /device:TPU:0, one launch (start us, length us, event | category | flops | bytes accessed | tf_op | source)
XLA Modules:
  0.0 28.0 jit_solution(10343437544952352557)
XLA Ops:
  0.6 0.0 copy-start
  0.6 2.0 %shard_map.58 = (f32[64,8192]{1,0:T(8,128)S(1)}, bf16[64,8192]{1,0:T(8,128)(2,1)S(1)}, f32[2,32,8,128]{3,2,1,0:T(8,128)S(1)}, f32[2,32,8,128]{3,2,1,0:T(8,128)S(1)}, f32[2,8,128]{2,1,0:T(8,128)S(1)}) custom-call(f32[64,8192]{1,0:T(8,128)} %right_ref.1, bf16[64,8192]{1,0:T(8,128)(2,1)} %weight_ref.1, s32[2,256]{1,0:T(2,128)} %flag_ref.5), custom_call_target="tpu_custom_call" | custom-call | tf_op jit(solution)/shard_map/pallas_call | solution.py:1052
  2.6 5.5 %collective-permute-start = (f32[2,32,8,128]{3,2,1,0:T(8,128)S(1)}, f32[2,32,8,128]{3,2,1,0:T(8,128)S(1)}, u32[]{:S(2)}, u32[]{:S(2)}) collective-permute-start(f32[2,32,8,128]{3,2,1,0:T(8,128)S(1)} %get-tuple-element.32), channel_id=1, source_target_pairs={{0,15},{2,1},{4,3},{6,5},{8,7},{10,9},{12,11},{14,13},{15,0},{1,2}... | collective-permute-start | bytes 786440 | tf_op jit(solution)/shard_map/ppermute | solution.py:1067
  8.1 0.0 collective-permute-start.1
  8.1 0.0 copy-done
  8.1 0.4 %shard_map.59.polar_first = f32[2,32,128]{2,1,0:T(8,128)S(1)} custom-call(f32[64,8192]{1,0:T(8,128)S(1)} %get-tuple-element.23.right_ref, bf16[64,8192]{1,0:T(8,128)(2,1)S(1)} %get-tuple-element.24.weight_ref, s32[2,256]{1,0:T(2,128)S(1)} %copy-done, f32[2,8,128]{2,1,0:T(8,128)S(1)} %get-tuple-element.25.edges_first), custom_call_target="tpu_custom_call" | custom-call | tf_op jit(solution)/shard_map/pallas_call | solution.py:1052
  8.6 0.2 collective-permute-start.2
  8.8 0.8 %collective-permute-start.4 = (f32[2,8,128]{2,1,0:T(8,128)S(1)}, f32[2,8,128]{2,1,0:T(8,128)S(1)}, u32[]{:S(2)}, u32[]{:S(2)}) collective-permute-start(f32[2,8,128]{2,1,0:T(8,128)S(1)} %get-tuple-element.25.edges_first), channel_id=1, source_target_pairs={{0,7},{2,9},{4,11},{6,13},{8,15},{10,1},{12,3},{14,5},{7,0},{9,2},... | collective-permute-start | bytes 24584 | tf_op jit(solution)/shard_map/ppermute | solution.py:1067
  9.6 2.8 %collective-permute-start.3 = (f32[2,8,128]{2,1,0:T(8,128)S(1)}, f32[2,8,128]{2,1,0:T(8,128)S(1)}, u32[]{:S(2)}, u32[]{:S(2)}) collective-permute-start(f32[2,8,128]{2,1,0:T(8,128)S(1)} %get-tuple-element.25.edges_first), channel_id=1, source_target_pairs={{0,9},{2,11},{4,13},{6,15},{8,1},{10,3},{12,5},{14,7},{9,0},{11,2}... | collective-permute-start | bytes 24584 | tf_op jit(solution)/shard_map/ppermute | solution.py:1067
  12.4 1.5 %shard_map.60 = (f32[2,32,64,128]{3,2,1,0:T(8,128)S(1)}, f32[2,32,64,128]{3,2,1,0:T(8,128)S(1)}, f32[2,32,64,128]{3,2,1,0:T(8,128)S(1)}, f32[4,16,16,128]{3,2,1,...) custom-call(f32[64,8192]{1,0:T(8,128)S(1)} %get-tuple-element.23.right_ref, ...), custom_call_target="tpu_custom_call" | custom-call | tf_op jit(solution)/shard_map/pallas_call | solution.py:1052
  13.9 0.0 collective-permute-done.4.corner_far
  13.9 0.2 collective-permute-done.3.corner_near
  14.1 0.0 collective-permute-done.2.polar_ref
  14.1 0.0 collective-permute-done.from_other
  14.1 0.0 collective-permute-done.1.from_mate
  14.1 3.9 %shard_map.61 = (f32[2,32,80,128]{3,2,1,0:T(8,128)S(1)}, f32[4,17,16,128]{3,2,1,0:T(8,128)S(1)}, f32[4,16,128]{2,1,0:T(8,128)S(1)}, f32[16,128]{1,0:T(8,128)S(1)...) custom-call(f32[2,32,64,128]{3,2,1,0:T(8,128)S(1)} %get-tuple-element.26.s_ref, ...), custom_call_target="tpu_custom_call" | custom-call | tf_op jit(solution)/shard_map/pallas_call | solution.py:1052
  18.0 3.8 %collective-permute-start.5 = (f32[43,8,128]{2,1,0:T(8,128)S(1)}, f32[43,8,128]{2,1,0:T(8,128)S(1)}, u32[]{:S(2)}, u32[]{:S(2)}) collective-permute-start(f32[43,8,128]{2,1,0:T(8,128)S(1)} %get-tuple-element.39), channel_id=1, source_target_pairs={{0,15},{2,1},{4,3},{6,5},{8,7},{10,9},{12,11},{14,13},{15,0},{1,2}... | collective-permute-start | bytes 528392 | tf_op jit(solution)/shard_map/ppermute | solution.py:1067
  21.9 0.0 collective-permute-start.6
  21.9 1.7 %shard_map.62 = f32[64,8192]{1,0:T(8,128)} custom-call(f32[2,32,80,128]{3,2,1,0:T(8,128)S(1)} %get-tuple-element.34.r_ref), custom_call_target="tpu_custom_call" | custom-call | tf_op jit(solution)/shard_map/pallas_call | solution.py:1052
  23.5 2.2 %collective-permute-done.5.from_other = f32[43,8,128]{2,1,0:T(8,128)S(1)} collective-permute-done((f32[43,8,128]{2,1,0:T(8,128)S(1)}, f32[43,8,128]{2,1,0:T(8,128)S(1)}, u32[]{:S(2)}, u32[]{:S(2)}) %collective-permute-start.5) | collective-permute-done | bytes 176160 | tf_op jit(solution)/shard_map/ppermute | solution.py:1067
  25.8 0.0 collective-permute-done.6.from_mate
  25.8 2.2 %shard_map.63 = (f32[16,2048]{1,0:T(8,128)}, f32[16,2048]{1,0:T(8,128)}) custom-call(f32[4,17,16,128]{3,2,1,0:T(8,128)S(1)} %get-tuple-element.35.s_ref, f32[4,16,16,128]{3,2,1,0:T(8,128)S(1)} %get-tuple-element.29.d1_ref.d_ref, f32[4,16,16,128]{3,2,1,0:T(8,128)S(1)} %get-tuple-element.30.i1_ref.i_ref, f32[4,16,128]{2,1,0:T(8,128)S(1)} %get-tuple-element.36.d_virtual, ...), custom_call_target="tpu_custom_call" | custom-call | tf_op jit(solution)/shard_map/pallas_call | solution.py:1052
Async XLA Ops:
  0.6 7.5 %copy-start = (s32[2,256]{1,0:T(2,128)S(1)}, s32[2,256]{1,0:T(2,128)}, u32[]{:S(2)}) copy-start(s32[2,256]{1,0:T(2,128)} %flag_ref.5) | copy-start | bytes 6148
  2.6 11.5 %collective-permute-start = (f32[2,32,8,128]{3,2,1,0:T(8,128)S(1)}, f32[2,32,8,128]{3,2,1,0:T(8,128)S(1)}, u32[]{:S(2)}, u32[]{:S(2)}) collective-permute-start(f32[2,32,8,128]{3,2,1,0:T(8,128)S(1)} %get-tuple-element.32), channel_id=1, source_target_pairs={{0,15},{2,1},{4,3},{6,5},{8,7},{10,9},{12,11},{14,13},{15,0},{1,2}... | collective-permute-start | bytes 786440 | tf_op jit(solution)/shard_map/ppermute | solution.py:1067
  8.1 6.0 %collective-permute-start.1 = (f32[2,32,8,128]{3,2,1,0:T(8,128)S(1)}, f32[2,32,8,128]{3,2,1,0:T(8,128)S(1)}, u32[]{:S(2)}, u32[]{:S(2)}) collective-permute-start(f32[2,32,8,128]{3,2,1,0:T(8,128)S(1)} %get-tuple-element.33), channel_id=1, source_target_pairs={{0,1},{2,3},{4,5},{6,7},{8,9},{10,11},{12,13},{14,15},{1,0},{3,2},... | collective-permute-start | bytes 786440 | tf_op jit(solution)/shard_map/ppermute | solution.py:1067
  8.6 5.5 %collective-permute-start.2 = (f32[2,32,128]{2,1,0:T(8,128)S(1)}, f32[2,32,128]{2,1,0:T(8,128)S(1)}, u32[]{:S(2)}, u32[]{:S(2)}) collective-permute-start(f32[2,32,128]{2,1,0:T(8,128)S(1)} %shard_map.59.polar_first), channel_id=1, source_target_pairs={{0,8},{1,9},{2,10},{3,11},{4,12},{5,13},{6,14},{7,15},{8,0},{9,1},... | collective-permute-start | bytes 98312 | tf_op jit(solution)/shard_map/ppermute | solution.py:1104
  8.8 5.1 %collective-permute-start.4 = (f32[2,8,128]{2,1,0:T(8,128)S(1)}, f32[2,8,128]{2,1,0:T(8,128)S(1)}, u32[]{:S(2)}, u32[]{:S(2)}) collective-permute-start(f32[2,8,128]{2,1,0:T(8,128)S(1)} %get-tuple-element.25.edges_first), channel_id=1, source_target_pairs={{0,7},{2,9},{4,11},{6,13},{8,15},{10,1},{12,3},{14,5},{7,0},{9,2},... | collective-permute-start | bytes 24584 | tf_op jit(solution)/shard_map/ppermute | solution.py:1067
  9.6 4.5 %collective-permute-start.3 = (f32[2,8,128]{2,1,0:T(8,128)S(1)}, f32[2,8,128]{2,1,0:T(8,128)S(1)}, u32[]{:S(2)}, u32[]{:S(2)}) collective-permute-start(f32[2,8,128]{2,1,0:T(8,128)S(1)} %get-tuple-element.25.edges_first), channel_id=1, source_target_pairs={{0,9},{2,11},{4,13},{6,15},{8,1},{10,3},{12,5},{14,7},{9,0},{11,2}... | collective-permute-start | bytes 24584 | tf_op jit(solution)/shard_map/ppermute | solution.py:1067
  18.0 7.7 %collective-permute-start.5 = (f32[43,8,128]{2,1,0:T(8,128)S(1)}, f32[43,8,128]{2,1,0:T(8,128)S(1)}, u32[]{:S(2)}, u32[]{:S(2)}) collective-permute-start(f32[43,8,128]{2,1,0:T(8,128)S(1)} %get-tuple-element.39), channel_id=1, source_target_pairs={{0,15},{2,1},{4,3},{6,5},{8,7},{10,9},{12,11},{14,13},{15,0},{1,2}... | collective-permute-start | bytes 528392 | tf_op jit(solution)/shard_map/ppermute | solution.py:1067
  21.9 3.9 %collective-permute-start.6 = (f32[43,8,128]{2,1,0:T(8,128)S(1)}, f32[43,8,128]{2,1,0:T(8,128)S(1)}, u32[]{:S(2)}, u32[]{:S(2)}) collective-permute-start(f32[43,8,128]{2,1,0:T(8,128)S(1)} %get-tuple-element.40), channel_id=1, source_target_pairs={{0,1},{2,3},{4,5},{6,7},{8,9},{10,11},{12,13},{14,15},{1,0},{3,2},... | collective-permute-start | bytes 528392 | tf_op jit(solution)/shard_map/ppermute | solution.py:1067

commit v19 on v18

--- a/solution.py
+++ b/solution.py
@@ -576,12 +576,12 @@
         return self.part(q % 2, t, q // 2)
 
     def whole(self, q, t):
-        if t == self.tiles:
+        if isinstance(t, int) and t == self.tiles:
             return self.virtual[q][...]
         return jnp.concatenate([self.rows(q, t), self.halo[q][t]], 0)
 
     def ends(self, q, t):
-        if t == self.tiles:
+        if isinstance(t, int) and t == self.tiles:
             whole = self.virtual[q][...]
             return whole[: self.columns // 2], whole[self.columns // 2 :]
         return self.rows(q, t), self.halo[q][t]
@@ -633,9 +633,9 @@
     held = [
         (q, (whole_s(q, tiles) + beside_virtual(q)) * whole_i(q, tiles)) for q in (y, z)
     ]
-    y_before = [roll_up(x) for x in v.ends(y, tiles)]
-    z_here = [roll_down(x) for x in v.ends(z, 0)]
-    for t in range(tiles):
+
+    def body(t, carry):
+        y_before, z_here = carry
         vy, vz = v.ends(y, t), v.ends(z, t)
         y_here = [roll_up(x) for x in vy]
         z_after = [roll_down(x) for x in v.ends(z, t + 1)]
@@ -652,7 +652,10 @@
                 rest.put(q, t, *[x - d * u for x, d, u in zip(total, load_d(q, t), value)])
         for q, value in new:
             v.put(q, t, *value)
-        y_before, z_here = y_here, z_after
+        return y_here, z_after
+
+    start = [roll_up(x) for x in v.ends(y, tiles)], [roll_down(x) for x in v.ends(z, 0)]
+    body(tiles - 1, loop(tiles - 1, body, start, 10))
     for q, value in held:
         v.virtual[q][...] = value
 
@@ -695,9 +698,10 @@
             columns_summed(t)
 
     full(0)
-    up = [roll_up(x) for x in v.ends(1, 0)]
-    down = [roll_down(x) for x in v.ends(2, 1)]
-    for t in range(1, tiles - 1):
+
+    def body(i, carry):
+        t = i + 1
+        up, down = carry
         x = [v.ends(q, t) for q in range(4)]
         up_here = [roll_up(part) for part in x[1]]
         down_next = [roll_down(part) for part in v.ends(2, t + 1)]
@@ -712,7 +716,10 @@
                 r.append(s - (d * x[q][i] - beside))
             rest.put(q, t, *r)
         columns_summed(t)
-        up, down = up_here, down_next
+        return up_here, down_next
+
+    start = [roll_up(x) for x in v.ends(1, 0)], [roll_down(x) for x in v.ends(2, 1)]
+    loop(tiles - 2, body, start, 10)
     full(tiles - 1)
     full(tiles)
 
@@ -777,9 +784,13 @@
         )
 
     v, rest = held(v_ref, hv), held(r_ref, hr)
-    for t in range(tiles):
+
+    def first(t, _):
         for q in (0, 3):
             v.put(q, t, *[x * i for x, i in zip(load_s(q, t), load_i(q, t))])
+        return 0
+
+    loop(tiles, first, 0, 8)
     for q in (1, 2):
         for t in (0, tiles - 1):
             v.put(q, t, jnp.zeros((rows, LANES), F32), jnp.zeros((8, LANES), F32))
@@ -792,7 +803,7 @@
     def coarse(t, value):
         n1[t] = value
 
-    restrict(c0, c1, tiles, rows, coarse, tiles)
+    restrict(c0, c1, tiles, rows, coarse, 8)
 
     def use(c, source):
         for q in range(4):

time: 28.1 us -> 29.8 us (1.060)
  Pallas kernels: 11.7 us -> 13.4 us
    pallas_call x6, Pallas kernels: 11.7 us -> 13.4 us  [call(): pl.pallas_call(kernel, out_shape=[jax.ShapeDtypeStruct(x, F32) if isinsta...]
  transfers between devices with their start and end apart: 7 -> 7, of which waited for: 2 -> 2; matrix products, arithmetic and copies ran while one was open for 0% -> 0% of each run, Pallas kernels for 13% -> 12%
where the time goes in v19:
time: 29.8 us; the launch traced here: 29.7 us
  Pallas kernels  13.4 us (45%)
  starting transfers between devices  13.2 us (44%)
  waiting for transfers between devices  2.42 us (8%)
  between operations  0.69 us (2%)
    pallas_call x6, Pallas kernels, call(): pl.pallas_call(kernel, out_shape=[jax.ShapeDtypeStruct(x, F32) if isinsta...  13.4 us
    ppermute x6, starting transfers between devices, swapped_with(): return lax.ppermute(x, 'lon', pairs + [(b, a) for a, b in pairs])  12.9 us
    ppermute x6, waiting for transfers between devices, swapped_with(): return lax.ppermute(x, 'lon', pairs + [(b, a) for a, b in pairs])  2.41 us
  transfers between devices with their start and end apart: 7, of which 2 were waited for; matrix products, arithmetic and copies ran while one was open for 0% of the time, Pallas kernels for 12%

profile of v19, /device:TPU:0, one launch (start us, length us, event | category | flops | bytes accessed | tf_op | source)
XLA Modules:
  0.0 29.7 jit_solution(6074296271583599611)
XLA Ops:
  0.6 0.0 copy-start
  0.6 2.0 %shard_map.58 = (f32[64,8192]{1,0:T(8,128)S(1)}, bf16[64,8192]{1,0:T(8,128)(2,1)S(1)}, f32[2,32,8,128]{3,2,1,0:T(8,128)S(1)}, f32[2,32,8,128]{3,2,1,0:T(8,128)S(1)}, f32[2,8,128]{2,1,0:T(8,128)S(1)}) custom-call(f32[64,8192]{1,0:T(8,128)} %right_ref.1, bf16[64,8192]{1,0:T(8,128)(2,1)} %weight_ref.1, s32[2,256]{1,0:T(2,128)} %flag_ref.5), custom_call_target="tpu_custom_call" | custom-call | tf_op jit(solution)/shard_map/pallas_call | solution.py:1063
  2.6 5.5 %collective-permute-start = (f32[2,32,8,128]{3,2,1,0:T(8,128)S(1)}, f32[2,32,8,128]{3,2,1,0:T(8,128)S(1)}, u32[]{:S(2)}, u32[]{:S(2)}) collective-permute-start(f32[2,32,8,128]{3,2,1,0:T(8,128)S(1)} %get-tuple-element.32), channel_id=1, source_target_pairs={{0,15},{2,1},{4,3},{6,5},{8,7},{10,9},{12,11},{14,13},{15,0},{1,2}... | collective-permute-start | bytes 786440 | tf_op jit(solution)/shard_map/ppermute | solution.py:1078
  8.1 0.0 collective-permute-start.1
  8.1 0.0 copy-done
  8.1 0.4 %shard_map.59.polar_first = f32[2,32,128]{2,1,0:T(8,128)S(1)} custom-call(f32[64,8192]{1,0:T(8,128)S(1)} %get-tuple-element.23.right_ref, bf16[64,8192]{1,0:T(8,128)(2,1)S(1)} %get-tuple-element.24.weight_ref, s32[2,256]{1,0:T(2,128)S(1)} %copy-done, f32[2,8,128]{2,1,0:T(8,128)S(1)} %get-tuple-element.25.edges_first), custom_call_target="tpu_custom_call" | custom-call | tf_op jit(solution)/shard_map/pallas_call | solution.py:1063
  8.6 0.2 collective-permute-start.2
  8.8 0.8 %collective-permute-start.4 = (f32[2,8,128]{2,1,0:T(8,128)S(1)}, f32[2,8,128]{2,1,0:T(8,128)S(1)}, u32[]{:S(2)}, u32[]{:S(2)}) collective-permute-start(f32[2,8,128]{2,1,0:T(8,128)S(1)} %get-tuple-element.25.edges_first), channel_id=1, source_target_pairs={{0,7},{2,9},{4,11},{6,13},{8,15},{10,1},{12,3},{14,5},{7,0},{9,2},... | collective-permute-start | bytes 24584 | tf_op jit(solution)/shard_map/ppermute | solution.py:1078
  9.6 2.8 %collective-permute-start.3 = (f32[2,8,128]{2,1,0:T(8,128)S(1)}, f32[2,8,128]{2,1,0:T(8,128)S(1)}, u32[]{:S(2)}, u32[]{:S(2)}) collective-permute-start(f32[2,8,128]{2,1,0:T(8,128)S(1)} %get-tuple-element.25.edges_first), channel_id=1, source_target_pairs={{0,9},{2,11},{4,13},{6,15},{8,1},{10,3},{12,5},{14,7},{9,0},{11,2}... | collective-permute-start | bytes 24584 | tf_op jit(solution)/shard_map/ppermute | solution.py:1078
  12.4 1.5 %shard_map.60 = (f32[2,32,64,128]{3,2,1,0:T(8,128)S(1)}, f32[2,32,64,128]{3,2,1,0:T(8,128)S(1)}, f32[2,32,64,128]{3,2,1,0:T(8,128)S(1)}, f32[4,16,16,128]{3,2,1,...) custom-call(f32[64,8192]{1,0:T(8,128)S(1)} %get-tuple-element.23.right_ref, ...), custom_call_target="tpu_custom_call" | custom-call | tf_op jit(solution)/shard_map/pallas_call | solution.py:1063
  13.9 0.0 collective-permute-done.4.corner_far
  13.9 0.2 collective-permute-done.3.corner_near
  14.1 0.0 collective-permute-done.2.polar_ref
  14.1 0.0 collective-permute-done.from_other
  14.1 0.0 collective-permute-done.1.from_mate
  14.1 5.6 %shard_map.61 = (f32[2,32,80,128]{3,2,1,0:T(8,128)S(1)}, f32[4,17,16,128]{3,2,1,0:T(8,128)S(1)}, f32[4,16,128]{2,1,0:T(8,128)S(1)}, f32[16,128]{1,0:T(8,128)S(1)...) custom-call(f32[2,32,64,128]{3,2,1,0:T(8,128)S(1)} %get-tuple-element.26.s_ref, ...), custom_call_target="tpu_custom_call" | custom-call | tf_op jit(solution)/shard_map/pallas_call | solution.py:1063
  19.7 3.8 %collective-permute-start.5 = (f32[43,8,128]{2,1,0:T(8,128)S(1)}, f32[43,8,128]{2,1,0:T(8,128)S(1)}, u32[]{:S(2)}, u32[]{:S(2)}) collective-permute-start(f32[43,8,128]{2,1,0:T(8,128)S(1)} %get-tuple-element.39), channel_id=1, source_target_pairs={{0,15},{2,1},{4,3},{6,5},{8,7},{10,9},{12,11},{14,13},{15,0},{1,2}... | collective-permute-start | bytes 528392 | tf_op jit(solution)/shard_map/ppermute | solution.py:1078
  23.6 0.0 collective-permute-start.6
  23.6 1.7 %shard_map.62 = f32[64,8192]{1,0:T(8,128)} custom-call(f32[2,32,80,128]{3,2,1,0:T(8,128)S(1)} %get-tuple-element.34.r_ref), custom_call_target="tpu_custom_call" | custom-call | tf_op jit(solution)/shard_map/pallas_call | solution.py:1063
  25.2 2.2 %collective-permute-done.5.from_other = f32[43,8,128]{2,1,0:T(8,128)S(1)} collective-permute-done((f32[43,8,128]{2,1,0:T(8,128)S(1)}, f32[43,8,128]{2,1,0:T(8,128)S(1)}, u32[]{:S(2)}, u32[]{:S(2)}) %collective-permute-start.5) | collective-permute-done | bytes 176160 | tf_op jit(solution)/shard_map/ppermute | solution.py:1078
  27.5 0.0 collective-permute-done.6.from_mate
  27.5 2.2 %shard_map.63 = (f32[16,2048]{1,0:T(8,128)}, f32[16,2048]{1,0:T(8,128)}) custom-call(f32[4,17,16,128]{3,2,1,0:T(8,128)S(1)} %get-tuple-element.35.s_ref, f32[4,16,16,128]{3,2,1,0:T(8,128)S(1)} %get-tuple-element.29.d1_ref.d_ref, f32[4,16,16,128]{3,2,1,0:T(8,128)S(1)} %get-tuple-element.30.i1_ref.i_ref, f32[4,16,128]{2,1,0:T(8,128)S(1)} %get-tuple-element.36.d_virtual, ...), custom_call_target="tpu_custom_call" | custom-call | tf_op jit(solution)/shard_map/pallas_call | solution.py:1063
Async XLA Ops:
  0.6 7.5 %copy-start = (s32[2,256]{1,0:T(2,128)S(1)}, s32[2,256]{1,0:T(2,128)}, u32[]{:S(2)}) copy-start(s32[2,256]{1,0:T(2,128)} %flag_ref.5) | copy-start | bytes 6148
  2.6 11.5 %collective-permute-start = (f32[2,32,8,128]{3,2,1,0:T(8,128)S(1)}, f32[2,32,8,128]{3,2,1,0:T(8,128)S(1)}, u32[]{:S(2)}, u32[]{:S(2)}) collective-permute-start(f32[2,32,8,128]{3,2,1,0:T(8,128)S(1)} %get-tuple-element.32), channel_id=1, source_target_pairs={{0,15},{2,1},{4,3},{6,5},{8,7},{10,9},{12,11},{14,13},{15,0},{1,2}... | collective-permute-start | bytes 786440 | tf_op jit(solution)/shard_map/ppermute | solution.py:1078
  8.1 6.0 %collective-permute-start.1 = (f32[2,32,8,128]{3,2,1,0:T(8,128)S(1)}, f32[2,32,8,128]{3,2,1,0:T(8,128)S(1)}, u32[]{:S(2)}, u32[]{:S(2)}) collective-permute-start(f32[2,32,8,128]{3,2,1,0:T(8,128)S(1)} %get-tuple-element.33), channel_id=1, source_target_pairs={{0,1},{2,3},{4,5},{6,7},{8,9},{10,11},{12,13},{14,15},{1,0},{3,2},... | collective-permute-start | bytes 786440 | tf_op jit(solution)/shard_map/ppermute | solution.py:1078
  8.6 5.5 %collective-permute-start.2 = (f32[2,32,128]{2,1,0:T(8,128)S(1)}, f32[2,32,128]{2,1,0:T(8,128)S(1)}, u32[]{:S(2)}, u32[]{:S(2)}) collective-permute-start(f32[2,32,128]{2,1,0:T(8,128)S(1)} %shard_map.59.polar_first), channel_id=1, source_target_pairs={{0,8},{1,9},{2,10},{3,11},{4,12},{5,13},{6,14},{7,15},{8,0},{9,1},... | collective-permute-start | bytes 98312 | tf_op jit(solution)/shard_map/ppermute | solution.py:1115
  8.8 5.1 %collective-permute-start.4 = (f32[2,8,128]{2,1,0:T(8,128)S(1)}, f32[2,8,128]{2,1,0:T(8,128)S(1)}, u32[]{:S(2)}, u32[]{:S(2)}) collective-permute-start(f32[2,8,128]{2,1,0:T(8,128)S(1)} %get-tuple-element.25.edges_first), channel_id=1, source_target_pairs={{0,7},{2,9},{4,11},{6,13},{8,15},{10,1},{12,3},{14,5},{7,0},{9,2},... | collective-permute-start | bytes 24584 | tf_op jit(solution)/shard_map/ppermute | solution.py:1078
  9.6 4.5 %collective-permute-start.3 = (f32[2,8,128]{2,1,0:T(8,128)S(1)}, f32[2,8,128]{2,1,0:T(8,128)S(1)}, u32[]{:S(2)}, u32[]{:S(2)}) collective-permute-start(f32[2,8,128]{2,1,0:T(8,128)S(1)} %get-tuple-element.25.edges_first), channel_id=1, source_target_pairs={{0,9},{2,11},{4,13},{6,15},{8,1},{10,3},{12,5},{14,7},{9,0},{11,2}... | collective-permute-start | bytes 24584 | tf_op jit(solution)/shard_map/ppermute | solution.py:1078
  19.7 7.7 %collective-permute-start.5 = (f32[43,8,128]{2,1,0:T(8,128)S(1)}, f32[43,8,128]{2,1,0:T(8,128)S(1)}, u32[]{:S(2)}, u32[]{:S(2)}) collective-permute-start(f32[43,8,128]{2,1,0:T(8,128)S(1)} %get-tuple-element.39), channel_id=1, source_target_pairs={{0,15},{2,1},{4,3},{6,5},{8,7},{10,9},{12,11},{14,13},{15,0},{1,2}... | collective-permute-start | bytes 528392 | tf_op jit(solution)/shard_map/ppermute | solution.py:1078
  23.6 3.9 %collective-permute-start.6 = (f32[43,8,128]{2,1,0:T(8,128)S(1)}, f32[43,8,128]{2,1,0:T(8,128)S(1)}, u32[]{:S(2)}, u32[]{:S(2)}) collective-permute-start(f32[43,8,128]{2,1,0:T(8,128)S(1)} %get-tuple-element.40), channel_id=1, source_target_pairs={{0,1},{2,3},{4,5},{6,7},{8,9},{10,11},{12,13},{14,15},{1,0},{3,2},... | collective-permute-start | bytes 528392 | tf_op jit(solution)/shard_map/ppermute | solution.py:1078

commit v20 on v18

--- a/solution.py
+++ b/solution.py
@@ -318,29 +318,31 @@
     for copy in copies[1:5]:
         copy.wait()
     sub = row_ids(8)
-    lanes = [slice(c * 256, (c + 1) * 256) for c in range(tiles)]
-
     def ends(size):
         return slice(0, size), slice(columns - size, columns)
 
-    source, weight = moved(
-        jnp.concatenate([right_here[at, w] for w in lanes for at in ends(8)], 0),
-        matrix,
-        jnp.concatenate([weight_here[at, w] for w in lanes for at in ends(16)], 0),
-    )
-    weight = weight.reshape(tiles, 32, 256)
-    weight = jnp.concatenate([weight[:, :8], weight[:, 24:]], 1).reshape(tiles * 16, 256)
-    source = quarters_of(source, temp_s)
-    weight = quarters_of(weight, temp_w)
+    count = tiles // 4
     found = []
-    for c in range(tiles):
-        here = slice(c * 8, (c + 1) * 8)
-        scales = scale_ref[c]
-        scale = jnp.where(sub < 4, scales[:1], scales[flag_cols - 1 : flag_cols])
-        pair = [x[here] for x in source], [4.0 + w[here] * scale for w in weight]
-        store_edges(c, edge_packs(*pair, False), odd, to_mate, to_other)
-        if c in (0, tiles - 1):
-            found.append(pair)
+    for batch in range(4):
+        chunks = range(batch * count, (batch + 1) * count)
+        lanes = [slice(c * 256, (c + 1) * 256) for c in chunks]
+        source, weight = moved(
+            jnp.concatenate([right_here[at, w] for w in lanes for at in ends(8)], 0),
+            matrix,
+            jnp.concatenate([weight_here[at, w] for w in lanes for at in ends(16)], 0),
+        )
+        weight = weight.reshape(count, 32, 256)
+        weight = jnp.concatenate([weight[:, :8], weight[:, 24:]], 1).reshape(count * 16, 256)
+        source = quarters_of(source, temp_s.at[batch])
+        weight = quarters_of(weight, temp_w.at[batch])
+        for i, c in enumerate(chunks):
+            here = slice(i * 8, (i + 1) * 8)
+            scales = scale_ref[c]
+            scale = jnp.where(sub < 4, scales[:1], scales[flag_cols - 1 : flag_cols])
+            pair = [x[here] for x in source], [4.0 + w[here] * scale for w in weight]
+            store_edges(c, edge_packs(*pair, False), odd, to_mate, to_other)
+            if c in (0, tiles - 1):
+                found.append(pair)
     both = mirrored_ends(*found)
     for pc in (0, 1):
         corner_ref[pc] = both[8 * pc : 8 * (pc + 1)]
@@ -734,7 +736,7 @@
         fill_halo(t, from_mate, from_other, odd, False, hs, hd, hi)
         return 0
 
-    loop(tiles, halo, 0, 8)
+    loop(tiles, halo, 0, tiles)
     total = -16.0
     for q in range(4):
         own_s, own_d = polar_unpacked(polar_ref, q)
@@ -1081,7 +1083,7 @@
     natural = (2, tiles, columns, LANES)
     padded = (2, tiles, columns + 16, LANES)
     quarters1 = (4, tiles1, rows1, LANES)
-    split = (2, 16 * tiles, LANES)
+    split = (4, 2, 4 * tiles, LANES)
     right_here, weight_here, to_mate, to_other, corner = call(
         edge_kernel,
         [(columns, height), jax.ShapeDtypeStruct((columns, height), BF16)]

time: 28.1 us -> 28 us (level)
  no operation moved by 1% of the time
where the time goes in v20:
time: 28 us; the launch traced here: 27.9 us
  starting transfers between devices  13.2 us (47%)
  Pallas kernels  11.6 us (41%)
  waiting for transfers between devices  2.42 us (9%)
  between operations  0.69 us (2%)
    ppermute x6, starting transfers between devices, swapped_with(): return lax.ppermute(x, 'lon', pairs + [(b, a) for a, b in pairs])  12.9 us
    pallas_call x6, Pallas kernels, call(): pl.pallas_call(kernel, out_shape=[jax.ShapeDtypeStruct(x, F32) if isinsta...  11.6 us
    ppermute x6, waiting for transfers between devices, swapped_with(): return lax.ppermute(x, 'lon', pairs + [(b, a) for a, b in pairs])  2.42 us
  transfers between devices with their start and end apart: 7, of which 2 were waited for; matrix products, arithmetic and copies ran while one was open for 0% of the time, Pallas kernels for 13%

profile of v20, /device:TPU:0, one launch (start us, length us, event | category | flops | bytes accessed | tf_op | source)
XLA Modules:
  0.0 27.9 jit_solution(6407235843435783129)
XLA Ops:
  0.6 0.0 copy-start
  0.6 2.0 %shard_map.58 = (f32[64,8192]{1,0:T(8,128)S(1)}, bf16[64,8192]{1,0:T(8,128)(2,1)S(1)}, f32[2,32,8,128]{3,2,1,0:T(8,128)S(1)}, f32[2,32,8,128]{3,2,1,0:T(8,128)S(1)}, f32[2,8,128]{2,1,0:T(8,128)S(1)}) custom-call(f32[64,8192]{1,0:T(8,128)} %right_ref.1, bf16[64,8192]{1,0:T(8,128)(2,1)} %weight_ref.1, s32[2,256]{1,0:T(2,128)} %flag_ref.5), custom_call_target="tpu_custom_call" | custom-call | tf_op jit(solution)/shard_map/pallas_call | solution.py:1054
  2.6 5.5 %collective-permute-start = (f32[2,32,8,128]{3,2,1,0:T(8,128)S(1)}, f32[2,32,8,128]{3,2,1,0:T(8,128)S(1)}, u32[]{:S(2)}, u32[]{:S(2)}) collective-permute-start(f32[2,32,8,128]{3,2,1,0:T(8,128)S(1)} %get-tuple-element.32), channel_id=1, source_target_pairs={{0,15},{2,1},{4,3},{6,5},{8,7},{10,9},{12,11},{14,13},{15,0},{1,2}... | collective-permute-start | bytes 786440 | tf_op jit(solution)/shard_map/ppermute | solution.py:1069
  8.1 0.0 collective-permute-start.1
  8.1 0.0 copy-done
  8.1 0.4 %shard_map.59.polar_first = f32[2,32,128]{2,1,0:T(8,128)S(1)} custom-call(f32[64,8192]{1,0:T(8,128)S(1)} %get-tuple-element.23.right_ref, bf16[64,8192]{1,0:T(8,128)(2,1)S(1)} %get-tuple-element.24.weight_ref, s32[2,256]{1,0:T(2,128)S(1)} %copy-done, f32[2,8,128]{2,1,0:T(8,128)S(1)} %get-tuple-element.25.edges_first), custom_call_target="tpu_custom_call" | custom-call | tf_op jit(solution)/shard_map/pallas_call | solution.py:1054
  8.5 0.2 collective-permute-start.2
  8.8 0.8 %collective-permute-start.4 = (f32[2,8,128]{2,1,0:T(8,128)S(1)}, f32[2,8,128]{2,1,0:T(8,128)S(1)}, u32[]{:S(2)}, u32[]{:S(2)}) collective-permute-start(f32[2,8,128]{2,1,0:T(8,128)S(1)} %get-tuple-element.25.edges_first), channel_id=1, source_target_pairs={{0,7},{2,9},{4,11},{6,13},{8,15},{10,1},{12,3},{14,5},{7,0},{9,2},... | collective-permute-start | bytes 24584 | tf_op jit(solution)/shard_map/ppermute | solution.py:1069
  9.6 2.8 %collective-permute-start.3 = (f32[2,8,128]{2,1,0:T(8,128)S(1)}, f32[2,8,128]{2,1,0:T(8,128)S(1)}, u32[]{:S(2)}, u32[]{:S(2)}) collective-permute-start(f32[2,8,128]{2,1,0:T(8,128)S(1)} %get-tuple-element.25.edges_first), channel_id=1, source_target_pairs={{0,9},{2,11},{4,13},{6,15},{8,1},{10,3},{12,5},{14,7},{9,0},{11,2}... | collective-permute-start | bytes 24584 | tf_op jit(solution)/shard_map/ppermute | solution.py:1069
  12.4 1.5 %shard_map.60 = (f32[2,32,64,128]{3,2,1,0:T(8,128)S(1)}, f32[2,32,64,128]{3,2,1,0:T(8,128)S(1)}, f32[2,32,64,128]{3,2,1,0:T(8,128)S(1)}, f32[4,16,16,128]{3,2,1,...) custom-call(f32[64,8192]{1,0:T(8,128)S(1)} %get-tuple-element.23.right_ref, ...), custom_call_target="tpu_custom_call" | custom-call | tf_op jit(solution)/shard_map/pallas_call | solution.py:1054
  13.9 0.0 collective-permute-done.4.corner_far
  13.9 0.2 collective-permute-done.3.corner_near
  14.1 0.0 collective-permute-done.2.polar_ref
  14.1 0.0 collective-permute-done.from_other
  14.1 0.0 collective-permute-done.1.from_mate
  14.1 3.9 %shard_map.61 = (f32[2,32,80,128]{3,2,1,0:T(8,128)S(1)}, f32[4,17,16,128]{3,2,1,0:T(8,128)S(1)}, f32[4,16,128]{2,1,0:T(8,128)S(1)}, f32[16,128]{1,0:T(8,128)S(1)...) custom-call(f32[2,32,64,128]{3,2,1,0:T(8,128)S(1)} %get-tuple-element.26.s_ref, ...), custom_call_target="tpu_custom_call" | custom-call | tf_op jit(solution)/shard_map/pallas_call | solution.py:1054
  18.0 3.8 %collective-permute-start.5 = (f32[43,8,128]{2,1,0:T(8,128)S(1)}, f32[43,8,128]{2,1,0:T(8,128)S(1)}, u32[]{:S(2)}, u32[]{:S(2)}) collective-permute-start(f32[43,8,128]{2,1,0:T(8,128)S(1)} %get-tuple-element.39), channel_id=1, source_target_pairs={{0,15},{2,1},{4,3},{6,5},{8,7},{10,9},{12,11},{14,13},{15,0},{1,2}... | collective-permute-start | bytes 528392 | tf_op jit(solution)/shard_map/ppermute | solution.py:1069
  21.8 0.0 collective-permute-start.6
  21.8 1.7 %shard_map.62 = f32[64,8192]{1,0:T(8,128)} custom-call(f32[2,32,80,128]{3,2,1,0:T(8,128)S(1)} %get-tuple-element.34.r_ref), custom_call_target="tpu_custom_call" | custom-call | tf_op jit(solution)/shard_map/pallas_call | solution.py:1054
  23.5 2.2 %collective-permute-done.5.from_other = f32[43,8,128]{2,1,0:T(8,128)S(1)} collective-permute-done((f32[43,8,128]{2,1,0:T(8,128)S(1)}, f32[43,8,128]{2,1,0:T(8,128)S(1)}, u32[]{:S(2)}, u32[]{:S(2)}) %collective-permute-start.5) | collective-permute-done | bytes 176160 | tf_op jit(solution)/shard_map/ppermute | solution.py:1069
  25.7 0.0 collective-permute-done.6.from_mate
  25.7 2.2 %shard_map.63 = (f32[16,2048]{1,0:T(8,128)}, f32[16,2048]{1,0:T(8,128)}) custom-call(f32[4,17,16,128]{3,2,1,0:T(8,128)S(1)} %get-tuple-element.35.s_ref, f32[4,16,16,128]{3,2,1,0:T(8,128)S(1)} %get-tuple-element.29.d1_ref.d_ref, f32[4,16,16,128]{3,2,1,0:T(8,128)S(1)} %get-tuple-element.30.i1_ref.i_ref, f32[4,16,128]{2,1,0:T(8,128)S(1)} %get-tuple-element.36.d_virtual, ...), custom_call_target="tpu_custom_call" | custom-call | tf_op jit(solution)/shard_map/pallas_call | solution.py:1054
Async XLA Ops:
  0.6 7.5 %copy-start = (s32[2,256]{1,0:T(2,128)S(1)}, s32[2,256]{1,0:T(2,128)}, u32[]{:S(2)}) copy-start(s32[2,256]{1,0:T(2,128)} %flag_ref.5) | copy-start | bytes 6148
  2.6 11.5 %collective-permute-start = (f32[2,32,8,128]{3,2,1,0:T(8,128)S(1)}, f32[2,32,8,128]{3,2,1,0:T(8,128)S(1)}, u32[]{:S(2)}, u32[]{:S(2)}) collective-permute-start(f32[2,32,8,128]{3,2,1,0:T(8,128)S(1)} %get-tuple-element.32), channel_id=1, source_target_pairs={{0,15},{2,1},{4,3},{6,5},{8,7},{10,9},{12,11},{14,13},{15,0},{1,2}... | collective-permute-start | bytes 786440 | tf_op jit(solution)/shard_map/ppermute | solution.py:1069
  8.1 6.0 %collective-permute-start.1 = (f32[2,32,8,128]{3,2,1,0:T(8,128)S(1)}, f32[2,32,8,128]{3,2,1,0:T(8,128)S(1)}, u32[]{:S(2)}, u32[]{:S(2)}) collective-permute-start(f32[2,32,8,128]{3,2,1,0:T(8,128)S(1)} %get-tuple-element.33), channel_id=1, source_target_pairs={{0,1},{2,3},{4,5},{6,7},{8,9},{10,11},{12,13},{14,15},{1,0},{3,2},... | collective-permute-start | bytes 786440 | tf_op jit(solution)/shard_map/ppermute | solution.py:1069
  8.5 5.5 %collective-permute-start.2 = (f32[2,32,128]{2,1,0:T(8,128)S(1)}, f32[2,32,128]{2,1,0:T(8,128)S(1)}, u32[]{:S(2)}, u32[]{:S(2)}) collective-permute-start(f32[2,32,128]{2,1,0:T(8,128)S(1)} %shard_map.59.polar_first), channel_id=1, source_target_pairs={{0,8},{1,9},{2,10},{3,11},{4,12},{5,13},{6,14},{7,15},{8,0},{9,1},... | collective-permute-start | bytes 98312 | tf_op jit(solution)/shard_map/ppermute | solution.py:1106
  8.8 5.1 %collective-permute-start.4 = (f32[2,8,128]{2,1,0:T(8,128)S(1)}, f32[2,8,128]{2,1,0:T(8,128)S(1)}, u32[]{:S(2)}, u32[]{:S(2)}) collective-permute-start(f32[2,8,128]{2,1,0:T(8,128)S(1)} %get-tuple-element.25.edges_first), channel_id=1, source_target_pairs={{0,7},{2,9},{4,11},{6,13},{8,15},{10,1},{12,3},{14,5},{7,0},{9,2},... | collective-permute-start | bytes 24584 | tf_op jit(solution)/shard_map/ppermute | solution.py:1069
  9.6 4.5 %collective-permute-start.3 = (f32[2,8,128]{2,1,0:T(8,128)S(1)}, f32[2,8,128]{2,1,0:T(8,128)S(1)}, u32[]{:S(2)}, u32[]{:S(2)}) collective-permute-start(f32[2,8,128]{2,1,0:T(8,128)S(1)} %get-tuple-element.25.edges_first), channel_id=1, source_target_pairs={{0,9},{2,11},{4,13},{6,15},{8,1},{10,3},{12,5},{14,7},{9,0},{11,2}... | collective-permute-start | bytes 24584 | tf_op jit(solution)/shard_map/ppermute | solution.py:1069
  18.0 7.7 %collective-permute-start.5 = (f32[43,8,128]{2,1,0:T(8,128)S(1)}, f32[43,8,128]{2,1,0:T(8,128)S(1)}, u32[]{:S(2)}, u32[]{:S(2)}) collective-permute-start(f32[43,8,128]{2,1,0:T(8,128)S(1)} %get-tuple-element.39), channel_id=1, source_target_pairs={{0,15},{2,1},{4,3},{6,5},{8,7},{10,9},{12,11},{14,13},{15,0},{1,2}... | collective-permute-start | bytes 528392 | tf_op jit(solution)/shard_map/ppermute | solution.py:1069
  21.8 3.9 %collective-permute-start.6 = (f32[43,8,128]{2,1,0:T(8,128)S(1)}, f32[43,8,128]{2,1,0:T(8,128)S(1)}, u32[]{:S(2)}, u32[]{:S(2)}) collective-permute-start(f32[43,8,128]{2,1,0:T(8,128)S(1)} %get-tuple-element.40), channel_id=1, source_target_pairs={{0,1},{2,3},{4,5},{6,7},{8,9},{10,11},{12,13},{14,15},{1,0},{3,2},... | collective-permute-start | bytes 528392 | tf_op jit(solution)/shard_map/ppermute | solution.py:1069

commit v21 on v20

--- a/solution.py
+++ b/solution.py
@@ -291,8 +291,8 @@
 
 def edge_kernel(
     right_ref, weight_ref, flag_ref,
-    right_here, weight_here, to_mate, to_other, corner_ref,
-    flags, temp_s, temp_w, scale_ref, sems,
+    right_here, weight_here, scale_ref, to_mate, to_other, corner_ref,
+    flags, temp_s, temp_w, sems,
 ):
     columns, height = right_ref.shape
     tiles = height // 256
@@ -360,10 +360,10 @@
     return moved(jnp.concatenate(polar_packs(ends), 0), mirror)
 
 
-def polar_kernel(right_ref, weight_ref, flag_ref, edges_first, polar_ref, temp_s, temp_w):
+def polar_kernel(right_ref, weight_ref, scale_ref, edges_first, polar_ref, temp_s, temp_w):
     columns, height = right_ref.shape
     rows, tiles = columns // 2, height // 256
-    scales = seam_scales(flag_ref[...], (0, tiles - 1))
+    flag_cols = columns // TILE
     lanes = slice(0, 256), slice(height - 256, height)
     source, weight = moved(
         jnp.concatenate([right_ref[:, w] for w in lanes], 0),
@@ -373,7 +373,7 @@
     found = []
     for end in (0, 1):
         here = slice(end * columns, (end + 1) * columns)
-        scale = seam_rows(scales[end], flag_ref.shape[0], rows)
+        scale = seam_rows(scale_ref[end * (tiles - 1)], flag_cols, rows)
         found.append(
             (
                 quarters_of(source[here], temp_s.at[end]),
@@ -386,14 +386,13 @@
 
 
 def bulk_kernel(
-    right_ref, weight_ref, flag_ref, polar_first,
+    right_ref, weight_ref, scale_ref, polar_first,
     s_ref, d_ref, i_ref, d1_ref, i1_ref, d2_ref,
-    temp, scale_ref, e_ref, split_temp,
+    temp, e_ref, split_temp,
 ):
     tiles, columns = s_ref.shape[1], s_ref.shape[2]
     rows = columns // 2
     matrix = splitter()
-    scale_ref[...] = seam_scales(flag_ref[...], range(tiles))
     for start in range(0, tiles, BATCH):
         lanes = [slice((start + i) * 256, (start + i + 1) * 256) for i in range(BATCH)]
         source, weight = moved(
@@ -404,7 +403,7 @@
         for i in range(BATCH):
             c = start + i
             here = slice(i * columns, (i + 1) * columns)
-            scale = seam_rows(scale_ref[c], flag_ref.shape[0], columns)
+            scale = seam_rows(scale_ref[c], columns // TILE, columns)
             screens = []
             for pr in (0, 1):
                 half = slice(pr * LANES, (pr + 1) * LANES)
@@ -873,7 +872,11 @@
     restrict(e0, e1, tiles1, rows1, edges, 16)
 
 
-def merge_kernel(r_ref, out_ref, out_buf, sems):
+def merge_kernel(
+    r_ref, s_ref, d_ref, i_ref, d_virtual, d2_ref, d2_virtual,
+    out_ref, rim_s, rim_d, rim_i, inverse2,
+    out_buf, sems,
+):
     tiles = r_ref.shape[1]
     columns = out_ref.shape[0]
     matrix = merger()
@@ -895,24 +898,38 @@
         copy = pltpu.make_async_copy(out_buf.at[:, part], out_ref.at[:, part], sems.at[group])
         copy.start()
         copies.append(copy)
+
+    sub = row_ids(8)
+    tiles1, own = d_ref.shape[1], d_ref.shape[2]
+
+    def rim(x):
+        return jnp.where(sub < 4, x[:8], x[own - 8 :])
+
+    for t in range(tiles1 + 1):
+        for q in range(4):
+            rim_s[q, t] = rim(s_ref[q, t])
+            if t == tiles1:
+                rim_d[q, t] = rim(d_virtual[q])
+                rim_i[q, t] = inverse_of(rim(d_virtual[q]))
+            else:
+                rim_d[q, t] = rim(d_ref[q, t])
+                rim_i[q, t] = rim(i_ref[q, t])
+        inverse2[t] = inverse_of(d2_virtual[...] if t == tiles1 else d2_ref[t])
     for copy in copies:
         copy.wait()
 
 
 def coarse_kernel(
-    s_ref, d_ref, i_ref, d_virtual, d2_ref, d2_virtual, s2_ref, from_other, from_mate,
+    rim_s, rim_d, rim_i, inverse2, d2_ref, d2_virtual, s2_ref, from_other, from_mate,
     solution_ref, residual_ref,
     v0, v1, v2, v3, c0, c1, hs, hd, hi, part, fixes, rest1, rest2, s, d, inv, va, vb,
 ):
     v = [v0, v1, v2, v3]
-    tiles, own = d_ref.shape[1], d_ref.shape[2]
+    tiles, own = d2_ref.shape[:2]
     rows = own + 8
     count = tiles + 1
     sub = row_ids(8)
     odd_band = is_odd()
-    def rim(x):
-        return jnp.where(sub < 4, x[:8], x[own - 8 :])
-
     for t in range(count):
         places = t, count + t, 2 * count + t // 2
         packs = [chosen(odd_band, from_mate[i], from_other[i]) for i in places]
@@ -953,17 +970,16 @@
                 known = (sub == near) | (sub == far) if q == bb else sub == near
                 inverse[q] = jnp.where(known, inverse_of(diag[q]), inverse[q])
         for q in range(4):
-            own_d = rim(d_virtual[q] if t == tiles else d_ref[q, t])
-            own_i = inverse_of(own_d) if t == tiles else rim(i_ref[q, t])
-            hs[q, t] = jnp.concatenate([source[q], rim(s_ref[q, t])], 0)
-            hd[q, t] = jnp.concatenate([diag[q], own_d], 0)
-            hi[q, t] = jnp.concatenate([inverse[q], own_i], 0)
+            hs[q, t] = source[q]
+            hd[q, t] = diag[q]
+            hi[q, t] = inverse[q]
             fixes[q, t] = fixed[q]
         part[t] = more
         near_total = (diag[0] + diag[1]) + (diag[2] + diag[3]) - 12.0
         total = jnp.where((sub == 0) | (sub == 7), near_total, total)
         here = d2_virtual[...] if t == tiles else d2_ref[t]
         d[t] = jnp.concatenate([here, total], 0)
+        inv[t] = jnp.concatenate([inverse2[t], inverse_of(total)], 0)
     def after_sweep(sweep):
         if sweep == 2:
             return
@@ -977,11 +993,12 @@
             for q, mask in todo.items():
                 v[q][t, :8] = jnp.where(mask, fixes[q, t], v[q][t, :8])
 
-    def of(ref):
-        return lambda q, t: ref[q, t]
-
-    left = of(hd), {1: rest1, 2: rest2}
-    smooth(v, of(hs), of(hi), tiles, 16, left, after_sweep)
+    def of(halo, own_rows):
+        return lambda q, t: jnp.concatenate([halo[q, t], own_rows[q, t]], 0)
+
+    load_s = of(hs, rim_s)
+    left = of(hd, rim_d), {1: rest1, 2: rest2}
+    smooth(v, load_s, of(hi, rim_i), tiles, 16, left, after_sweep)
     row = row_ids(16)
 
     def valid(q, virtual):
@@ -992,7 +1009,7 @@
         last = 15 if q == even ^ 1 else 14
         return (row <= after_band) | ((row >= before_band) & (row <= first)) | (row >= last)
 
-    residuals(v, of(hs), left, tiles, c0, c1, lambda t, r: None, 16, valid)
+    residuals(v, load_s, left, tiles, c0, c1, lambda t, r: None, 16, valid)
 
     lane, row = lane_ids(rows), row_ids(rows)
     even = (lane + row) % 2 == 0
@@ -1008,11 +1025,9 @@
             ],
             0,
         )
-        inverse = inverse_of(d[t])
         s[t] = source
-        inv[t] = inverse
         virtual = isinstance(t, int) and t == tiles
-        va[t] = jnp.where(odd if virtual else even, source * inverse, 0.0)
+        va[t] = jnp.where(odd if virtual else even, source * inv[t], 0.0)
 
     restrict(c0, c1, tiles, 16, start, 16)
 
@@ -1084,11 +1099,11 @@
     padded = (2, tiles, columns + 16, LANES)
     quarters1 = (4, tiles1, rows1, LANES)
     split = (4, 2, 4 * tiles, LANES)
-    right_here, weight_here, to_mate, to_other, corner = call(
+    right_here, weight_here, scales, to_mate, to_other, corner = call(
         edge_kernel,
         [(columns, height), jax.ShapeDtypeStruct((columns, height), BF16)]
-        + [(2, tiles, 8, LANES), (2, tiles, 8, LANES), (2, 8, LANES)],
-        [pltpu.VMEM(seam_flags.shape, jnp.int32), split, split, (tiles, 8, LANES)],
+        + [(tiles, 8, LANES), (2, tiles, 8, LANES), (2, tiles, 8, LANES), (2, 8, LANES)],
+        [pltpu.VMEM(seam_flags.shape, jnp.int32), split, split],
         *[
             pltpu.with_memory_space_constraint(x, pltpu.HBM)
             for x in (right_side, texel_weight, seam_flags)
@@ -1101,7 +1116,7 @@
     ends = (2, 2, columns, LANES)
     (polar_own,) = call(
         polar_kernel, [(2, rows, LANES)], [ends, ends],
-        right_here, weight_here, seam_flags, corner,
+        right_here, weight_here, scales, corner,
     )
     polar = lax.ppermute(
         polar_own, "lon", [(i, (i + half_turn) % (2 * half_turn)) for i in range(2 * half_turn)]
@@ -1109,8 +1124,8 @@
     s, d, inverse, d1, i1, d2 = call(
         bulk_kernel,
         [natural] * 3 + [quarters1, quarters1, quarters1[1:]],
-        [(BATCH, columns, LANES), (tiles, 8, LANES), (tiles, rows, LANES), (BATCH, 2, rows, LANES)],
-        right_here, weight_here, seam_flags, polar_own,
+        [(BATCH, columns, LANES), (tiles, rows, LANES), (BATCH, 2, rows, LANES)],
+        right_here, weight_here, scales, polar_own,
     )
 
     def level_scratch(tiles, rows):
@@ -1136,8 +1151,12 @@
         s, d, inverse, d1, i1, d2, from_other, from_mate, polar, corner_near, corner_far,
     )
     from_mate, from_other = swapped_edges(to_mate, to_other)
-    (fine_residual,) = call(
-        merge_kernel, [(columns, height)], [(columns, height)], r,
+    rim = (4, tiles1 + 1, 8, LANES)
+    fine_residual, rim_s, rim_d, rim_i, inverse2 = call(
+        merge_kernel,
+        [(columns, height), rim, rim, rim, (tiles1 + 1, rows1, LANES)],
+        [(columns, height)],
+        r, s1, d1, i1, d1_virtual, d2, d2_virtual,
         sems=(GROUPS,), far_out=1,
     )
     wide = (tiles1 + 1, rows1 + 8, LANES)
@@ -1145,11 +1164,11 @@
         coarse_kernel,
         [(columns // 4, height // 4)] * 2,
         level_scratch(tiles1, 16)
-        + [(4, tiles1 + 1, 16, LANES)] * 3
+        + [(4, tiles1 + 1, 8, LANES)] * 3
         + [(tiles1 + 1, 8, LANES), (4, tiles1 + 1, 8, LANES)]
         + [(tiles1, 16, LANES)] * 2
         + [wide] * 5,
-        s1, d1, i1, d1_virtual, d2, d2_virtual, s2_own, from_other, from_mate,
+        rim_s, rim_d, rim_i, inverse2, d2, d2_virtual, s2_own, from_other, from_mate,
     )
     return fine_residual, solution_2, residual_2
 

time: 28 us -> 27.7 us (0.989)
  Pallas kernels: 11.6 us -> 11.2 us
    pallas_call x6, Pallas kernels: 11.6 us -> 11.2 us  [call(): pl.pallas_call(kernel, out_shape=[jax.ShapeDtypeStruct(x, F32) if isinsta...]
where the time goes in v21:
time: 27.7 us; the launch traced here: 27.5 us
  starting transfers between devices  13.2 us (48%)
  Pallas kernels  11.2 us (40%)
  waiting for transfers between devices  2.45 us (9%)
  between operations  0.68 us (2%)
    ppermute x6, starting transfers between devices, swapped_with(): return lax.ppermute(x, 'lon', pairs + [(b, a) for a, b in pairs])  12.9 us
    pallas_call x6, Pallas kernels, call(): pl.pallas_call(kernel, out_shape=[jax.ShapeDtypeStruct(x, F32) if isinsta...  11.2 us
    ppermute x6, waiting for transfers between devices, swapped_with(): return lax.ppermute(x, 'lon', pairs + [(b, a) for a, b in pairs])  2.44 us
  transfers between devices with their start and end apart: 7, of which 2 were waited for; matrix products, arithmetic and copies ran while one was open for 0% of the time, Pallas kernels for 13%

profile of v21, /device:TPU:0, one launch (start us, length us, event | category | flops | bytes accessed | tf_op | source)
XLA Modules:
  0.0 27.5 jit_solution(10564069346751664609)
XLA Ops:
  0.6 1.9 %shard_map.58 = (f32[64,8192]{1,0:T(8,128)S(1)}, bf16[64,8192]{1,0:T(8,128)(2,1)S(1)}, f32[32,8,128]{2,1,0:T(8,128)S(1)}, f32[2,32,8,128]{3,2,1,0:T(8,128)S(1)},...) custom-call(f32[64,8192]{1,0:T(8,128)} %right_ref.1, bf16[64,8192]{1,0:T(8,128)(2,1)} %weight_ref.1, ...), custom_call_target="tpu_custom_call" | custom-call | tf_op jit(solution)/shard_map/pallas_call | solution.py:1069
  2.6 5.5 %collective-permute-start = (f32[2,32,8,128]{3,2,1,0:T(8,128)S(1)}, f32[2,32,8,128]{3,2,1,0:T(8,128)S(1)}, u32[]{:S(2)}, u32[]{:S(2)}) collective-permute-start(f32[2,32,8,128]{3,2,1,0:T(8,128)S(1)} %get-tuple-element.39), channel_id=1, source_target_pairs={{0,15},{2,1},{4,3},{6,5},{8,7},{10,9},{12,11},{14,13},{15,0},{1,2}... | collective-permute-start | bytes 786440 | tf_op jit(solution)/shard_map/ppermute | solution.py:1084
  8.1 0.0 collective-permute-start.1
  8.1 0.4 %shard_map.59.polar_first = f32[2,32,128]{2,1,0:T(8,128)S(1)} custom-call(f32[64,8192]{1,0:T(8,128)S(1)} %get-tuple-element.29.right_ref, bf16[64,8192]{1,0:T(8,128)(2,1)S(1)} %get-tuple-element.30.weight_ref, f32[32,8,128]{2,1,0:T(8,128)S(1)} %get-tuple-element.31.scale_ref, f32[2,8,128]{2,1,0:T(8,128)S(1)} %get-tuple-element.32.edges_first), custom_call_target="tpu_custom_call" | custom-call | tf_op jit(solution)/shard_map/pallas_call | solution.py:1069
  8.5 0.2 collective-permute-start.2
  8.7 0.8 %collective-permute-start.4 = (f32[2,8,128]{2,1,0:T(8,128)S(1)}, f32[2,8,128]{2,1,0:T(8,128)S(1)}, u32[]{:S(2)}, u32[]{:S(2)}) collective-permute-start(f32[2,8,128]{2,1,0:T(8,128)S(1)} %get-tuple-element.32.edges_first), channel_id=1, source_target_pairs={{0,7},{2,9},{4,11},{6,13},{8,15},{10,1},{12,3},{14,5},{7,0},{9,2},... | collective-permute-start | bytes 24584 | tf_op jit(solution)/shard_map/ppermute | solution.py:1084
  9.5 2.8 %collective-permute-start.3 = (f32[2,8,128]{2,1,0:T(8,128)S(1)}, f32[2,8,128]{2,1,0:T(8,128)S(1)}, u32[]{:S(2)}, u32[]{:S(2)}) collective-permute-start(f32[2,8,128]{2,1,0:T(8,128)S(1)} %get-tuple-element.32.edges_first), channel_id=1, source_target_pairs={{0,9},{2,11},{4,13},{6,15},{8,1},{10,3},{12,5},{14,7},{9,0},{11,2}... | collective-permute-start | bytes 24584 | tf_op jit(solution)/shard_map/ppermute | solution.py:1084
  12.4 1.5 %shard_map.60 = (f32[2,32,64,128]{3,2,1,0:T(8,128)S(1)}, f32[2,32,64,128]{3,2,1,0:T(8,128)S(1)}, f32[2,32,64,128]{3,2,1,0:T(8,128)S(1)}, f32[4,16,16,128]{3,2,1,...) custom-call(f32[64,8192]{1,0:T(8,128)S(1)} %get-tuple-element.29.right_ref, ...), custom_call_target="tpu_custom_call" | custom-call | tf_op jit(solution)/shard_map/pallas_call | solution.py:1069
  13.8 0.0 collective-permute-done.4.corner_far
  13.8 0.2 collective-permute-done.3.corner_near
  14.0 0.0 collective-permute-done.2.polar_ref
  14.0 0.0 collective-permute-done.from_other
  14.0 0.0 collective-permute-done.1.from_mate
  14.0 3.6 %shard_map.61 = (f32[2,32,80,128]{3,2,1,0:T(8,128)S(1)}, f32[4,17,16,128]{3,2,1,0:T(8,128)S(1)}, f32[4,16,128]{2,1,0:T(8,128)S(1)}, f32[16,128]{1,0:T(8,128)S(1)...) custom-call(f32[2,32,64,128]{3,2,1,0:T(8,128)S(1)} %get-tuple-element.33.s_ref, ...), custom_call_target="tpu_custom_call" | custom-call | tf_op jit(solution)/shard_map/pallas_call | solution.py:1069
  17.7 3.8 %collective-permute-start.5 = (f32[43,8,128]{2,1,0:T(8,128)S(1)}, f32[43,8,128]{2,1,0:T(8,128)S(1)}, u32[]{:S(2)}, u32[]{:S(2)}) collective-permute-start(f32[43,8,128]{2,1,0:T(8,128)S(1)} %get-tuple-element.51), channel_id=1, source_target_pairs={{0,15},{2,1},{4,3},{6,5},{8,7},{10,9},{12,11},{14,13},{15,0},{1,2}... | collective-permute-start | bytes 528392 | tf_op jit(solution)/shard_map/ppermute | solution.py:1084
  21.5 0.0 collective-permute-start.6
  21.5 1.7 %shard_map.62 = (f32[64,8192]{1,0:T(8,128)}, f32[4,17,8,128]{3,2,1,0:T(8,128)S(1)}, f32[4,17,8,128]{3,2,1,0:T(8,128)S(1)}, f32[4,17,8,128]{3,2,1,0:T(8,128)S(1)}, f32[17,16,128]{2,1,0:T(8,128)S(1)}) custom-call(f32[2,32,80,128]{3,2,1,0:T(8,128)S(1)} %get-tuple-element.41.r_ref, f32[4,17,16,128]{3,2,1,0:T(8,128)S(1)} %get-tuple-element.42.s_ref, ...), custom_call_target="tpu_custom_call" | custom-call | tf_op jit(solution)/shard_map/pallas_call | solution.py:1069
  23.2 2.2 %collective-permute-done.5.from_other = f32[43,8,128]{2,1,0:T(8,128)S(1)} collective-permute-done((f32[43,8,128]{2,1,0:T(8,128)S(1)}, f32[43,8,128]{2,1,0:T(8,128)S(1)}, u32[]{:S(2)}, u32[]{:S(2)}) %collective-permute-start.5) | collective-permute-done | bytes 176160 | tf_op jit(solution)/shard_map/ppermute | solution.py:1084
  25.4 0.0 collective-permute-done.6.from_mate
  25.4 2.1 %shard_map.63 = (f32[16,2048]{1,0:T(8,128)}, f32[16,2048]{1,0:T(8,128)}) custom-call(f32[4,17,8,128]{3,2,1,0:T(8,128)S(1)} %get-tuple-element.46.rim_s, f32[4,17,8,128]{3,2,1,0:T(8,128)S(1)} %get-tuple-element.47.rim_d, f32[4,17,8,128]{3,2,1,0:T(8,128)S(1)} %get-tuple-element.48.rim_i, f32[17,16,128]{2,1,0:T(8,128)S(1)} %get-tuple-element.49.inverse2, ...), custom_call_target="tpu_custom_call" | custom-call | tf_op jit(solution)/shard_map/pallas_call | solution.py:1069
Async XLA Ops:
  2.6 11.5 %collective-permute-start = (f32[2,32,8,128]{3,2,1,0:T(8,128)S(1)}, f32[2,32,8,128]{3,2,1,0:T(8,128)S(1)}, u32[]{:S(2)}, u32[]{:S(2)}) collective-permute-start(f32[2,32,8,128]{3,2,1,0:T(8,128)S(1)} %get-tuple-element.39), channel_id=1, source_target_pairs={{0,15},{2,1},{4,3},{6,5},{8,7},{10,9},{12,11},{14,13},{15,0},{1,2}... | collective-permute-start | bytes 786440 | tf_op jit(solution)/shard_map/ppermute | solution.py:1084
  8.1 6.0 %collective-permute-start.1 = (f32[2,32,8,128]{3,2,1,0:T(8,128)S(1)}, f32[2,32,8,128]{3,2,1,0:T(8,128)S(1)}, u32[]{:S(2)}, u32[]{:S(2)}) collective-permute-start(f32[2,32,8,128]{3,2,1,0:T(8,128)S(1)} %get-tuple-element.40), channel_id=1, source_target_pairs={{0,1},{2,3},{4,5},{6,7},{8,9},{10,11},{12,13},{14,15},{1,0},{3,2},... | collective-permute-start | bytes 786440 | tf_op jit(solution)/shard_map/ppermute | solution.py:1084
  8.5 5.5 %collective-permute-start.2 = (f32[2,32,128]{2,1,0:T(8,128)S(1)}, f32[2,32,128]{2,1,0:T(8,128)S(1)}, u32[]{:S(2)}, u32[]{:S(2)}) collective-permute-start(f32[2,32,128]{2,1,0:T(8,128)S(1)} %shard_map.59.polar_first), channel_id=1, source_target_pairs={{0,8},{1,9},{2,10},{3,11},{4,12},{5,13},{6,14},{7,15},{8,0},{9,1},... | collective-permute-start | bytes 98312 | tf_op jit(solution)/shard_map/ppermute | solution.py:1121
  8.7 5.1 %collective-permute-start.4 = (f32[2,8,128]{2,1,0:T(8,128)S(1)}, f32[2,8,128]{2,1,0:T(8,128)S(1)}, u32[]{:S(2)}, u32[]{:S(2)}) collective-permute-start(f32[2,8,128]{2,1,0:T(8,128)S(1)} %get-tuple-element.32.edges_first), channel_id=1, source_target_pairs={{0,7},{2,9},{4,11},{6,13},{8,15},{10,1},{12,3},{14,5},{7,0},{9,2},... | collective-permute-start | bytes 24584 | tf_op jit(solution)/shard_map/ppermute | solution.py:1084
  9.5 4.5 %collective-permute-start.3 = (f32[2,8,128]{2,1,0:T(8,128)S(1)}, f32[2,8,128]{2,1,0:T(8,128)S(1)}, u32[]{:S(2)}, u32[]{:S(2)}) collective-permute-start(f32[2,8,128]{2,1,0:T(8,128)S(1)} %get-tuple-element.32.edges_first), channel_id=1, source_target_pairs={{0,9},{2,11},{4,13},{6,15},{8,1},{10,3},{12,5},{14,7},{9,0},{11,2}... | collective-permute-start | bytes 24584 | tf_op jit(solution)/shard_map/ppermute | solution.py:1084
  17.7 7.7 %collective-permute-start.5 = (f32[43,8,128]{2,1,0:T(8,128)S(1)}, f32[43,8,128]{2,1,0:T(8,128)S(1)}, u32[]{:S(2)}, u32[]{:S(2)}) collective-permute-start(f32[43,8,128]{2,1,0:T(8,128)S(1)} %get-tuple-element.51), channel_id=1, source_target_pairs={{0,15},{2,1},{4,3},{6,5},{8,7},{10,9},{12,11},{14,13},{15,0},{1,2}... | collective-permute-start | bytes 528392 | tf_op jit(solution)/shard_map/ppermute | solution.py:1084
  21.5 3.9 %collective-permute-start.6 = (f32[43,8,128]{2,1,0:T(8,128)S(1)}, f32[43,8,128]{2,1,0:T(8,128)S(1)}, u32[]{:S(2)}, u32[]{:S(2)}) collective-permute-start(f32[43,8,128]{2,1,0:T(8,128)S(1)} %get-tuple-element.52), channel_id=1, source_target_pairs={{0,1},{2,3},{4,5},{6,7},{8,9},{10,11},{12,13},{14,15},{1,0},{3,2},... | collective-permute-start | bytes 528392 | tf_op jit(solution)/shard_map/ppermute | solution.py:1084

commit v22 on v21

--- a/solution.py
+++ b/solution.py
@@ -601,10 +601,11 @@
             at = 8 + self.columns
             self.own[pr][t, at : at + 1] = halo[0:1]
 
-    def beside_columns(self, q, t, halo):
+    def beside_columns(self, q, t, near):
         sub = row_ids(8)
         pr, pc = q % 2, q // 2
-        own = self.part(pr, t, pc - 1) + self.part(pr, t, pc + 1)
+        rows, halo = near
+        own = rows + self.part(pr, t, 2 if pc else -1)
         if pc == 0:
             other = jnp.where(sub == 0, self.line(pr, t, self.columns - 1), col_prev(halo))
         else:
@@ -635,25 +636,26 @@
         (q, (whole_s(q, tiles) + beside_virtual(q)) * whole_i(q, tiles)) for q in (y, z)
     ]
     y_before = [roll_up(x) for x in v.ends(y, tiles)]
-    z_here = [roll_down(x) for x in v.ends(z, 0)]
+    vz = v.ends(z, 0)
+    z_here = [roll_down(x) for x in vz]
     for t in range(tiles):
-        vy, vz = v.ends(y, t), v.ends(z, t)
+        vy, z_next = v.ends(y, t), v.ends(z, t + 1)
         y_here = [roll_up(x) for x in vy]
-        z_after = [roll_down(x) for x in v.ends(z, t + 1)]
+        z_after = [roll_down(x) for x in z_next]
         lat_a = lane_sum(vy, y_here, y_before, 0)
         lat_b = lane_sum(vz, z_here, z_after, LANES - 1)
         new = []
-        for q, lat, halo in ((qa, lat_a, vz[1]), (qb, lat_b, vy[1])):
-            cols = v.beside_columns(q, t, halo)
+        for q, lat, near in ((qa, lat_a, vz), (qb, lat_b, vy)):
+            cols = v.beside_columns(q, t, near)
             total = [x + (l + c) for x, l, c in zip(load_s(q, t), lat, cols)]
             value = [x * i for x, i in zip(total, load_i(q, t))]
             new.append((q, value))
-            if left is not None:
+            if left is not None and 0 < t < tiles - 1:
                 load_d, rest = left
                 rest.put(q, t, *[x - d * u for x, d, u in zip(total, load_d(q, t), value)])
         for q, value in new:
             v.put(q, t, *value)
-        y_before, z_here = y_here, z_after
+        y_before, z_here, vz = y_here, z_after, z_next
     for q, value in held:
         v.virtual[q][...] = value
 
@@ -697,15 +699,17 @@
 
     full(0)
     up = [roll_up(x) for x in v.ends(1, 0)]
-    down = [roll_down(x) for x in v.ends(2, 1)]
+    x2 = v.ends(2, 1)
+    down = [roll_down(x) for x in x2]
     for t in range(1, tiles - 1):
-        x = [v.ends(q, t) for q in range(4)]
+        x = [v.ends(0, t), v.ends(1, t), x2, v.ends(3, t)]
+        x2 = v.ends(2, t + 1)
         up_here = [roll_up(part) for part in x[1]]
-        down_next = [roll_down(part) for part in v.ends(2, t + 1)]
+        down_next = [roll_down(part) for part in x2]
         for q, ns, near, edge, lane_at in (
             (0, 1, up_here, up, 0), (3, 2, down, down_next, LANES - 1)
         ):
-            cols = v.beside_columns(q, t, x[q ^ 2][1])
+            cols = v.beside_columns(q, t, x[q ^ 2])
             r = []
             for i, (s, d) in enumerate(zip(load_s(q, t), load_d(q, t))):
                 lane = lane_ids(s.shape[0])

time: 27.7 us -> 27.7 us (level)
  no operation moved by 1% of the time
where the time goes in v22:
time: 27.7 us; the launch traced here: 27.5 us
  starting transfers between devices  13.2 us (48%)
  Pallas kernels  11.2 us (40%)
  waiting for transfers between devices  2.45 us (9%)
  between operations  0.68 us (2%)
    ppermute x6, starting transfers between devices, swapped_with(): return lax.ppermute(x, 'lon', pairs + [(b, a) for a, b in pairs])  12.9 us
    pallas_call x6, Pallas kernels, call(): pl.pallas_call(kernel, out_shape=[jax.ShapeDtypeStruct(x, F32) if isinsta...  11.2 us
    ppermute x6, waiting for transfers between devices, swapped_with(): return lax.ppermute(x, 'lon', pairs + [(b, a) for a, b in pairs])  2.44 us
  transfers between devices with their start and end apart: 7, of which 2 were waited for; matrix products, arithmetic and copies ran while one was open for 0% of the time, Pallas kernels for 13%

profile of v22, /device:TPU:0, one launch (start us, length us, event | category | flops | bytes accessed | tf_op | source)
XLA Modules:
  0.0 27.5 jit_solution(3448753677054559836)
XLA Ops:
  0.6 1.9 %shard_map.58 = (f32[64,8192]{1,0:T(8,128)S(1)}, bf16[64,8192]{1,0:T(8,128)(2,1)S(1)}, f32[32,8,128]{2,1,0:T(8,128)S(1)}, f32[2,32,8,128]{3,2,1,0:T(8,128)S(1)},...) custom-call(f32[64,8192]{1,0:T(8,128)} %right_ref.1, bf16[64,8192]{1,0:T(8,128)(2,1)} %weight_ref.1, ...), custom_call_target="tpu_custom_call" | custom-call | tf_op jit(solution)/shard_map/pallas_call | solution.py:1073
  2.6 5.5 %collective-permute-start = (f32[2,32,8,128]{3,2,1,0:T(8,128)S(1)}, f32[2,32,8,128]{3,2,1,0:T(8,128)S(1)}, u32[]{:S(2)}, u32[]{:S(2)}) collective-permute-start(f32[2,32,8,128]{3,2,1,0:T(8,128)S(1)} %get-tuple-element.39), channel_id=1, source_target_pairs={{0,15},{2,1},{4,3},{6,5},{8,7},{10,9},{12,11},{14,13},{15,0},{1,2}... | collective-permute-start | bytes 786440 | tf_op jit(solution)/shard_map/ppermute | solution.py:1088
  8.1 0.0 collective-permute-start.1
  8.1 0.4 %shard_map.59.polar_first = f32[2,32,128]{2,1,0:T(8,128)S(1)} custom-call(f32[64,8192]{1,0:T(8,128)S(1)} %get-tuple-element.29.right_ref, bf16[64,8192]{1,0:T(8,128)(2,1)S(1)} %get-tuple-element.30.weight_ref, f32[32,8,128]{2,1,0:T(8,128)S(1)} %get-tuple-element.31.scale_ref, f32[2,8,128]{2,1,0:T(8,128)S(1)} %get-tuple-element.32.edges_first), custom_call_target="tpu_custom_call" | custom-call | tf_op jit(solution)/shard_map/pallas_call | solution.py:1073
  8.5 0.2 collective-permute-start.2
  8.7 0.8 %collective-permute-start.4 = (f32[2,8,128]{2,1,0:T(8,128)S(1)}, f32[2,8,128]{2,1,0:T(8,128)S(1)}, u32[]{:S(2)}, u32[]{:S(2)}) collective-permute-start(f32[2,8,128]{2,1,0:T(8,128)S(1)} %get-tuple-element.32.edges_first), channel_id=1, source_target_pairs={{0,7},{2,9},{4,11},{6,13},{8,15},{10,1},{12,3},{14,5},{7,0},{9,2},... | collective-permute-start | bytes 24584 | tf_op jit(solution)/shard_map/ppermute | solution.py:1088
  9.5 2.8 %collective-permute-start.3 = (f32[2,8,128]{2,1,0:T(8,128)S(1)}, f32[2,8,128]{2,1,0:T(8,128)S(1)}, u32[]{:S(2)}, u32[]{:S(2)}) collective-permute-start(f32[2,8,128]{2,1,0:T(8,128)S(1)} %get-tuple-element.32.edges_first), channel_id=1, source_target_pairs={{0,9},{2,11},{4,13},{6,15},{8,1},{10,3},{12,5},{14,7},{9,0},{11,2}... | collective-permute-start | bytes 24584 | tf_op jit(solution)/shard_map/ppermute | solution.py:1088
  12.4 1.5 %shard_map.60 = (f32[2,32,64,128]{3,2,1,0:T(8,128)S(1)}, f32[2,32,64,128]{3,2,1,0:T(8,128)S(1)}, f32[2,32,64,128]{3,2,1,0:T(8,128)S(1)}, f32[4,16,16,128]{3,2,1,...) custom-call(f32[64,8192]{1,0:T(8,128)S(1)} %get-tuple-element.29.right_ref, ...), custom_call_target="tpu_custom_call" | custom-call | tf_op jit(solution)/shard_map/pallas_call | solution.py:1073
  13.8 0.0 collective-permute-done.4.corner_far
  13.8 0.2 collective-permute-done.3.corner_near
  14.0 0.0 collective-permute-done.2.polar_ref
  14.0 0.0 collective-permute-done.from_other
  14.0 0.0 collective-permute-done.1.from_mate
  14.0 3.6 %shard_map.61 = (f32[2,32,80,128]{3,2,1,0:T(8,128)S(1)}, f32[4,17,16,128]{3,2,1,0:T(8,128)S(1)}, f32[4,16,128]{2,1,0:T(8,128)S(1)}, f32[16,128]{1,0:T(8,128)S(1)...) custom-call(f32[2,32,64,128]{3,2,1,0:T(8,128)S(1)} %get-tuple-element.33.s_ref, ...), custom_call_target="tpu_custom_call" | custom-call | tf_op jit(solution)/shard_map/pallas_call | solution.py:1073
  17.7 3.8 %collective-permute-start.5 = (f32[43,8,128]{2,1,0:T(8,128)S(1)}, f32[43,8,128]{2,1,0:T(8,128)S(1)}, u32[]{:S(2)}, u32[]{:S(2)}) collective-permute-start(f32[43,8,128]{2,1,0:T(8,128)S(1)} %get-tuple-element.51), channel_id=1, source_target_pairs={{0,15},{2,1},{4,3},{6,5},{8,7},{10,9},{12,11},{14,13},{15,0},{1,2}... | collective-permute-start | bytes 528392 | tf_op jit(solution)/shard_map/ppermute | solution.py:1088
  21.5 0.0 collective-permute-start.6
  21.5 1.7 %shard_map.62 = (f32[64,8192]{1,0:T(8,128)}, f32[4,17,8,128]{3,2,1,0:T(8,128)S(1)}, f32[4,17,8,128]{3,2,1,0:T(8,128)S(1)}, f32[4,17,8,128]{3,2,1,0:T(8,128)S(1)}, f32[17,16,128]{2,1,0:T(8,128)S(1)}) custom-call(f32[2,32,80,128]{3,2,1,0:T(8,128)S(1)} %get-tuple-element.41.r_ref, f32[4,17,16,128]{3,2,1,0:T(8,128)S(1)} %get-tuple-element.42.s_ref, ...), custom_call_target="tpu_custom_call" | custom-call | tf_op jit(solution)/shard_map/pallas_call | solution.py:1073
  23.2 2.2 %collective-permute-done.5.from_other = f32[43,8,128]{2,1,0:T(8,128)S(1)} collective-permute-done((f32[43,8,128]{2,1,0:T(8,128)S(1)}, f32[43,8,128]{2,1,0:T(8,128)S(1)}, u32[]{:S(2)}, u32[]{:S(2)}) %collective-permute-start.5) | collective-permute-done | bytes 176160 | tf_op jit(solution)/shard_map/ppermute | solution.py:1088
  25.4 0.0 collective-permute-done.6.from_mate
  25.4 2.1 %shard_map.63 = (f32[16,2048]{1,0:T(8,128)}, f32[16,2048]{1,0:T(8,128)}) custom-call(f32[4,17,8,128]{3,2,1,0:T(8,128)S(1)} %get-tuple-element.46.rim_s, f32[4,17,8,128]{3,2,1,0:T(8,128)S(1)} %get-tuple-element.47.rim_d, f32[4,17,8,128]{3,2,1,0:T(8,128)S(1)} %get-tuple-element.48.rim_i, f32[17,16,128]{2,1,0:T(8,128)S(1)} %get-tuple-element.49.inverse2, ...), custom_call_target="tpu_custom_call" | custom-call | tf_op jit(solution)/shard_map/pallas_call | solution.py:1073
Async XLA Ops:
  2.6 11.5 %collective-permute-start = (f32[2,32,8,128]{3,2,1,0:T(8,128)S(1)}, f32[2,32,8,128]{3,2,1,0:T(8,128)S(1)}, u32[]{:S(2)}, u32[]{:S(2)}) collective-permute-start(f32[2,32,8,128]{3,2,1,0:T(8,128)S(1)} %get-tuple-element.39), channel_id=1, source_target_pairs={{0,15},{2,1},{4,3},{6,5},{8,7},{10,9},{12,11},{14,13},{15,0},{1,2}... | collective-permute-start | bytes 786440 | tf_op jit(solution)/shard_map/ppermute | solution.py:1088
  8.1 6.0 %collective-permute-start.1 = (f32[2,32,8,128]{3,2,1,0:T(8,128)S(1)}, f32[2,32,8,128]{3,2,1,0:T(8,128)S(1)}, u32[]{:S(2)}, u32[]{:S(2)}) collective-permute-start(f32[2,32,8,128]{3,2,1,0:T(8,128)S(1)} %get-tuple-element.40), channel_id=1, source_target_pairs={{0,1},{2,3},{4,5},{6,7},{8,9},{10,11},{12,13},{14,15},{1,0},{3,2},... | collective-permute-start | bytes 786440 | tf_op jit(solution)/shard_map/ppermute | solution.py:1088
  8.5 5.5 %collective-permute-start.2 = (f32[2,32,128]{2,1,0:T(8,128)S(1)}, f32[2,32,128]{2,1,0:T(8,128)S(1)}, u32[]{:S(2)}, u32[]{:S(2)}) collective-permute-start(f32[2,32,128]{2,1,0:T(8,128)S(1)} %shard_map.59.polar_first), channel_id=1, source_target_pairs={{0,8},{1,9},{2,10},{3,11},{4,12},{5,13},{6,14},{7,15},{8,0},{9,1},... | collective-permute-start | bytes 98312 | tf_op jit(solution)/shard_map/ppermute | solution.py:1125
  8.7 5.1 %collective-permute-start.4 = (f32[2,8,128]{2,1,0:T(8,128)S(1)}, f32[2,8,128]{2,1,0:T(8,128)S(1)}, u32[]{:S(2)}, u32[]{:S(2)}) collective-permute-start(f32[2,8,128]{2,1,0:T(8,128)S(1)} %get-tuple-element.32.edges_first), channel_id=1, source_target_pairs={{0,7},{2,9},{4,11},{6,13},{8,15},{10,1},{12,3},{14,5},{7,0},{9,2},... | collective-permute-start | bytes 24584 | tf_op jit(solution)/shard_map/ppermute | solution.py:1088
  9.5 4.5 %collective-permute-start.3 = (f32[2,8,128]{2,1,0:T(8,128)S(1)}, f32[2,8,128]{2,1,0:T(8,128)S(1)}, u32[]{:S(2)}, u32[]{:S(2)}) collective-permute-start(f32[2,8,128]{2,1,0:T(8,128)S(1)} %get-tuple-element.32.edges_first), channel_id=1, source_target_pairs={{0,9},{2,11},{4,13},{6,15},{8,1},{10,3},{12,5},{14,7},{9,0},{11,2}... | collective-permute-start | bytes 24584 | tf_op jit(solution)/shard_map/ppermute | solution.py:1088
  17.7 7.7 %collective-permute-start.5 = (f32[43,8,128]{2,1,0:T(8,128)S(1)}, f32[43,8,128]{2,1,0:T(8,128)S(1)}, u32[]{:S(2)}, u32[]{:S(2)}) collective-permute-start(f32[43,8,128]{2,1,0:T(8,128)S(1)} %get-tuple-element.51), channel_id=1, source_target_pairs={{0,15},{2,1},{4,3},{6,5},{8,7},{10,9},{12,11},{14,13},{15,0},{1,2}... | collective-permute-start | bytes 528392 | tf_op jit(solution)/shard_map/ppermute | solution.py:1088
  21.5 3.9 %collective-permute-start.6 = (f32[43,8,128]{2,1,0:T(8,128)S(1)}, f32[43,8,128]{2,1,0:T(8,128)S(1)}, u32[]{:S(2)}, u32[]{:S(2)}) collective-permute-start(f32[43,8,128]{2,1,0:T(8,128)S(1)} %get-tuple-element.52), channel_id=1, source_target_pairs={{0,1},{2,3},{4,5},{6,7},{8,9},{10,11},{12,13},{14,15},{1,0},{3,2},... | collective-permute-start | bytes 528392 | tf_op jit(solution)/shard_map/ppermute | solution.py:1088

commit v23 on v22

--- a/solution.py
+++ b/solution.py
@@ -457,10 +457,10 @@
     ]
 
     def body(t, carry):
-        y_before, z_here = carry
-        vy, vz = v[y][t], v[z][t]
+        y_before, z_here, vz = carry
+        vy, z_next = v[y][t], v[z][t + 1]
         y_here = roll_up(vy)
-        z_after = roll_down(v[z][t + 1])
+        z_after = roll_down(z_next)
         lat_a = vy + jnp.where(lane == 0, y_before, y_here)
         lat_b = vz + jnp.where(lane == LANES - 1, z_after, z_here)
         all_a = load_s(qa, t) + (lat_a + (vz + col_a(vz)))
@@ -471,9 +471,10 @@
             load_d, rest = left
             rest[qa][t] = all_a - load_d(qa, t) * new_a
             rest[qb][t] = all_b - load_d(qb, t) * new_b
-        return y_here, z_after
-
-    loop(tiles, body, (roll_up(v[y][tiles]), roll_down(v[z][0])), unroll)
+        return y_here, z_after, z_next
+
+    first = v[z][0]
+    loop(tiles, body, (roll_up(v[y][tiles]), roll_down(first), first), unroll)
     for q, value in held:
         v[q][tiles] = value
 
@@ -530,9 +531,10 @@
 
     def body(i, carry):
         t = i + 1
-        up, down = carry
-        x = [v[q][t] for q in range(4)]
-        up_here, down_next = roll_up(x[1]), roll_down(v[2][t + 1])
+        up, down, x2 = carry
+        x = [v[0][t], v[1][t], x2, v[3][t]]
+        next2 = v[2][t + 1]
+        up_here, down_next = roll_up(x[1]), roll_down(next2)
         beside0 = (x[1] + jnp.where(lane == 0, up, up_here)) + (x[2] + col_prev(x[2]))
         beside3 = (x[2] + jnp.where(lane == LANES - 1, down_next, down)) + (
             x[1] + col_next(x[1])
@@ -540,10 +542,11 @@
         r0 = load_s(0, t) - (load_d(0, t) * x[0] - beside0)
         r3 = load_s(3, t) - (load_d(3, t) * x[3] - beside3)
         use(t, [r0, rest[1][t], rest[2][t], r3])
-        return up_here, down_next
+        return up_here, down_next, next2
 
     full(0)
-    loop(tiles - 2, body, (roll_up(v[1][0]), roll_down(v[2][1])), unroll)
+    first = v[2][1]
+    loop(tiles - 2, body, (roll_up(v[1][0]), roll_down(first), first), unroll)
     full(tiles - 1)
     full(tiles)
 

time: 27.7 us -> 27.7 us (level)
  no operation moved by 1% of the time
where the time goes in v23:
time: 27.7 us; the launch traced here: 27.5 us
  starting transfers between devices  13.2 us (48%)
  Pallas kernels  11.2 us (40%)
  waiting for transfers between devices  2.45 us (9%)
  between operations  0.68 us (2%)
    ppermute x6, starting transfers between devices, swapped_with(): return lax.ppermute(x, 'lon', pairs + [(b, a) for a, b in pairs])  12.9 us
    pallas_call x6, Pallas kernels, call(): pl.pallas_call(kernel, out_shape=[jax.ShapeDtypeStruct(x, F32) if isinsta...  11.2 us
    ppermute x6, waiting for transfers between devices, swapped_with(): return lax.ppermute(x, 'lon', pairs + [(b, a) for a, b in pairs])  2.44 us
  transfers between devices with their start and end apart: 7, of which 2 were waited for; matrix products, arithmetic and copies ran while one was open for 0% of the time, Pallas kernels for 13%

profile of v23, /device:TPU:0, one launch (start us, length us, event | category | flops | bytes accessed | tf_op | source)
XLA Modules:
  0.0 27.5 jit_solution(3448753677054559836)
XLA Ops:
  0.6 1.9 %shard_map.58 = (f32[64,8192]{1,0:T(8,128)S(1)}, bf16[64,8192]{1,0:T(8,128)(2,1)S(1)}, f32[32,8,128]{2,1,0:T(8,128)S(1)}, f32[2,32,8,128]{3,2,1,0:T(8,128)S(1)},...) custom-call(f32[64,8192]{1,0:T(8,128)} %right_ref.1, bf16[64,8192]{1,0:T(8,128)(2,1)} %weight_ref.1, ...), custom_call_target="tpu_custom_call" | custom-call | tf_op jit(solution)/shard_map/pallas_call | solution.py:1076
  2.6 5.5 %collective-permute-start = (f32[2,32,8,128]{3,2,1,0:T(8,128)S(1)}, f32[2,32,8,128]{3,2,1,0:T(8,128)S(1)}, u32[]{:S(2)}, u32[]{:S(2)}) collective-permute-start(f32[2,32,8,128]{3,2,1,0:T(8,128)S(1)} %get-tuple-element.39), channel_id=1, source_target_pairs={{0,15},{2,1},{4,3},{6,5},{8,7},{10,9},{12,11},{14,13},{15,0},{1,2}... | collective-permute-start | bytes 786440 | tf_op jit(solution)/shard_map/ppermute | solution.py:1091
  8.1 0.0 collective-permute-start.1
  8.1 0.4 %shard_map.59.polar_first = f32[2,32,128]{2,1,0:T(8,128)S(1)} custom-call(f32[64,8192]{1,0:T(8,128)S(1)} %get-tuple-element.29.right_ref, bf16[64,8192]{1,0:T(8,128)(2,1)S(1)} %get-tuple-element.30.weight_ref, f32[32,8,128]{2,1,0:T(8,128)S(1)} %get-tuple-element.31.scale_ref, f32[2,8,128]{2,1,0:T(8,128)S(1)} %get-tuple-element.32.edges_first), custom_call_target="tpu_custom_call" | custom-call | tf_op jit(solution)/shard_map/pallas_call | solution.py:1076
  8.5 0.2 collective-permute-start.2
  8.7 0.8 %collective-permute-start.4 = (f32[2,8,128]{2,1,0:T(8,128)S(1)}, f32[2,8,128]{2,1,0:T(8,128)S(1)}, u32[]{:S(2)}, u32[]{:S(2)}) collective-permute-start(f32[2,8,128]{2,1,0:T(8,128)S(1)} %get-tuple-element.32.edges_first), channel_id=1, source_target_pairs={{0,7},{2,9},{4,11},{6,13},{8,15},{10,1},{12,3},{14,5},{7,0},{9,2},... | collective-permute-start | bytes 24584 | tf_op jit(solution)/shard_map/ppermute | solution.py:1091
  9.5 2.8 %collective-permute-start.3 = (f32[2,8,128]{2,1,0:T(8,128)S(1)}, f32[2,8,128]{2,1,0:T(8,128)S(1)}, u32[]{:S(2)}, u32[]{:S(2)}) collective-permute-start(f32[2,8,128]{2,1,0:T(8,128)S(1)} %get-tuple-element.32.edges_first), channel_id=1, source_target_pairs={{0,9},{2,11},{4,13},{6,15},{8,1},{10,3},{12,5},{14,7},{9,0},{11,2}... | collective-permute-start | bytes 24584 | tf_op jit(solution)/shard_map/ppermute | solution.py:1091
  12.4 1.5 %shard_map.60 = (f32[2,32,64,128]{3,2,1,0:T(8,128)S(1)}, f32[2,32,64,128]{3,2,1,0:T(8,128)S(1)}, f32[2,32,64,128]{3,2,1,0:T(8,128)S(1)}, f32[4,16,16,128]{3,2,1,...) custom-call(f32[64,8192]{1,0:T(8,128)S(1)} %get-tuple-element.29.right_ref, ...), custom_call_target="tpu_custom_call" | custom-call | tf_op jit(solution)/shard_map/pallas_call | solution.py:1076
  13.8 0.0 collective-permute-done.4.corner_far
  13.8 0.2 collective-permute-done.3.corner_near
  14.0 0.0 collective-permute-done.2.polar_ref
  14.0 0.0 collective-permute-done.from_other
  14.0 0.0 collective-permute-done.1.from_mate
  14.0 3.6 %shard_map.61 = (f32[2,32,80,128]{3,2,1,0:T(8,128)S(1)}, f32[4,17,16,128]{3,2,1,0:T(8,128)S(1)}, f32[4,16,128]{2,1,0:T(8,128)S(1)}, f32[16,128]{1,0:T(8,128)S(1)...) custom-call(f32[2,32,64,128]{3,2,1,0:T(8,128)S(1)} %get-tuple-element.33.s_ref, ...), custom_call_target="tpu_custom_call" | custom-call | tf_op jit(solution)/shard_map/pallas_call | solution.py:1076
  17.7 3.8 %collective-permute-start.5 = (f32[43,8,128]{2,1,0:T(8,128)S(1)}, f32[43,8,128]{2,1,0:T(8,128)S(1)}, u32[]{:S(2)}, u32[]{:S(2)}) collective-permute-start(f32[43,8,128]{2,1,0:T(8,128)S(1)} %get-tuple-element.51), channel_id=1, source_target_pairs={{0,15},{2,1},{4,3},{6,5},{8,7},{10,9},{12,11},{14,13},{15,0},{1,2}... | collective-permute-start | bytes 528392 | tf_op jit(solution)/shard_map/ppermute | solution.py:1091
  21.5 0.0 collective-permute-start.6
  21.5 1.7 %shard_map.62 = (f32[64,8192]{1,0:T(8,128)}, f32[4,17,8,128]{3,2,1,0:T(8,128)S(1)}, f32[4,17,8,128]{3,2,1,0:T(8,128)S(1)}, f32[4,17,8,128]{3,2,1,0:T(8,128)S(1)}, f32[17,16,128]{2,1,0:T(8,128)S(1)}) custom-call(f32[2,32,80,128]{3,2,1,0:T(8,128)S(1)} %get-tuple-element.41.r_ref, f32[4,17,16,128]{3,2,1,0:T(8,128)S(1)} %get-tuple-element.42.s_ref, ...), custom_call_target="tpu_custom_call" | custom-call | tf_op jit(solution)/shard_map/pallas_call | solution.py:1076
  23.2 2.2 %collective-permute-done.5.from_other = f32[43,8,128]{2,1,0:T(8,128)S(1)} collective-permute-done((f32[43,8,128]{2,1,0:T(8,128)S(1)}, f32[43,8,128]{2,1,0:T(8,128)S(1)}, u32[]{:S(2)}, u32[]{:S(2)}) %collective-permute-start.5) | collective-permute-done | bytes 176160 | tf_op jit(solution)/shard_map/ppermute | solution.py:1091
  25.4 0.0 collective-permute-done.6.from_mate
  25.4 2.1 %shard_map.63 = (f32[16,2048]{1,0:T(8,128)}, f32[16,2048]{1,0:T(8,128)}) custom-call(f32[4,17,8,128]{3,2,1,0:T(8,128)S(1)} %get-tuple-element.46.rim_s, f32[4,17,8,128]{3,2,1,0:T(8,128)S(1)} %get-tuple-element.47.rim_d, f32[4,17,8,128]{3,2,1,0:T(8,128)S(1)} %get-tuple-element.48.rim_i, f32[17,16,128]{2,1,0:T(8,128)S(1)} %get-tuple-element.49.inverse2, ...), custom_call_target="tpu_custom_call" | custom-call | tf_op jit(solution)/shard_map/pallas_call | solution.py:1076
Async XLA Ops:
  2.6 11.5 %collective-permute-start = (f32[2,32,8,128]{3,2,1,0:T(8,128)S(1)}, f32[2,32,8,128]{3,2,1,0:T(8,128)S(1)}, u32[]{:S(2)}, u32[]{:S(2)}) collective-permute-start(f32[2,32,8,128]{3,2,1,0:T(8,128)S(1)} %get-tuple-element.39), channel_id=1, source_target_pairs={{0,15},{2,1},{4,3},{6,5},{8,7},{10,9},{12,11},{14,13},{15,0},{1,2}... | collective-permute-start | bytes 786440 | tf_op jit(solution)/shard_map/ppermute | solution.py:1091
  8.1 6.0 %collective-permute-start.1 = (f32[2,32,8,128]{3,2,1,0:T(8,128)S(1)}, f32[2,32,8,128]{3,2,1,0:T(8,128)S(1)}, u32[]{:S(2)}, u32[]{:S(2)}) collective-permute-start(f32[2,32,8,128]{3,2,1,0:T(8,128)S(1)} %get-tuple-element.40), channel_id=1, source_target_pairs={{0,1},{2,3},{4,5},{6,7},{8,9},{10,11},{12,13},{14,15},{1,0},{3,2},... | collective-permute-start | bytes 786440 | tf_op jit(solution)/shard_map/ppermute | solution.py:1091
  8.5 5.5 %collective-permute-start.2 = (f32[2,32,128]{2,1,0:T(8,128)S(1)}, f32[2,32,128]{2,1,0:T(8,128)S(1)}, u32[]{:S(2)}, u32[]{:S(2)}) collective-permute-start(f32[2,32,128]{2,1,0:T(8,128)S(1)} %shard_map.59.polar_first), channel_id=1, source_target_pairs={{0,8},{1,9},{2,10},{3,11},{4,12},{5,13},{6,14},{7,15},{8,0},{9,1},... | collective-permute-start | bytes 98312 | tf_op jit(solution)/shard_map/ppermute | solution.py:1128
  8.7 5.1 %collective-permute-start.4 = (f32[2,8,128]{2,1,0:T(8,128)S(1)}, f32[2,8,128]{2,1,0:T(8,128)S(1)}, u32[]{:S(2)}, u32[]{:S(2)}) collective-permute-start(f32[2,8,128]{2,1,0:T(8,128)S(1)} %get-tuple-element.32.edges_first), channel_id=1, source_target_pairs={{0,7},{2,9},{4,11},{6,13},{8,15},{10,1},{12,3},{14,5},{7,0},{9,2},... | collective-permute-start | bytes 24584 | tf_op jit(solution)/shard_map/ppermute | solution.py:1091
  9.5 4.5 %collective-permute-start.3 = (f32[2,8,128]{2,1,0:T(8,128)S(1)}, f32[2,8,128]{2,1,0:T(8,128)S(1)}, u32[]{:S(2)}, u32[]{:S(2)}) collective-permute-start(f32[2,8,128]{2,1,0:T(8,128)S(1)} %get-tuple-element.32.edges_first), channel_id=1, source_target_pairs={{0,9},{2,11},{4,13},{6,15},{8,1},{10,3},{12,5},{14,7},{9,0},{11,2}... | collective-permute-start | bytes 24584 | tf_op jit(solution)/shard_map/ppermute | solution.py:1091
  17.7 7.7 %collective-permute-start.5 = (f32[43,8,128]{2,1,0:T(8,128)S(1)}, f32[43,8,128]{2,1,0:T(8,128)S(1)}, u32[]{:S(2)}, u32[]{:S(2)}) collective-permute-start(f32[43,8,128]{2,1,0:T(8,128)S(1)} %get-tuple-element.51), channel_id=1, source_target_pairs={{0,15},{2,1},{4,3},{6,5},{8,7},{10,9},{12,11},{14,13},{15,0},{1,2}... | collective-permute-start | bytes 528392 | tf_op jit(solution)/shard_map/ppermute | solution.py:1091
  21.5 3.9 %collective-permute-start.6 = (f32[43,8,128]{2,1,0:T(8,128)S(1)}, f32[43,8,128]{2,1,0:T(8,128)S(1)}, u32[]{:S(2)}, u32[]{:S(2)}) collective-permute-start(f32[43,8,128]{2,1,0:T(8,128)S(1)} %get-tuple-element.52), channel_id=1, source_target_pairs={{0,1},{2,3},{4,5},{6,7},{8,9},{10,11},{12,13},{14,15},{1,0},{3,2},... | collective-permute-start | bytes 528392 | tf_op jit(solution)/shard_map/ppermute | solution.py:1091
